TPU v7x, 32 devices: a whole 2x2x4 slice. The times are simulated.
32 devices in a mesh: gx: 4 (over y, core), gy: 4 (over z), gz: 2 (over x).
Axes of the slice: x: 2, y: 2, z: 4, core: 2. Of those that a mesh axis runs over, the one named last changes fastest.
Arguments:
- wavefunctions: float32 [48, 48, 24, 256], P('gx', 'gy', 'gz'), may hold values from -6 to 6
- cell_matrices: bfloat16 [8, 8, 4, 343, 343], P('gx', 'gy', 'gz'), may hold values from -0.078125 to 0.078125
- projectors: float32 [32, 16, 1728], P(('gx', 'gy', 'gz')), may hold values from -0.14433756 to 0.14433756
- slot_atoms: int32 [32, 16], P(('gx', 'gy', 'gz')), may hold values from 0 to 64, as said below
- atom_coupling: float32 [64], replicated, may hold values from 0.5 to 3
Outputs:
- filtered: float32 [48, 48, 24, 256], P('gx', 'gy', 'gz')
Inputs may be any that keep to these rules, and one draw needn't show every extreme that they name: `slot_atoms`: atom a belongs to device a // 2. The live slots of device d name distinct atoms whose owners lie 0 or 1 below d along each of gx, gy, gz (periodically); 64 marks an empty slot, and some device has all 16 slots live.
All inputs are finite; a program needn't handle non-finite values.
Results may differ from a plain program's by a relative error of at most 0.00045.
Values may be sent and summed in bfloat16 or wider, within the bound.
No kernel may reach another device: no remote copies, remote signals or barrier semaphores. Data moves between devices by JAX's collectives and lax.ppermute only.
A program may use at most 64 MiB of HBM per device.

v0:
```python
import jax
import jax.numpy as jnp
from jax import lax
from jax.sharding import PartitionSpec as P


def passed_along(value, axis, by):
    count = lax.axis_size(axis)
    return lax.ppermute(value, axis, [(i, (i + by) % count) for i in range(count)])


def extend(values, axis_pos, neighbour):
    first_plane = lax.slice_in_dim(values, 0, 1, axis=axis_pos + 1)
    cell_count = first_plane.shape[axis_pos]
    head_plane = lax.slice_in_dim(first_plane, 0, 1, axis=axis_pos)
    rest_planes = lax.slice_in_dim(first_plane, 1, cell_count, axis=axis_pos)
    upper_planes = jnp.concatenate([rest_planes, neighbour(head_plane)], axis=axis_pos)
    return jnp.concatenate([values, upper_planes], axis=axis_pos + 1)


def fold(values, axis_pos, neighbour):
    span_nodes = values.shape[axis_pos + 1]
    cell_count = values.shape[axis_pos]
    inner_part = lax.slice_in_dim(values, 0, span_nodes - 1, axis=axis_pos + 1)
    last_plane = lax.slice_in_dim(values, span_nodes - 1, span_nodes, axis=axis_pos + 1)
    tail_plane = lax.slice_in_dim(last_plane, cell_count - 1, cell_count, axis=axis_pos)
    lead_planes = lax.slice_in_dim(last_plane, 0, cell_count - 1, axis=axis_pos)
    incoming = jnp.concatenate([neighbour(tail_plane), lead_planes], axis=axis_pos)
    front_plane = lax.slice_in_dim(inner_part, 0, 1, axis=axis_pos + 1) + incoming
    return jnp.concatenate(
        [front_plane, lax.slice_in_dim(inner_part, 1, span_nodes - 1, axis=axis_pos + 1)],
        axis=axis_pos + 1,
    )


def cell_part(field_now, cell_matrices):
    cells_x, cells_y, cells_z = (
        cell_matrices.shape[0],
        cell_matrices.shape[1],
        cell_matrices.shape[2],
    )
    wave_count = field_now.shape[3]
    node_order = field_now.shape[0] // cells_x
    side_nodes = node_order + 1
    values = field_now.astype(jnp.bfloat16).reshape(
        cells_x, node_order, cells_y, node_order, cells_z, node_order, wave_count
    )
    values = extend(values, 0, lambda plane_part: passed_along(plane_part, "gx", -1))
    values = extend(values, 2, lambda plane_part: passed_along(plane_part, "gy", -1))
    values = extend(values, 4, lambda plane_part: passed_along(plane_part, "gz", -1))
    stacked = values.transpose(0, 2, 4, 1, 3, 5, 6).reshape(
        cells_x, cells_y, cells_z, side_nodes**3, wave_count
    )
    product = jnp.einsum(
        "xyzmn,xyznw->xyzmw", cell_matrices, stacked, preferred_element_type=jnp.float32
    )
    product = product.reshape(
        cells_x, cells_y, cells_z, side_nodes, side_nodes, side_nodes, wave_count
    )
    product = product.transpose(0, 3, 1, 4, 2, 5, 6)
    product = fold(
        product,
        4,
        lambda plane_part: passed_along(plane_part.astype(jnp.bfloat16), "gz", 1).astype(
            plane_part.dtype
        ),
    )
    product = fold(
        product,
        2,
        lambda plane_part: passed_along(plane_part.astype(jnp.bfloat16), "gy", 1).astype(
            plane_part.dtype
        ),
    )
    product = fold(
        product,
        0,
        lambda plane_part: passed_along(plane_part.astype(jnp.bfloat16), "gx", 1).astype(
            plane_part.dtype
        ),
    )
    return product.reshape(field_now.shape)


def nonlocal_part(field_now, projectors, slot_atoms, atom_coupling):
    wave_count = field_now.shape[3]
    flat_field = field_now.reshape(-1, wave_count)
    proj_rows = projectors[0]
    slot_ids = slot_atoms[0]
    highest = lax.Precision.HIGHEST
    contract_first = (((0,), (0,)), ((), ()))
    coefficients = jnp.dot(
        proj_rows, flat_field, precision=highest, preferred_element_type=jnp.float32
    )
    atom_count = atom_coupling.shape[0]
    size_x = lax.axis_size("gx")
    size_y = lax.axis_size("gy")
    size_z = lax.axis_size("gz")
    per_device = atom_count // (size_x * size_y * size_z)
    index_x = lax.axis_index("gx")
    index_y = lax.axis_index("gy")
    index_z = lax.axis_index("gz")
    owner = slot_ids // per_device
    owner_x = owner // (size_y * size_z)
    owner_y = owner // size_z % size_y
    owner_z = owner % size_z
    delta_x = (index_x - owner_x) % size_x
    delta_y = (index_y - owner_y) % size_y
    delta_z = (index_z - owner_z) % size_z
    local_slot = ((delta_x * 2 + delta_y) * 2 + delta_z) * per_device + slot_ids % per_device
    local_slot = jnp.where(slot_ids < atom_count, local_slot, -1)
    columns = lax.iota(jnp.int32, 8 * per_device)
    selector = (local_slot[:, None] == columns[None, :]).astype(jnp.float32)
    partial_sums = lax.dot_general(
        selector,
        coefficients,
        contract_first,
        precision=highest,
        preferred_element_type=jnp.float32,
    )
    grouped = partial_sums.reshape(2, 2, 2, per_device, wave_count)
    device_index = (index_x * size_y + index_y) * size_z + index_z
    own_coupling = lax.dynamic_slice_in_dim(atom_coupling, device_index * per_device, per_device)
    grouped = grouped[0] + passed_along(grouped[1], "gx", -1)
    grouped = grouped[0] + passed_along(grouped[1], "gy", -1)
    own_totals = grouped[0] + passed_along(grouped[1], "gz", -1)
    own_weighted = own_totals * own_coupling[:, None]
    spread = jnp.stack([own_weighted, passed_along(own_weighted, "gz", 1)])
    spread = jnp.stack([spread, passed_along(spread, "gy", 1)])
    spread = jnp.stack([spread, passed_along(spread, "gx", 1)])
    weighted = spread.reshape(8 * per_device, wave_count)
    back = jnp.dot(selector, weighted, precision=highest, preferred_element_type=jnp.float32)
    image = lax.dot_general(
        proj_rows, back, contract_first, precision=highest, preferred_element_type=jnp.float32
    )
    return image.reshape(field_now.shape)


def local(wavefunctions, cell_matrices, projectors, slot_atoms, atom_coupling):

    def apply_operator(field_now):
        return cell_part(field_now, cell_matrices) + nonlocal_part(
            field_now, projectors, slot_atoms, atom_coupling
        )

    previous = wavefunctions
    current = apply_operator(wavefunctions)
    following = 2.0 * apply_operator(current) - previous
    previous, current = (current, following)
    return current


def solution(mesh):
    return jax.shard_map(
        local,
        mesh=mesh,
        in_specs=(
            P("gx", "gy", "gz", None),
            P("gx", "gy", "gz", None, None),
            P(("gx", "gy", "gz"), None, None),
            P(("gx", "gy", "gz"), None),
            P(),
        ),
        out_specs=P("gx", "gy", "gz", None),
        check_vma=False,
    )
```

profile of v0, /device:TPU:0, one launch (start us, length us, event | category | flops | bytes accessed | tf_op | source)
XLA Modules:
  0.0 162.4 jit_solution(3663006300573108786)
XLA Ops:
  0.0 2.8 %reshape.196 = f32[1728,256]{1,0:T(8,128)} reshape(f32[12,12,12,256]{3,2,1,0:T(8,128)} %param.5) | data formatting | bytes 3538944 | tf_op jit(solution)/shard_map/reshape | solution.py:87
  2.8 2.3 %fusion.39 = f32[16,256]{1,0:T(8,128)S(1)} fusion(f32[1728,256]{1,0:T(8,128)} %reshape.196, f32[1,16,1728]{2,1,0:T(8,128)S(1)} %copy-done.6), kind=kOutput, calls=%fused_computation.79 | convolution fusion | flops 84934656 | bytes 1896448 | tf_op jit(solution)/shard_map/dot_general | solution.py:92
  5.5 2.5 %collective-permute-start.6 = (f32[2,2,2,256]{3,2,1,0:T(2,128)S(1)}, f32[2,2,2,256]{3,2,1,0:T(2,128)S(1)}, u32[]{:S(2)}, u32[]{:S(2)}) collective-permute-start(f32[2,2,2,256]{3,2,1,0:T(2,128)S(1)} %squeeze.47), channel_id=1, source_target_pairs={{0,24},{8,0},{16,8},{24,16},{1,25},{9,1},{17,9},{25,17},{2,26},{10... | collective-permute-start | bytes 24584 | tf_op jit(solution)/shard_map/ppermute | solution.py:9
  9.3 3.6 %collective-permute-start.7 = (f32[2,2,256]{2,1,0:T(2,128)S(1)}, f32[2,2,256]{2,1,0:T(2,128)S(1)}, u32[]{:S(2)}, u32[]{:S(2)}) collective-permute-start(f32[2,2,256]{2,1,0:T(2,128)S(1)} %slice_bitcast_fusion.2), channel_id=1, source_target_pairs={{0,6},{2,0},{4,2},{6,4},{1,7},{3,1},{5,3},{7,5},{8,14},{10,8},{12,... | collective-permute-start | bytes 12296 | tf_op jit(solution)/shard_map/ppermute | solution.py:9
  15.8 2.8 %convert_element_type.33 = bf16[12,12,12,256]{3,2,1,0:T(8,128)(2,1)} convert(f32[12,12,12,256]{3,2,1,0:T(8,128)} %param.5) | non-fusion elementwise | flops 442368 | bytes 2654208 | tf_op jit(solution)/shard_map/convert_element_type | solution.py:45
  21.9 2.7 %collective-permute-done.9 = f32[2,256]{1,0:T(2,128)S(1)} collective-permute-done((f32[2,256]{1,0:T(2,128)S(1)}, f32[2,256]{1,0:T(2,128)S(1)}, u32[]{:S(2)}, u32[]{:S(2)}) %collective-permute-start.9) | collective-permute-done | bytes 2080 | tf_op jit(solution)/shard_map/ppermute | solution.py:9
  24.9 3.9 %collective-permute-start.1 = (bf16[2,7,1,1,2,6,256]{6,5,4,3,2,1,0:T(8,128)(2,1)S(1)}, bf16[2,7,1,1,2,6,256]{6,5,4,3,2,1,0:T(8,128)(2,1)S(1)}, u32[]{:S(2)}, u32[]{:S(2)}) collective-permute-start(bf16[2,7,1,1,2,6,256]{6,5,4,3,2,1,0:T(8,128)(2,1)S(1)} %get-tuple-element.8), channel_id=1, source_target_pairs={{0,6},{2,0},{4,2},{6,4},{1,7},{3,1},{5,3},{7,5},{8,14},{10,8},{12,... | collective-permute-start | bytes 258056 | tf_op jit(solution)/shard_map/ppermute | solution.py:9
  33.7 5.4 %collective-permute-done.2 = bf16[2,7,2,7,1,1,256]{6,5,4,3,2,1,0:T(2,128)(2,1)} collective-permute-done((bf16[2,7,2,7,1,1,256]{6,5,4,3,2,1,0:T(2,128)(2,1)}, bf16[2,7,2,7,1,1,256]{6,5,4,3,2,1,0:T(2,128)(2,1)}, u32[]{:S(2)}, u32[]{:S(2)}) %collective-permute-start.2) | collective-permute-done | bytes 100384 | tf_op jit(solution)/shard_map/ppermute | solution.py:9
  39.1 2.3 %fusion.18 = bf16[2,2,2,7,7,7,256]{6,5,2,4,1,3,0:T(8,128)(2,1)S(1)} fusion(bf16[2,7,1,1,2,6,256]{6,5,4,3,2,1,0:T(8,128)(2,1)} %copy-done.9, bf16[2,7,1,1,2,6,256]{6,5,4,3,2,1,0:T(8,128)(2,1)} %copy-done.7, bf16[2,6,2,6,2,6,256]{6,5,4,3,2,1,0:T(8,128)(2,1)S(1)} %reshape.193, bf16[1,1,2,6,2,6,256]{6,5,4,3,2,1,0:T(8,128)(2,1)} %copy-done.8, ...), kind=kLoop, calls=%fused_computation.36 | loop fusion | flops 15454208 | bytes 2709504 | tf_op jit(solution)/shard_map/transpose | solution.py:51
  48.2 3.1 %collective-permute-done.3 = bf16[2,7,2,7,1,1,256]{6,4,5,3,1,2,0:T(2,128)(2,1)S(1)} collective-permute-done((bf16[2,7,2,7,1,1,256]{6,4,5,3,1,2,0:T(2,128)(2,1)S(1)}, bf16[2,7,2,7,1,1,256]{6,4,5,3,1,2,0:T(2,128)(2,1)S(1)}, u32[]{:S(2)}, u32[]{:S(2)}) %collective-permute-start.3) | collective-permute-done | bytes 100384 | tf_op jit(solution)/shard_map/ppermute | solution.py:9
  52.6 6.3 %collective-permute-done.4 = bf16[2,7,1,1,2,6,256]{6,4,5,3,1,2,0:T(2,128)(2,1)S(1)} collective-permute-done((bf16[2,7,1,1,2,6,256]{6,4,5,3,1,2,0:T(2,128)(2,1)S(1)}, bf16[2,7,1,1,2,6,256]{6,4,5,3,1,2,0:T(2,128)(2,1)S(1)}, u32[]{:S(2)}, u32[]{:S(2)}) %collective-permute-start.4) | collective-permute-done | bytes 86048 | tf_op jit(solution)/shard_map/ppermute | solution.py:9
  61.8 2.8 %convolution_bitcast_fusion.1 = f32[1728,256]{1,0:T(8,128)} fusion(f32[16,256]{1,0:T(8,128)S(1)} %fusion.43, f32[1,16,1728]{2,1,0:T(8,128)S(1)} %copy-done.6), kind=kOutput, calls=%fused_computation.7 | convolution fusion | flops 84934656 | bytes 1896448 | tf_op jit(solution)/shard_map/dot_general | solution.py:133
  64.6 2.7 %reshape.198 = f32[2,6,2,6,2,6,256]{6,5,4,3,2,1,0:T(8,128)} reshape(f32[1728,256]{1,0:T(8,128)} %convolution_bitcast_fusion.1) | data formatting | bytes 3538944 | tf_op jit(solution)/shard_map/reshape | solution.py:136
  73.8 2.7 %reshape.202 = f32[1728,256]{1,0:T(8,128)} reshape(f32[2,6,2,6,2,6,256]{6,5,4,3,2,1,0:T(8,128)} %copy.23) | data formatting | bytes 3538944 | tf_op jit(solution)/shard_map/reshape | solution.py:82
  76.4 5.0 %fusion.13 = f32[256,16]{1,0:T(8,128)S(1)} fusion(f32[1728,256]{1,0:T(8,128)} %reshape.202, f32[1728,256]{1,0:T(8,128)} %convolution_bitcast_fusion.1, f32[1,16,1728]{2,1,0:T(8,128)S(1)} %copy-done.6), kind=kOutput, calls=%fused_computation.24 | convolution fusion | flops 85377024 | bytes 3665920 | tf_op jit(solution)/shard_map/dot_general | solution.py:92
  96.4 3.9 %collective-permute-start.13 = (bf16[2,7,1,1,2,6,256]{6,4,5,3,1,2,0:T(2,128)(2,1)S(1)}, bf16[2,7,1,1,2,6,256]{6,4,5,3,1,2,0:T(2,128)(2,1)S(1)}, u32[]{:S(2)}, u32[]{:S(2)}) collective-permute-start(bf16[2,7,1,1,2,6,256]{6,4,5,3,1,2,0:T(2,128)(2,1)S(1)} %get-tuple-element.12), channel_id=1, source_target_pairs={{0,6},{2,0},{4,2},{6,4},{1,7},{3,1},{5,3},{7,5},{8,14},{10,8},{12,... | collective-permute-start | bytes 258056 | tf_op jit(solution)/shard_map/ppermute | solution.py:9
  105.5 6.0 %collective-permute-done.14 = bf16[2,7,2,7,1,1,256]{6,4,5,3,1,2,0:T(2,128)(2,1)} collective-permute-done((bf16[2,7,2,7,1,1,256]{6,4,5,3,1,2,0:T(2,128)(2,1)}, bf16[2,7,2,7,1,1,256]{6,4,5,3,1,2,0:T(2,128)(2,1)}, u32[]{:S(2)}, u32[]{:S(2)}) %collective-permute-start.14) | collective-permute-done | bytes 100384 | tf_op jit(solution)/shard_map/ppermute | solution.py:9
  111.5 12.9 %fusion.23 = bf16[2,7,2,7,2,7,256]{6,4,5,3,1,2,0:T(2,128)(2,1)S(1)} fusion(bf16[2,7,1,1,2,6,256]{6,4,5,3,1,2,0:T(2,128)(2,1)S(1)} %collective-permute-done.13, bf16[2,7,1,1,2,6,256]{6,4,5,3,1,2,0:T(2,128)(2,1)S(1)} %get-tuple-element.11, bf16[1,1,2,6,2,6,256]{6,4,5,3,1,2,0:T(2,128)(2,1)S(1)} %collective-permute-done.12, ...), kind=kLoop, calls=%fused_computation.46 | loop fusion | flops 15454208 | bytes 2709504 | tf_op jit(solution)/shard_map/concatenate | solution.py:18
  129.6 4.5 %collective-permute-done.15 = bf16[2,7,2,7,1,1,256]{6,4,5,3,1,2,0:T(2,128)(2,1)S(1)} collective-permute-done((bf16[2,7,2,7,1,1,256]{6,4,5,3,1,2,0:T(2,128)(2,1)S(1)}, bf16[2,7,2,7,1,1,256]{6,4,5,3,1,2,0:T(2,128)(2,1)S(1)}, u32[]{:S(2)}, u32[]{:S(2)}) %collective-permute-start.15) | collective-permute-done | bytes 100384 | tf_op jit(solution)/shard_map/ppermute | solution.py:9
  135.0 6.2 %collective-permute-done.16 = bf16[2,7,1,1,2,6,256]{6,4,5,3,1,2,0:T(2,128)(2,1)S(1)} collective-permute-done((bf16[2,7,1,1,2,6,256]{6,4,5,3,1,2,0:T(2,128)(2,1)S(1)}, bf16[2,7,1,1,2,6,256]{6,4,5,3,1,2,0:T(2,128)(2,1)S(1)}, u32[]{:S(2)}, u32[]{:S(2)}) %collective-permute-start.16) | collective-permute-done | bytes 86048 | tf_op jit(solution)/shard_map/ppermute | solution.py:9
  143.9 2.8 %convolution_bitcast_fusion = f32[1728,256]{1,0:T(8,128)} fusion(f32[16,256]{1,0:T(8,128)S(1)} %fusion.41, f32[1,16,1728]{2,1,0:T(8,128)S(1)} %copy-done.6), kind=kOutput, calls=%fused_computation.6 | convolution fusion | flops 84934656 | bytes 1896448 | tf_op jit(solution)/shard_map/dot_general | solution.py:133
  146.8 2.8 %reshape.204 = f32[12,12,12,256]{3,2,1,0:T(8,128)} reshape(f32[1728,256]{1,0:T(8,128)} %convolution_bitcast_fusion) | data formatting | bytes 3538944 | tf_op jit(solution)/shard_map/reshape | solution.py:136
  153.6 3.3 %reshape.201 = f32[12,12,12,256]{3,2,1,0:T(8,128)} reshape(f32[2,6,2,6,2,6,256]{6,5,4,3,2,1,0:T(8,128)} %copy.22) | data formatting | bytes 3538944 | tf_op jit(solution)/shard_map/reshape | solution.py:82
  156.9 5.5 %multiply_subtract_fusion = f32[12,12,12,256]{3,2,1,0:T(8,128)} fusion(f32[12,12,12,256]{3,2,1,0:T(8,128)} %param.5, f32[12,12,12,256]{3,2,1,0:T(8,128)} %reshape.201, f32[12,12,12,256]{3,2,1,0:T(8,128)} %reshape.204), kind=kLoop, calls=%fused_computation.8 | loop fusion | flops 1327104 | bytes 7077888 | tf_op jit(solution)/shard_map/sub | solution.py:148
  (139 shorter events, 62.9 us)
Async XLA Ops:
  5.5 3.8 %collective-permute-start.6 = (f32[2,2,2,256]{3,2,1,0:T(2,128)S(1)}, f32[2,2,2,256]{3,2,1,0:T(2,128)S(1)}, u32[]{:S(2)}, u32[]{:S(2)}) collective-permute-start(f32[2,2,2,256]{3,2,1,0:T(2,128)S(1)} %squeeze.47), channel_id=1, source_target_pairs={{0,24},{8,0},{16,8},{24,16},{1,25},{9,1},{17,9},{25,17},{2,26},{10... | collective-permute-start | bytes 24584 | tf_op jit(solution)/shard_map/ppermute | solution.py:9
  9.3 5.0 %collective-permute-start.7 = (f32[2,2,256]{2,1,0:T(2,128)S(1)}, f32[2,2,256]{2,1,0:T(2,128)S(1)}, u32[]{:S(2)}, u32[]{:S(2)}) collective-permute-start(f32[2,2,256]{2,1,0:T(2,128)S(1)} %slice_bitcast_fusion.2), channel_id=1, source_target_pairs={{0,6},{2,0},{4,2},{6,4},{1,7},{3,1},{5,3},{7,5},{8,14},{10,8},{12,... | collective-permute-start | bytes 12296 | tf_op jit(solution)/shard_map/ppermute | solution.py:9
  14.3 6.6 %collective-permute-start.8 = (f32[2,256]{1,0:T(2,128)S(1)}, f32[2,256]{1,0:T(2,128)S(1)}, u32[]{:S(2)}, u32[]{:S(2)}) collective-permute-start(f32[2,256]{1,0:T(2,128)S(1)} %slice_bitcast_fusion.6), channel_id=1, source_target_pairs={{0,1},{1,0},{2,3},{3,2},{4,5},{5,4},{6,7},{7,6},{8,9},{9,8},{10,11... | collective-permute-start | bytes 6152 | tf_op jit(solution)/shard_map/ppermute | solution.py:9
  21.0 3.6 %collective-permute-start.9 = (f32[2,256]{1,0:T(2,128)S(1)}, f32[2,256]{1,0:T(2,128)S(1)}, u32[]{:S(2)}, u32[]{:S(2)}) collective-permute-start(f32[2,256]{1,0:T(2,128)S(1)} %fusion.56), channel_id=1, source_target_pairs={{0,1},{1,0},{2,3},{3,2},{4,5},{5,4},{6,7},{7,6},{8,9},{9,8},{10,11... | collective-permute-start | bytes 6152 | tf_op jit(solution)/shard_map/ppermute | solution.py:9
  21.5 3.3 %collective-permute-start = (bf16[1,1,2,6,2,6,256]{6,5,4,3,2,1,0:T(8,128)(2,1)S(1)}, bf16[1,1,2,6,2,6,256]{6,5,4,3,2,1,0:T(8,128)(2,1)S(1)}, u32[]{:S(2)}, u32[]{:S(2)}) collective-permute-start(bf16[1,1,2,6,2,6,256]{6,5,4,3,2,1,0:T(8,128)(2,1)S(1)} %get-tuple-element.10), channel_id=1, source_target_pairs={{0,24},{8,0},{16,8},{24,16},{1,25},{9,1},{17,9},{25,17},{2,26},{10... | collective-permute-start | bytes 221192 | tf_op jit(solution)/shard_map/ppermute | solution.py:9
  24.6 5.7 %collective-permute-start.10 = (f32[2,2,256]{2,1,0:T(2,128)S(1)}, f32[2,2,256]{2,1,0:T(2,128)S(1)}, u32[]{:S(2)}, u32[]{:S(2)}) collective-permute-start(f32[2,2,256]{2,1,0:T(2,128)S(1)} %get-tuple-element.26), channel_id=1, source_target_pairs={{0,2},{2,4},{4,6},{6,0},{1,3},{3,5},{5,7},{7,1},{8,10},{10,12},{12... | collective-permute-start | bytes 12296 | tf_op jit(solution)/shard_map/ppermute | solution.py:9
  24.9 6.6 %collective-permute-start.1 = (bf16[2,7,1,1,2,6,256]{6,5,4,3,2,1,0:T(8,128)(2,1)S(1)}, bf16[2,7,1,1,2,6,256]{6,5,4,3,2,1,0:T(8,128)(2,1)S(1)}, u32[]{:S(2)}, u32[]{:S(2)}) collective-permute-start(bf16[2,7,1,1,2,6,256]{6,5,4,3,2,1,0:T(8,128)(2,1)S(1)} %get-tuple-element.8), channel_id=1, source_target_pairs={{0,6},{2,0},{4,2},{6,4},{1,7},{3,1},{5,3},{7,5},{8,14},{10,8},{12,... | collective-permute-start | bytes 258056 | tf_op jit(solution)/shard_map/ppermute | solution.py:9
  30.2 3.4 %collective-permute-start.11 = (f32[2,2,2,256]{3,2,1,0:T(2,128)S(1)}, f32[2,2,2,256]{3,2,1,0:T(2,128)S(1)}, u32[]{:S(2)}, u32[]{:S(2)}) collective-permute-start(f32[2,2,2,256]{3,2,1,0:T(2,128)S(1)} %get-tuple-element.22), channel_id=1, source_target_pairs={{0,8},{8,16},{16,24},{24,0},{1,9},{9,17},{17,25},{25,1},{2,10},{10... | collective-permute-start | bytes 24584 | tf_op jit(solution)/shard_map/ppermute | solution.py:9
  32.3 6.8 %collective-permute-start.2 = (bf16[2,7,2,7,1,1,256]{6,5,4,3,2,1,0:T(2,128)(2,1)}, bf16[2,7,2,7,1,1,256]{6,5,4,3,2,1,0:T(2,128)(2,1)}, u32[]{:S(2)}, u32[]{:S(2)}) collective-permute-start(bf16[2,7,2,7,1,1,256]{6,5,4,3,2,1,0:T(2,128)(2,1)} %fusion.29), channel_id=1, source_target_pairs={{0,1},{1,0},{2,3},{3,2},{4,5},{5,4},{6,7},{7,6},{8,9},{9,8},{10,11... | collective-permute-start | bytes 301064 | tf_op jit(solution)/shard_map/ppermute | solution.py:9
  45.5 5.8 %collective-permute-start.3 = (bf16[2,7,2,7,1,1,256]{6,4,5,3,1,2,0:T(2,128)(2,1)S(1)}, bf16[2,7,2,7,1,1,256]{6,4,5,3,1,2,0:T(2,128)(2,1)S(1)}, u32[]{:S(2)}, u32[]{:S(2)}) collective-permute-start(bf16[2,7,2,7,1,1,256]{6,4,5,3,1,2,0:T(2,128)(2,1)S(1)} %slice.381), channel_id=1, source_target_pairs={{0,1},{1,0},{2,3},{3,2},{4,5},{5,4},{6,7},{7,6},{8,9},{9,8},{10,11... | collective-permute-start | bytes 301064 | tf_op jit(solution)/shard_map/ppermute | solution.py:9
  52.1 6.8 %collective-permute-start.4 = (bf16[2,7,1,1,2,6,256]{6,4,5,3,1,2,0:T(2,128)(2,1)S(1)}, bf16[2,7,1,1,2,6,256]{6,4,5,3,1,2,0:T(2,128)(2,1)S(1)}, u32[]{:S(2)}, u32[]{:S(2)}) collective-permute-start(bf16[2,7,1,1,2,6,256]{6,4,5,3,1,2,0:T(2,128)(2,1)S(1)} %fusion.34), channel_id=1, source_target_pairs={{0,2},{2,4},{4,6},{6,0},{1,3},{3,5},{5,7},{7,1},{8,10},{10,12},{12... | collective-permute-start | bytes 258056 | tf_op jit(solution)/shard_map/ppermute | solution.py:9
  61.6 6.7 %collective-permute-start.5 = (bf16[1,1,2,6,2,6,256]{6,4,5,3,1,2,0:T(2,128)(2,1)S(1)}, bf16[1,1,2,6,2,6,256]{6,4,5,3,1,2,0:T(2,128)(2,1)S(1)}, u32[]{:S(2)}, u32[]{:S(2)}) collective-permute-start(bf16[1,1,2,6,2,6,256]{6,4,5,3,1,2,0:T(2,128)(2,1)S(1)} %slice.383), channel_id=1, source_target_pairs={{0,8},{8,16},{16,24},{24,0},{1,9},{9,17},{17,25},{25,1},{2,10},{10... | collective-permute-start | bytes 221192 | tf_op jit(solution)/shard_map/ppermute | solution.py:9
  81.8 3.2 %collective-permute-start.18 = (f32[2,2,2,256]{3,2,1,0:T(2,128)S(1)}, f32[2,2,2,256]{3,2,1,0:T(2,128)S(1)}, u32[]{:S(2)}, u32[]{:S(2)}) collective-permute-start(f32[2,2,2,256]{3,2,1,0:T(2,128)S(1)} %squeeze.53), channel_id=1, source_target_pairs={{0,24},{8,0},{16,8},{24,16},{1,25},{9,1},{17,9},{25,17},{2,26},{10... | collective-permute-start | bytes 24584 | tf_op jit(solution)/shard_map/ppermute | solution.py:9
  84.9 3.7 %collective-permute-start.19 = (f32[2,2,256]{2,1,0:T(2,128)S(1)}, f32[2,2,256]{2,1,0:T(2,128)S(1)}, u32[]{:S(2)}, u32[]{:S(2)}) collective-permute-start(f32[2,2,256]{2,1,0:T(2,128)S(1)} %slice_bitcast_fusion), channel_id=1, source_target_pairs={{0,6},{2,0},{4,2},{6,4},{1,7},{3,1},{5,3},{7,5},{8,14},{10,8},{12,... | collective-permute-start | bytes 12296 | tf_op jit(solution)/shard_map/ppermute | solution.py:9
  88.6 3.6 %collective-permute-start.20 = (f32[2,256]{1,0:T(2,128)S(1)}, f32[2,256]{1,0:T(2,128)S(1)}, u32[]{:S(2)}, u32[]{:S(2)}) collective-permute-start(f32[2,256]{1,0:T(2,128)S(1)} %slice_bitcast_fusion.4), channel_id=1, source_target_pairs={{0,1},{1,0},{2,3},{3,2},{4,5},{5,4},{6,7},{7,6},{8,9},{9,8},{10,11... | collective-permute-start | bytes 6152 | tf_op jit(solution)/shard_map/ppermute | solution.py:9
  92.3 3.6 %collective-permute-start.21 = (f32[2,256]{1,0:T(2,128)S(1)}, f32[2,256]{1,0:T(2,128)S(1)}, u32[]{:S(2)}, u32[]{:S(2)}) collective-permute-start(f32[2,256]{1,0:T(2,128)S(1)} %fusion.54), channel_id=1, source_target_pairs={{0,1},{1,0},{2,3},{3,2},{4,5},{5,4},{6,7},{7,6},{8,9},{9,8},{10,11... | collective-permute-start | bytes 6152 | tf_op jit(solution)/shard_map/ppermute | solution.py:9
  94.1 2.0 %collective-permute-start.12 = (bf16[1,1,2,6,2,6,256]{6,4,5,3,1,2,0:T(2,128)(2,1)S(1)}, bf16[1,1,2,6,2,6,256]{6,4,5,3,1,2,0:T(2,128)(2,1)S(1)}, u32[]{:S(2)}, u32[]{:S(2)}) collective-permute-start(bf16[1,1,2,6,2,6,256]{6,4,5,3,1,2,0:T(2,128)(2,1)S(1)} %get-tuple-element.14), channel_id=1, source_target_pairs={{0,24},{8,0},{16,8},{24,16},{1,25},{9,1},{17,9},{25,17},{2,26},{10... | collective-permute-start | bytes 221192 | tf_op jit(solution)/shard_map/ppermute | solution.py:9
  95.9 5.5 %collective-permute-start.22 = (f32[2,2,256]{2,1,0:T(2,128)S(1)}, f32[2,2,256]{2,1,0:T(2,128)S(1)}, u32[]{:S(2)}, u32[]{:S(2)}) collective-permute-start(f32[2,2,256]{2,1,0:T(2,128)S(1)} %get-tuple-element.24), channel_id=1, source_target_pairs={{0,2},{2,4},{4,6},{6,0},{1,3},{3,5},{5,7},{7,1},{8,10},{10,12},{12... | collective-permute-start | bytes 12296 | tf_op jit(solution)/shard_map/ppermute | solution.py:9
  96.4 6.2 %collective-permute-start.13 = (bf16[2,7,1,1,2,6,256]{6,4,5,3,1,2,0:T(2,128)(2,1)S(1)}, bf16[2,7,1,1,2,6,256]{6,4,5,3,1,2,0:T(2,128)(2,1)S(1)}, u32[]{:S(2)}, u32[]{:S(2)}) collective-permute-start(bf16[2,7,1,1,2,6,256]{6,4,5,3,1,2,0:T(2,128)(2,1)S(1)} %get-tuple-element.12), channel_id=1, source_target_pairs={{0,6},{2,0},{4,2},{6,4},{1,7},{3,1},{5,3},{7,5},{8,14},{10,8},{12,... | collective-permute-start | bytes 258056 | tf_op jit(solution)/shard_map/ppermute | solution.py:9
  101.4 4.1 %collective-permute-start.23 = (f32[2,2,2,256]{3,2,1,0:T(2,128)S(1)}, f32[2,2,2,256]{3,2,1,0:T(2,128)S(1)}, u32[]{:S(2)}, u32[]{:S(2)}) collective-permute-start(f32[2,2,2,256]{3,2,1,0:T(2,128)S(1)} %get-tuple-element.20), channel_id=1, source_target_pairs={{0,8},{8,16},{16,24},{24,0},{1,9},{9,17},{17,25},{25,1},{2,10},{10... | collective-permute-start | bytes 24584 | tf_op jit(solution)/shard_map/ppermute | solution.py:9
  103.5 8.0 %collective-permute-start.14 = (bf16[2,7,2,7,1,1,256]{6,4,5,3,1,2,0:T(2,128)(2,1)}, bf16[2,7,2,7,1,1,256]{6,4,5,3,1,2,0:T(2,128)(2,1)}, u32[]{:S(2)}, u32[]{:S(2)}) collective-permute-start(bf16[2,7,2,7,1,1,256]{6,4,5,3,1,2,0:T(2,128)(2,1)} %fusion.28), channel_id=1, source_target_pairs={{0,1},{1,0},{2,3},{3,2},{4,5},{5,4},{6,7},{7,6},{8,9},{9,8},{10,11... | collective-permute-start | bytes 301064 | tf_op jit(solution)/shard_map/ppermute | solution.py:9
  127.0 7.1 %collective-permute-start.15 = (bf16[2,7,2,7,1,1,256]{6,4,5,3,1,2,0:T(2,128)(2,1)S(1)}, bf16[2,7,2,7,1,1,256]{6,4,5,3,1,2,0:T(2,128)(2,1)S(1)}, u32[]{:S(2)}, u32[]{:S(2)}) collective-permute-start(bf16[2,7,2,7,1,1,256]{6,4,5,3,1,2,0:T(2,128)(2,1)S(1)} %slice.380), channel_id=1, source_target_pairs={{0,1},{1,0},{2,3},{3,2},{4,5},{5,4},{6,7},{7,6},{8,9},{9,8},{10,11... | collective-permute-start | bytes 301064 | tf_op jit(solution)/shard_map/ppermute | solution.py:9
  134.9 6.3 %collective-permute-start.16 = (bf16[2,7,1,1,2,6,256]{6,4,5,3,1,2,0:T(2,128)(2,1)S(1)}, bf16[2,7,1,1,2,6,256]{6,4,5,3,1,2,0:T(2,128)(2,1)S(1)}, u32[]{:S(2)}, u32[]{:S(2)}) collective-permute-start(bf16[2,7,1,1,2,6,256]{6,4,5,3,1,2,0:T(2,128)(2,1)S(1)} %fusion.35), channel_id=1, source_target_pairs={{0,2},{2,4},{4,6},{6,0},{1,3},{3,5},{5,7},{7,1},{8,10},{10,12},{12... | collective-permute-start | bytes 258056 | tf_op jit(solution)/shard_map/ppermute | solution.py:9
  143.9 5.8 %collective-permute-start.17 = (bf16[1,1,2,6,2,6,256]{6,4,5,3,1,2,0:T(2,128)(2,1)S(1)}, bf16[1,1,2,6,2,6,256]{6,4,5,3,1,2,0:T(2,128)(2,1)S(1)}, u32[]{:S(2)}, u32[]{:S(2)}) collective-permute-start(bf16[1,1,2,6,2,6,256]{6,4,5,3,1,2,0:T(2,128)(2,1)S(1)} %slice.382), channel_id=1, source_target_pairs={{0,8},{8,16},{16,24},{24,0},{1,9},{9,17},{17,25},{25,1},{2,10},{10... | collective-permute-start | bytes 221192 | tf_op jit(solution)/shard_map/ppermute | solution.py:9
  (14 other events, 85.5 us)
where the time goes:
time: 163 us; the launch traced here: 162 us
  waiting for transfers between devices  48.1 us (30%)
  other arithmetic  34 us (21%)
  local copies, waits for them, and re-layouts  32.4 us (20%)
  starting transfers between devices  31.8 us (20%)
  matrix products  15.6 us (10%)
    ppermute x24, waiting for transfers between devices, passed_along(): lax.ppermute(value, axis, [(i, (i + by) % count) for i in range(count)])  48.1 us
    ppermute x24, starting transfers between devices, passed_along(): lax.ppermute(value, axis, [(i, (i + by) % count) for i in range(count)])  31.8 us
    concatenate x3, other arithmetic, extend(): return jnp.concatenate([values, upper_planes], axis=axis_pos + 1)  14.6 us
    dot_general x2, matrix products, nonlocal_part(): jnp.dot(proj_rows, flat_field, precision=highest, preferred_element_type=...  7.36 us
    reshape x2, local copies, waits for them, and re-layouts, cell_part(): return product.reshape(field_now.shape)  5.95 us
    dot_general x2, matrix products, nonlocal_part(): lax.dot_general(proj_rows, back, contract_first, precision=highest, prefe...  5.63 us
    reshape x2, local copies, waits for them, and re-layouts, nonlocal_part(): return image.reshape(field_now.shape)  5.55 us
    sub x1, other arithmetic, local(): following = 2.0 * apply_operator(current) - previous  5.52 us
  transfers between devices with their start and end apart: 24, of which 18 were waited for; matrix products, arithmetic and copies ran while one was open for 13% of the time, Pallas kernels for 0%

commit v1 on v0

v1 whole, which is shorter than its diff:
```python
import functools

import jax
import jax.numpy as jnp
from jax import lax
from jax.experimental import pallas as pl
from jax.experimental.pallas import tpu as pltpu
from jax.sharding import PartitionSpec as P

AXES = ("gx", "gy", "gz")
F32 = jnp.float32
BF16 = jnp.bfloat16
LIMIT = 32 * 1024 * 1024


def up_to(value, unit):
    return -(-value // unit) * unit


def shifted(value, shift):
    sizes = [lax.axis_size(axis) for axis in AXES]
    pairs = []
    for x in range(sizes[0]):
        for y in range(sizes[1]):
            for z in range(sizes[2]):
                here = (x * sizes[1] + y) * sizes[2] + z
                there = [(p + s) % n for p, s, n in zip((x, y, z), shift, sizes)]
                pairs.append((here, (there[0] * sizes[1] + there[1]) * sizes[2] + there[2]))
    return lax.ppermute(value, AXES, pairs)


def halves(value):
    high = value.astype(BF16).astype(F32)
    return high, value - high


def put_split(rows_ref, start, value):
    count = value.shape[0]
    high, low = halves(value)
    rows_ref[start : start + count] = high
    rows_ref[start + count : start + 2 * count] = low


def get_split(rows_ref, start, count):
    return rows_ref[start : start + count] + rows_ref[start + count : start + 2 * count]


class Sizes:
    def __init__(self, field_shape, cell_shape, locals_count):
        self.bx, self.by, self.bz, self.waves = field_shape
        self.cells = cell_shape[:3]
        self.order = self.bx // cell_shape[0]
        self.side = self.order + 1
        self.group = up_to(self.side, 8)
        self.padded = up_to(self.side * self.side * self.group, 16)
        self.bzp = up_to(self.bz, 16)
        self.locals = locals_count
        self.half = locals_count // 2
        self.quarter = locals_count // 4
        self.own = locals_count // 8
        self.x_rows = self.by * self.bz
        self.y_rows = (self.bx + 1) * self.bz
        self.z_rows = (self.bx + 1) * self.by
        self.yz_rows = self.bx + 1
        self.x_msg = up_to(self.x_rows + 2 * self.half, 16)
        self.y_msg = up_to(self.y_rows + 2 * self.own, 16)
        self.z_msg = up_to(self.z_rows + 2 * self.own, 16)
        self.yz_msg = up_to(self.yz_rows + 2 * self.own, 16)
        self.nodes_padded = self.bx * self.by * self.bzp

    def rows(self, count, dtype=F32):
        return jax.ShapeDtypeStruct((count, self.waves), dtype)

    def scratch(self, *shape):
        return pltpu.VMEM(shape + (self.waves,), F32)


def call(body, sizes, outs, scratch, args):
    return pl.pallas_call(
        functools.partial(body, sizes),
        out_shape=outs,
        in_specs=[pl.BlockSpec(memory_space=pltpu.VMEM) for _ in args],
        out_specs=[pl.BlockSpec(memory_space=pltpu.VMEM) for _ in outs],
        scratch_shapes=scratch,
        compiler_params=pltpu.CompilerParams(vmem_limit_bytes=LIMIT),
    )(*args)


def projector_body(s, rows_ref, by_node_ref, by_atom_ref, tall_ref, wide_ref):
    rows = rows_ref[...]
    high, low = halves(rows)
    low = low.astype(BF16).astype(F32)
    tall_ref[...] = jnp.concatenate([high, low, high], axis=0).T
    wide_ref[...] = jnp.zeros(wide_ref.shape, F32)
    for g in range(s.bx * s.by):
        wide_ref[g, 0 : s.bz, :] = tall_ref[g * s.bz : (g + 1) * s.bz, :]
    wide = wide_ref[...].reshape(s.nodes_padded, 3 * s.locals)
    by_node_ref[...] = wide.astype(BF16)
    by_atom_ref[...] = wide.T[0 : 2 * s.locals].astype(BF16)


def coefficients(s, by_atom_ref, wide_ref):
    field = wide_ref[...].reshape(s.nodes_padded, s.waves)
    high = field.astype(BF16)
    low = (field - high.astype(F32)).astype(BF16)
    with_high = jnp.dot(by_atom_ref[...], high, preferred_element_type=F32)
    with_low = jnp.dot(by_atom_ref[0 : s.locals], low, preferred_element_type=F32)
    return with_high[0 : s.locals] + with_high[s.locals : 2 * s.locals] + with_low


def send_down_x(s, by_atom_ref, wide_ref, rows_ref, msg_ref, kept_ref):
    total = coefficients(s, by_atom_ref, wide_ref)
    kept_ref[...] = total[0 : s.half]
    rows_ref[...] = jnp.zeros(rows_ref.shape, F32)
    for y in range(s.by):
        rows_ref[y * s.bz : (y + 1) * s.bz] = wide_ref[0, y, 0 : s.bz]
    put_split(rows_ref, s.x_rows, total[s.half : 2 * s.half])
    msg_ref[...] = rows_ref[...].astype(BF16)


def first_body(s, field_ref, by_atom_ref, msg_ref, kept_ref, wide_ref, rows_ref):
    wide_ref[:, :, 0 : s.bz, :] = field_ref[...]
    wide_ref[:, :, s.bz : s.bzp, :] = jnp.zeros((s.bx, s.by, s.bzp - s.bz, s.waves), F32)
    send_down_x(s, by_atom_ref, wide_ref, rows_ref, msg_ref, kept_ref)


def down_body(s, field_ref, from_x_ref, kept_ref, y_msg_ref, z_msg_ref, yz_msg_ref, part_ref, x_ref, y_ref, z_ref, yz_ref):
    x_ref[...] = from_x_ref[...].astype(F32)
    total = kept_ref[...] + get_split(x_ref, s.x_rows, s.half)
    y_ref[...] = jnp.zeros(y_ref.shape, F32)
    z_ref[...] = jnp.zeros(z_ref.shape, F32)
    yz_ref[...] = jnp.zeros(yz_ref.shape, F32)
    for x in range(s.bx):
        y_ref[x * s.bz : (x + 1) * s.bz] = field_ref[x, 0]
        z_ref[x * s.by : (x + 1) * s.by] = field_ref[x, :, 0, :]
        yz_ref[x : x + 1] = field_ref[x, 0, 0:1, :]
    y_ref[s.bx * s.bz : s.y_rows] = x_ref[0 : s.bz]
    for y in range(s.by):
        z_ref[s.bx * s.by + y : s.bx * s.by + y + 1] = x_ref[y * s.bz : y * s.bz + 1]
    yz_ref[s.bx : s.bx + 1] = x_ref[0:1]
    own = s.own
    part_ref[...] = total[0:own]
    put_split(z_ref, s.z_rows, total[own : 2 * own])
    put_split(y_ref, s.y_rows, total[2 * own : 3 * own])
    put_split(yz_ref, s.yz_rows, total[3 * own : 4 * own])
    y_msg_ref[...] = y_ref[...].astype(BF16)
    z_msg_ref[...] = z_ref[...].astype(BF16)
    yz_msg_ref[...] = yz_ref[...].astype(BF16)


def cell_body(
    s, field_ref, matrix_ref, from_x_ref, from_y_ref, from_z_ref, from_yz_ref, part_ref, weight_ref,
    block_ref, y_msg_ref, z_msg_ref, yz_msg_ref, own_ref,
    values_ref, sums_ref, x_ref, y_ref, z_ref, yz_ref,
):
    order, side, group = s.order, s.side, s.group
    cells_x, cells_y, cells_z = s.cells
    x_ref[...] = from_x_ref[...].astype(F32)
    y_ref[...] = from_y_ref[...].astype(F32)
    z_ref[...] = from_z_ref[...].astype(F32)
    yz_ref[...] = from_yz_ref[...].astype(F32)
    for k in range(cells_z):
        first = k * order
        count = min(group, s.bz - first)
        values_ref[k, 0 : s.bx, 0 : s.by, 0:count, :] = field_ref[:, :, first : first + count, :]
        for y in range(s.by):
            values_ref[k, s.bx, y, 0:count, :] = x_ref[y * s.bz + first : y * s.bz + first + count]
        for x in range(s.bx + 1):
            values_ref[k, x, s.by, 0:count, :] = y_ref[x * s.bz + first : x * s.bz + first + count]
        if count < group:
            values_ref[k, :, :, count:group, :] = jnp.zeros((s.bx + 1, s.by + 1, group - count, s.waves), F32)
    k = cells_z - 1
    for x in range(s.bx + 1):
        values_ref[k, x, 0 : s.by, order, :] = z_ref[x * s.by : (x + 1) * s.by]
        values_ref[k, x, s.by, order : order + 1, :] = yz_ref[x : x + 1]
    sums_ref[...] = jnp.zeros(sums_ref.shape, F32)
    used = side * side * group
    for i in range(cells_x):
        for j in range(cells_y):
            for k in range(cells_z):
                span_x = slice(i * order, i * order + side)
                span_y = slice(j * order, j * order + side)
                values = values_ref[k, span_x, span_y].reshape(used, s.waves)
                if s.padded > used:
                    values = jnp.concatenate([values, jnp.zeros((s.padded - used, s.waves), F32)], axis=0)
                product = jnp.dot(matrix_ref[i, j, k], values.astype(BF16), preferred_element_type=F32)
                sums_ref[k, span_x, span_y] += product[0:used].reshape(side, side, group, s.waves)
    own = s.own
    total = part_ref[...] + get_split(z_ref, s.z_rows, own) + get_split(y_ref, s.y_rows, own) + get_split(yz_ref, s.yz_rows, own)
    total = total * weight_ref[...]
    own_ref[...] = total
    for k in range(cells_z):
        first = k * order
        block_ref[:, :, first : first + order, :] = sums_ref[k, :, 0 : s.by, 0:order, :]
        if k:
            block_ref[:, :, first : first + 1, :] += sums_ref[k - 1, :, 0 : s.by, order : order + 1, :]
    y_ref[...] = jnp.zeros(y_ref.shape, F32)
    z_ref[...] = jnp.zeros(z_ref.shape, F32)
    yz_ref[...] = jnp.zeros(yz_ref.shape, F32)
    last = cells_z - 1
    for x in range(s.bx + 1):
        for k in range(cells_z):
            at = x * s.bz + k * order
            y_ref[at : at + order] = sums_ref[k, x, s.by, 0:order, :]
            if k:
                y_ref[at : at + 1] += sums_ref[k - 1, x, s.by, order : order + 1, :]
        z_ref[x * s.by : (x + 1) * s.by] = sums_ref[last, x, 0 : s.by, order, :]
        yz_ref[x : x + 1] = sums_ref[last, x, s.by, order : order + 1, :]
    put_split(y_ref, s.y_rows, total)
    put_split(z_ref, s.z_rows, total)
    put_split(yz_ref, s.yz_rows, total)
    y_msg_ref[...] = y_ref[...].astype(BF16)
    z_msg_ref[...] = z_ref[...].astype(BF16)
    yz_msg_ref[...] = yz_ref[...].astype(BF16)


def up_body(s, block_ref, from_y_ref, from_z_ref, from_yz_ref, own_ref, x_msg_ref, spread_ref, x_ref, y_ref, z_ref, yz_ref):
    y_ref[...] = from_y_ref[...].astype(F32)
    z_ref[...] = from_z_ref[...].astype(F32)
    yz_ref[...] = from_yz_ref[...].astype(F32)
    x_ref[...] = jnp.zeros(x_ref.shape, F32)
    for y in range(s.by):
        x_ref[y * s.bz : (y + 1) * s.bz] = block_ref[s.bx, y]
    x_ref[0 : s.bz] += y_ref[s.bx * s.bz : s.y_rows]
    for y in range(s.by):
        x_ref[y * s.bz : y * s.bz + 1] += z_ref[s.bx * s.by + y : s.bx * s.by + y + 1]
    x_ref[0:1] += yz_ref[s.bx : s.bx + 1]
    own = s.own
    spread = jnp.concatenate(
        [own_ref[...], get_split(z_ref, s.z_rows, own), get_split(y_ref, s.y_rows, own), get_split(yz_ref, s.yz_rows, own)], axis=0
    )
    spread_ref[...] = spread
    put_split(x_ref, s.x_rows, spread)
    x_msg_ref[...] = x_ref[...].astype(BF16)


def assemble(s, block_ref, from_x_ref, from_y_ref, from_z_ref, from_yz_ref, spread_ref, by_node_ref, wide_ref, x_ref, y_ref, z_ref, yz_ref):
    x_ref[...] = from_x_ref[...].astype(F32)
    y_ref[...] = from_y_ref[...].astype(F32)
    z_ref[...] = from_z_ref[...].astype(F32)
    yz_ref[...] = from_yz_ref[...].astype(F32)
    totals = jnp.concatenate([spread_ref[...], get_split(x_ref, s.x_rows, s.half)], axis=0)
    high, low = halves(totals)
    stacked = jnp.concatenate([high, high, low], axis=0).astype(BF16)
    image = jnp.dot(by_node_ref[...], stacked, preferred_element_type=F32)
    wide_ref[...] = image.reshape(s.bx, s.by, s.bzp, s.waves)
    wide_ref[:, :, 0 : s.bz, :] += block_ref[0 : s.bx]
    for y in range(s.by):
        wide_ref[0, y, 0 : s.bz, :] += x_ref[y * s.bz : (y + 1) * s.bz]
    for x in range(s.bx):
        wide_ref[x, 0, 0 : s.bz, :] += y_ref[x * s.bz : (x + 1) * s.bz]
        wide_ref[x, :, 0, :] += z_ref[x * s.by : (x + 1) * s.by]
        wide_ref[x, 0, 0:1, :] += yz_ref[x : x + 1]


def middle_body(
    s, block_ref, from_x_ref, from_y_ref, from_z_ref, from_yz_ref, spread_ref, by_node_ref, by_atom_ref,
    field_ref, msg_ref, kept_ref, wide_ref, x_ref, y_ref, z_ref, yz_ref,
):
    assemble(s, block_ref, from_x_ref, from_y_ref, from_z_ref, from_yz_ref, spread_ref, by_node_ref, wide_ref, x_ref, y_ref, z_ref, yz_ref)
    field_ref[...] = wide_ref[:, :, 0 : s.bz, :]
    send_down_x(s, by_atom_ref, wide_ref, x_ref, msg_ref, kept_ref)


def last_body(
    s, start_ref, block_ref, from_x_ref, from_y_ref, from_z_ref, from_yz_ref, spread_ref, by_node_ref,
    out_ref, wide_ref, x_ref, y_ref, z_ref, yz_ref,
):
    assemble(s, block_ref, from_x_ref, from_y_ref, from_z_ref, from_yz_ref, spread_ref, by_node_ref, wide_ref, x_ref, y_ref, z_ref, yz_ref)
    out_ref[...] = 2.0 * wide_ref[:, :, 0 : s.bz, :] - start_ref[...]


def atom_rows(proj_rows, slot_ids, atom_count):
    size_x, size_y, size_z = (lax.axis_size(axis) for axis in AXES)
    index_x, index_y, index_z = (lax.axis_index(axis) for axis in AXES)
    per_device = atom_count // (size_x * size_y * size_z)
    owner = slot_ids // per_device
    delta_x = (index_x - owner // (size_y * size_z)) % size_x
    delta_y = (index_y - owner // size_z % size_y) % size_y
    delta_z = (index_z - owner % size_z) % size_z
    local_slot = ((delta_x * 2 + delta_y) * 2 + delta_z) * per_device + slot_ids % per_device
    local_slot = jnp.where(slot_ids < atom_count, local_slot, -1)
    columns = lax.iota(jnp.int32, 8 * per_device)
    selector = (columns[:, None] == local_slot[None, :]).astype(F32)
    return jnp.dot(selector, proj_rows, precision=lax.Precision.HIGHEST, preferred_element_type=F32)


def regrouped(s, cell_matrices):
    row = lax.iota(jnp.int32, s.padded)
    node = jnp.where(row % s.group < s.side, row // s.group * s.side + row % s.group, -1)
    spread = (node[:, None] == lax.iota(jnp.int32, cell_matrices.shape[3])[None, :]).astype(BF16)
    wide = jnp.einsum("xyzmn,cn->xyzmc", cell_matrices, spread, preferred_element_type=BF16)
    return jnp.einsum("rm,xyzmc->xyzrc", spread, wide, preferred_element_type=BF16)


def local(wavefunctions, cell_matrices, projectors, slot_atoms, atom_coupling):
    atom_count = atom_coupling.shape[0]
    devices = 1
    for axis in AXES:
        devices *= lax.axis_size(axis)
    per_device = atom_count // devices
    s = Sizes(wavefunctions.shape, cell_matrices.shape, 8 * per_device)
    index = (lax.axis_index("gx") * lax.axis_size("gy") + lax.axis_index("gy")) * lax.axis_size("gz") + lax.axis_index("gz")
    weight = lax.dynamic_slice_in_dim(atom_coupling, index * per_device, per_device)
    weight = jnp.broadcast_to(weight[:, None], (per_device, s.waves))
    rows = atom_rows(projectors[0], slot_atoms[0], atom_count)
    by_node, by_atom = call(
        projector_body,
        s,
        [jax.ShapeDtypeStruct((s.nodes_padded, 3 * s.locals), BF16), jax.ShapeDtypeStruct((2 * s.locals, s.nodes_padded), BF16)],
        [pltpu.VMEM((s.bx * s.by * s.bz, 3 * s.locals), F32), pltpu.VMEM((s.bx * s.by, s.bzp, 3 * s.locals), F32)],
        [rows],
    )
    matrices = regrouped(s, cell_matrices)
    wide = s.scratch(s.bx, s.by, s.bzp)
    x_rows, y_rows, z_rows, yz_rows = (s.scratch(n) for n in (s.x_msg, s.y_msg, s.z_msg, s.yz_msg))
    side_msgs = [s.rows(s.y_msg, BF16), s.rows(s.z_msg, BF16), s.rows(s.yz_msg, BF16)]
    sum_shape = (s.cells[2], s.bx + 1, s.by + 1, s.group)
    down_x, kept = call(first_body, s, [s.rows(s.x_msg, BF16), s.rows(s.half)], [wide, x_rows], [wavefunctions, by_atom])
    field = wavefunctions
    for step in range(2):
        from_x = shifted(down_x, (-1, 0, 0))
        y_msg, z_msg, yz_msg, part = call(
            down_body, s, side_msgs + [s.rows(s.own)], [x_rows, y_rows, z_rows, yz_rows], [field, from_x, kept]
        )
        from_y = shifted(y_msg, (0, -1, 0))
        from_z = shifted(z_msg, (0, 0, -1))
        from_yz = shifted(yz_msg, (0, -1, -1))
        block, y_msg, z_msg, yz_msg, own = call(
            cell_body,
            s,
            [jax.ShapeDtypeStruct((s.bx + 1, s.by, s.bz, s.waves), F32)] + side_msgs + [s.rows(s.own)],
            [s.scratch(*sum_shape), s.scratch(*sum_shape), x_rows, y_rows, z_rows, yz_rows],
            [field, matrices, from_x, from_y, from_z, from_yz, part, weight],
        )
        from_y = shifted(y_msg, (0, 1, 0))
        from_z = shifted(z_msg, (0, 0, 1))
        from_yz = shifted(yz_msg, (0, 1, 1))
        up_x, spread = call(
            up_body,
            s,
            [s.rows(s.x_msg, BF16), s.rows(s.half)],
            [x_rows, y_rows, z_rows, yz_rows],
            [block, from_y, from_z, from_yz, own],
        )
        from_x = shifted(up_x, (1, 0, 0))
        scratch = [wide, x_rows, y_rows, z_rows, yz_rows]
        received = [block, from_x, from_y, from_z, from_yz, spread, by_node]
        if step == 0:
            field, down_x, kept = call(
                middle_body,
                s,
                [jax.ShapeDtypeStruct(field.shape, F32), s.rows(s.x_msg, BF16), s.rows(s.half)],
                scratch,
                received + [by_atom],
            )
        else:
            (out,) = call(last_body, s, [jax.ShapeDtypeStruct(field.shape, F32)], scratch, [wavefunctions] + received)
    return out


def solution(mesh):
    return jax.shard_map(
        local,
        mesh=mesh,
        in_specs=(
            P("gx", "gy", "gz", None),
            P("gx", "gy", "gz", None, None),
            P(("gx", "gy", "gz"), None, None),
            P(("gx", "gy", "gz"), None),
            P(),
        ),
        out_specs=P("gx", "gy", "gz", None),
        check_vma=False,
    )
```

time: 163 us -> 66.1 us (0.41)
  other arithmetic: 34 us -> 0.85 us
  local copies, waits for them, and re-layouts: 32.4 us -> 5.42 us
  waiting for transfers between devices: 48.1 us -> 28.3 us
  starting transfers between devices: 31.8 us -> 16.5 us
  matrix products: 15.6 us -> 5.93 us
  Pallas kernels: 0 us -> 8.75 us
    ppermute x24 -> x16, waiting for transfers between devices: 48.1 us -> 28.3 us  [shifted(): return lax.ppermute(value, AXES, pairs)]
    concatenate x9 -> x0, other arithmetic: 19 us -> none  [the longest x3 14.6 us: extend(): return jnp.concatenate([values, upper_planes], axis=axis_pos + 1)]
    reshape x8 -> x0, local copies, waits for them, and re-layouts: 16.5 us -> none  [the longest x2 5.95 us: cell_part(): return product.reshape(field_now.shape)]
    ppermute x24 -> x16, starting transfers between devices: 31.8 us -> 16.5 us  [shifted(): return lax.ppermute(value, AXES, pairs)]
    dot_general x10 -> x2, matrix products: 15.6 us -> 5.93 us  [the longest x1 4.85 us: regrouped(): jnp.einsum('rm,xyzmc->xyzrc', spread, wide, preferred_element_type=BF16)]
    pallas_call x0 -> x10, Pallas kernels: none -> 8.75 us  [call(): pl.pallas_call(functools.partial(body, sizes), out_shape=outs, in_specs=[...]
    sub x1 -> x0, other arithmetic: 5.52 us -> none  [local(): following = 2.0 * apply_operator(current) - previous]
    slice x18 -> x0, local copies, waits for them, and re-layouts: 4.79 us -> none  [the longest x6 2.89 us: fold(): lax.slice_in_dim(inner_part, 1, span_nodes - 1, axis=axis_pos + 1)]
  transfers between devices with their start and end apart: 24 -> 16, of which waited for: 18 -> 7; matrix products, arithmetic and copies ran while one was open for 13% -> 7% of each run, Pallas kernels for 0% -> 0%
where the time goes in v1:
time: 66.1 us; the launch traced here: 65.8 us
  waiting for transfers between devices  28.3 us (43%)
  starting transfers between devices  16.5 us (25%)
  Pallas kernels  8.75 us (13%)
  matrix products  5.93 us (9%)
  local copies, waits for them, and re-layouts  5.42 us (8%)
  other arithmetic  0.85 us (1%)
    ppermute x16, waiting for transfers between devices, shifted(): return lax.ppermute(value, AXES, pairs)  28.3 us
    ppermute x16, starting transfers between devices, shifted(): return lax.ppermute(value, AXES, pairs)  16.5 us
    pallas_call x10, Pallas kernels, call(): pl.pallas_call(functools.partial(body, sizes), out_shape=outs, in_specs=[...  8.75 us
    unnamed x16, local copies, waits for them, and re-layouts  5.28 us
    dot_general x1, matrix products, regrouped(): jnp.einsum('rm,xyzmc->xyzrc', spread, wide, preferred_element_type=BF16)  4.85 us
  transfers between devices with their start and end apart: 16, of which 7 were waited for; matrix products, arithmetic and copies ran while one was open for 7% of the time, Pallas kernels for 0%

profile of v1, /device:TPU:0, one launch (start us, length us, event | category | flops | bytes accessed | tf_op | source)
XLA Modules:
  0.0 65.8 jit_solution(14870162210319672161)
XLA Ops:
  0.0 0.8 %fusion.39 = s32[16]{0:T(128)S(1)} fusion(s32[1,16]{1,0:T(1,128)} %param.8, s32[]{:T(128)S(6)} %axis_index.50, s32[]{:T(128)S(6)} %axis_index.48, s32[]{:T(128)S(6)} %axis_index.21), kind=kLoop, calls=%fused_computation.62 | loop fusion | flops 1648 | bytes 140 | tf_op jit(solution)/shard_map/eq | solution.py:284
  0.8 1.1 %fusion.16.rows_ref = f32[16,1728]{1,0:T(8,128)S(1)} fusion(f32[1,16,1728]{2,1,0:T(8,128)} %param.7, s32[16]{0:T(128)S(1)} %fusion.39), kind=kOutput, calls=%fused_computation.8 | convolution fusion | flops 5308672 | bytes 221248 | tf_op jit(solution)/shard_map/dot_general | solution.py:285
  2.5 1.7 %copy-done.1 = f32[12,12,12,256]{3,2,1,0:T(8,128)S(1)} copy-done((f32[12,12,12,256]{3,2,1,0:T(8,128)S(1)}, f32[12,12,12,256]{3,2,1,0:T(8,128)}, u32[]{:S(2)}) %copy-start.1) | copy-done | bytes 1769496
  4.7 2.5 %collective-permute-start = (bf16[160,256]{1,0:T(8,128)(2,1)S(1)}, bf16[160,256]{1,0:T(8,128)(2,1)S(1)}, u32[]{:S(2)}, u32[]{:S(2)}) collective-permute-start(bf16[160,256]{1,0:T(8,128)(2,1)S(1)} %get-tuple-element.35), channel_id=1, source_target_pairs={{0,24},{1,25},{2,26},{3,27},{4,28},{5,29},{6,30},{7,31},{8,0},{9,1... | collective-permute-start | bytes 245768 | tf_op jit(solution)/shard_map/ppermute | solution.py:29
  7.2 2.1 %collective-permute-done.from_x_ref = bf16[160,256]{1,0:T(8,128)(2,1)S(1)} collective-permute-done((bf16[160,256]{1,0:T(8,128)(2,1)S(1)}, bf16[160,256]{1,0:T(8,128)(2,1)S(1)}, u32[]{:S(2)}, u32[]{:S(2)}) %collective-permute-start) | collective-permute-done | bytes 81952 | tf_op jit(solution)/shard_map/ppermute | solution.py:29
  9.3 4.6 %collective-permute-start.3 = (bf16[32,256]{1,0:T(8,128)(2,1)S(1)}, bf16[32,256]{1,0:T(8,128)(2,1)S(1)}, u32[]{:S(2)}, u32[]{:S(2)}) collective-permute-start(bf16[32,256]{1,0:T(8,128)(2,1)S(1)} %get-tuple-element.39), channel_id=1, source_target_pairs={{0,7},{1,6},{2,1},{3,0},{4,3},{5,2},{6,5},{7,4},{8,15},{9,14},{10,... | collective-permute-start | bytes 49160 | tf_op jit(solution)/shard_map/ppermute | solution.py:29
  14.9 4.9 %fusion.4.matrix_ref = bf16[2,2,2,400,400]{4,3,2,1,0:T(8,128)(2,1)} fusion(bf16[2,2,2,343,343]{4,2,3,1,0:T(2,128)(2,1)S(1)} %copy-done, s32[400]{0:T(512)S(1)} %fusion.25), kind=kOutput, calls=%fused_computation.4 | convolution fusion | flops 1631308032 | bytes 4443984 | tf_op jit(solution)/shard_map/rm,xyzmc->xyzrc/dot_general | solution.py:293
  19.9 1.7 %copy-done.3 = f32[12,12,12,256]{3,2,1,0:T(8,128)S(1)} copy-done((f32[12,12,12,256]{3,2,1,0:T(8,128)S(1)}, f32[12,12,12,256]{3,2,1,0:T(8,128)}, u32[]{:S(2)}) %copy-start.3) | copy-done | bytes 1769496
  21.6 1.9 %copy-done.5 = bf16[2,2,2,400,400]{4,3,2,1,0:T(8,128)(2,1)S(1)} copy-done((bf16[2,2,2,400,400]{4,3,2,1,0:T(8,128)(2,1)S(1)}, bf16[2,2,2,400,400]{4,3,2,1,0:T(8,128)(2,1)}, u32[]{:S(2)}) %copy-start.5) | copy-done | bytes 2560024
  23.5 1.7 %shard_map.58 = (f32[13,12,12,256]{3,2,1,0:T(8,128)S(1)}, bf16[160,256]{1,0:T(8,128)(2,1)S(1)}, bf16[160,256]{1,0:T(8,128)(2,1)S(1)}, bf16[32,256]{1,0:T(8,128)(2,1)S(1)}, f32[2,256]{1,0:T(2,128)S(1)}) custom-call(f32[12,12,12,256]{3,2,1,0:T(8,128)S(1)} %copy-done.3, bf16[2,2,2,400,400]{4,3,2,1,0:T(8,128)(2,1)S(1)} %copy-done.5, ...), custom_call_target="tpu_custom_call" | custom-call | tf_op jit(solution)/shard_map/pallas_call | solution.py:79
  25.2 1.6 %collective-permute-start.4 = (bf16[160,256]{1,0:T(8,128)(2,1)S(1)}, bf16[160,256]{1,0:T(8,128)(2,1)S(1)}, u32[]{:S(2)}, u32[]{:S(2)}) collective-permute-start(bf16[160,256]{1,0:T(8,128)(2,1)S(1)} %get-tuple-element.42), channel_id=1, source_target_pairs={{0,2},{1,3},{2,4},{3,5},{4,6},{5,7},{6,0},{7,1},{8,10},{9,11},{10,... | collective-permute-start | bytes 245768 | tf_op jit(solution)/shard_map/ppermute | solution.py:29
  26.8 1.5 %collective-permute-start.5 = (bf16[160,256]{1,0:T(8,128)(2,1)S(1)}, bf16[160,256]{1,0:T(8,128)(2,1)S(1)}, u32[]{:S(2)}, u32[]{:S(2)}) collective-permute-start(bf16[160,256]{1,0:T(8,128)(2,1)S(1)} %get-tuple-element.43), channel_id=1, source_target_pairs={{0,1},{1,0},{2,3},{3,2},{4,5},{5,4},{6,7},{7,6},{8,9},{9,8},{10,11... | collective-permute-start | bytes 245768 | tf_op jit(solution)/shard_map/ppermute | solution.py:29
  28.4 6.4 %collective-permute-done.6.from_yz_ref = bf16[32,256]{1,0:T(8,128)(2,1)S(1)} collective-permute-done((bf16[32,256]{1,0:T(8,128)(2,1)S(1)}, bf16[32,256]{1,0:T(8,128)(2,1)S(1)}, u32[]{:S(2)}, u32[]{:S(2)}) %collective-permute-start.6) | collective-permute-done | bytes 16416 | tf_op jit(solution)/shard_map/ppermute | solution.py:29
  34.9 3.9 %collective-permute-done.7.from_x_ref = bf16[160,256]{1,0:T(8,128)(2,1)S(1)} collective-permute-done((bf16[160,256]{1,0:T(8,128)(2,1)S(1)}, bf16[160,256]{1,0:T(8,128)(2,1)S(1)}, u32[]{:S(2)}, u32[]{:S(2)}) %collective-permute-start.7) | collective-permute-done | bytes 81952 | tf_op jit(solution)/shard_map/ppermute | solution.py:29
  38.7 1.6 %shard_map.60 = (f32[12,12,12,256]{3,2,1,0:T(8,128)S(1)}, bf16[160,256]{1,0:T(8,128)(2,1)S(1)}, f32[8,256]{1,0:T(8,128)S(1)}) custom-call(f32[13,12,12,256]{3,2,1,0:T(8,128)S(1)} %get-tuple-element.41.block_ref, bf16[160,256]{1,0:T(8,128)(2,1)S(1)} %collective-permute-done.7.from_x_ref, bf16[160,256]{1,0:T(8,128)(2,1)S(1)} %collective-permute-done.4.from_y_ref, ...), custom_call_target="tpu_custom_call" | custom-call | tf_op jit(solution)/shard_map/pallas_call | solution.py:79
  40.3 2.1 %collective-permute-done.8.from_x_ref = bf16[160,256]{1,0:T(8,128)(2,1)S(1)} collective-permute-done((bf16[160,256]{1,0:T(8,128)(2,1)S(1)}, bf16[160,256]{1,0:T(8,128)(2,1)S(1)}, u32[]{:S(2)}, u32[]{:S(2)}) %collective-permute-start.8) | collective-permute-done | bytes 81952 | tf_op jit(solution)/shard_map/ppermute | solution.py:29
  43.5 1.0 %collective-permute-start.11 = (bf16[32,256]{1,0:T(8,128)(2,1)S(1)}, bf16[32,256]{1,0:T(8,128)(2,1)S(1)}, u32[]{:S(2)}, u32[]{:S(2)}) collective-permute-start(bf16[32,256]{1,0:T(8,128)(2,1)S(1)} %get-tuple-element.54), channel_id=1, source_target_pairs={{0,7},{1,6},{2,1},{3,0},{4,3},{5,2},{6,5},{7,4},{8,15},{9,14},{10,... | collective-permute-start | bytes 49160 | tf_op jit(solution)/shard_map/ppermute | solution.py:29
  44.6 3.6 %collective-permute-done.11.from_yz_ref = bf16[32,256]{1,0:T(8,128)(2,1)S(1)} collective-permute-done((bf16[32,256]{1,0:T(8,128)(2,1)S(1)}, bf16[32,256]{1,0:T(8,128)(2,1)S(1)}, u32[]{:S(2)}, u32[]{:S(2)}) %collective-permute-start.11) | collective-permute-done | bytes 16416 | tf_op jit(solution)/shard_map/ppermute | solution.py:29
  48.2 1.7 %shard_map.62 = (f32[13,12,12,256]{3,2,1,0:T(8,128)S(1)}, bf16[160,256]{1,0:T(8,128)(2,1)S(1)}, bf16[160,256]{1,0:T(8,128)(2,1)S(1)}, bf16[32,256]{1,0:T(8,128)(2,1)S(1)}, f32[2,256]{1,0:T(2,128)S(1)}) custom-call(f32[12,12,12,256]{3,2,1,0:T(8,128)S(1)} %get-tuple-element.49.field_ref, bf16[2,2,2,400,400]{4,3,2,1,0:T(8,128)(2,1)S(1)} %copy-done.6, ...), custom_call_target="tpu_custom_call" | custom-call | tf_op jit(solution)/shard_map/pallas_call | solution.py:79
  49.9 1.6 %collective-permute-start.12 = (bf16[160,256]{1,0:T(8,128)(2,1)S(1)}, bf16[160,256]{1,0:T(8,128)(2,1)S(1)}, u32[]{:S(2)}, u32[]{:S(2)}) collective-permute-start(bf16[160,256]{1,0:T(8,128)(2,1)S(1)} %get-tuple-element.57), channel_id=1, source_target_pairs={{0,2},{1,3},{2,4},{3,5},{4,6},{5,7},{6,0},{7,1},{8,10},{9,11},{10,... | collective-permute-start | bytes 245768 | tf_op jit(solution)/shard_map/ppermute | solution.py:29
  51.5 1.5 %collective-permute-start.13 = (bf16[160,256]{1,0:T(8,128)(2,1)S(1)}, bf16[160,256]{1,0:T(8,128)(2,1)S(1)}, u32[]{:S(2)}, u32[]{:S(2)}) collective-permute-start(bf16[160,256]{1,0:T(8,128)(2,1)S(1)} %get-tuple-element.58), channel_id=1, source_target_pairs={{0,1},{1,0},{2,3},{3,2},{4,5},{5,4},{6,7},{7,6},{8,9},{9,8},{10,11... | collective-permute-start | bytes 245768 | tf_op jit(solution)/shard_map/ppermute | solution.py:29
  53.0 6.4 %collective-permute-done.14.from_yz_ref = bf16[32,256]{1,0:T(8,128)(2,1)S(1)} collective-permute-done((bf16[32,256]{1,0:T(8,128)(2,1)S(1)}, bf16[32,256]{1,0:T(8,128)(2,1)S(1)}, u32[]{:S(2)}, u32[]{:S(2)}) %collective-permute-start.14) | collective-permute-done | bytes 16416 | tf_op jit(solution)/shard_map/ppermute | solution.py:29
  59.6 3.9 %collective-permute-done.15.from_x_ref = bf16[160,256]{1,0:T(8,128)(2,1)S(1)} collective-permute-done((bf16[160,256]{1,0:T(8,128)(2,1)S(1)}, bf16[160,256]{1,0:T(8,128)(2,1)S(1)}, u32[]{:S(2)}, u32[]{:S(2)}) %collective-permute-start.15) | collective-permute-done | bytes 81952 | tf_op jit(solution)/shard_map/ppermute | solution.py:29
  63.4 2.4 %shard_map.64 = f32[12,12,12,256]{3,2,1,0:T(8,128)} custom-call(f32[12,12,12,256]{3,2,1,0:T(8,128)S(1)} %copy-done.4, f32[13,12,12,256]{3,2,1,0:T(8,128)S(1)} %get-tuple-element.56.block_ref, bf16[160,256]{1,0:T(8,128)(2,1)S(1)} %collective-permute-done.15.from_x_ref, bf16[160,256]{1,0:T(8,128)(2,1)S(1)} %collective-permute-done.12.from_y_ref, ...), custom_call_target="tpu_custom_call" | custom-call | tf_op jit(solution)/shard_map/pallas_call | solution.py:79
  (40 shorter events, 3.9 us)
Async XLA Ops:
  0.0 14.9 %copy-start = (bf16[2,2,2,343,343]{4,2,3,1,0:T(2,128)(2,1)S(1)}, bf16[2,2,2,343,343]{4,2,3,1,0:T(2,128)(2,1)}, u32[]{:S(2)}) copy-start(bf16[2,2,2,343,343]{4,2,3,1,0:T(2,128)(2,1)} %param.6) | copy-start | bytes 5647156
  2.5 1.7 %copy-start.1 = (f32[12,12,12,256]{3,2,1,0:T(8,128)S(1)}, f32[12,12,12,256]{3,2,1,0:T(8,128)}, u32[]{:S(2)}) copy-start(f32[12,12,12,256]{3,2,1,0:T(8,128)} %start_ref.1) | copy-start | bytes 5308420
  4.1 5.1 %copy-start.2 = (f32[12,12,12,256]{3,2,1,0:T(8,128)S(1)}, f32[12,12,12,256]{3,2,1,0:T(8,128)}, u32[]{:S(2)}) copy-start(f32[12,12,12,256]{3,2,1,0:T(8,128)} %start_ref.1) | copy-start | bytes 5308420
  4.7 4.5 %collective-permute-start = (bf16[160,256]{1,0:T(8,128)(2,1)S(1)}, bf16[160,256]{1,0:T(8,128)(2,1)S(1)}, u32[]{:S(2)}, u32[]{:S(2)}) collective-permute-start(bf16[160,256]{1,0:T(8,128)(2,1)S(1)} %get-tuple-element.35), channel_id=1, source_target_pairs={{0,24},{1,25},{2,26},{3,27},{4,28},{5,29},{6,30},{7,31},{8,0},{9,1... | collective-permute-start | bytes 245768 | tf_op jit(solution)/shard_map/ppermute | solution.py:29
  9.3 10.5 %collective-permute-start.3 = (bf16[32,256]{1,0:T(8,128)(2,1)S(1)}, bf16[32,256]{1,0:T(8,128)(2,1)S(1)}, u32[]{:S(2)}, u32[]{:S(2)}) collective-permute-start(bf16[32,256]{1,0:T(8,128)(2,1)S(1)} %get-tuple-element.39), channel_id=1, source_target_pairs={{0,7},{1,6},{2,1},{3,0},{4,3},{5,2},{6,5},{7,4},{8,15},{9,14},{10,... | collective-permute-start | bytes 49160 | tf_op jit(solution)/shard_map/ppermute | solution.py:29
  13.9 5.9 %collective-permute-start.1 = (bf16[160,256]{1,0:T(8,128)(2,1)S(1)}, bf16[160,256]{1,0:T(8,128)(2,1)S(1)}, u32[]{:S(2)}, u32[]{:S(2)}) collective-permute-start(bf16[160,256]{1,0:T(8,128)(2,1)S(1)} %get-tuple-element.37), channel_id=1, source_target_pairs={{0,6},{1,7},{2,0},{3,1},{4,2},{5,3},{6,4},{7,5},{8,14},{9,15},{10,... | collective-permute-start | bytes 245768 | tf_op jit(solution)/shard_map/ppermute | solution.py:29
  14.4 5.4 %copy-start.7 = (f32[64]{0:T(128)S(1)}, f32[64]{0:T(128)}, u32[]{:S(2)}) copy-start(f32[64]{0:T(128)} %param.9) | copy-start | bytes 772
  14.4 5.5 %collective-permute-start.2 = (bf16[160,256]{1,0:T(8,128)(2,1)S(1)}, bf16[160,256]{1,0:T(8,128)(2,1)S(1)}, u32[]{:S(2)}, u32[]{:S(2)}) collective-permute-start(bf16[160,256]{1,0:T(8,128)(2,1)S(1)} %get-tuple-element.38), channel_id=1, source_target_pairs={{0,1},{1,0},{2,3},{3,2},{4,5},{5,4},{6,7},{7,6},{8,9},{9,8},{10,11... | collective-permute-start | bytes 245768 | tf_op jit(solution)/shard_map/ppermute | solution.py:29
  19.9 1.7 %copy-start.3 = (f32[12,12,12,256]{3,2,1,0:T(8,128)S(1)}, f32[12,12,12,256]{3,2,1,0:T(8,128)}, u32[]{:S(2)}) copy-start(f32[12,12,12,256]{3,2,1,0:T(8,128)} %start_ref.1) | copy-start | bytes 5308420
  21.6 1.9 %copy-start.5 = (bf16[2,2,2,400,400]{4,3,2,1,0:T(8,128)(2,1)S(1)}, bf16[2,2,2,400,400]{4,3,2,1,0:T(8,128)(2,1)}, u32[]{:S(2)}) copy-start(bf16[2,2,2,400,400]{4,3,2,1,0:T(8,128)(2,1)} %fusion.4.matrix_ref) | copy-start | bytes 7680004
  25.2 9.6 %collective-permute-start.4 = (bf16[160,256]{1,0:T(8,128)(2,1)S(1)}, bf16[160,256]{1,0:T(8,128)(2,1)S(1)}, u32[]{:S(2)}, u32[]{:S(2)}) collective-permute-start(bf16[160,256]{1,0:T(8,128)(2,1)S(1)} %get-tuple-element.42), channel_id=1, source_target_pairs={{0,2},{1,3},{2,4},{3,5},{4,6},{5,7},{6,0},{7,1},{8,10},{9,11},{10,... | collective-permute-start | bytes 245768 | tf_op jit(solution)/shard_map/ppermute | solution.py:29
  26.8 7.9 %collective-permute-start.5 = (bf16[160,256]{1,0:T(8,128)(2,1)S(1)}, bf16[160,256]{1,0:T(8,128)(2,1)S(1)}, u32[]{:S(2)}, u32[]{:S(2)}) collective-permute-start(bf16[160,256]{1,0:T(8,128)(2,1)S(1)} %get-tuple-element.43), channel_id=1, source_target_pairs={{0,1},{1,0},{2,3},{3,2},{4,5},{5,4},{6,7},{7,6},{8,9},{9,8},{10,11... | collective-permute-start | bytes 245768 | tf_op jit(solution)/shard_map/ppermute | solution.py:29
  28.3 6.4 %collective-permute-start.6 = (bf16[32,256]{1,0:T(8,128)(2,1)S(1)}, bf16[32,256]{1,0:T(8,128)(2,1)S(1)}, u32[]{:S(2)}, u32[]{:S(2)}) collective-permute-start(bf16[32,256]{1,0:T(8,128)(2,1)S(1)} %get-tuple-element.44), channel_id=1, source_target_pairs={{0,3},{1,2},{2,5},{3,4},{4,7},{5,6},{6,1},{7,0},{8,11},{9,10},{10,... | collective-permute-start | bytes 49160 | tf_op jit(solution)/shard_map/ppermute | solution.py:29
  34.8 3.9 %collective-permute-start.7 = (bf16[160,256]{1,0:T(8,128)(2,1)S(1)}, bf16[160,256]{1,0:T(8,128)(2,1)S(1)}, u32[]{:S(2)}, u32[]{:S(2)}) collective-permute-start(bf16[160,256]{1,0:T(8,128)(2,1)S(1)} %get-tuple-element.46), channel_id=1, source_target_pairs={{0,8},{1,9},{2,10},{3,11},{4,12},{5,13},{6,14},{7,15},{8,16},{9,17... | collective-permute-start | bytes 245768 | tf_op jit(solution)/shard_map/ppermute | solution.py:29
  38.7 9.5 %copy-start.6 = (bf16[2,2,2,400,400]{4,3,2,1,0:T(8,128)(2,1)S(1)}, bf16[2,2,2,400,400]{4,3,2,1,0:T(8,128)(2,1)}, u32[]{:S(2)}) copy-start(bf16[2,2,2,400,400]{4,3,2,1,0:T(8,128)(2,1)} %fusion.4.matrix_ref) | copy-start | bytes 7680004
  40.3 2.1 %collective-permute-start.8 = (bf16[160,256]{1,0:T(8,128)(2,1)S(1)}, bf16[160,256]{1,0:T(8,128)(2,1)S(1)}, u32[]{:S(2)}, u32[]{:S(2)}) collective-permute-start(bf16[160,256]{1,0:T(8,128)(2,1)S(1)} %get-tuple-element.50), channel_id=1, source_target_pairs={{0,24},{1,25},{2,26},{3,27},{4,28},{5,29},{6,30},{7,31},{8,0},{9,1... | collective-permute-start | bytes 245768 | tf_op jit(solution)/shard_map/ppermute | solution.py:29
  42.5 5.7 %collective-permute-start.9 = (bf16[160,256]{1,0:T(8,128)(2,1)S(1)}, bf16[160,256]{1,0:T(8,128)(2,1)S(1)}, u32[]{:S(2)}, u32[]{:S(2)}) collective-permute-start(bf16[160,256]{1,0:T(8,128)(2,1)S(1)} %get-tuple-element.52), channel_id=1, source_target_pairs={{0,6},{1,7},{2,0},{3,1},{4,2},{5,3},{6,4},{7,5},{8,14},{9,15},{10,... | collective-permute-start | bytes 245768 | tf_op jit(solution)/shard_map/ppermute | solution.py:29
  43.0 5.2 %collective-permute-start.10 = (bf16[160,256]{1,0:T(8,128)(2,1)S(1)}, bf16[160,256]{1,0:T(8,128)(2,1)S(1)}, u32[]{:S(2)}, u32[]{:S(2)}) collective-permute-start(bf16[160,256]{1,0:T(8,128)(2,1)S(1)} %get-tuple-element.53), channel_id=1, source_target_pairs={{0,1},{1,0},{2,3},{3,2},{4,5},{5,4},{6,7},{7,6},{8,9},{9,8},{10,11... | collective-permute-start | bytes 245768 | tf_op jit(solution)/shard_map/ppermute | solution.py:29
  43.5 4.6 %collective-permute-start.11 = (bf16[32,256]{1,0:T(8,128)(2,1)S(1)}, bf16[32,256]{1,0:T(8,128)(2,1)S(1)}, u32[]{:S(2)}, u32[]{:S(2)}) collective-permute-start(bf16[32,256]{1,0:T(8,128)(2,1)S(1)} %get-tuple-element.54), channel_id=1, source_target_pairs={{0,7},{1,6},{2,1},{3,0},{4,3},{5,2},{6,5},{7,4},{8,15},{9,14},{10,... | collective-permute-start | bytes 49160 | tf_op jit(solution)/shard_map/ppermute | solution.py:29
  49.9 13.5 %copy-start.4 = (f32[12,12,12,256]{3,2,1,0:T(8,128)S(1)}, f32[12,12,12,256]{3,2,1,0:T(8,128)}, u32[]{:S(2)}) copy-start(f32[12,12,12,256]{3,2,1,0:T(8,128)} %start_ref.1) | copy-start | bytes 5308420
  49.9 9.6 %collective-permute-start.12 = (bf16[160,256]{1,0:T(8,128)(2,1)S(1)}, bf16[160,256]{1,0:T(8,128)(2,1)S(1)}, u32[]{:S(2)}, u32[]{:S(2)}) collective-permute-start(bf16[160,256]{1,0:T(8,128)(2,1)S(1)} %get-tuple-element.57), channel_id=1, source_target_pairs={{0,2},{1,3},{2,4},{3,5},{4,6},{5,7},{6,0},{7,1},{8,10},{9,11},{10,... | collective-permute-start | bytes 245768 | tf_op jit(solution)/shard_map/ppermute | solution.py:29
  51.5 7.9 %collective-permute-start.13 = (bf16[160,256]{1,0:T(8,128)(2,1)S(1)}, bf16[160,256]{1,0:T(8,128)(2,1)S(1)}, u32[]{:S(2)}, u32[]{:S(2)}) collective-permute-start(bf16[160,256]{1,0:T(8,128)(2,1)S(1)} %get-tuple-element.58), channel_id=1, source_target_pairs={{0,1},{1,0},{2,3},{3,2},{4,5},{5,4},{6,7},{7,6},{8,9},{9,8},{10,11... | collective-permute-start | bytes 245768 | tf_op jit(solution)/shard_map/ppermute | solution.py:29
  53.0 6.4 %collective-permute-start.14 = (bf16[32,256]{1,0:T(8,128)(2,1)S(1)}, bf16[32,256]{1,0:T(8,128)(2,1)S(1)}, u32[]{:S(2)}, u32[]{:S(2)}) collective-permute-start(bf16[32,256]{1,0:T(8,128)(2,1)S(1)} %get-tuple-element.59), channel_id=1, source_target_pairs={{0,3},{1,2},{2,5},{3,4},{4,7},{5,6},{6,1},{7,0},{8,11},{9,10},{10,... | collective-permute-start | bytes 49160 | tf_op jit(solution)/shard_map/ppermute | solution.py:29
  59.5 3.9 %collective-permute-start.15 = (bf16[160,256]{1,0:T(8,128)(2,1)S(1)}, bf16[160,256]{1,0:T(8,128)(2,1)S(1)}, u32[]{:S(2)}, u32[]{:S(2)}) collective-permute-start(bf16[160,256]{1,0:T(8,128)(2,1)S(1)} %get-tuple-element.61), channel_id=1, source_target_pairs={{0,8},{1,9},{2,10},{3,11},{4,12},{5,13},{6,14},{7,15},{8,16},{9,17... | collective-permute-start | bytes 245768 | tf_op jit(solution)/shard_map/ppermute | solution.py:29

commit v2 on v1

v2 whole, which is shorter than its diff:
```python
import functools

import jax
import jax.numpy as jnp
from jax import lax
from jax.experimental import pallas as pl
from jax.experimental.pallas import tpu as pltpu
from jax.sharding import PartitionSpec as P

AXES = ("gx", "gy", "gz")
F32 = jnp.float32
BF16 = jnp.bfloat16
LIMIT = 12 * 1024 * 1024


def up_to(value, unit):
    return -(-value // unit) * unit


def shifted(value, shift):
    sizes = [lax.axis_size(axis) for axis in AXES]
    pairs = []
    for x in range(sizes[0]):
        for y in range(sizes[1]):
            for z in range(sizes[2]):
                here = (x * sizes[1] + y) * sizes[2] + z
                there = [(p + s) % n for p, s, n in zip((x, y, z), shift, sizes)]
                pairs.append((here, (there[0] * sizes[1] + there[1]) * sizes[2] + there[2]))
    return lax.ppermute(value, AXES, pairs)


def halves(value):
    high = value.astype(BF16).astype(F32)
    return high, value - high


def put_split(rows_ref, start, value):
    count = value.shape[0]
    high, low = halves(value)
    rows_ref[start : start + count] = high
    rows_ref[start + count : start + 2 * count] = low


def get_split(rows_ref, start, count):
    return rows_ref[start : start + count] + rows_ref[start + count : start + 2 * count]


class Sizes:
    def __init__(self, field_shape, cell_shape, locals_count):
        self.bx, self.by, self.bz, self.waves = field_shape
        self.cells = cell_shape[:3]
        self.order = self.bx // cell_shape[0]
        self.side = self.order + 1
        self.group = up_to(self.side, 8)
        self.padded = up_to(self.side * self.side * self.group, 16)
        self.bzp = up_to(max(self.bz + 1, (cell_shape[2] - 1) * self.order + self.group), 16)
        self.locals = locals_count
        self.half = locals_count // 2
        self.quarter = locals_count // 4
        self.own = locals_count // 8
        self.x_rows = self.by * self.bz
        self.y_rows = (self.bx + 1) * self.bz
        self.z_rows = (self.bx + 1) * self.by
        self.yz_rows = self.bx + 1
        self.x_msg = up_to(self.x_rows + 2 * self.half, 16)
        self.y_msg = up_to(self.y_rows + 2 * self.own, 16)
        self.z_msg = up_to(self.z_rows + 2 * self.own, 16)
        self.yz_msg = up_to(self.yz_rows + 2 * self.own, 16)
        self.nodes_padded = self.bx * self.by * self.bzp

    def extended(self):
        return jax.ShapeDtypeStruct((self.bx + 1, self.by + 1, self.bzp, self.waves), F32)

    def rows(self, count, dtype=F32):
        return jax.ShapeDtypeStruct((count, self.waves), dtype)

    def scratch(self, *shape):
        return pltpu.VMEM(shape + (self.waves,), F32)


VMEM = pltpu.VMEM


def call(body, sizes, outs, scratch, args, spaces=None, out_spaces=None, aliases=None):
    spaces = spaces or {}
    out_spaces = out_spaces or {}
    outs = [out_spaces.get(n, VMEM)(out.shape, out.dtype) for n, out in enumerate(outs)]
    args = [pltpu.with_memory_space_constraint(arg, spaces.get(n, VMEM)) for n, arg in enumerate(args)]
    return pl.pallas_call(
        functools.partial(body, sizes),
        out_shape=outs,
        in_specs=[pl.BlockSpec(memory_space=spaces.get(n, VMEM)) for n in range(len(args))],
        out_specs=[pl.BlockSpec(memory_space=out_spaces.get(n, VMEM)) for n in range(len(outs))],
        scratch_shapes=scratch,
        input_output_aliases=aliases or {},
        compiler_params=pltpu.CompilerParams(vmem_limit_bytes=LIMIT),
    )(*args)


def own_index():
    return (lax.axis_index("gx") * lax.axis_size("gy") + lax.axis_index("gy")) * lax.axis_size("gz") + lax.axis_index("gz")


def local_atoms(own):
    sizes = [lax.axis_size(axis) for axis in AXES]
    here = [lax.axis_index(axis) for axis in AXES]
    ids = []
    for dx in range(2):
        for dy in range(2):
            for dz in range(2):
                x, y, z = (lax.rem(h + n - d, n) for h, n, d in zip(here, sizes, (dx, dy, dz)))
                owner = (x * sizes[1] + y) * sizes[2] + z
                ids += [owner * own + a for a in range(own)]
    return jnp.stack(ids).astype(jnp.int32)


def put_face(s, rows_ref, field_ref):
    for y in range(s.by):
        rows_ref[y * s.bz : (y + 1) * s.bz] = field_ref[0, y, 0 : s.bz]


def plane_sums(s, by_atom_ref, x, plane):
    high = plane.astype(BF16)
    low = (plane - high.astype(F32)).astype(BF16)
    with_high = jnp.dot(by_atom_ref[x], high, preferred_element_type=F32)
    with_low = jnp.dot(by_atom_ref[x, 0 : s.locals], low, preferred_element_type=F32)
    return with_high[0 : s.locals] + with_high[s.locals : 2 * s.locals] + with_low


def send_down_x(s, total, field_ref, rows_ref, msg_ref, kept_ref):
    kept_ref[...] = total[0 : s.half]
    put_face(s, rows_ref, field_ref)
    rows_ref[s.x_rows :] = jnp.zeros((s.x_msg - s.x_rows, s.waves), F32)
    put_split(rows_ref, s.x_rows, total[s.half : 2 * s.half])
    msg_ref[...] = rows_ref[...].astype(BF16)


def first_body(
    s, start_hbm, rows_hbm, slots_hbm, ids_ref,
    field_ref, by_node_ref, by_atom_ref, msg_ref, kept_ref,
    start_ref, rows_ref, slots_ref, tall_ref, wide_ref, x_ref, sems, small_sems,
):
    small = [
        pltpu.make_async_copy(rows_hbm, rows_ref, small_sems.at[0]),
        pltpu.make_async_copy(slots_hbm, slots_ref, small_sems.at[1]),
    ]
    for copy in small:
        copy.start()
    copies = [pltpu.make_async_copy(start_hbm.at[x], start_ref.at[x], sems.at[x]) for x in range(s.bx)]
    for copy in copies:
        copy.start()
    for copy in small:
        copy.wait()
    selector = (ids_ref[...] == slots_ref[...]).astype(F32)
    rows = jnp.dot(selector, rows_ref[0], precision=lax.Precision.HIGHEST, preferred_element_type=F32)
    high, low = halves(rows)
    low = low.astype(BF16).astype(F32)
    tall_ref[...] = jnp.concatenate([high, low, high], axis=0).T
    wide_ref[:, s.bz : s.bzp, :] = jnp.zeros((s.bx * s.by, s.bzp - s.bz, 3 * s.locals), F32)
    for g in range(s.bx * s.by):
        wide_ref[g, 0 : s.bz, :] = tall_ref[g * s.bz : (g + 1) * s.bz, :]
    for x in range(s.bx):
        wide = wide_ref[x * s.by : (x + 1) * s.by].reshape(s.by * s.bzp, 3 * s.locals)
        by_node_ref[x] = wide.astype(BF16)
        by_atom_ref[x] = wide.T[0 : 2 * s.locals].astype(BF16)
    total = jnp.zeros((s.locals, s.waves), F32)
    for x in range(s.bx):
        copies[x].wait()
        plane = start_ref[x]
        plane = jnp.concatenate([plane, jnp.zeros((s.by, s.bzp - s.bz, s.waves), F32)], axis=1)
        field_ref[x, 0 : s.by] = plane
        total = total + plane_sums(s, by_atom_ref, x, plane.reshape(s.by * s.bzp, s.waves))
    send_down_x(s, total, field_ref, x_ref, msg_ref, kept_ref)


def down_body(s, field_ref, from_x_ref, kept_ref, y_msg_ref, z_msg_ref, yz_msg_ref, part_ref, x_ref, y_ref, z_ref, yz_ref):
    x_ref[...] = from_x_ref[...].astype(F32)
    total = kept_ref[...] + get_split(x_ref, s.x_rows, s.half)
    for ref, used in ((y_ref, s.y_rows), (z_ref, s.z_rows), (yz_ref, s.yz_rows)):
        ref[used:] = jnp.zeros((ref.shape[0] - used, s.waves), F32)
    for x in range(s.bx):
        y_ref[x * s.bz : (x + 1) * s.bz] = field_ref[x, 0, 0 : s.bz]
        z_ref[x * s.by : (x + 1) * s.by] = field_ref[x, 0 : s.by, 0, :]
        yz_ref[x : x + 1] = field_ref[x, 0, 0:1, :]
    y_ref[s.bx * s.bz : s.y_rows] = x_ref[0 : s.bz]
    for y in range(s.by):
        z_ref[s.bx * s.by + y : s.bx * s.by + y + 1] = x_ref[y * s.bz : y * s.bz + 1]
    yz_ref[s.bx : s.bx + 1] = x_ref[0:1]
    own = s.own
    part_ref[...] = total[0:own]
    put_split(z_ref, s.z_rows, total[own : 2 * own])
    put_split(y_ref, s.y_rows, total[2 * own : 3 * own])
    put_split(yz_ref, s.yz_rows, total[3 * own : 4 * own])
    y_msg_ref[...] = y_ref[...].astype(BF16)
    z_msg_ref[...] = z_ref[...].astype(BF16)
    yz_msg_ref[...] = yz_ref[...].astype(BF16)


def cell_body(
    s, before_ref, matrix_ref, from_x_ref, from_y_ref, from_z_ref, from_yz_ref, part_ref, weight_ref,
    field_ref, block_ref, y_msg_ref, z_msg_ref, yz_msg_ref, own_ref,
    sums_ref, x_ref, y_ref, z_ref, yz_ref,
):
    del before_ref
    order, side, group = s.order, s.side, s.group
    cells_x, cells_y, cells_z = s.cells
    x_ref[...] = from_x_ref[...].astype(F32)
    y_ref[...] = from_y_ref[...].astype(F32)
    z_ref[...] = from_z_ref[...].astype(F32)
    yz_ref[...] = from_yz_ref[...].astype(F32)
    rest = jnp.zeros((s.bzp - s.bz, s.waves), F32)
    for y in range(s.by):
        field_ref[s.bx, y, 0 : s.bz, :] = x_ref[y * s.bz : (y + 1) * s.bz]
        field_ref[s.bx, y, s.bz :, :] = rest
    for x in range(s.bx + 1):
        field_ref[x, s.by, 0 : s.bz, :] = y_ref[x * s.bz : (x + 1) * s.bz]
        field_ref[x, s.by, s.bz :, :] = rest
        field_ref[x, 0 : s.by, s.bz, :] = z_ref[x * s.by : (x + 1) * s.by]
        field_ref[x, s.by, s.bz : s.bz + 1, :] = yz_ref[x : x + 1]
    used = side * side * group
    for i in range(cells_x):
        for j in range(cells_y):
            for k in range(cells_z):
                first = k * order
                values = field_ref[i * order : i * order + side, j * order : j * order + side, first : first + group]
                values = values.reshape(used, s.waves)
                if s.padded > used:
                    values = jnp.concatenate([values, jnp.zeros((s.padded - used, s.waves), F32)], axis=0)
                product = jnp.dot(matrix_ref[i, j, k], values.astype(BF16), preferred_element_type=F32)
                product = product[0:used].reshape(side, side, group, s.waves)
                x0, x1, y0, y1 = i * order, i * order + side, j * order, j * order + side
                a, b = int(i > 0), int(j > 0)
                sums_ref[k, x0 + a : x1, y0 + b : y1] = product[a:, b:]
                if a:
                    sums_ref[k, x0, y0 + b : y1] += product[0, b:]
                if b:
                    sums_ref[k, x0 + a : x1, y0] += product[a:, 0]
                if a and b:
                    sums_ref[k, x0, y0] += product[0, 0]
    own = s.own
    total = part_ref[...] + get_split(z_ref, s.z_rows, own) + get_split(y_ref, s.y_rows, own) + get_split(yz_ref, s.yz_rows, own)
    total = total * weight_ref[...]
    own_ref[...] = total
    last = cells_z - 1
    for x in range(s.bx + 1):
        z_ref[x * s.by : (x + 1) * s.by] = sums_ref[last, x, 0 : s.by, order, :]
        yz_ref[x : x + 1] = sums_ref[last, x, s.by, order : order + 1, :]
        for k in range(cells_z):
            at = x * s.bz + k * order
            y_ref[at : at + order] = sums_ref[k, x, s.by, 0:order, :]
            if k:
                y_ref[at : at + 1] += sums_ref[k - 1, x, s.by, order : order + 1, :]
    put_split(y_ref, s.y_rows, total)
    put_split(z_ref, s.z_rows, total)
    put_split(yz_ref, s.yz_rows, total)
    y_msg_ref[...] = y_ref[...].astype(BF16)
    z_msg_ref[...] = z_ref[...].astype(BF16)
    yz_msg_ref[...] = yz_ref[...].astype(BF16)
    for x in range(s.bx + 1):
        block_ref[x, :, 0:group, :] = sums_ref[0, x, 0 : s.by]
        block_ref[x, :, group:, :] = jnp.zeros((s.by, s.bzp - group, s.waves), F32)
        for k in range(1, cells_z):
            block_ref[x, :, k * order : k * order + group, :] += sums_ref[k, x, 0 : s.by]


def up_body(s, block_ref, from_y_ref, from_z_ref, from_yz_ref, own_ref, x_msg_ref, spread_ref, x_ref, y_ref, z_ref, yz_ref):
    y_ref[...] = from_y_ref[...].astype(F32)
    z_ref[...] = from_z_ref[...].astype(F32)
    yz_ref[...] = from_yz_ref[...].astype(F32)
    x_ref[s.x_rows :] = jnp.zeros((s.x_msg - s.x_rows, s.waves), F32)
    for y in range(s.by):
        x_ref[y * s.bz : (y + 1) * s.bz] = block_ref[s.bx, y, 0 : s.bz]
    x_ref[0 : s.bz] += y_ref[s.bx * s.bz : s.y_rows]
    for y in range(s.by):
        x_ref[y * s.bz : y * s.bz + 1] += z_ref[s.bx * s.by + y : s.bx * s.by + y + 1]
    x_ref[0:1] += yz_ref[s.bx : s.bx + 1]
    own = s.own
    spread = jnp.concatenate(
        [own_ref[...], get_split(z_ref, s.z_rows, own), get_split(y_ref, s.y_rows, own), get_split(yz_ref, s.yz_rows, own)], axis=0
    )
    spread_ref[...] = spread
    put_split(x_ref, s.x_rows, spread)
    x_msg_ref[...] = x_ref[...].astype(BF16)


def stacked_totals(s, from_x_ref, spread_ref, x_ref):
    totals = jnp.concatenate([spread_ref[...], get_split(x_ref, s.x_rows, s.half)], axis=0)
    high, low = halves(totals)
    return jnp.concatenate([high, high, low], axis=0).astype(BF16)


def widen(s, received_ref, rows_ref, wide_ref, count):
    rows_ref[...] = received_ref[...].astype(F32)
    wide_ref[:, s.bz :, :] = jnp.zeros((count, s.bzp - s.bz, s.waves), F32)
    for n in range(count):
        wide_ref[n, 0 : s.bz] = rows_ref[n * s.bz : (n + 1) * s.bz]


def image_plane(s, x, block_ref, by_node_ref, stacked, wide_x_ref, wide_y_ref, z_ref, yz_ref, plane_ref):
    image = jnp.dot(by_node_ref[x], stacked, preferred_element_type=F32).reshape(s.by, s.bzp, s.waves)
    plane = image + block_ref[x]
    if x == 0:
        plane = plane + wide_x_ref[...]
    plane_ref[...] = plane
    plane_ref[0] += wide_y_ref[x]
    plane_ref[:, 0, :] += z_ref[x * s.by : (x + 1) * s.by]
    plane_ref[0, 0:1, :] += yz_ref[x : x + 1]


def middle_body(
    s, block_ref, from_x_ref, from_y_ref, from_z_ref, from_yz_ref, spread_ref, by_node_ref, by_atom_ref,
    field_ref, msg_ref, kept_ref, x_ref, y_ref, z_ref, yz_ref, wide_x_ref, wide_y_ref,
):
    widen(s, from_x_ref, x_ref, wide_x_ref, s.by)
    widen(s, from_y_ref, y_ref, wide_y_ref, s.bx)
    z_ref[...] = from_z_ref[...].astype(F32)
    yz_ref[...] = from_yz_ref[...].astype(F32)
    stacked = stacked_totals(s, from_x_ref, spread_ref, x_ref)
    total = jnp.zeros((s.locals, s.waves), F32)
    for x in range(s.bx):
        plane_ref = field_ref.at[x, 0 : s.by]
        image_plane(s, x, block_ref, by_node_ref, stacked, wide_x_ref, wide_y_ref, z_ref, yz_ref, plane_ref)
        total = total + plane_sums(s, by_atom_ref, x, plane_ref[...].reshape(s.by * s.bzp, s.waves))
    send_down_x(s, total, field_ref, x_ref, msg_ref, kept_ref)


def last_body(
    s, start_ref, block_ref, from_x_ref, from_y_ref, from_z_ref, from_yz_ref, spread_ref, by_node_ref,
    out_hbm, x_ref, y_ref, z_ref, yz_ref, wide_x_ref, wide_y_ref, plane_ref, out_ref, sems,
):
    widen(s, from_x_ref, x_ref, wide_x_ref, s.by)
    widen(s, from_y_ref, y_ref, wide_y_ref, s.bx)
    z_ref[...] = from_z_ref[...].astype(F32)
    yz_ref[...] = from_yz_ref[...].astype(F32)
    stacked = stacked_totals(s, from_x_ref, spread_ref, x_ref)
    copies = []
    for x in range(s.bx):
        image_plane(s, x, block_ref, by_node_ref, stacked, wide_x_ref, wide_y_ref, z_ref, yz_ref, plane_ref)
        out_ref[x] = 2.0 * plane_ref[:, 0 : s.bz] - start_ref[x]
        copies.append(pltpu.make_async_copy(out_ref.at[x], out_hbm.at[x], sems.at[x]))
        copies[x].start()
    for copy in copies:
        copy.wait()


def node_of(s, rows):
    return jnp.where(rows % s.group < s.side, rows // s.group * s.side + rows % s.group, -1)


def matrix_body(s, wide_ref, spread_ref, out_ref):
    nodes = wide_ref.shape[3]
    for i in range(s.cells[0]):
        for j in range(s.cells[1]):
            for k in range(s.cells[2]):
                for first in range(0, s.padded, 256):
                    end = min(first + 256, s.padded)
                    low = first // s.group * s.side // 16 * 16
                    high = min(nodes, up_to(-(-end // s.group) * s.side, 16))
                    part = jnp.dot(spread_ref[first:end, low:high], wide_ref[i, j, k, low:high], preferred_element_type=F32)
                    out_ref[i, j, k, first:end] = part.astype(BF16)


def regrouped(s, cell_matrices):
    nodes = cell_matrices.shape[3]
    spread = (node_of(s, lax.iota(jnp.int32, s.padded))[:, None] == lax.iota(jnp.int32, nodes)[None, :]).astype(BF16)
    wide = jnp.einsum("xyzmn,cn->xyzmc", cell_matrices, spread, preferred_element_type=BF16)
    shape = cell_matrices.shape[:3] + (s.padded, s.padded)
    return call(matrix_body, s, [jax.ShapeDtypeStruct(shape, BF16)], [], [wide, spread])[0]


def local(wavefunctions, cell_matrices, projectors, slot_atoms, atom_coupling):
    atom_count = atom_coupling.shape[0]
    devices = 1
    for axis in AXES:
        devices *= lax.axis_size(axis)
    per_device = atom_count // devices
    s = Sizes(wavefunctions.shape, cell_matrices.shape, 8 * per_device)
    weight = lax.dynamic_slice_in_dim(atom_coupling, own_index() * per_device, per_device)
    weight = jnp.broadcast_to(weight[:, None], (per_device, s.waves))
    ids = local_atoms(per_device)[:, None]
    matrices = regrouped(s, cell_matrices)
    x_rows, y_rows, z_rows, yz_rows = (s.scratch(n) for n in (s.x_msg, s.y_msg, s.z_msg, s.yz_msg))
    wide_x, wide_y = s.scratch(s.by, s.bzp), s.scratch(s.bx, s.bzp)
    side_msgs = [s.rows(s.y_msg, BF16), s.rows(s.z_msg, BF16), s.rows(s.yz_msg, BF16)]
    plane = s.by * s.bzp
    field, by_node, by_atom, down_x, kept = call(
        first_body,
        s,
        [
            s.extended(),
            jax.ShapeDtypeStruct((s.bx, plane, 3 * s.locals), BF16),
            jax.ShapeDtypeStruct((s.bx, 2 * s.locals, plane), BF16),
            s.rows(s.x_msg, BF16),
            s.rows(s.half),
        ],
        [
            s.scratch(s.bx, s.by, s.bz),
            pltpu.VMEM(projectors.shape, F32),
            pltpu.VMEM(slot_atoms.shape, jnp.int32),
            pltpu.VMEM((s.bx * s.by * s.bz, 3 * s.locals), F32),
            pltpu.VMEM((s.bx * s.by, s.bzp, 3 * s.locals), F32),
            x_rows,
            pltpu.SemaphoreType.DMA((s.bx,)),
            pltpu.SemaphoreType.DMA((2,)),
        ],
        [wavefunctions, projectors, slot_atoms, ids],
        spaces={0: pltpu.HBM, 1: pltpu.HBM, 2: pltpu.HBM},
    )
    for step in range(2):
        from_x = shifted(down_x, (-1, 0, 0))
        y_msg, z_msg, yz_msg, part = call(
            down_body, s, side_msgs + [s.rows(s.own)], [x_rows, y_rows, z_rows, yz_rows], [field, from_x, kept]
        )
        from_y = shifted(y_msg, (0, -1, 0))
        from_z = shifted(z_msg, (0, 0, -1))
        from_yz = shifted(yz_msg, (0, -1, -1))
        field, block, y_msg, z_msg, yz_msg, own = call(
            cell_body,
            s,
            [s.extended(), jax.ShapeDtypeStruct((s.bx + 1, s.by, s.bzp, s.waves), F32)] + side_msgs + [s.rows(s.own)],
            [s.scratch(s.cells[2], s.bx + 1, s.by + 1, s.group), x_rows, y_rows, z_rows, yz_rows],
            [field, matrices, from_x, from_y, from_z, from_yz, part, weight],
            aliases={0: 0},
        )
        from_y = shifted(y_msg, (0, 1, 0))
        from_z = shifted(z_msg, (0, 0, 1))
        from_yz = shifted(yz_msg, (0, 1, 1))
        up_x, spread = call(
            up_body,
            s,
            [s.rows(s.x_msg, BF16), s.rows(s.half)],
            [x_rows, y_rows, z_rows, yz_rows],
            [block, from_y, from_z, from_yz, own],
        )
        from_x = shifted(up_x, (1, 0, 0))
        scratch = [x_rows, y_rows, z_rows, yz_rows, wide_x, wide_y]
        received = [block, from_x, from_y, from_z, from_yz, spread, by_node]
        if step == 0:
            field, down_x, kept = call(
                middle_body, s, [s.extended(), s.rows(s.x_msg, BF16), s.rows(s.half)], scratch, received + [by_atom]
            )
        else:
            (out,) = call(
                last_body,
                s,
                [jax.ShapeDtypeStruct(wavefunctions.shape, F32)],
                scratch
                + [s.scratch(s.by, s.bzp)]
                + [s.scratch(s.bx, s.by, s.bz), pltpu.SemaphoreType.DMA((s.bx,))],
                [wavefunctions] + received,
                out_spaces={0: pltpu.HBM},
            )
    return out


def solution(mesh):
    return jax.shard_map(
        local,
        mesh=mesh,
        in_specs=(
            P("gx", "gy", "gz", None),
            P("gx", "gy", "gz", None, None),
            P(("gx", "gy", "gz"), None, None),
            P(("gx", "gy", "gz"), None),
            P(),
        ),
        out_specs=P("gx", "gy", "gz", None),
        check_vma=False,
    )
```

time: 66.1 us -> 60.2 us (0.911)
  local copies, waits for them, and re-layouts: 5.42 us -> 2.13 us
  matrix products: 5.93 us -> 3.32 us
  Pallas kernels: 8.75 us -> 11.1 us
  waiting for transfers between devices: 28.3 us -> 26.9 us
  other arithmetic: 0.85 us -> 0.12 us
    unnamed x16 -> x12, local copies, waits for them, and re-layouts: 5.28 us -> 1.82 us
    dot_general x2 -> x1, matrix products: 5.93 us -> 3.32 us  [regrouped(): jnp.einsum('xyzmn,cn->xyzmc', cell_matrices, spread, preferred_element_ty...]
    pallas_call x10, Pallas kernels: 8.75 us -> 11.1 us  [call(): pl.pallas_call(functools.partial(body, sizes), out_shape=outs, in_specs=[...]
    ppermute x16, waiting for transfers between devices: 28.3 us -> 26.9 us  [shifted(): return lax.ppermute(value, AXES, pairs)]
    eq x1 -> x0, other arithmetic: 0.84 us -> none  [atom_rows(): selector = (columns[:, None] == local_slot[None, :]).astype(F32)]
  transfers between devices with their start and end apart: 16 -> 16, of which waited for: 7 -> 8; matrix products, arithmetic and copies ran while one was open for 7% -> 6% of each run, Pallas kernels for 0% -> 2%
where the time goes in v2:
time: 60.2 us; the launch traced here: 60.1 us
  waiting for transfers between devices  26.9 us (45%)
  starting transfers between devices  16.5 us (27%)
  Pallas kernels  11.1 us (18%)
  matrix products  3.32 us (6%)
  local copies, waits for them, and re-layouts  2.13 us (4%)
    ppermute x16, waiting for transfers between devices, shifted(): return lax.ppermute(value, AXES, pairs)  26.9 us
    ppermute x16, starting transfers between devices, shifted(): return lax.ppermute(value, AXES, pairs)  16.5 us
    pallas_call x10, Pallas kernels, call(): pl.pallas_call(functools.partial(body, sizes), out_shape=outs, in_specs=[...  11.1 us
    dot_general x1, matrix products, regrouped(): jnp.einsum('xyzmn,cn->xyzmc', cell_matrices, spread, preferred_element_ty...  3.32 us
    unnamed x12, local copies, waits for them, and re-layouts  1.82 us
  transfers between devices with their start and end apart: 16, of which 8 were waited for; matrix products, arithmetic and copies ran while one was open for 6% of the time, Pallas kernels for 2%

profile of v2, /device:TPU:0, one launch (start us, length us, event | category | flops | bytes accessed | tf_op | source)
XLA Modules:
  0.0 60.1 jit_solution(1736215987149457537)
XLA Ops:
  0.2 3.5 %shard_map.55 = (f32[13,13,16,256]{3,2,1,0:T(8,128)S(1)}, bf16[12,192,48]{2,1,0:T(8,128)(2,1)S(1)}, bf16[12,32,192]{2,1,0:T(8,128)(2,1)S(1)}, bf16[160,256]{1,0:T(8,128)(2,1)S(1)}, f32[8,256]{1,0:T(8,128)S(1)}) custom-call(f32[12,12,12,256]{3,2,1,0:T(8,128)} %start_ref.1, f32[1,16,1728]{2,1,0:T(8,128)} %rows_hbm.1, s32[1,16]{1,0:T(1,128)} %slots_hbm.1, ...), custom_call_target="tpu_custom_call" | custom-call | tf_op jit(solution)/shard_map/pallas_call | solution.py:89
  3.7 2.5 %collective-permute-start = (bf16[160,256]{1,0:T(8,128)(2,1)S(1)}, bf16[160,256]{1,0:T(8,128)(2,1)S(1)}, u32[]{:S(2)}, u32[]{:S(2)}) collective-permute-start(bf16[160,256]{1,0:T(8,128)(2,1)S(1)} %get-tuple-element.36), channel_id=1, source_target_pairs={{0,24},{1,25},{2,26},{3,27},{4,28},{5,29},{6,30},{7,31},{8,0},{9,1... | collective-permute-start | bytes 245768 | tf_op jit(solution)/shard_map/ppermute | solution.py:29
  6.2 3.3 %fusion.2.wide_ref = bf16[2,2,2,343,400]{4,3,2,1,0:T(8,128)(2,1)} fusion(bf16[2,2,2,343,343]{4,2,3,1,0:T(2,128)(2,1)S(1)} %copy-done, s32[400]{0:T(512)S(1)} %fusion.15), kind=kOutput, calls=%fused_computation.2 | convolution fusion | flops 753090816 | bytes 4079184 | tf_op jit(solution)/shard_map/xyzmn,cn->xyzmc/dot_general | solution.py:366
  9.5 0.7 %shard_map.57 = (bf16[160,256]{1,0:T(8,128)(2,1)}, bf16[160,256]{1,0:T(8,128)(2,1)S(1)}, bf16[32,256]{1,0:T(8,128)(2,1)}, f32[2,256]{1,0:T(2,128)S(1)}) custom-call(f32[13,13,16,256]{3,2,1,0:T(8,128)S(1)} %get-tuple-element.35.field_ref.before_ref, bf16[160,256]{1,0:T(8,128)(2,1)S(1)} %collective-permute-done.from_x_ref, f32[8,256]{1,0:T(8,128)S(1)} %get-tuple-element.37.kept_ref), custom_call_target="tpu_custom_call" | custom-call | tf_op jit(solution)/shard_map/pallas_call | solution.py:89
  10.3 4.5 %collective-permute-start.3 = (bf16[32,256]{1,0:T(8,128)(2,1)}, bf16[32,256]{1,0:T(8,128)(2,1)S(1)}, u32[]{:S(2)}, u32[]{:S(2)}) collective-permute-start(bf16[32,256]{1,0:T(8,128)(2,1)} %get-tuple-element.40), channel_id=1, source_target_pairs={{0,7},{1,6},{2,1},{3,0},{4,3},{5,2},{6,5},{7,4},{8,15},{9,14},{10,... | collective-permute-start | bytes 49160 | tf_op jit(solution)/shard_map/ppermute | solution.py:29
  16.0 1.8 %copy-done.4 = bf16[2,2,2,343,400]{4,3,2,1,0:T(8,128)(2,1)S(1)} copy-done((bf16[2,2,2,343,400]{4,3,2,1,0:T(8,128)(2,1)S(1)}, bf16[2,2,2,343,400]{4,3,2,1,0:T(8,128)(2,1)}, u32[]{:S(2)}) %copy-start.4) | copy-done | bytes 2195224
  17.8 1.0 %shard_map.56.matrix_ref = bf16[2,2,2,400,400]{4,3,2,1,0:T(8,128)(2,1)S(1)} custom-call(bf16[2,2,2,343,400]{4,3,2,1,0:T(8,128)(2,1)S(1)} %copy-done.4, bf16[400,343]{1,0:T(8,128)(2,1)S(1)} %fusion.5.spread_ref), custom_call_target="tpu_custom_call" | custom-call | tf_op jit(solution)/shard_map/pallas_call | solution.py:89
  18.8 0.6 %collective-permute-done.1.from_y_ref = bf16[160,256]{1,0:T(8,128)(2,1)S(1)} collective-permute-done((bf16[160,256]{1,0:T(8,128)(2,1)}, bf16[160,256]{1,0:T(8,128)(2,1)S(1)}, u32[]{:S(2)}, u32[]{:S(2)}) %collective-permute-start.1) | collective-permute-done | bytes 81952 | tf_op jit(solution)/shard_map/ppermute | solution.py:29
  19.8 1.4 %shard_map.58 = (f32[13,13,16,256]{3,2,1,0:T(8,128)S(1)}, f32[13,12,16,256]{3,2,1,0:T(8,128)S(1)}, bf16[160,256]{1,0:T(8,128)(2,1)S(1)}, bf16[160,256]{1,0:T(8,1...) custom-call(f32[13,13,16,256]{3,2,1,0:T(8,128)S(1)} %copy-done.2, ...), custom_call_target="tpu_custom_call", output_to_operand_aliasing={{0}: (0, {})} | custom-call | tf_op jit(solution)/shard_map/pallas_call | solution.py:89
  21.1 1.6 %collective-permute-start.4 = (bf16[160,256]{1,0:T(8,128)(2,1)S(1)}, bf16[160,256]{1,0:T(8,128)(2,1)S(1)}, u32[]{:S(2)}, u32[]{:S(2)}) collective-permute-start(bf16[160,256]{1,0:T(8,128)(2,1)S(1)} %get-tuple-element.43), channel_id=1, source_target_pairs={{0,2},{1,3},{2,4},{3,5},{4,6},{5,7},{6,0},{7,1},{8,10},{9,11},{10,... | collective-permute-start | bytes 245768 | tf_op jit(solution)/shard_map/ppermute | solution.py:29
  22.7 1.3 %collective-permute-start.5 = (bf16[160,256]{1,0:T(8,128)(2,1)S(1)}, bf16[160,256]{1,0:T(8,128)(2,1)S(1)}, u32[]{:S(2)}, u32[]{:S(2)}) collective-permute-start(bf16[160,256]{1,0:T(8,128)(2,1)S(1)} %get-tuple-element.44), channel_id=1, source_target_pairs={{0,1},{1,0},{2,3},{3,2},{4,5},{5,4},{6,7},{7,6},{8,9},{9,8},{10,11... | collective-permute-start | bytes 245768 | tf_op jit(solution)/shard_map/ppermute | solution.py:29
  24.3 6.2 %collective-permute-done.6.from_yz_ref = bf16[32,256]{1,0:T(8,128)(2,1)S(1)} collective-permute-done((bf16[32,256]{1,0:T(8,128)(2,1)S(1)}, bf16[32,256]{1,0:T(8,128)(2,1)S(1)}, u32[]{:S(2)}, u32[]{:S(2)}) %collective-permute-start.6) | collective-permute-done | bytes 16416 | tf_op jit(solution)/shard_map/ppermute | solution.py:29
  30.6 3.9 %collective-permute-done.7.from_x_ref = bf16[160,256]{1,0:T(8,128)(2,1)S(1)} collective-permute-done((bf16[160,256]{1,0:T(8,128)(2,1)S(1)}, bf16[160,256]{1,0:T(8,128)(2,1)S(1)}, u32[]{:S(2)}, u32[]{:S(2)}) %collective-permute-start.7) | collective-permute-done | bytes 81952 | tf_op jit(solution)/shard_map/ppermute | solution.py:29
  34.5 1.1 %shard_map.60 = (f32[13,13,16,256]{3,2,1,0:T(8,128)S(1)}, bf16[160,256]{1,0:T(8,128)(2,1)S(1)}, f32[8,256]{1,0:T(8,128)S(1)}) custom-call(f32[13,12,16,256]{3,2,1,0:T(8,128)S(1)} %get-tuple-element.42.block_ref, bf16[160,256]{1,0:T(8,128)(2,1)S(1)} %collective-permute-done.7.from_x_ref, bf16[160,256]{1,0:T(8,128)(2,1)S(1)} %collective-permute-done.4.from_y_ref, ...), custom_call_target="tpu_custom_call" | custom-call | tf_op jit(solution)/shard_map/pallas_call | solution.py:89
  35.5 2.1 %collective-permute-done.8.from_x_ref = bf16[160,256]{1,0:T(8,128)(2,1)S(1)} collective-permute-done((bf16[160,256]{1,0:T(8,128)(2,1)S(1)}, bf16[160,256]{1,0:T(8,128)(2,1)S(1)}, u32[]{:S(2)}, u32[]{:S(2)}) %collective-permute-start.8) | collective-permute-done | bytes 81952 | tf_op jit(solution)/shard_map/ppermute | solution.py:29
  38.2 0.7 %collective-permute-start.10 = (bf16[160,256]{1,0:T(8,128)(2,1)S(1)}, bf16[160,256]{1,0:T(8,128)(2,1)S(1)}, u32[]{:S(2)}, u32[]{:S(2)}) collective-permute-start(bf16[160,256]{1,0:T(8,128)(2,1)S(1)} %get-tuple-element.55), channel_id=1, source_target_pairs={{0,1},{1,0},{2,3},{3,2},{4,5},{5,4},{6,7},{7,6},{8,9},{9,8},{10,11... | collective-permute-start | bytes 245768 | tf_op jit(solution)/shard_map/ppermute | solution.py:29
  38.9 0.8 %collective-permute-start.11 = (bf16[32,256]{1,0:T(8,128)(2,1)S(1)}, bf16[32,256]{1,0:T(8,128)(2,1)S(1)}, u32[]{:S(2)}, u32[]{:S(2)}) collective-permute-start(bf16[32,256]{1,0:T(8,128)(2,1)S(1)} %get-tuple-element.56), channel_id=1, source_target_pairs={{0,7},{1,6},{2,1},{3,0},{4,3},{5,2},{6,5},{7,4},{8,15},{9,14},{10,... | collective-permute-start | bytes 49160 | tf_op jit(solution)/shard_map/ppermute | solution.py:29
  39.8 3.8 %collective-permute-done.11.from_yz_ref = bf16[32,256]{1,0:T(8,128)(2,1)S(1)} collective-permute-done((bf16[32,256]{1,0:T(8,128)(2,1)S(1)}, bf16[32,256]{1,0:T(8,128)(2,1)S(1)}, u32[]{:S(2)}, u32[]{:S(2)}) %collective-permute-start.11) | collective-permute-done | bytes 16416 | tf_op jit(solution)/shard_map/ppermute | solution.py:29
  43.6 1.4 %shard_map.62 = (f32[13,13,16,256]{3,2,1,0:T(8,128)S(1)}, f32[13,12,16,256]{3,2,1,0:T(8,128)S(1)}, bf16[160,256]{1,0:T(8,128)(2,1)S(1)}, bf16[160,256]{1,0:T(8,1...) custom-call(f32[13,13,16,256]{3,2,1,0:T(8,128)S(1)} %get-tuple-element.51.field_r, ...), custom_call_target="tpu_custom_call", output_to_operand_aliasing={{0}: (0, {})} | custom-call | tf_op jit(solution)/shard_map/pallas_call | solution.py:89
  45.0 1.6 %collective-permute-start.12 = (bf16[160,256]{1,0:T(8,128)(2,1)S(1)}, bf16[160,256]{1,0:T(8,128)(2,1)S(1)}, u32[]{:S(2)}, u32[]{:S(2)}) collective-permute-start(bf16[160,256]{1,0:T(8,128)(2,1)S(1)} %get-tuple-element.59), channel_id=1, source_target_pairs={{0,2},{1,3},{2,4},{3,5},{4,6},{5,7},{6,0},{7,1},{8,10},{9,11},{10,... | collective-permute-start | bytes 245768 | tf_op jit(solution)/shard_map/ppermute | solution.py:29
  46.6 1.3 %collective-permute-start.13 = (bf16[160,256]{1,0:T(8,128)(2,1)S(1)}, bf16[160,256]{1,0:T(8,128)(2,1)S(1)}, u32[]{:S(2)}, u32[]{:S(2)}) collective-permute-start(bf16[160,256]{1,0:T(8,128)(2,1)S(1)} %get-tuple-element.60), channel_id=1, source_target_pairs={{0,1},{1,0},{2,3},{3,2},{4,5},{5,4},{6,7},{7,6},{8,9},{9,8},{10,11... | collective-permute-start | bytes 245768 | tf_op jit(solution)/shard_map/ppermute | solution.py:29
  48.1 6.2 %collective-permute-done.14.from_yz_ref = bf16[32,256]{1,0:T(8,128)(2,1)S(1)} collective-permute-done((bf16[32,256]{1,0:T(8,128)(2,1)S(1)}, bf16[32,256]{1,0:T(8,128)(2,1)S(1)}, u32[]{:S(2)}, u32[]{:S(2)}) %collective-permute-start.14) | collective-permute-done | bytes 16416 | tf_op jit(solution)/shard_map/ppermute | solution.py:29
  54.5 3.9 %collective-permute-done.15.from_x_ref = bf16[160,256]{1,0:T(8,128)(2,1)S(1)} collective-permute-done((bf16[160,256]{1,0:T(8,128)(2,1)S(1)}, bf16[160,256]{1,0:T(8,128)(2,1)S(1)}, u32[]{:S(2)}, u32[]{:S(2)}) %collective-permute-start.15) | collective-permute-done | bytes 81952 | tf_op jit(solution)/shard_map/ppermute | solution.py:29
  58.3 1.8 %shard_map.64 = f32[12,12,12,256]{3,2,1,0:T(8,128)} custom-call(f32[12,12,12,256]{3,2,1,0:T(8,128)S(1)} %copy-done.3, f32[13,12,16,256]{3,2,1,0:T(8,128)S(1)} %get-tuple-element.58.block_ref, bf16[160,256]{1,0:T(8,128)(2,1)S(1)} %collective-permute-done.15.from_x_ref, bf16[160,256]{1,0:T(8,128)(2,1)S(1)} %collective-permute-done.12.from_y_ref, ...), custom_call_target="tpu_custom_call" | custom-call | tf_op jit(solution)/shard_map/pallas_call | solution.py:89
  (37 shorter events, 3.0 us)
Async XLA Ops:
  0.0 6.2 %copy-start = (bf16[2,2,2,343,343]{4,2,3,1,0:T(2,128)(2,1)S(1)}, bf16[2,2,2,343,343]{4,2,3,1,0:T(2,128)(2,1)}, u32[]{:S(2)}) copy-start(bf16[2,2,2,343,343]{4,2,3,1,0:T(2,128)(2,1)} %param.6) | copy-start | bytes 5647156
  3.7 5.8 %copy-start.1 = (f32[13,13,16,256]{3,2,1,0:T(8,128)}, f32[13,13,16,256]{3,2,1,0:T(8,128)S(1)}, u32[]{:S(2)}) copy-start(f32[13,13,16,256]{3,2,1,0:T(8,128)S(1)} %get-tuple-element.35.field_ref.before_ref) | copy-start | bytes 8306692
  3.7 5.8 %collective-permute-start = (bf16[160,256]{1,0:T(8,128)(2,1)S(1)}, bf16[160,256]{1,0:T(8,128)(2,1)S(1)}, u32[]{:S(2)}, u32[]{:S(2)}) collective-permute-start(bf16[160,256]{1,0:T(8,128)(2,1)S(1)} %get-tuple-element.36), channel_id=1, source_target_pairs={{0,24},{1,25},{2,26},{3,27},{4,28},{5,29},{6,30},{7,31},{8,0},{9,1... | collective-permute-start | bytes 245768 | tf_op jit(solution)/shard_map/ppermute | solution.py:29
  9.5 6.4 %copy-start.5 = (f32[64]{0:T(128)S(1)}, f32[64]{0:T(128)}, u32[]{:S(2)}) copy-start(f32[64]{0:T(128)} %param.9) | copy-start | bytes 772
  10.3 8.6 %collective-permute-start.3 = (bf16[32,256]{1,0:T(8,128)(2,1)}, bf16[32,256]{1,0:T(8,128)(2,1)S(1)}, u32[]{:S(2)}, u32[]{:S(2)}) collective-permute-start(bf16[32,256]{1,0:T(8,128)(2,1)} %get-tuple-element.40), channel_id=1, source_target_pairs={{0,7},{1,6},{2,1},{3,0},{4,3},{5,2},{6,5},{7,4},{8,15},{9,14},{10,... | collective-permute-start | bytes 49160 | tf_op jit(solution)/shard_map/ppermute | solution.py:29
  14.8 4.7 %collective-permute-start.1 = (bf16[160,256]{1,0:T(8,128)(2,1)}, bf16[160,256]{1,0:T(8,128)(2,1)S(1)}, u32[]{:S(2)}, u32[]{:S(2)}) collective-permute-start(bf16[160,256]{1,0:T(8,128)(2,1)} %get-tuple-element.38), channel_id=1, source_target_pairs={{0,6},{1,7},{2,0},{3,1},{4,2},{5,3},{6,4},{7,5},{8,14},{9,15},{10,... | collective-permute-start | bytes 245768 | tf_op jit(solution)/shard_map/ppermute | solution.py:29
  15.3 4.4 %collective-permute-start.2 = (bf16[160,256]{1,0:T(8,128)(2,1)S(1)}, bf16[160,256]{1,0:T(8,128)(2,1)S(1)}, u32[]{:S(2)}, u32[]{:S(2)}) collective-permute-start(bf16[160,256]{1,0:T(8,128)(2,1)S(1)} %get-tuple-element.39), channel_id=1, source_target_pairs={{0,1},{1,0},{2,3},{3,2},{4,5},{5,4},{6,7},{7,6},{8,9},{9,8},{10,11... | collective-permute-start | bytes 245768 | tf_op jit(solution)/shard_map/ppermute | solution.py:29
  16.0 1.8 %copy-start.4 = (bf16[2,2,2,343,400]{4,3,2,1,0:T(8,128)(2,1)S(1)}, bf16[2,2,2,343,400]{4,3,2,1,0:T(8,128)(2,1)}, u32[]{:S(2)}) copy-start(bf16[2,2,2,343,400]{4,3,2,1,0:T(8,128)(2,1)} %fusion.2.wide_ref) | copy-start | bytes 6585604
  17.8 2.0 %copy-start.2 = (f32[13,13,16,256]{3,2,1,0:T(8,128)S(1)}, f32[13,13,16,256]{3,2,1,0:T(8,128)}, u32[]{:S(2)}) copy-start(f32[13,13,16,256]{3,2,1,0:T(8,128)} %copy-done.1) | copy-start | bytes 8306692
  21.1 9.4 %collective-permute-start.4 = (bf16[160,256]{1,0:T(8,128)(2,1)S(1)}, bf16[160,256]{1,0:T(8,128)(2,1)S(1)}, u32[]{:S(2)}, u32[]{:S(2)}) collective-permute-start(bf16[160,256]{1,0:T(8,128)(2,1)S(1)} %get-tuple-element.43), channel_id=1, source_target_pairs={{0,2},{1,3},{2,4},{3,5},{4,6},{5,7},{6,0},{7,1},{8,10},{9,11},{10,... | collective-permute-start | bytes 245768 | tf_op jit(solution)/shard_map/ppermute | solution.py:29
  22.7 7.8 %collective-permute-start.5 = (bf16[160,256]{1,0:T(8,128)(2,1)S(1)}, bf16[160,256]{1,0:T(8,128)(2,1)S(1)}, u32[]{:S(2)}, u32[]{:S(2)}) collective-permute-start(bf16[160,256]{1,0:T(8,128)(2,1)S(1)} %get-tuple-element.44), channel_id=1, source_target_pairs={{0,1},{1,0},{2,3},{3,2},{4,5},{5,4},{6,7},{7,6},{8,9},{9,8},{10,11... | collective-permute-start | bytes 245768 | tf_op jit(solution)/shard_map/ppermute | solution.py:29
  24.1 6.4 %collective-permute-start.6 = (bf16[32,256]{1,0:T(8,128)(2,1)S(1)}, bf16[32,256]{1,0:T(8,128)(2,1)S(1)}, u32[]{:S(2)}, u32[]{:S(2)}) collective-permute-start(bf16[32,256]{1,0:T(8,128)(2,1)S(1)} %get-tuple-element.45), channel_id=1, source_target_pairs={{0,3},{1,2},{2,5},{3,4},{4,7},{5,6},{6,1},{7,0},{8,11},{9,10},{10,... | collective-permute-start | bytes 49160 | tf_op jit(solution)/shard_map/ppermute | solution.py:29
  30.6 3.9 %collective-permute-start.7 = (bf16[160,256]{1,0:T(8,128)(2,1)S(1)}, bf16[160,256]{1,0:T(8,128)(2,1)S(1)}, u32[]{:S(2)}, u32[]{:S(2)}) collective-permute-start(bf16[160,256]{1,0:T(8,128)(2,1)S(1)} %get-tuple-element.47), channel_id=1, source_target_pairs={{0,8},{1,9},{2,10},{3,11},{4,12},{5,13},{6,14},{7,15},{8,16},{9,17... | collective-permute-start | bytes 245768 | tf_op jit(solution)/shard_map/ppermute | solution.py:29
  35.5 2.1 %collective-permute-start.8 = (bf16[160,256]{1,0:T(8,128)(2,1)S(1)}, bf16[160,256]{1,0:T(8,128)(2,1)S(1)}, u32[]{:S(2)}, u32[]{:S(2)}) collective-permute-start(bf16[160,256]{1,0:T(8,128)(2,1)S(1)} %get-tuple-element.52), channel_id=1, source_target_pairs={{0,24},{1,25},{2,26},{3,27},{4,28},{5,29},{6,30},{7,31},{8,0},{9,1... | collective-permute-start | bytes 245768 | tf_op jit(solution)/shard_map/ppermute | solution.py:29
  37.7 5.9 %collective-permute-start.9 = (bf16[160,256]{1,0:T(8,128)(2,1)S(1)}, bf16[160,256]{1,0:T(8,128)(2,1)S(1)}, u32[]{:S(2)}, u32[]{:S(2)}) collective-permute-start(bf16[160,256]{1,0:T(8,128)(2,1)S(1)} %get-tuple-element.54), channel_id=1, source_target_pairs={{0,6},{1,7},{2,0},{3,1},{4,2},{5,3},{6,4},{7,5},{8,14},{9,15},{10,... | collective-permute-start | bytes 245768 | tf_op jit(solution)/shard_map/ppermute | solution.py:29
  38.2 5.4 %collective-permute-start.10 = (bf16[160,256]{1,0:T(8,128)(2,1)S(1)}, bf16[160,256]{1,0:T(8,128)(2,1)S(1)}, u32[]{:S(2)}, u32[]{:S(2)}) collective-permute-start(bf16[160,256]{1,0:T(8,128)(2,1)S(1)} %get-tuple-element.55), channel_id=1, source_target_pairs={{0,1},{1,0},{2,3},{3,2},{4,5},{5,4},{6,7},{7,6},{8,9},{9,8},{10,11... | collective-permute-start | bytes 245768 | tf_op jit(solution)/shard_map/ppermute | solution.py:29
  38.9 4.6 %collective-permute-start.11 = (bf16[32,256]{1,0:T(8,128)(2,1)S(1)}, bf16[32,256]{1,0:T(8,128)(2,1)S(1)}, u32[]{:S(2)}, u32[]{:S(2)}) collective-permute-start(bf16[32,256]{1,0:T(8,128)(2,1)S(1)} %get-tuple-element.56), channel_id=1, source_target_pairs={{0,7},{1,6},{2,1},{3,0},{4,3},{5,2},{6,5},{7,4},{8,15},{9,14},{10,... | collective-permute-start | bytes 49160 | tf_op jit(solution)/shard_map/ppermute | solution.py:29
  45.0 13.4 %copy-start.3 = (f32[12,12,12,256]{3,2,1,0:T(8,128)S(1)}, f32[12,12,12,256]{3,2,1,0:T(8,128)}, u32[]{:S(2)}) copy-start(f32[12,12,12,256]{3,2,1,0:T(8,128)} %start_ref.1) | copy-start | bytes 5308420
  45.0 9.4 %collective-permute-start.12 = (bf16[160,256]{1,0:T(8,128)(2,1)S(1)}, bf16[160,256]{1,0:T(8,128)(2,1)S(1)}, u32[]{:S(2)}, u32[]{:S(2)}) collective-permute-start(bf16[160,256]{1,0:T(8,128)(2,1)S(1)} %get-tuple-element.59), channel_id=1, source_target_pairs={{0,2},{1,3},{2,4},{3,5},{4,6},{5,7},{6,0},{7,1},{8,10},{9,11},{10,... | collective-permute-start | bytes 245768 | tf_op jit(solution)/shard_map/ppermute | solution.py:29
  46.6 7.8 %collective-permute-start.13 = (bf16[160,256]{1,0:T(8,128)(2,1)S(1)}, bf16[160,256]{1,0:T(8,128)(2,1)S(1)}, u32[]{:S(2)}, u32[]{:S(2)}) collective-permute-start(bf16[160,256]{1,0:T(8,128)(2,1)S(1)} %get-tuple-element.60), channel_id=1, source_target_pairs={{0,1},{1,0},{2,3},{3,2},{4,5},{5,4},{6,7},{7,6},{8,9},{9,8},{10,11... | collective-permute-start | bytes 245768 | tf_op jit(solution)/shard_map/ppermute | solution.py:29
  47.9 6.4 %collective-permute-start.14 = (bf16[32,256]{1,0:T(8,128)(2,1)S(1)}, bf16[32,256]{1,0:T(8,128)(2,1)S(1)}, u32[]{:S(2)}, u32[]{:S(2)}) collective-permute-start(bf16[32,256]{1,0:T(8,128)(2,1)S(1)} %get-tuple-element.61), channel_id=1, source_target_pairs={{0,3},{1,2},{2,5},{3,4},{4,7},{5,6},{6,1},{7,0},{8,11},{9,10},{10,... | collective-permute-start | bytes 49160 | tf_op jit(solution)/shard_map/ppermute | solution.py:29
  54.4 3.9 %collective-permute-start.15 = (bf16[160,256]{1,0:T(8,128)(2,1)S(1)}, bf16[160,256]{1,0:T(8,128)(2,1)S(1)}, u32[]{:S(2)}, u32[]{:S(2)}) collective-permute-start(bf16[160,256]{1,0:T(8,128)(2,1)S(1)} %get-tuple-element.63), channel_id=1, source_target_pairs={{0,8},{1,9},{2,10},{3,11},{4,12},{5,13},{6,14},{7,15},{8,16},{9,17... | collective-permute-start | bytes 245768 | tf_op jit(solution)/shard_map/ppermute | solution.py:29

commit v3 on v2

--- a/solution.py
+++ b/solution.py
@@ -55,6 +55,7 @@
         self.padded = up_to(self.side * self.side * self.group, 16)
         self.bzp = up_to(max(self.bz + 1, (cell_shape[2] - 1) * self.order + self.group), 16)
         self.locals = locals_count
+        self.few = max(n for n in (1, 2, 3, 4) if self.bx % n == 0)
         self.half = locals_count // 2
         self.quarter = locals_count // 4
         self.own = locals_count // 8
@@ -81,13 +82,13 @@
 VMEM = pltpu.VMEM
 
 
-def call(body, sizes, outs, scratch, args, spaces=None, out_spaces=None, aliases=None):
+def call(body, sizes, outs, scratch, args, spaces=None, out_spaces=None, aliases=None, extra=()):
     spaces = spaces or {}
     out_spaces = out_spaces or {}
     outs = [out_spaces.get(n, VMEM)(out.shape, out.dtype) for n, out in enumerate(outs)]
     args = [pltpu.with_memory_space_constraint(arg, spaces.get(n, VMEM)) for n, arg in enumerate(args)]
     return pl.pallas_call(
-        functools.partial(body, sizes),
+        functools.partial(body, sizes, *extra),
         out_shape=outs,
         in_specs=[pl.BlockSpec(memory_space=spaces.get(n, VMEM)) for n in range(len(args))],
         out_specs=[pl.BlockSpec(memory_space=out_spaces.get(n, VMEM)) for n in range(len(outs))],
@@ -95,10 +96,6 @@
         input_output_aliases=aliases or {},
         compiler_params=pltpu.CompilerParams(vmem_limit_bytes=LIMIT),
     )(*args)
-
-
-def own_index():
-    return (lax.axis_index("gx") * lax.axis_size("gy") + lax.axis_index("gy")) * lax.axis_size("gz") + lax.axis_index("gz")
 
 
 def local_atoms(own):
@@ -136,19 +133,23 @@
 
 
 def first_body(
-    s, start_hbm, rows_hbm, slots_hbm, ids_ref,
-    field_ref, by_node_ref, by_atom_ref, msg_ref, kept_ref,
-    start_ref, rows_ref, slots_ref, tall_ref, wide_ref, x_ref, sems, small_sems,
+    s, start_hbm, rows_hbm, slots_hbm, coupling_hbm, ids_ref,
+    field_ref, by_node_ref, by_atom_ref, msg_ref, kept_ref, weight_ref,
+    start_ref, rows_ref, slots_ref, coupling_ref, tall_ref, wide_ref, x_ref, sems, small_sems,
 ):
     small = [
         pltpu.make_async_copy(rows_hbm, rows_ref, small_sems.at[0]),
         pltpu.make_async_copy(slots_hbm, slots_ref, small_sems.at[1]),
+        pltpu.make_async_copy(coupling_hbm, coupling_ref, small_sems.at[2]),
     ]
     for copy in small:
         copy.start()
-    copies = [pltpu.make_async_copy(start_hbm.at[x], start_ref.at[x], sems.at[x]) for x in range(s.bx)]
-    for copy in copies:
-        copy.start()
+    few = s.few
+    copies = []
+    for n in range(s.bx // few):
+        span = pl.ds(n * few, few)
+        copies.append(pltpu.make_async_copy(start_hbm.at[span], start_ref.at[span], sems.at[n]))
+        copies[n].start()
     for copy in small:
         copy.wait()
     selector = (ids_ref[...] == slots_ref[...]).astype(F32)
@@ -164,16 +165,21 @@
         by_node_ref[x] = wide.astype(BF16)
         by_atom_ref[x] = wide.T[0 : 2 * s.locals].astype(BF16)
     total = jnp.zeros((s.locals, s.waves), F32)
-    for x in range(s.bx):
-        copies[x].wait()
-        plane = start_ref[x]
-        plane = jnp.concatenate([plane, jnp.zeros((s.by, s.bzp - s.bz, s.waves), F32)], axis=1)
-        field_ref[x, 0 : s.by] = plane
-        total = total + plane_sums(s, by_atom_ref, x, plane.reshape(s.by * s.bzp, s.waves))
+    for n in range(s.bx // few):
+        copies[n].wait()
+        planes = start_ref[n * few : (n + 1) * few]
+        planes = jnp.concatenate([planes, jnp.zeros((few, s.by, s.bzp - s.bz, s.waves), F32)], axis=2)
+        field_ref[n * few : (n + 1) * few, 0 : s.by] = planes
+        for x in range(few):
+            total = total + plane_sums(s, by_atom_ref, n * few + x, planes[x].reshape(s.by * s.bzp, s.waves))
     send_down_x(s, total, field_ref, x_ref, msg_ref, kept_ref)
-
-
-def down_body(s, field_ref, from_x_ref, kept_ref, y_msg_ref, z_msg_ref, yz_msg_ref, part_ref, x_ref, y_ref, z_ref, yz_ref):
+    atoms = lax.broadcasted_iota(jnp.int32, (s.own, coupling_ref.shape[1]), 1)
+    weight = jnp.sum(jnp.where(atoms == ids_ref[0 : s.own], coupling_ref[...], 0.0), axis=1, keepdims=True)
+    weight_ref[...] = jnp.broadcast_to(weight, weight_ref.shape)
+
+
+def down_body(s, field_ref, from_x_ref, kept_ref, early_ref, y_msg_ref, z_msg_ref, yz_msg_ref, part_ref, x_ref, y_ref, z_ref, yz_ref):
+    del early_ref
     x_ref[...] = from_x_ref[...].astype(F32)
     total = kept_ref[...] + get_split(x_ref, s.x_rows, s.half)
     for ref, used in ((y_ref, s.y_rows), (z_ref, s.z_rows), (yz_ref, s.yz_rows)):
@@ -197,10 +203,11 @@
 
 
 def cell_body(
-    s, before_ref, matrix_ref, from_x_ref, from_y_ref, from_z_ref, from_yz_ref, part_ref, weight_ref,
-    field_ref, block_ref, y_msg_ref, z_msg_ref, yz_msg_ref, own_ref,
-    sums_ref, x_ref, y_ref, z_ref, yz_ref,
+    s, before_ref, from_x_ref, from_y_ref, from_z_ref, from_yz_ref, part_ref, weight_ref, *refs
 ):
+    matrix_refs, refs = refs[: s.cells[0]], refs[s.cells[0] :]
+    (field_ref, block_ref, y_msg_ref, z_msg_ref, yz_msg_ref, own_ref,
+     sums_ref, x_ref, y_ref, z_ref, yz_ref) = refs
     del before_ref
     order, side, group = s.order, s.side, s.group
     cells_x, cells_y, cells_z = s.cells
@@ -226,7 +233,7 @@
                 values = values.reshape(used, s.waves)
                 if s.padded > used:
                     values = jnp.concatenate([values, jnp.zeros((s.padded - used, s.waves), F32)], axis=0)
-                product = jnp.dot(matrix_ref[i, j, k], values.astype(BF16), preferred_element_type=F32)
+                product = jnp.dot(matrix_refs[i][j, k], values.astype(BF16), preferred_element_type=F32)
                 product = product[0:used].reshape(side, side, group, s.waves)
                 x0, x1, y0, y1 = i * order, i * order + side, j * order, j * order + side
                 a, b = int(i > 0), int(j > 0)
@@ -343,29 +350,67 @@
         copy.wait()
 
 
-def node_of(s, rows):
-    return jnp.where(rows % s.group < s.side, rows // s.group * s.side + rows % s.group, -1)
-
-
-def matrix_body(s, wide_ref, spread_ref, out_ref):
-    nodes = wide_ref.shape[3]
-    for i in range(s.cells[0]):
-        for j in range(s.cells[1]):
-            for k in range(s.cells[2]):
-                for first in range(0, s.padded, 256):
-                    end = min(first + 256, s.padded)
-                    low = first // s.group * s.side // 16 * 16
-                    high = min(nodes, up_to(-(-end // s.group) * s.side, 16))
-                    part = jnp.dot(spread_ref[first:end, low:high], wide_ref[i, j, k, low:high], preferred_element_type=F32)
-                    out_ref[i, j, k, first:end] = part.astype(BF16)
-
-
-def regrouped(s, cell_matrices):
-    nodes = cell_matrices.shape[3]
-    spread = (node_of(s, lax.iota(jnp.int32, s.padded))[:, None] == lax.iota(jnp.int32, nodes)[None, :]).astype(BF16)
-    wide = jnp.einsum("xyzmn,cn->xyzmc", cell_matrices, spread, preferred_element_type=BF16)
-    shape = cell_matrices.shape[:3] + (s.padded, s.padded)
-    return call(matrix_body, s, [jax.ShapeDtypeStruct(shape, BF16)], [], [wide, spread])[0]
+def selector(count, chosen):
+    row = lax.broadcasted_iota(jnp.int32, count, 0)
+    column = lax.broadcasted_iota(jnp.int32, count, 1)
+    return chosen(row, column).astype(F32).astype(BF16)
+
+
+def matrix_body(s, part, matrix_hbm, out_ref, raw_ref, flat_ref, half_ref, sems):
+    cells_y, cells_z = s.cells[1:]
+    side, group = s.side, s.group
+    nodes = side**3
+    copies = [pltpu.make_async_copy(matrix_hbm.at[part, j], raw_ref.at[j], sems.at[j]) for j in range(cells_y)]
+    for copy in copies:
+        copy.start()
+    wide = 256 // group * side
+    spans = []
+    for first in range(0, s.padded, 256):
+        low = first // group * side // 128 * 128
+        high = min(nodes, first // group * side + wide)
+        width = min(256, s.padded - first)
+        spans.append((first, low, high, selector((high - low, width), lambda m, c, low=low, first=first: (
+            ((c + first) % group < side) & (m + low == (c + first) // group * side + (c + first) % group)))))
+    tall = 128 // group * side
+    picks = jnp.concatenate(
+        [
+            selector((128, tall * cells_z), lambda r, m, k=k: (r % group < side) & (m == (r // group * side + r % group) * cells_z + k))
+            for k in range(cells_z)
+        ],
+        axis=0,
+    )
+    for j in range(cells_y):
+        copies[j].wait()
+        flat_ref[...] = raw_ref[j].reshape(nodes * cells_z, nodes)
+        for first, low, high, spread in spans:
+            half = jnp.dot(flat_ref[:, low:high], spread, preferred_element_type=F32)
+            half_ref[:, first : first + spread.shape[1]] = half.astype(BF16)
+        for first in range(0, s.padded, 128):
+            count = min(128, s.padded - first)
+            low = first // group * side * cells_z
+            high = min(nodes * cells_z, low + tall * cells_z)
+            rows = jnp.dot(picks[:, 0 : high - low], half_ref[low:high], preferred_element_type=F32).astype(BF16)
+            for k in range(cells_z):
+                out_ref[j, k, first : first + count] = rows[128 * k : 128 * k + count]
+
+
+def regrouped(s, cell_matrices, part):
+    shape = cell_matrices.shape
+    nodes = shape[3]
+    return call(
+        matrix_body,
+        s,
+        [jax.ShapeDtypeStruct(shape[1:3] + (s.padded, s.padded), BF16)],
+        [
+            pltpu.VMEM((shape[1], nodes, shape[2], nodes), BF16),
+            pltpu.VMEM((nodes * shape[2], nodes), BF16),
+            pltpu.VMEM((nodes * shape[2], s.padded), BF16),
+            pltpu.SemaphoreType.DMA((shape[1],)),
+        ],
+        [cell_matrices.transpose(0, 1, 3, 2, 4)],
+        spaces={0: pltpu.HBM},
+        extra=(part,),
+    )[0]
 
 
 def local(wavefunctions, cell_matrices, projectors, slot_atoms, atom_coupling):
@@ -375,15 +420,13 @@
         devices *= lax.axis_size(axis)
     per_device = atom_count // devices
     s = Sizes(wavefunctions.shape, cell_matrices.shape, 8 * per_device)
-    weight = lax.dynamic_slice_in_dim(atom_coupling, own_index() * per_device, per_device)
-    weight = jnp.broadcast_to(weight[:, None], (per_device, s.waves))
     ids = local_atoms(per_device)[:, None]
-    matrices = regrouped(s, cell_matrices)
+    matrices = [regrouped(s, cell_matrices, part) for part in range(s.cells[0])]
     x_rows, y_rows, z_rows, yz_rows = (s.scratch(n) for n in (s.x_msg, s.y_msg, s.z_msg, s.yz_msg))
     wide_x, wide_y = s.scratch(s.by, s.bzp), s.scratch(s.bx, s.bzp)
     side_msgs = [s.rows(s.y_msg, BF16), s.rows(s.z_msg, BF16), s.rows(s.yz_msg, BF16)]
     plane = s.by * s.bzp
-    field, by_node, by_atom, down_x, kept = call(
+    field, by_node, by_atom, down_x, kept, weight = call(
         first_body,
         s,
         [
@@ -392,24 +435,26 @@
             jax.ShapeDtypeStruct((s.bx, 2 * s.locals, plane), BF16),
             s.rows(s.x_msg, BF16),
             s.rows(s.half),
+            s.rows(s.own),
         ],
         [
             s.scratch(s.bx, s.by, s.bz),
             pltpu.VMEM(projectors.shape, F32),
             pltpu.VMEM(slot_atoms.shape, jnp.int32),
+            pltpu.VMEM((1, atom_count), F32),
             pltpu.VMEM((s.bx * s.by * s.bz, 3 * s.locals), F32),
             pltpu.VMEM((s.bx * s.by, s.bzp, 3 * s.locals), F32),
             x_rows,
             pltpu.SemaphoreType.DMA((s.bx,)),
-            pltpu.SemaphoreType.DMA((2,)),
+            pltpu.SemaphoreType.DMA((3,)),
         ],
-        [wavefunctions, projectors, slot_atoms, ids],
-        spaces={0: pltpu.HBM, 1: pltpu.HBM, 2: pltpu.HBM},
+        [wavefunctions, projectors, slot_atoms, atom_coupling[None, :], ids],
+        spaces={0: pltpu.HBM, 1: pltpu.HBM, 2: pltpu.HBM, 3: pltpu.HBM},
     )
     for step in range(2):
         from_x = shifted(down_x, (-1, 0, 0))
         y_msg, z_msg, yz_msg, part = call(
-            down_body, s, side_msgs + [s.rows(s.own)], [x_rows, y_rows, z_rows, yz_rows], [field, from_x, kept]
+            down_body, s, side_msgs + [s.rows(s.own)], [x_rows, y_rows, z_rows, yz_rows], [field, from_x, kept, matrices[0]]
         )
         from_y = shifted(y_msg, (0, -1, 0))
         from_z = shifted(z_msg, (0, 0, -1))
@@ -419,7 +464,7 @@
             s,
             [s.extended(), jax.ShapeDtypeStruct((s.bx + 1, s.by, s.bzp, s.waves), F32)] + side_msgs + [s.rows(s.own)],
             [s.scratch(s.cells[2], s.bx + 1, s.by + 1, s.group), x_rows, y_rows, z_rows, yz_rows],
-            [field, matrices, from_x, from_y, from_z, from_yz, part, weight],
+            [field, from_x, from_y, from_z, from_yz, part, weight] + matrices,
             aliases={0: 0},
         )
         from_y = shifted(y_msg, (0, 1, 0))

time: 60.2 us -> 57 us (0.947)
  matrix products: 3.32 us -> 0 us
  Pallas kernels: 11.1 us -> 13.8 us
  starting transfers between devices: 16.5 us -> 14.5 us
  local copies, waits for them, and re-layouts: 2.13 us -> 0.18 us
  waiting for transfers between devices: 26.9 us -> 28.2 us
    dot_general x1 -> x0, matrix products: 3.32 us -> none  [regrouped(): jnp.einsum('xyzmn,cn->xyzmc', cell_matrices, spread, preferred_element_ty...]
    pallas_call x10 -> x11, Pallas kernels: 11.1 us -> 13.8 us  [call(): pl.pallas_call(functools.partial(body, sizes, *extra), out_shape=outs, in...]
    ppermute x16, starting transfers between devices: 16.5 us -> 14.5 us  [shifted(): return lax.ppermute(value, AXES, pairs)]
    unnamed x12 -> x2, local copies, waits for them, and re-layouts: 1.82 us -> 0.01 us
    ppermute x16, waiting for transfers between devices: 26.9 us -> 28.2 us  [shifted(): return lax.ppermute(value, AXES, pairs)]
  transfers between devices with their start and end apart: 16 -> 16, of which waited for: 8 -> 7; matrix products, arithmetic and copies ran while one was open for 6% -> 0% of each run, Pallas kernels for 2% -> 9%
where the time goes in v3:
time: 57 us; the launch traced here: 56.8 us
  waiting for transfers between devices  28.2 us (49%)
  starting transfers between devices  14.5 us (25%)
  Pallas kernels  13.8 us (24%)
    ppermute x16, waiting for transfers between devices, shifted(): return lax.ppermute(value, AXES, pairs)  28.2 us
    ppermute x16, starting transfers between devices, shifted(): return lax.ppermute(value, AXES, pairs)  14.5 us
    pallas_call x11, Pallas kernels, call(): pl.pallas_call(functools.partial(body, sizes, *extra), out_shape=outs, in...  13.8 us
  transfers between devices with their start and end apart: 16, of which 7 were waited for; matrix products, arithmetic and copies ran while one was open for 0% of the time, Pallas kernels for 9%

profile of v3, /device:TPU:0, one launch (start us, length us, event | category | flops | bytes accessed | tf_op | source)
XLA Modules:
  0.0 56.8 jit_solution(14176979994907212295)
XLA Ops:
  0.2 3.0 %shard_map.55 = (f32[13,13,16,256]{3,2,1,0:T(8,128)S(1)}, bf16[12,192,48]{2,1,0:T(8,128)(2,1)S(1)}, bf16[12,32,192]{2,1,0:T(8,128)(2,1)S(1)}, bf16[160,256]{1,0:...) custom-call(f32[12,12,12,256]{3,2,1,0:T(8,128)} %start_ref.1, f32[1,16,1728]{2,1,0:T(8,128)} %rows_hbm.1, ...), custom_call_target="tpu_custom_call" | custom-call | tf_op jit(solution)/shard_map/pallas_call | solution.py:90
  3.2 2.5 %collective-permute-start = (bf16[160,256]{1,0:T(8,128)(2,1)S(1)}, bf16[160,256]{1,0:T(8,128)(2,1)S(1)}, u32[]{:S(2)}, u32[]{:S(2)}) collective-permute-start(bf16[160,256]{1,0:T(8,128)(2,1)S(1)} %get-tuple-element.37), channel_id=1, source_target_pairs={{0,24},{1,25},{2,26},{3,27},{4,28},{5,29},{6,30},{7,31},{8,0},{9,1... | collective-permute-start | bytes 245768 | tf_op jit(solution)/shard_map/ppermute | solution.py:29
  5.6 2.4 %shard_map.56.early_ref.refs_0_ = bf16[2,2,400,400]{3,2,1,0:T(8,128)(2,1)S(1)} custom-call(bf16[2,2,343,2,343]{4,3,2,1,0:T(2,128)(2,1)} %bitcast.19), custom_call_target="tpu_custom_call" | custom-call | tf_op jit(solution)/shard_map/pallas_call | solution.py:90
  8.2 3.7 %collective-permute-start.1 = (bf16[160,256]{1,0:T(8,128)(2,1)S(1)}, bf16[160,256]{1,0:T(8,128)(2,1)S(1)}, u32[]{:S(2)}, u32[]{:S(2)}) collective-permute-start(bf16[160,256]{1,0:T(8,128)(2,1)S(1)} %get-tuple-element.39), channel_id=1, source_target_pairs={{0,6},{1,7},{2,0},{3,1},{4,2},{5,3},{6,4},{7,5},{8,14},{9,15},{10,... | collective-permute-start | bytes 245768 | tf_op jit(solution)/shard_map/ppermute | solution.py:29
  11.9 1.5 %collective-permute-start.2 = (bf16[160,256]{1,0:T(8,128)(2,1)S(1)}, bf16[160,256]{1,0:T(8,128)(2,1)S(1)}, u32[]{:S(2)}, u32[]{:S(2)}) collective-permute-start(bf16[160,256]{1,0:T(8,128)(2,1)S(1)} %get-tuple-element.40), channel_id=1, source_target_pairs={{0,1},{1,0},{2,3},{3,2},{4,5},{5,4},{6,7},{7,6},{8,9},{9,8},{10,11... | collective-permute-start | bytes 245768 | tf_op jit(solution)/shard_map/ppermute | solution.py:29
  13.4 0.4 collective-permute-start.3
  13.8 2.4 %shard_map.58.refs_1_ = bf16[2,2,400,400]{3,2,1,0:T(8,128)(2,1)S(1)} custom-call(bf16[2,2,343,2,343]{4,3,2,1,0:T(2,128)(2,1)} %bitcast.20), custom_call_target="tpu_custom_call" | custom-call | tf_op jit(solution)/shard_map/pallas_call | solution.py:90
  16.2 1.8 %collective-permute-done.3.from_yz_ref = bf16[32,256]{1,0:T(8,128)(2,1)S(1)} collective-permute-done((bf16[32,256]{1,0:T(8,128)(2,1)S(1)}, bf16[32,256]{1,0:T(8,128)(2,1)S(1)}, u32[]{:S(2)}, u32[]{:S(2)}) %collective-permute-start.3) | collective-permute-done | bytes 16416 | tf_op jit(solution)/shard_map/ppermute | solution.py:29
  18.0 1.4 %shard_map.59 = (f32[13,13,16,256]{3,2,1,0:T(8,128)S(1)}, f32[13,12,16,256]{3,2,1,0:T(8,128)S(1)}, bf16[160,256]{1,0:T(8,128)(2,1)S(1)}, bf16[160,256]{1,0:T(8,1...) custom-call(f32[13,13,16,256]{3,2,1,0:T(8,128)S(1)} %get-tuple-element.36.field_r, ...), custom_call_target="tpu_custom_call", output_to_operand_aliasing={{0}: (0, {})} | custom-call | tf_op jit(solution)/shard_map/pallas_call | solution.py:90
  19.4 1.3 %collective-permute-start.5 = (bf16[160,256]{1,0:T(8,128)(2,1)S(1)}, bf16[160,256]{1,0:T(8,128)(2,1)S(1)}, u32[]{:S(2)}, u32[]{:S(2)}) collective-permute-start(bf16[160,256]{1,0:T(8,128)(2,1)S(1)} %get-tuple-element.46), channel_id=1, source_target_pairs={{0,1},{1,0},{2,3},{3,2},{4,5},{5,4},{6,7},{7,6},{8,9},{9,8},{10,11... | collective-permute-start | bytes 245768 | tf_op jit(solution)/shard_map/ppermute | solution.py:29
  20.9 6.3 %collective-permute-done.6.from_yz_ref = bf16[32,256]{1,0:T(8,128)(2,1)S(1)} collective-permute-done((bf16[32,256]{1,0:T(8,128)(2,1)S(1)}, bf16[32,256]{1,0:T(8,128)(2,1)S(1)}, u32[]{:S(2)}, u32[]{:S(2)}) %collective-permute-start.6) | collective-permute-done | bytes 16416 | tf_op jit(solution)/shard_map/ppermute | solution.py:29
  27.3 3.9 %collective-permute-done.7.from_x_ref = bf16[160,256]{1,0:T(8,128)(2,1)S(1)} collective-permute-done((bf16[160,256]{1,0:T(8,128)(2,1)S(1)}, bf16[160,256]{1,0:T(8,128)(2,1)S(1)}, u32[]{:S(2)}, u32[]{:S(2)}) %collective-permute-start.7) | collective-permute-done | bytes 81952 | tf_op jit(solution)/shard_map/ppermute | solution.py:29
  31.1 1.1 %shard_map.61 = (f32[13,13,16,256]{3,2,1,0:T(8,128)S(1)}, bf16[160,256]{1,0:T(8,128)(2,1)S(1)}, f32[8,256]{1,0:T(8,128)S(1)}) custom-call(f32[13,12,16,256]{3,2,1,0:T(8,128)S(1)} %get-tuple-element.44.block_ref, bf16[160,256]{1,0:T(8,128)(2,1)S(1)} %collective-permute-done.7.from_x_ref, bf16[160,256]{1,0:T(8,128)(2,1)S(1)} %collective-permute-done.4.from_y_ref, ...), custom_call_target="tpu_custom_call" | custom-call | tf_op jit(solution)/shard_map/pallas_call | solution.py:90
  32.2 2.1 %collective-permute-done.8.from_x_ref = bf16[160,256]{1,0:T(8,128)(2,1)S(1)} collective-permute-done((bf16[160,256]{1,0:T(8,128)(2,1)S(1)}, bf16[160,256]{1,0:T(8,128)(2,1)S(1)}, u32[]{:S(2)}, u32[]{:S(2)}) %collective-permute-start.8) | collective-permute-done | bytes 81952 | tf_op jit(solution)/shard_map/ppermute | solution.py:29
  34.4 1.3 %collective-permute-start.9 = (bf16[160,256]{1,0:T(8,128)(2,1)S(1)}, bf16[160,256]{1,0:T(8,128)(2,1)S(1)}, u32[]{:S(2)}, u32[]{:S(2)}) collective-permute-start(bf16[160,256]{1,0:T(8,128)(2,1)S(1)} %get-tuple-element.56), channel_id=1, source_target_pairs={{0,6},{1,7},{2,0},{3,1},{4,2},{5,3},{6,4},{7,5},{8,14},{9,15},{10,... | collective-permute-start | bytes 245768 | tf_op jit(solution)/shard_map/ppermute | solution.py:29
  35.7 1.5 %collective-permute-start.10 = (bf16[160,256]{1,0:T(8,128)(2,1)S(1)}, bf16[160,256]{1,0:T(8,128)(2,1)S(1)}, u32[]{:S(2)}, u32[]{:S(2)}) collective-permute-start(bf16[160,256]{1,0:T(8,128)(2,1)S(1)} %get-tuple-element.57), channel_id=1, source_target_pairs={{0,1},{1,0},{2,3},{3,2},{4,5},{5,4},{6,7},{7,6},{8,9},{9,8},{10,11... | collective-permute-start | bytes 245768 | tf_op jit(solution)/shard_map/ppermute | solution.py:29
  37.2 0.4 collective-permute-start.11
  37.6 4.2 %collective-permute-done.11.from_yz_ref = bf16[32,256]{1,0:T(8,128)(2,1)S(1)} collective-permute-done((bf16[32,256]{1,0:T(8,128)(2,1)S(1)}, bf16[32,256]{1,0:T(8,128)(2,1)S(1)}, u32[]{:S(2)}, u32[]{:S(2)}) %collective-permute-start.11) | collective-permute-done | bytes 16416 | tf_op jit(solution)/shard_map/ppermute | solution.py:29
  41.8 1.4 %shard_map.63 = (f32[13,13,16,256]{3,2,1,0:T(8,128)S(1)}, f32[13,12,16,256]{3,2,1,0:T(8,128)S(1)}, bf16[160,256]{1,0:T(8,128)(2,1)S(1)}, bf16[160,256]{1,0:T(8,1...) custom-call(f32[13,13,16,256]{3,2,1,0:T(8,128)S(1)} %get-tuple-element.53.field_r, ...), custom_call_target="tpu_custom_call", output_to_operand_aliasing={{0}: (0, {})} | custom-call | tf_op jit(solution)/shard_map/pallas_call | solution.py:90
  43.4 1.2 %collective-permute-start.13 = (bf16[160,256]{1,0:T(8,128)(2,1)S(1)}, bf16[160,256]{1,0:T(8,128)(2,1)S(1)}, u32[]{:S(2)}, u32[]{:S(2)}) collective-permute-start(bf16[160,256]{1,0:T(8,128)(2,1)S(1)} %get-tuple-element.62), channel_id=1, source_target_pairs={{0,1},{1,0},{2,3},{3,2},{4,5},{5,4},{6,7},{7,6},{8,9},{9,8},{10,11... | collective-permute-start | bytes 245768 | tf_op jit(solution)/shard_map/ppermute | solution.py:29
  44.6 0.3 collective-permute-start.14
  44.9 6.1 %collective-permute-done.14.from_yz_ref = bf16[32,256]{1,0:T(8,128)(2,1)S(1)} collective-permute-done((bf16[32,256]{1,0:T(8,128)(2,1)S(1)}, bf16[32,256]{1,0:T(8,128)(2,1)S(1)}, u32[]{:S(2)}, u32[]{:S(2)}) %collective-permute-start.14) | collective-permute-done | bytes 16416 | tf_op jit(solution)/shard_map/ppermute | solution.py:29
  51.2 3.9 %collective-permute-done.15.from_x_ref = bf16[160,256]{1,0:T(8,128)(2,1)S(1)} collective-permute-done((bf16[160,256]{1,0:T(8,128)(2,1)S(1)}, bf16[160,256]{1,0:T(8,128)(2,1)S(1)}, u32[]{:S(2)}, u32[]{:S(2)}) %collective-permute-start.15) | collective-permute-done | bytes 81952 | tf_op jit(solution)/shard_map/ppermute | solution.py:29
  55.0 1.8 %shard_map.65 = f32[12,12,12,256]{3,2,1,0:T(8,128)} custom-call(f32[12,12,12,256]{3,2,1,0:T(8,128)S(1)} %copy-done, f32[13,12,16,256]{3,2,1,0:T(8,128)S(1)} %get-tuple-element.60.block_ref, bf16[160,256]{1,0:T(8,128)(2,1)S(1)} %collective-permute-done.15.from_x_ref, bf16[160,256]{1,0:T(8,128)(2,1)S(1)} %collective-permute-done.12.from_y_ref, ...), custom_call_target="tpu_custom_call" | custom-call | tf_op jit(solution)/shard_map/pallas_call | solution.py:90
  (23 shorter events, 1.0 us)
Async XLA Ops:
  3.2 4.9 %collective-permute-start = (bf16[160,256]{1,0:T(8,128)(2,1)S(1)}, bf16[160,256]{1,0:T(8,128)(2,1)S(1)}, u32[]{:S(2)}, u32[]{:S(2)}) collective-permute-start(bf16[160,256]{1,0:T(8,128)(2,1)S(1)} %get-tuple-element.37), channel_id=1, source_target_pairs={{0,24},{1,25},{2,26},{3,27},{4,28},{5,29},{6,30},{7,31},{8,0},{9,1... | collective-permute-start | bytes 245768 | tf_op jit(solution)/shard_map/ppermute | solution.py:29
  8.2 9.8 %collective-permute-start.1 = (bf16[160,256]{1,0:T(8,128)(2,1)S(1)}, bf16[160,256]{1,0:T(8,128)(2,1)S(1)}, u32[]{:S(2)}, u32[]{:S(2)}) collective-permute-start(bf16[160,256]{1,0:T(8,128)(2,1)S(1)} %get-tuple-element.39), channel_id=1, source_target_pairs={{0,6},{1,7},{2,0},{3,1},{4,2},{5,3},{6,4},{7,5},{8,14},{9,15},{10,... | collective-permute-start | bytes 245768 | tf_op jit(solution)/shard_map/ppermute | solution.py:29
  11.9 6.1 %collective-permute-start.2 = (bf16[160,256]{1,0:T(8,128)(2,1)S(1)}, bf16[160,256]{1,0:T(8,128)(2,1)S(1)}, u32[]{:S(2)}, u32[]{:S(2)}) collective-permute-start(bf16[160,256]{1,0:T(8,128)(2,1)S(1)} %get-tuple-element.40), channel_id=1, source_target_pairs={{0,1},{1,0},{2,3},{3,2},{4,5},{5,4},{6,7},{7,6},{8,9},{9,8},{10,11... | collective-permute-start | bytes 245768 | tf_op jit(solution)/shard_map/ppermute | solution.py:29
  13.4 4.6 %collective-permute-start.3 = (bf16[32,256]{1,0:T(8,128)(2,1)S(1)}, bf16[32,256]{1,0:T(8,128)(2,1)S(1)}, u32[]{:S(2)}, u32[]{:S(2)}) collective-permute-start(bf16[32,256]{1,0:T(8,128)(2,1)S(1)} %get-tuple-element.41), channel_id=1, source_target_pairs={{0,7},{1,6},{2,1},{3,0},{4,3},{5,2},{6,5},{7,4},{8,15},{9,14},{10,... | collective-permute-start | bytes 49160 | tf_op jit(solution)/shard_map/ppermute | solution.py:29
  19.4 7.8 %collective-permute-start.4 = (bf16[160,256]{1,0:T(8,128)(2,1)S(1)}, bf16[160,256]{1,0:T(8,128)(2,1)S(1)}, u32[]{:S(2)}, u32[]{:S(2)}) collective-permute-start(bf16[160,256]{1,0:T(8,128)(2,1)S(1)} %get-tuple-element.45), channel_id=1, source_target_pairs={{0,2},{1,3},{2,4},{3,5},{4,6},{5,7},{6,0},{7,1},{8,10},{9,11},{10,... | collective-permute-start | bytes 245768 | tf_op jit(solution)/shard_map/ppermute | solution.py:29
  19.4 7.8 %collective-permute-start.5 = (bf16[160,256]{1,0:T(8,128)(2,1)S(1)}, bf16[160,256]{1,0:T(8,128)(2,1)S(1)}, u32[]{:S(2)}, u32[]{:S(2)}) collective-permute-start(bf16[160,256]{1,0:T(8,128)(2,1)S(1)} %get-tuple-element.46), channel_id=1, source_target_pairs={{0,1},{1,0},{2,3},{3,2},{4,5},{5,4},{6,7},{7,6},{8,9},{9,8},{10,11... | collective-permute-start | bytes 245768 | tf_op jit(solution)/shard_map/ppermute | solution.py:29
  20.7 6.4 %collective-permute-start.6 = (bf16[32,256]{1,0:T(8,128)(2,1)S(1)}, bf16[32,256]{1,0:T(8,128)(2,1)S(1)}, u32[]{:S(2)}, u32[]{:S(2)}) collective-permute-start(bf16[32,256]{1,0:T(8,128)(2,1)S(1)} %get-tuple-element.47), channel_id=1, source_target_pairs={{0,3},{1,2},{2,5},{3,4},{4,7},{5,6},{6,1},{7,0},{8,11},{9,10},{10,... | collective-permute-start | bytes 49160 | tf_op jit(solution)/shard_map/ppermute | solution.py:29
  27.2 3.9 %collective-permute-start.7 = (bf16[160,256]{1,0:T(8,128)(2,1)S(1)}, bf16[160,256]{1,0:T(8,128)(2,1)S(1)}, u32[]{:S(2)}, u32[]{:S(2)}) collective-permute-start(bf16[160,256]{1,0:T(8,128)(2,1)S(1)} %get-tuple-element.49), channel_id=1, source_target_pairs={{0,8},{1,9},{2,10},{3,11},{4,12},{5,13},{6,14},{7,15},{8,16},{9,17... | collective-permute-start | bytes 245768 | tf_op jit(solution)/shard_map/ppermute | solution.py:29
  32.2 2.1 %collective-permute-start.8 = (bf16[160,256]{1,0:T(8,128)(2,1)S(1)}, bf16[160,256]{1,0:T(8,128)(2,1)S(1)}, u32[]{:S(2)}, u32[]{:S(2)}) collective-permute-start(bf16[160,256]{1,0:T(8,128)(2,1)S(1)} %get-tuple-element.54), channel_id=1, source_target_pairs={{0,24},{1,25},{2,26},{3,27},{4,28},{5,29},{6,30},{7,31},{8,0},{9,1... | collective-permute-start | bytes 245768 | tf_op jit(solution)/shard_map/ppermute | solution.py:29
  34.4 7.4 %collective-permute-start.9 = (bf16[160,256]{1,0:T(8,128)(2,1)S(1)}, bf16[160,256]{1,0:T(8,128)(2,1)S(1)}, u32[]{:S(2)}, u32[]{:S(2)}) collective-permute-start(bf16[160,256]{1,0:T(8,128)(2,1)S(1)} %get-tuple-element.56), channel_id=1, source_target_pairs={{0,6},{1,7},{2,0},{3,1},{4,2},{5,3},{6,4},{7,5},{8,14},{9,15},{10,... | collective-permute-start | bytes 245768 | tf_op jit(solution)/shard_map/ppermute | solution.py:29
  35.7 6.1 %collective-permute-start.10 = (bf16[160,256]{1,0:T(8,128)(2,1)S(1)}, bf16[160,256]{1,0:T(8,128)(2,1)S(1)}, u32[]{:S(2)}, u32[]{:S(2)}) collective-permute-start(bf16[160,256]{1,0:T(8,128)(2,1)S(1)} %get-tuple-element.57), channel_id=1, source_target_pairs={{0,1},{1,0},{2,3},{3,2},{4,5},{5,4},{6,7},{7,6},{8,9},{9,8},{10,11... | collective-permute-start | bytes 245768 | tf_op jit(solution)/shard_map/ppermute | solution.py:29
  37.2 4.6 %collective-permute-start.11 = (bf16[32,256]{1,0:T(8,128)(2,1)S(1)}, bf16[32,256]{1,0:T(8,128)(2,1)S(1)}, u32[]{:S(2)}, u32[]{:S(2)}) collective-permute-start(bf16[32,256]{1,0:T(8,128)(2,1)S(1)} %get-tuple-element.58), channel_id=1, source_target_pairs={{0,7},{1,6},{2,1},{3,0},{4,3},{5,2},{6,5},{7,4},{8,15},{9,14},{10,... | collective-permute-start | bytes 49160 | tf_op jit(solution)/shard_map/ppermute | solution.py:29
  43.2 11.8 %copy-start = (f32[12,12,12,256]{3,2,1,0:T(8,128)S(1)}, f32[12,12,12,256]{3,2,1,0:T(8,128)}, u32[]{:S(2)}) copy-start(f32[12,12,12,256]{3,2,1,0:T(8,128)} %start_ref.1) | copy-start | bytes 5308420
  43.2 7.8 %collective-permute-start.12 = (bf16[160,256]{1,0:T(8,128)(2,1)S(1)}, bf16[160,256]{1,0:T(8,128)(2,1)S(1)}, u32[]{:S(2)}, u32[]{:S(2)}) collective-permute-start(bf16[160,256]{1,0:T(8,128)(2,1)S(1)} %get-tuple-element.61), channel_id=1, source_target_pairs={{0,2},{1,3},{2,4},{3,5},{4,6},{5,7},{6,0},{7,1},{8,10},{9,11},{10,... | collective-permute-start | bytes 245768 | tf_op jit(solution)/shard_map/ppermute | solution.py:29
  43.4 7.7 %collective-permute-start.13 = (bf16[160,256]{1,0:T(8,128)(2,1)S(1)}, bf16[160,256]{1,0:T(8,128)(2,1)S(1)}, u32[]{:S(2)}, u32[]{:S(2)}) collective-permute-start(bf16[160,256]{1,0:T(8,128)(2,1)S(1)} %get-tuple-element.62), channel_id=1, source_target_pairs={{0,1},{1,0},{2,3},{3,2},{4,5},{5,4},{6,7},{7,6},{8,9},{9,8},{10,11... | collective-permute-start | bytes 245768 | tf_op jit(solution)/shard_map/ppermute | solution.py:29
  44.6 6.4 %collective-permute-start.14 = (bf16[32,256]{1,0:T(8,128)(2,1)S(1)}, bf16[32,256]{1,0:T(8,128)(2,1)S(1)}, u32[]{:S(2)}, u32[]{:S(2)}) collective-permute-start(bf16[32,256]{1,0:T(8,128)(2,1)S(1)} %get-tuple-element.63), channel_id=1, source_target_pairs={{0,3},{1,2},{2,5},{3,4},{4,7},{5,6},{6,1},{7,0},{8,11},{9,10},{10,... | collective-permute-start | bytes 49160 | tf_op jit(solution)/shard_map/ppermute | solution.py:29
  51.1 3.9 %collective-permute-start.15 = (bf16[160,256]{1,0:T(8,128)(2,1)S(1)}, bf16[160,256]{1,0:T(8,128)(2,1)S(1)}, u32[]{:S(2)}, u32[]{:S(2)}) collective-permute-start(bf16[160,256]{1,0:T(8,128)(2,1)S(1)} %get-tuple-element.65), channel_id=1, source_target_pairs={{0,8},{1,9},{2,10},{3,11},{4,12},{5,13},{6,14},{7,15},{8,16},{9,17... | collective-permute-start | bytes 245768 | tf_op jit(solution)/shard_map/ppermute | solution.py:29

commit v4 on v3

v4 whole, which is shorter than its diff:
```python
import functools

import jax
import jax.numpy as jnp
from jax import lax
from jax.experimental import pallas as pl
from jax.experimental.pallas import tpu as pltpu
from jax.sharding import PartitionSpec as P

AXES = ("gx", "gy", "gz")
F32 = jnp.float32
BF16 = jnp.bfloat16
LIMIT = 12 * 1024 * 1024


def up_to(value, unit):
    return -(-value // unit) * unit


def shifted(value, shift):
    sizes = [lax.axis_size(axis) for axis in AXES]
    pairs = []
    for x in range(sizes[0]):
        for y in range(sizes[1]):
            for z in range(sizes[2]):
                here = (x * sizes[1] + y) * sizes[2] + z
                there = [(p + s) % n for p, s, n in zip((x, y, z), shift, sizes)]
                pairs.append((here, (there[0] * sizes[1] + there[1]) * sizes[2] + there[2]))
    return lax.ppermute(value, AXES, pairs)


def halves(value):
    high = value.astype(BF16).astype(F32)
    return high, value - high


def put_split(rows_ref, start, value):
    count = value.shape[0]
    high, low = halves(value)
    rows_ref[start : start + count] = high
    rows_ref[start + count : start + 2 * count] = low


def get_split(rows_ref, start, count):
    return rows_ref[start : start + count] + rows_ref[start + count : start + 2 * count]


class Sizes:
    def __init__(self, field_shape, cell_shape, own, pairs):
        self.bx, self.by, self.bz, self.waves = field_shape
        self.cells = cell_shape[:3]
        self.order = self.bx // cell_shape[0]
        self.side = self.order + 1
        self.group = up_to(self.side, 8)
        self.padded = up_to(self.side * self.side * self.group, 16)
        self.bzp = up_to(max(self.bz + 1, (cell_shape[2] - 1) * self.order + self.group), 16)
        self.few = max(n for n in (1, 2, 3, 4) if self.bx % n == 0)
        self.pairs = pairs
        self.own = own
        self.locals = 8 * own
        self.span = self.bz + 1
        self.z_rows = self.bx * self.by
        self.x_rows = self.by * self.span
        self.y_rows = self.bx * self.span
        self.x_msg = up_to(self.x_rows + 4 * own, 16)
        self.y_msg = up_to(self.y_rows + 4 * own, 16)
        self.xy_msg = up_to(self.span + 4 * own, 16)
        self.z_plane = up_to(self.z_rows, 16)
        self.z_sums = up_to(8 * own, 16)
        self.z_both = up_to(self.z_rows + 8 * own, 16)

    def extended(self):
        return jax.ShapeDtypeStruct((self.bx + 1, self.by + 1, self.bzp, self.waves), F32)

    def block(self):
        return jax.ShapeDtypeStruct((self.bx, self.by, self.bzp, self.waves), F32)

    def rows(self, count, dtype=F32):
        return jax.ShapeDtypeStruct((count, self.waves), dtype)

    def scratch(self, *shape):
        return pltpu.VMEM(shape + (self.waves,), F32)

    def z_msgs(self, down, up):
        return [self.rows(down + up, BF16)] if self.pairs else [self.rows(down, BF16), self.rows(up, BF16)]

    def side_msgs(self):
        return [self.rows(n, BF16) for n in (self.x_msg, self.y_msg, self.xy_msg)]

    def side_rows(self):
        return [self.scratch(n) for n in (self.x_msg, self.y_msg, self.xy_msg)]


VMEM = pltpu.VMEM


def call(body, sizes, outs, scratch, args, spaces=None, out_spaces=None, aliases=None, extra=()):
    spaces = spaces or {}
    out_spaces = out_spaces or {}
    outs = [out_spaces.get(n, VMEM)(out.shape, out.dtype) for n, out in enumerate(outs)]
    args = [pltpu.with_memory_space_constraint(arg, spaces.get(n, VMEM)) for n, arg in enumerate(args)]
    return pl.pallas_call(
        functools.partial(body, sizes, *extra),
        out_shape=outs,
        in_specs=[pl.BlockSpec(memory_space=spaces.get(n, VMEM)) for n in range(len(args))],
        out_specs=[pl.BlockSpec(memory_space=out_spaces.get(n, VMEM)) for n in range(len(outs))],
        scratch_shapes=scratch,
        input_output_aliases=aliases or {},
        compiler_params=pltpu.CompilerParams(vmem_limit_bytes=LIMIT),
    )(*args)


def local_atoms(own):
    sizes = [lax.axis_size(axis) for axis in AXES]
    here = [lax.axis_index(axis) for axis in AXES]
    ids = []
    for dz in (1, 0):
        for dx in (1, 0):
            for dy in (1, 0):
                x, y, z = (lax.rem(h + n - d, n) for h, n, d in zip(here, sizes, (dx, dy, dz)))
                owner = (x * sizes[1] + y) * sizes[2] + z
                ids += [owner * own + a for a in range(own)]
    return jnp.stack(ids).astype(jnp.int32)


def blank(rows_ref, first):
    count = rows_ref.shape[0] - first
    if count:
        rows_ref[first:] = jnp.zeros((count,) + rows_ref.shape[1:], F32)


def split_sums(by_atom, count, field):
    high = field.astype(BF16)
    low = (field - high.astype(F32)).astype(BF16)
    with_high = jnp.dot(by_atom, high, preferred_element_type=F32)
    with_low = jnp.dot(by_atom[0:count], low, preferred_element_type=F32)
    return with_high[0:count] + with_high[count : 2 * count] + with_low


def put_z(s, msg_refs, down_ref, up_ref):
    if s.pairs:
        count = down_ref.shape[0]
        msg_refs[0][0:count] = down_ref[...].astype(BF16)
        msg_refs[0][count:] = up_ref[...].astype(BF16)
    else:
        msg_refs[0][...] = down_ref[...].astype(BF16)
        msg_refs[1][...] = up_ref[...].astype(BF16)


def get_z(s, msg_refs, above_ref, below_ref):
    if s.pairs:
        count = above_ref.shape[0]
        above_ref[...] = msg_refs[0][0:count].astype(F32)
        below_ref[...] = msg_refs[0][count:].astype(F32)
    else:
        above_ref[...] = msg_refs[0][...].astype(F32)
        below_ref[...] = msg_refs[1][...].astype(F32)


def columns(s, totals):
    own, half = s.own, 4 * s.own
    return [
        jnp.concatenate([totals[n * own : (n + 1) * own], totals[half + n * own : half + (n + 1) * own]], axis=0) for n in range(4)
    ]


def from_columns(s, parts):
    own = s.own
    return jnp.concatenate([part[0:own] for part in parts] + [part[own : 2 * own] for part in parts], axis=0)


def first_body(
    s, start_hbm, rows_hbm, slots_hbm, coupling_hbm, ids_ref,
    field_ref, by_node_ref, by_atom_ref, line_ref, *refs
):
    *msg_refs, total_ref, weight_ref, start_ref, rows_ref, slots_ref, coupling_ref, tall_ref, wide_ref, low_ref, high_ref, sems, small_sems = refs
    small = [
        pltpu.make_async_copy(rows_hbm, rows_ref, small_sems.at[0]),
        pltpu.make_async_copy(slots_hbm, slots_ref, small_sems.at[1]),
        pltpu.make_async_copy(coupling_hbm, coupling_ref, small_sems.at[2]),
    ]
    for copy in small:
        copy.start()
    few = s.few
    copies = []
    for n in range(s.bx // few):
        span = pl.ds(n * few, few)
        copies.append(pltpu.make_async_copy(start_hbm.at[span], start_ref.at[span], sems.at[n]))
        copies[n].start()
    for copy in small:
        copy.wait()
    selector = (ids_ref[...] == slots_ref[...]).astype(F32)
    rows = jnp.dot(selector, rows_ref[0], precision=lax.Precision.HIGHEST, preferred_element_type=F32)
    high, low = halves(rows)
    low = low.astype(BF16).astype(F32)
    tall_ref[...] = jnp.concatenate([high, low, high], axis=0).T
    wide_ref[:, s.bz : s.bzp, :] = jnp.zeros((s.bx * s.by, s.bzp - s.bz, 3 * s.locals), F32)
    for g in range(s.bx * s.by):
        wide_ref[g, 0 : s.bz, :] = tall_ref[g * s.bz : (g + 1) * s.bz, :]
    for x in range(s.bx):
        wide = wide_ref[x * s.by : (x + 1) * s.by].reshape(s.by * s.bzp, 3 * s.locals)
        by_node_ref[x] = wide.astype(BF16)
        by_atom_ref[x] = wide.T[0 : 2 * s.locals].astype(BF16)
    line_ref[...] = wide_ref[:, 0, :]
    total = jnp.zeros((s.locals, s.waves), F32)
    for n in range(s.bx // few):
        copies[n].wait()
        planes = start_ref[n * few : (n + 1) * few]
        planes = jnp.concatenate([planes, jnp.zeros((few, s.by, s.bzp - s.bz, s.waves), F32)], axis=2)
        field_ref[n * few : (n + 1) * few, 0 : s.by] = planes
        for x in range(few):
            total = total + split_sums(by_atom_ref[n * few + x], s.locals, planes[x].reshape(s.by * s.bzp, s.waves))
    total_ref[...] = total
    half = 4 * s.own
    for x in range(s.bx):
        low_ref[x * s.by : (x + 1) * s.by] = field_ref[x, 0 : s.by, 0, :]
    blank(low_ref, s.z_rows)
    blank(high_ref, 0)
    put_split(low_ref, s.z_rows, total[0:half])
    put_split(high_ref, 0, total[half:])
    put_z(s, msg_refs, low_ref, high_ref)
    atoms = lax.broadcasted_iota(jnp.int32, (s.locals, coupling_ref.shape[1]), 1)
    weight = jnp.sum(jnp.where(atoms == ids_ref[...], coupling_ref[...], 0.0), axis=1, keepdims=True)
    weight_ref[...] = jnp.broadcast_to(weight, weight_ref.shape)


def put_sides(s, field_ref, x, y, x_ref, y_ref, xy_ref):
    for n in range(s.by):
        x_ref[n * s.span : (n + 1) * s.span] = field_ref[x, n, 0 : s.span, :]
    for n in range(s.bx):
        y_ref[n * s.span : (n + 1) * s.span] = field_ref[n, y, 0 : s.span, :]
    xy_ref[0 : s.span] = field_ref[x, y, 0 : s.span, :]
    for ref, used in ((x_ref, s.x_rows), (y_ref, s.y_rows), (xy_ref, s.span)):
        blank(ref, used)


def send_sides(s, x_ref, y_ref, xy_ref, msg_refs, parts):
    for ref, used, part, msg_ref in zip((x_ref, y_ref, xy_ref), (s.x_rows, s.y_rows, s.span), parts, msg_refs):
        put_split(ref, used, part)
        msg_ref[...] = ref[...].astype(BF16)


def get_sides(s, received, x_ref, y_ref, xy_ref):
    parts = []
    for ref, used, msg_ref in zip((x_ref, y_ref, xy_ref), (s.x_rows, s.y_rows, s.span), received):
        ref[...] = msg_ref[...].astype(F32)
        parts.append(get_split(ref, used, 2 * s.own))
    return parts


def add_sides(s, field_ref, x_ref, y_ref, xy_ref):
    for n in range(s.by):
        field_ref[0, n, 0 : s.span, :] += x_ref[n * s.span : (n + 1) * s.span]
    for n in range(s.bx):
        field_ref[n, 0, 0 : s.span, :] += y_ref[n * s.span : (n + 1) * s.span]
    field_ref[0, 0, 0 : s.span, :] += xy_ref[0 : s.span]


def send_down(s, total, field_ref, msg_refs, part_ref, x_ref, y_ref, xy_ref):
    put_sides(s, field_ref, 0, 0, x_ref, y_ref, xy_ref)
    corner, x_part, y_part, own_part = columns(s, total)
    part_ref[...] = own_part
    send_sides(s, x_ref, y_ref, xy_ref, msg_refs, (x_part, y_part, corner))


def first_down_body(s, before_ref, total_ref, early_ref, *refs):
    del before_ref, early_ref
    count = 2 - s.pairs
    received, refs = refs[:count], refs[count:]
    field_ref, *msg_refs, part_ref, above_ref, below_ref, x_ref, y_ref, xy_ref = refs
    get_z(s, received, above_ref, below_ref)
    half = 4 * s.own
    total = total_ref[...] + jnp.concatenate([get_split(below_ref, 0, half), get_split(above_ref, s.z_rows, half)], axis=0)
    for x in range(s.bx):
        field_ref[x, 0 : s.by, s.bz, :] = above_ref[x * s.by : (x + 1) * s.by]
    send_down(s, total, field_ref, msg_refs, part_ref, x_ref, y_ref, xy_ref)


def cell_body(s, before_ref, from_x_ref, from_y_ref, from_xy_ref, part_ref, weight_ref, *refs):
    matrix_refs, refs = refs[: s.cells[0]], refs[s.cells[0] :]
    field_ref, block_ref, *msg_refs, own_ref, sums_ref, x_ref, y_ref, xy_ref = refs
    del before_ref
    parts = get_sides(s, (from_x_ref, from_y_ref, from_xy_ref), x_ref, y_ref, xy_ref)
    rest = jnp.zeros((s.bzp - s.span, s.waves), F32)
    for n in range(s.by):
        field_ref[s.bx, n, 0 : s.span, :] = x_ref[n * s.span : (n + 1) * s.span]
        field_ref[s.bx, n, s.span :, :] = rest
    for n in range(s.bx):
        field_ref[n, s.by, 0 : s.span, :] = y_ref[n * s.span : (n + 1) * s.span]
        field_ref[n, s.by, s.span :, :] = rest
    field_ref[s.bx, s.by, 0 : s.span, :] = xy_ref[0 : s.span]
    field_ref[s.bx, s.by, s.span :, :] = rest
    weight = columns(s, weight_ref[...])[3]
    total = (part_ref[...] + parts[0] + parts[1] + parts[2]) * weight
    own_ref[...] = total
    apply_cells(s, field_ref, matrix_refs, sums_ref)
    join_sides(s, sums_ref, x_ref, y_ref, xy_ref)
    send_sides(s, x_ref, y_ref, xy_ref, msg_refs, (total, total, total))
    join_cells(s, sums_ref, block_ref)


def apply_cells(s, field_ref, matrix_refs, sums_ref):
    order, side, group = s.order, s.side, s.group
    used = side * side * group
    for i in range(s.cells[0]):
        for j in range(s.cells[1]):
            for k in range(s.cells[2]):
                first = k * order
                values = field_ref[i * order : i * order + side, j * order : j * order + side, first : first + group]
                values = values.reshape(used, s.waves)
                if s.padded > used:
                    values = jnp.concatenate([values, jnp.zeros((s.padded - used, s.waves), F32)], axis=0)
                product = jnp.dot(matrix_refs[i][j, k], values.astype(BF16), preferred_element_type=F32)
                product = product[0:used].reshape(side, side, group, s.waves)
                x0, x1, y0, y1 = i * order, i * order + side, j * order, j * order + side
                a, b = int(i > 0), int(j > 0)
                sums_ref[k, x0 + a : x1, y0 + b : y1] = product[a:, b:]
                if a:
                    sums_ref[k, x0, y0 + b : y1] += product[0, b:]
                if b:
                    sums_ref[k, x0 + a : x1, y0] += product[a:, 0]
                if a and b:
                    sums_ref[k, x0, y0] += product[0, 0]


def join_cells(s, sums_ref, out_ref):
    count = s.by
    for x in range(s.bx):
        out_ref[x, :, 0 : s.group, :] = sums_ref[0, x, 0:count]
        out_ref[x, :, s.group :, :] = jnp.zeros((count, s.bzp - s.group, s.waves), F32)
        for k in range(1, s.cells[2]):
            out_ref[x, :, k * s.order : k * s.order + s.group, :] += sums_ref[k, x, 0:count]


def join_sides(s, sums_ref, x_ref, y_ref, xy_ref):
    last = s.cells[2] - 1

    def join(rows_ref, at, x, y):
        for k in range(s.cells[2]):
            count = s.order + int(k == last)
            first = at + k * s.order
            rows_ref[first : first + count] = sums_ref[k, x, y, 0:count, :]
            if k:
                rows_ref[first : first + 1] += sums_ref[k - 1, x, y, s.order : s.order + 1, :]

    for n in range(s.by):
        join(x_ref, n * s.span, s.bx, n)
    for n in range(s.bx):
        join(y_ref, n * s.span, n, s.by)
    join(xy_ref, 0, s.bx, s.by)
    for ref, used in ((x_ref, s.x_rows), (y_ref, s.y_rows), (xy_ref, s.span)):
        blank(ref, used)


def stacked(totals):
    high, low = halves(totals)
    return jnp.concatenate([high, high, low], axis=0).astype(BF16)


def middle_body(s, block_ref, from_x_ref, from_y_ref, from_xy_ref, own_ref, by_node_ref, *refs):
    field_ref, *msg_refs, x_ref, y_ref, xy_ref, low_ref, high_ref = refs
    x_part, y_part, corner = get_sides(s, (from_x_ref, from_y_ref, from_xy_ref), x_ref, y_ref, xy_ref)
    stack = stacked(from_columns(s, [corner, x_part, y_part, own_ref[...]]))
    for x in range(s.bx):
        image = jnp.dot(by_node_ref[x], stack, preferred_element_type=F32)
        field_ref[x, 0 : s.by] = image.reshape(s.by, s.bzp, s.waves) + block_ref[x]
    add_sides(s, field_ref, x_ref, y_ref, xy_ref)
    for x in range(s.bx):
        low_ref[x * s.by : (x + 1) * s.by] = field_ref[x, 0 : s.by, 0, :]
        high_ref[x * s.by : (x + 1) * s.by] = field_ref[x, 0 : s.by, s.bz, :]
    blank(low_ref, s.z_rows)
    blank(high_ref, s.z_rows)
    put_z(s, msg_refs, low_ref, high_ref)


def sums_body(s, field_ref, by_atom_ref, line_ref, total_ref, lowest_ref):
    total = jnp.zeros((s.locals, s.waves), F32)
    for x in range(s.bx):
        total = total + split_sums(by_atom_ref[x], s.locals, field_ref[x, 0 : s.by].reshape(s.by * s.bzp, s.waves))
    total_ref[...] = total
    lowest = line_ref[...].T[0 : 2 * s.locals]
    if s.z_plane > s.z_rows:
        lowest = jnp.concatenate([lowest, jnp.zeros((2 * s.locals, s.z_plane - s.z_rows), F32)], axis=1)
    lowest_ref[...] = lowest.astype(BF16)


def second_down_body(s, before_ref, total_ref, lowest_ref, *refs):
    del before_ref
    count = 2 - s.pairs
    received, refs = refs[:count], refs[count:]
    field_ref, *msg_refs, part_ref, above_ref, below_ref, x_ref, y_ref, xy_ref = refs
    get_z(s, received, above_ref, below_ref)
    for x in range(s.bx):
        field_ref[x, 0 : s.by, s.bz, :] += above_ref[x * s.by : (x + 1) * s.by]
        field_ref[x, 0 : s.by, 0, :] += below_ref[x * s.by : (x + 1) * s.by]
    total = total_ref[...] + split_sums(lowest_ref[...], s.locals, below_ref[...])
    send_down(s, total, field_ref, msg_refs, part_ref, x_ref, y_ref, xy_ref)


def fold_body(s, before_ref, from_x_ref, from_y_ref, from_xy_ref, own_ref, *refs):
    del before_ref
    block_ref, *msg_refs, total_ref, x_ref, y_ref, xy_ref, low_ref, high_ref = refs
    x_part, y_part, corner = get_sides(s, (from_x_ref, from_y_ref, from_xy_ref), x_ref, y_ref, xy_ref)
    total = from_columns(s, [corner, x_part, y_part, own_ref[...]])
    total_ref[...] = total
    add_sides(s, block_ref, x_ref, y_ref, xy_ref)
    half = 4 * s.own
    for x in range(s.bx):
        high_ref[x * s.by : (x + 1) * s.by] = block_ref[x, :, s.bz, :]
    blank(high_ref, s.z_rows)
    blank(low_ref, 0)
    put_split(low_ref, 0, total[0:half])
    put_split(high_ref, s.z_rows, total[half:])
    put_z(s, msg_refs, low_ref, high_ref)


def last_body(s, start_ref, block_ref, total_ref, by_node_ref, *refs):
    count = 2 - s.pairs
    received, refs = refs[:count], refs[count:]
    out_hbm, above_ref, below_ref, plane_ref, out_ref, sems = refs
    get_z(s, received, above_ref, below_ref)
    half = 4 * s.own
    total = total_ref[...] + jnp.concatenate([get_split(below_ref, s.z_rows, half), get_split(above_ref, 0, half)], axis=0)
    stack = stacked(total)
    copies = []
    for x in range(s.bx):
        image = jnp.dot(by_node_ref[x], stack, preferred_element_type=F32)
        plane_ref[...] = image.reshape(s.by, s.bzp, s.waves) + block_ref[x]
        plane_ref[:, 0, :] += below_ref[x * s.by : (x + 1) * s.by]
        out_ref[x] = 2.0 * plane_ref[:, 0 : s.bz] - start_ref[x]
        copies.append(pltpu.make_async_copy(out_ref.at[x], out_hbm.at[x], sems.at[x]))
        copies[x].start()
    for copy in copies:
        copy.wait()


def selector(count, chosen):
    row = lax.broadcasted_iota(jnp.int32, count, 0)
    column = lax.broadcasted_iota(jnp.int32, count, 1)
    return chosen(row, column).astype(F32).astype(BF16)


def matrix_body(s, part, matrix_hbm, out_ref, raw_ref, flat_ref, half_ref, sems):
    cells_y, cells_z = s.cells[1:]
    side, group = s.side, s.group
    nodes = side**3
    copies = [pltpu.make_async_copy(matrix_hbm.at[part, j], raw_ref.at[j], sems.at[j]) for j in range(cells_y)]
    for copy in copies:
        copy.start()
    wide = 256 // group * side
    spans = []
    for first in range(0, s.padded, 256):
        low = first // group * side // 128 * 128
        high = min(nodes, first // group * side + wide)
        width = min(256, s.padded - first)
        spans.append((first, low, high, selector((high - low, width), lambda m, c, low=low, first=first: (
            ((c + first) % group < side) & (m + low == (c + first) // group * side + (c + first) % group)))))
    tall = 128 // group * side
    picks = jnp.concatenate(
        [
            selector((128, tall * cells_z), lambda r, m, k=k: (r % group < side) & (m == (r // group * side + r % group) * cells_z + k))
            for k in range(cells_z)
        ],
        axis=0,
    )
    for j in range(cells_y):
        copies[j].wait()
        flat_ref[...] = raw_ref[j].reshape(nodes * cells_z, nodes)
        for first, low, high, spread in spans:
            half = jnp.dot(flat_ref[:, low:high], spread, preferred_element_type=F32)
            half_ref[:, first : first + spread.shape[1]] = half.astype(BF16)
        for first in range(0, s.padded, 128):
            count = min(128, s.padded - first)
            low = first // group * side * cells_z
            high = min(nodes * cells_z, low + tall * cells_z)
            rows = jnp.dot(picks[:, 0 : high - low], half_ref[low:high], preferred_element_type=F32).astype(BF16)
            for k in range(cells_z):
                out_ref[j, k, first : first + count] = rows[128 * k : 128 * k + count]


def regrouped(s, cell_matrices, part):
    shape = cell_matrices.shape
    nodes = shape[3]
    return call(
        matrix_body,
        s,
        [jax.ShapeDtypeStruct(shape[1:3] + (s.padded, s.padded), BF16)],
        [
            pltpu.VMEM((shape[1], nodes, shape[2], nodes), BF16),
            pltpu.VMEM((nodes * shape[2], nodes), BF16),
            pltpu.VMEM((nodes * shape[2], s.padded), BF16),
            pltpu.SemaphoreType.DMA((shape[1],)),
        ],
        [cell_matrices.transpose(0, 1, 3, 2, 4)],
        spaces={0: pltpu.HBM},
        extra=(part,),
    )[0]


def along_z(s, msgs):
    if s.pairs:
        return [shifted(msgs[0], (0, 0, 1))]
    return [shifted(msgs[0], (0, 0, -1)), shifted(msgs[1], (0, 0, 1))]


def along_xy(msgs, by):
    return [shifted(msg, (by * dx, by * dy, 0)) for msg, dx, dy in zip(msgs, (1, 0, 1), (0, 1, 1))]


def local(wavefunctions, cell_matrices, projectors, slot_atoms, atom_coupling):
    atom_count = atom_coupling.shape[0]
    devices = 1
    for axis in AXES:
        devices *= lax.axis_size(axis)
    own = atom_count // devices
    s = Sizes(wavefunctions.shape, cell_matrices.shape, own, lax.axis_size("gz") == 2)
    ids = local_atoms(own)[:, None]
    plane = s.by * s.bzp
    sides = s.side_rows()
    sums = s.scratch(s.cells[2], s.bx + 1, s.by + 1, s.group)
    field, by_node, by_atom, line, *msgs, total, weight = call(
        first_body,
        s,
        [
            s.extended(),
            jax.ShapeDtypeStruct((s.bx, plane, 3 * s.locals), BF16),
            jax.ShapeDtypeStruct((s.bx, 2 * s.locals, plane), BF16),
            jax.ShapeDtypeStruct((s.z_rows, 3 * s.locals), F32),
        ]
        + s.z_msgs(s.z_both, s.z_sums)
        + [s.rows(s.locals), s.rows(s.locals)],
        [
            s.scratch(s.bx, s.by, s.bz),
            pltpu.VMEM(projectors.shape, F32),
            pltpu.VMEM(slot_atoms.shape, jnp.int32),
            pltpu.VMEM((1, atom_count), F32),
            pltpu.VMEM((s.bx * s.by * s.bz, 3 * s.locals), F32),
            pltpu.VMEM((s.bx * s.by, s.bzp, 3 * s.locals), F32),
            s.scratch(s.z_both),
            s.scratch(s.z_sums),
            pltpu.SemaphoreType.DMA((s.bx // s.few,)),
            pltpu.SemaphoreType.DMA((3,)),
        ],
        [wavefunctions, projectors, slot_atoms, atom_coupling[None, :], ids],
        spaces={0: pltpu.HBM, 1: pltpu.HBM, 2: pltpu.HBM, 3: pltpu.HBM},
    )
    matrices = [regrouped(s, cell_matrices, part) for part in range(s.cells[0])]
    received = along_z(s, msgs)
    field, *msgs, part = call(
        first_down_body,
        s,
        [s.extended()] + s.side_msgs() + [s.rows(2 * own)],
        [s.scratch(s.z_both), s.scratch(s.z_sums)] + sides,
        [field, total, matrices[0]] + received,
        aliases={0: 0},
    )

    def cells(field, msgs, part):
        received = along_xy(msgs, -1)
        _, block, *msgs, mine = call(
            cell_body,
            s,
            [s.extended(), s.block()] + s.side_msgs() + [s.rows(2 * own)],
            [sums] + sides,
            [field] + received + [part, weight] + matrices,
            aliases={0: 0},
        )
        return block, along_xy(msgs, 1), mine

    block, received, mine = cells(field, msgs, part)
    field, *msgs = call(
        middle_body,
        s,
        [s.extended()] + s.z_msgs(s.z_plane, s.z_plane),
        sides + [s.scratch(s.z_plane), s.scratch(s.z_plane)],
        [block] + received + [mine, by_node],
    )
    received = along_z(s, msgs)
    total, lowest = call(
        sums_body,
        s,
        [s.rows(s.locals), jax.ShapeDtypeStruct((2 * s.locals, s.z_plane), BF16)],
        [],
        [field, by_atom, line],
    )
    field, *msgs, part = call(
        second_down_body,
        s,
        [s.extended()] + s.side_msgs() + [s.rows(2 * own)],
        [s.scratch(s.z_plane), s.scratch(s.z_plane)] + sides,
        [field, total, lowest] + received,
        aliases={0: 0},
    )
    block, received, mine = cells(field, msgs, part)
    block, *msgs, total = call(
        fold_body,
        s,
        [s.block()] + s.z_msgs(s.z_sums, s.z_both) + [s.rows(s.locals)],
        sides + [s.scratch(s.z_sums), s.scratch(s.z_both)],
        [block] + received + [mine],
        aliases={0: 0},
    )
    received = along_z(s, msgs)
    (out,) = call(
        last_body,
        s,
        [jax.ShapeDtypeStruct(wavefunctions.shape, F32)],
        [
            s.scratch(s.z_sums),
            s.scratch(s.z_both),
            s.scratch(s.by, s.bzp),
            s.scratch(s.bx, s.by, s.bz),
            pltpu.SemaphoreType.DMA((s.bx,)),
        ],
        [wavefunctions, block, total, by_node] + received,
        out_spaces={0: pltpu.HBM},
    )
    return out


def solution(mesh):
    return jax.shard_map(
        local,
        mesh=mesh,
        in_specs=(
            P("gx", "gy", "gz", None),
            P("gx", "gy", "gz", None, None),
            P(("gx", "gy", "gz"), None, None),
            P(("gx", "gy", "gz"), None),
            P(),
        ),
        out_specs=P("gx", "gy", "gz", None),
        check_vma=False,
    )
```

time: 57 us -> 54.3 us (0.953)
  waiting for transfers between devices: 28.2 us -> 23 us
  starting transfers between devices: 14.5 us -> 16.7 us
    ppermute x16 -> x15, waiting for transfers between devices: 28.2 us -> 23 us  [shifted(): return lax.ppermute(value, AXES, pairs)]
    ppermute x16 -> x15, starting transfers between devices: 14.5 us -> 16.7 us  [shifted(): return lax.ppermute(value, AXES, pairs)]
  transfers between devices with their start and end apart: 16 -> 15, of which waited for: 7 -> 7; matrix products, arithmetic and copies ran while one was open for 0% -> 0% of each run, Pallas kernels for 9% -> 10%
where the time goes in v4:
time: 54.3 us; the launch traced here: 54.1 us
  waiting for transfers between devices  23 us (42%)
  starting transfers between devices  16.7 us (31%)
  Pallas kernels  14.1 us (26%)
    ppermute x15, waiting for transfers between devices, shifted(): return lax.ppermute(value, AXES, pairs)  23 us
    ppermute x15, starting transfers between devices, shifted(): return lax.ppermute(value, AXES, pairs)  16.7 us
    pallas_call x11, Pallas kernels, call(): pl.pallas_call(functools.partial(body, sizes, *extra), out_shape=outs, in...  14.1 us
  transfers between devices with their start and end apart: 15, of which 7 were waited for; matrix products, arithmetic and copies ran while one was open for 0% of the time, Pallas kernels for 10%

profile of v4, /device:TPU:0, one launch (start us, length us, event | category | flops | bytes accessed | tf_op | source)
XLA Modules:
  0.0 54.1 jit_solution(4134380733162825022)
XLA Ops:
  0.2 2.9 %shard_map.55 = (f32[13,13,16,256]{3,2,1,0:T(8,128)S(1)}, bf16[12,192,48]{2,1,0:T(8,128)(2,1)S(1)}, bf16[12,32,192]{2,1,0:T(8,128)(2,1)S(1)}, f32[144,48]{1,0:T(...) custom-call(f32[12,12,12,256]{3,2,1,0:T(8,128)} %start_ref.1, ...), custom_call_target="tpu_custom_call" | custom-call | tf_op jit(solution)/shard_map/pallas_call | solution.py:102
  3.1 3.0 %collective-permute-start = (bf16[176,256]{1,0:T(8,128)(2,1)S(1)}, bf16[176,256]{1,0:T(8,128)(2,1)S(1)}, u32[]{:S(2)}, u32[]{:S(2)}) collective-permute-start(bf16[176,256]{1,0:T(8,128)(2,1)S(1)} %get-tuple-element.41), channel_id=1, source_target_pairs={{0,1},{1,0},{2,3},{3,2},{4,5},{5,4},{6,7},{7,6},{8,9},{9,8},{10,11... | collective-permute-start | bytes 270344 | tf_op jit(solution)/shard_map/ppermute | solution.py:29
  6.1 2.4 %shard_map.56.early_ref.refs_0_ = bf16[2,2,400,400]{3,2,1,0:T(8,128)(2,1)S(1)} custom-call(bf16[2,2,343,2,343]{4,3,2,1,0:T(2,128)(2,1)} %bitcast.19), custom_call_target="tpu_custom_call" | custom-call | tf_op jit(solution)/shard_map/pallas_call | solution.py:102
  8.9 0.6 %collective-permute-start.1 = (bf16[176,256]{1,0:T(8,128)(2,1)S(1)}, bf16[176,256]{1,0:T(8,128)(2,1)S(1)}, u32[]{:S(2)}, u32[]{:S(2)}) collective-permute-start(bf16[176,256]{1,0:T(8,128)(2,1)S(1)} %get-tuple-element.43), channel_id=1, source_target_pairs={{0,24},{1,25},{2,26},{3,27},{4,28},{5,29},{6,30},{7,31},{8,0},{9,1... | collective-permute-start | bytes 270344 | tf_op jit(solution)/shard_map/ppermute | solution.py:29
  9.5 3.6 %collective-permute-start.2 = (bf16[176,256]{1,0:T(8,128)(2,1)S(1)}, bf16[176,256]{1,0:T(8,128)(2,1)S(1)}, u32[]{:S(2)}, u32[]{:S(2)}) collective-permute-start(bf16[176,256]{1,0:T(8,128)(2,1)S(1)} %get-tuple-element.44), channel_id=1, source_target_pairs={{0,6},{1,7},{2,0},{3,1},{4,2},{5,3},{6,4},{7,5},{8,14},{9,15},{10,... | collective-permute-start | bytes 270344 | tf_op jit(solution)/shard_map/ppermute | solution.py:29
  13.1 1.2 %collective-permute-start.3 = (bf16[32,256]{1,0:T(8,128)(2,1)S(1)}, bf16[32,256]{1,0:T(8,128)(2,1)S(1)}, u32[]{:S(2)}, u32[]{:S(2)}) collective-permute-start(bf16[32,256]{1,0:T(8,128)(2,1)S(1)} %get-tuple-element.45), channel_id=1, source_target_pairs={{0,30},{1,31},{2,24},{3,25},{4,26},{5,27},{6,28},{7,29},{8,6},{9,7... | collective-permute-start | bytes 49160 | tf_op jit(solution)/shard_map/ppermute | solution.py:29
  14.2 2.4 %shard_map.58.refs_1_ = bf16[2,2,400,400]{3,2,1,0:T(8,128)(2,1)S(1)} custom-call(bf16[2,2,343,2,343]{4,3,2,1,0:T(2,128)(2,1)} %bitcast.20), custom_call_target="tpu_custom_call" | custom-call | tf_op jit(solution)/shard_map/pallas_call | solution.py:102
  16.7 1.4 %shard_map.59 = (f32[13,13,16,256]{3,2,1,0:T(8,128)S(1)}, f32[12,12,16,256]{3,2,1,0:T(8,128)S(1)}, bf16[176,256]{1,0:T(8,128)(2,1)S(1)}, bf16[176,256]{1,0:T(8,1...) custom-call(f32[13,13,16,256]{3,2,1,0:T(8,128)S(1)} %get-tuple-element.42.before_, ...), custom_call_target="tpu_custom_call", output_to_operand_aliasing={{0}: (0, {})} | custom-call | tf_op jit(solution)/shard_map/pallas_call | solution.py:102
  18.1 0.7 %collective-permute-start.4 = (bf16[176,256]{1,0:T(8,128)(2,1)S(1)}, bf16[176,256]{1,0:T(8,128)(2,1)S(1)}, u32[]{:S(2)}, u32[]{:S(2)}) collective-permute-start(bf16[176,256]{1,0:T(8,128)(2,1)S(1)} %get-tuple-element.49), channel_id=1, source_target_pairs={{0,8},{1,9},{2,10},{3,11},{4,12},{5,13},{6,14},{7,15},{8,16},{9,17... | collective-permute-start | bytes 270344 | tf_op jit(solution)/shard_map/ppermute | solution.py:29
  18.7 1.1 %collective-permute-start.5 = (bf16[176,256]{1,0:T(8,128)(2,1)S(1)}, bf16[176,256]{1,0:T(8,128)(2,1)S(1)}, u32[]{:S(2)}, u32[]{:S(2)}) collective-permute-start(bf16[176,256]{1,0:T(8,128)(2,1)S(1)} %get-tuple-element.50), channel_id=1, source_target_pairs={{0,2},{1,3},{2,4},{3,5},{4,6},{5,7},{6,0},{7,1},{8,10},{9,11},{10,... | collective-permute-start | bytes 270344 | tf_op jit(solution)/shard_map/ppermute | solution.py:29
  20.1 5.6 %collective-permute-done.6.from_xy_ref = bf16[32,256]{1,0:T(8,128)(2,1)S(1)} collective-permute-done((bf16[32,256]{1,0:T(8,128)(2,1)S(1)}, bf16[32,256]{1,0:T(8,128)(2,1)S(1)}, u32[]{:S(2)}, u32[]{:S(2)}) %collective-permute-start.6) | collective-permute-done | bytes 16416 | tf_op jit(solution)/shard_map/ppermute | solution.py:29
  26.0 0.6 %shard_map.60 = (f32[13,13,16,256]{3,2,1,0:T(8,128)S(1)}, bf16[288,256]{1,0:T(8,128)(2,1)S(1)}) custom-call(f32[12,12,16,256]{3,2,1,0:T(8,128)S(1)} %get-tuple-element.48.block_ref, bf16[176,256]{1,0:T(8,128)(2,1)S(1)} %collective-permute-done.4.from_x_ref, bf16[176,256]{1,0:T(8,128)(2,1)S(1)} %collective-permute-done.5.from_y_ref, ...), custom_call_target="tpu_custom_call" | custom-call | tf_op jit(solution)/shard_map/pallas_call | solution.py:102
  26.6 1.5 %collective-permute-start.7 = (bf16[288,256]{1,0:T(8,128)(2,1)S(1)}, bf16[288,256]{1,0:T(8,128)(2,1)S(1)}, u32[]{:S(2)}, u32[]{:S(2)}) collective-permute-start(bf16[288,256]{1,0:T(8,128)(2,1)S(1)} %get-tuple-element.59), channel_id=1, source_target_pairs={{0,1},{1,0},{2,3},{3,2},{4,5},{5,4},{6,7},{7,6},{8,9},{9,8},{10,11... | collective-permute-start | bytes 442376 | tf_op jit(solution)/shard_map/ppermute | solution.py:29
  28.2 0.5 shard_map.61
  28.6 3.9 %collective-permute-done.7.refs_0_ = bf16[288,256]{1,0:T(8,128)(2,1)S(1)} collective-permute-done((bf16[288,256]{1,0:T(8,128)(2,1)S(1)}, bf16[288,256]{1,0:T(8,128)(2,1)S(1)}, u32[]{:S(2)}, u32[]{:S(2)}) %collective-permute-start.7) | collective-permute-done | bytes 147488 | tf_op jit(solution)/shard_map/ppermute | solution.py:29
  32.6 0.4 shard_map.62
  33.0 1.8 %collective-permute-start.9 = (bf16[176,256]{1,0:T(8,128)(2,1)S(1)}, bf16[176,256]{1,0:T(8,128)(2,1)S(1)}, u32[]{:S(2)}, u32[]{:S(2)}) collective-permute-start(bf16[176,256]{1,0:T(8,128)(2,1)S(1)} %get-tuple-element.62), channel_id=1, source_target_pairs={{0,6},{1,7},{2,0},{3,1},{4,2},{5,3},{6,4},{7,5},{8,14},{9,15},{10,... | collective-permute-start | bytes 270344 | tf_op jit(solution)/shard_map/ppermute | solution.py:29
  34.9 3.2 %collective-permute-done.10.from_xy_ref = bf16[32,256]{1,0:T(8,128)(2,1)S(1)} collective-permute-done((bf16[32,256]{1,0:T(8,128)(2,1)S(1)}, bf16[32,256]{1,0:T(8,128)(2,1)S(1)}, u32[]{:S(2)}, u32[]{:S(2)}) %collective-permute-start.10) | collective-permute-done | bytes 16416 | tf_op jit(solution)/shard_map/ppermute | solution.py:29
  38.2 1.3 %shard_map.63 = (f32[13,13,16,256]{3,2,1,0:T(8,128)S(1)}, f32[12,12,16,256]{3,2,1,0:T(8,128)S(1)}, bf16[176,256]{1,0:T(8,128)(2,1)S(1)}, bf16[176,256]{1,0:T(8,1...) custom-call(f32[13,13,16,256]{3,2,1,0:T(8,128)S(1)} %get-tuple-element.60.before_, ...), custom_call_target="tpu_custom_call", output_to_operand_aliasing={{0}: (0, {})} | custom-call | tf_op jit(solution)/shard_map/pallas_call | solution.py:102
  39.6 0.9 %collective-permute-start.11 = (bf16[176,256]{1,0:T(8,128)(2,1)S(1)}, bf16[176,256]{1,0:T(8,128)(2,1)S(1)}, u32[]{:S(2)}, u32[]{:S(2)}) collective-permute-start(bf16[176,256]{1,0:T(8,128)(2,1)S(1)} %get-tuple-element.66), channel_id=1, source_target_pairs={{0,8},{1,9},{2,10},{3,11},{4,12},{5,13},{6,14},{7,15},{8,16},{9,17... | collective-permute-start | bytes 270344 | tf_op jit(solution)/shard_map/ppermute | solution.py:29
  40.8 6.8 %collective-permute-done.13.from_xy_ref = bf16[32,256]{1,0:T(8,128)(2,1)S(1)} collective-permute-done((bf16[32,256]{1,0:T(8,128)(2,1)S(1)}, bf16[32,256]{1,0:T(8,128)(2,1)S(1)}, u32[]{:S(2)}, u32[]{:S(2)}) %collective-permute-start.13) | collective-permute-done | bytes 16416 | tf_op jit(solution)/shard_map/ppermute | solution.py:29
  47.8 1.6 %collective-permute-start.14 = (bf16[176,256]{1,0:T(8,128)(2,1)S(1)}, bf16[176,256]{1,0:T(8,128)(2,1)S(1)}, u32[]{:S(2)}, u32[]{:S(2)}) collective-permute-start(bf16[176,256]{1,0:T(8,128)(2,1)S(1)} %get-tuple-element.72), channel_id=1, source_target_pairs={{0,1},{1,0},{2,3},{3,2},{4,5},{5,4},{6,7},{7,6},{8,9},{9,8},{10,11... | collective-permute-start | bytes 270344 | tf_op jit(solution)/shard_map/ppermute | solution.py:29
  49.4 3.0 %collective-permute-done.14.refs_0_ = bf16[176,256]{1,0:T(8,128)(2,1)S(1)} collective-permute-done((bf16[176,256]{1,0:T(8,128)(2,1)S(1)}, bf16[176,256]{1,0:T(8,128)(2,1)S(1)}, u32[]{:S(2)}, u32[]{:S(2)}) %collective-permute-start.14) | collective-permute-done | bytes 90144 | tf_op jit(solution)/shard_map/ppermute | solution.py:29
  52.4 1.8 %shard_map.65 = f32[12,12,12,256]{3,2,1,0:T(8,128)} custom-call(f32[12,12,12,256]{3,2,1,0:T(8,128)S(1)} %copy-done, f32[12,12,16,256]{3,2,1,0:T(8,128)S(1)} %get-tuple-element.70.block_ref, f32[16,256]{1,0:T(8,128)S(1)} %get-tuple-element.71.total_ref, bf16[12,192,48]{2,1,0:T(8,128)(2,1)S(1)} %get-tuple-element.53.by_node_ref, ...), custom_call_target="tpu_custom_call" | custom-call | tf_op jit(solution)/shard_map/pallas_call | solution.py:102
  (21 shorter events, 1.9 us)
Async XLA Ops:
  3.1 5.6 %collective-permute-start = (bf16[176,256]{1,0:T(8,128)(2,1)S(1)}, bf16[176,256]{1,0:T(8,128)(2,1)S(1)}, u32[]{:S(2)}, u32[]{:S(2)}) collective-permute-start(bf16[176,256]{1,0:T(8,128)(2,1)S(1)} %get-tuple-element.41), channel_id=1, source_target_pairs={{0,1},{1,0},{2,3},{3,2},{4,5},{5,4},{6,7},{7,6},{8,9},{9,8},{10,11... | collective-permute-start | bytes 270344 | tf_op jit(solution)/shard_map/ppermute | solution.py:29
  8.9 7.8 %collective-permute-start.1 = (bf16[176,256]{1,0:T(8,128)(2,1)S(1)}, bf16[176,256]{1,0:T(8,128)(2,1)S(1)}, u32[]{:S(2)}, u32[]{:S(2)}) collective-permute-start(bf16[176,256]{1,0:T(8,128)(2,1)S(1)} %get-tuple-element.43), channel_id=1, source_target_pairs={{0,24},{1,25},{2,26},{3,27},{4,28},{5,29},{6,30},{7,31},{8,0},{9,1... | collective-permute-start | bytes 270344 | tf_op jit(solution)/shard_map/ppermute | solution.py:29
  9.5 7.2 %collective-permute-start.2 = (bf16[176,256]{1,0:T(8,128)(2,1)S(1)}, bf16[176,256]{1,0:T(8,128)(2,1)S(1)}, u32[]{:S(2)}, u32[]{:S(2)}) collective-permute-start(bf16[176,256]{1,0:T(8,128)(2,1)S(1)} %get-tuple-element.44), channel_id=1, source_target_pairs={{0,6},{1,7},{2,0},{3,1},{4,2},{5,3},{6,4},{7,5},{8,14},{9,15},{10,... | collective-permute-start | bytes 270344 | tf_op jit(solution)/shard_map/ppermute | solution.py:29
  13.1 3.6 %collective-permute-start.3 = (bf16[32,256]{1,0:T(8,128)(2,1)S(1)}, bf16[32,256]{1,0:T(8,128)(2,1)S(1)}, u32[]{:S(2)}, u32[]{:S(2)}) collective-permute-start(bf16[32,256]{1,0:T(8,128)(2,1)S(1)} %get-tuple-element.45), channel_id=1, source_target_pairs={{0,30},{1,31},{2,24},{3,25},{4,26},{5,27},{6,28},{7,29},{8,6},{9,7... | collective-permute-start | bytes 49160 | tf_op jit(solution)/shard_map/ppermute | solution.py:29
  18.1 7.7 %collective-permute-start.4 = (bf16[176,256]{1,0:T(8,128)(2,1)S(1)}, bf16[176,256]{1,0:T(8,128)(2,1)S(1)}, u32[]{:S(2)}, u32[]{:S(2)}) collective-permute-start(bf16[176,256]{1,0:T(8,128)(2,1)S(1)} %get-tuple-element.49), channel_id=1, source_target_pairs={{0,8},{1,9},{2,10},{3,11},{4,12},{5,13},{6,14},{7,15},{8,16},{9,17... | collective-permute-start | bytes 270344 | tf_op jit(solution)/shard_map/ppermute | solution.py:29
  18.7 7.3 %collective-permute-start.5 = (bf16[176,256]{1,0:T(8,128)(2,1)S(1)}, bf16[176,256]{1,0:T(8,128)(2,1)S(1)}, u32[]{:S(2)}, u32[]{:S(2)}) collective-permute-start(bf16[176,256]{1,0:T(8,128)(2,1)S(1)} %get-tuple-element.50), channel_id=1, source_target_pairs={{0,2},{1,3},{2,4},{3,5},{4,6},{5,7},{6,0},{7,1},{8,10},{9,11},{10,... | collective-permute-start | bytes 270344 | tf_op jit(solution)/shard_map/ppermute | solution.py:29
  19.8 6.0 %collective-permute-start.6 = (bf16[32,256]{1,0:T(8,128)(2,1)S(1)}, bf16[32,256]{1,0:T(8,128)(2,1)S(1)}, u32[]{:S(2)}, u32[]{:S(2)}) collective-permute-start(bf16[32,256]{1,0:T(8,128)(2,1)S(1)} %get-tuple-element.51), channel_id=1, source_target_pairs={{0,10},{1,11},{2,12},{3,13},{4,14},{5,15},{6,8},{7,9},{8,18},{9,19... | collective-permute-start | bytes 49160 | tf_op jit(solution)/shard_map/ppermute | solution.py:29
  26.6 5.9 %collective-permute-start.7 = (bf16[288,256]{1,0:T(8,128)(2,1)S(1)}, bf16[288,256]{1,0:T(8,128)(2,1)S(1)}, u32[]{:S(2)}, u32[]{:S(2)}) collective-permute-start(bf16[288,256]{1,0:T(8,128)(2,1)S(1)} %get-tuple-element.59), channel_id=1, source_target_pairs={{0,1},{1,0},{2,3},{3,2},{4,5},{5,4},{6,7},{7,6},{8,9},{9,8},{10,11... | collective-permute-start | bytes 442376 | tf_op jit(solution)/shard_map/ppermute | solution.py:29
  33.0 5.2 %collective-permute-start.8 = (bf16[176,256]{1,0:T(8,128)(2,1)S(1)}, bf16[176,256]{1,0:T(8,128)(2,1)S(1)}, u32[]{:S(2)}, u32[]{:S(2)}) collective-permute-start(bf16[176,256]{1,0:T(8,128)(2,1)S(1)} %get-tuple-element.61), channel_id=1, source_target_pairs={{0,24},{1,25},{2,26},{3,27},{4,28},{5,29},{6,30},{7,31},{8,0},{9,1... | collective-permute-start | bytes 270344 | tf_op jit(solution)/shard_map/ppermute | solution.py:29
  33.0 5.2 %collective-permute-start.9 = (bf16[176,256]{1,0:T(8,128)(2,1)S(1)}, bf16[176,256]{1,0:T(8,128)(2,1)S(1)}, u32[]{:S(2)}, u32[]{:S(2)}) collective-permute-start(bf16[176,256]{1,0:T(8,128)(2,1)S(1)} %get-tuple-element.62), channel_id=1, source_target_pairs={{0,6},{1,7},{2,0},{3,1},{4,2},{5,3},{6,4},{7,5},{8,14},{9,15},{10,... | collective-permute-start | bytes 270344 | tf_op jit(solution)/shard_map/ppermute | solution.py:29
  34.8 3.4 %collective-permute-start.10 = (bf16[32,256]{1,0:T(8,128)(2,1)S(1)}, bf16[32,256]{1,0:T(8,128)(2,1)S(1)}, u32[]{:S(2)}, u32[]{:S(2)}) collective-permute-start(bf16[32,256]{1,0:T(8,128)(2,1)S(1)} %get-tuple-element.63), channel_id=1, source_target_pairs={{0,30},{1,31},{2,24},{3,25},{4,26},{5,27},{6,28},{7,29},{8,6},{9,7... | collective-permute-start | bytes 49160 | tf_op jit(solution)/shard_map/ppermute | solution.py:29
  39.6 12.8 %copy-start = (f32[12,12,12,256]{3,2,1,0:T(8,128)S(1)}, f32[12,12,12,256]{3,2,1,0:T(8,128)}, u32[]{:S(2)}) copy-start(f32[12,12,12,256]{3,2,1,0:T(8,128)} %start_ref.1) | copy-start | bytes 5308420
  39.6 8.0 %collective-permute-start.11 = (bf16[176,256]{1,0:T(8,128)(2,1)S(1)}, bf16[176,256]{1,0:T(8,128)(2,1)S(1)}, u32[]{:S(2)}, u32[]{:S(2)}) collective-permute-start(bf16[176,256]{1,0:T(8,128)(2,1)S(1)} %get-tuple-element.66), channel_id=1, source_target_pairs={{0,8},{1,9},{2,10},{3,11},{4,12},{5,13},{6,14},{7,15},{8,16},{9,17... | collective-permute-start | bytes 270344 | tf_op jit(solution)/shard_map/ppermute | solution.py:29
  40.5 7.1 %collective-permute-start.12 = (bf16[176,256]{1,0:T(8,128)(2,1)S(1)}, bf16[176,256]{1,0:T(8,128)(2,1)S(1)}, u32[]{:S(2)}, u32[]{:S(2)}) collective-permute-start(bf16[176,256]{1,0:T(8,128)(2,1)S(1)} %get-tuple-element.67), channel_id=1, source_target_pairs={{0,2},{1,3},{2,4},{3,5},{4,6},{5,7},{6,0},{7,1},{8,10},{9,11},{10,... | collective-permute-start | bytes 270344 | tf_op jit(solution)/shard_map/ppermute | solution.py:29
  40.8 6.8 %collective-permute-start.13 = (bf16[32,256]{1,0:T(8,128)(2,1)S(1)}, bf16[32,256]{1,0:T(8,128)(2,1)S(1)}, u32[]{:S(2)}, u32[]{:S(2)}) collective-permute-start(bf16[32,256]{1,0:T(8,128)(2,1)S(1)} %get-tuple-element.68), channel_id=1, source_target_pairs={{0,10},{1,11},{2,12},{3,13},{4,14},{5,15},{6,8},{7,9},{8,18},{9,19... | collective-permute-start | bytes 49160 | tf_op jit(solution)/shard_map/ppermute | solution.py:29
  47.8 4.6 %collective-permute-start.14 = (bf16[176,256]{1,0:T(8,128)(2,1)S(1)}, bf16[176,256]{1,0:T(8,128)(2,1)S(1)}, u32[]{:S(2)}, u32[]{:S(2)}) collective-permute-start(bf16[176,256]{1,0:T(8,128)(2,1)S(1)} %get-tuple-element.72), channel_id=1, source_target_pairs={{0,1},{1,0},{2,3},{3,2},{4,5},{5,4},{6,7},{7,6},{8,9},{9,8},{10,11... | collective-permute-start | bytes 270344 | tf_op jit(solution)/shard_map/ppermute | solution.py:29

commit v5 on v4

--- a/solution.py
+++ b/solution.py
@@ -54,7 +54,7 @@
         self.group = up_to(self.side, 8)
         self.padded = up_to(self.side * self.side * self.group, 16)
         self.bzp = up_to(max(self.bz + 1, (cell_shape[2] - 1) * self.order + self.group), 16)
-        self.few = max(n for n in (1, 2, 3, 4) if self.bx % n == 0)
+        self.few_out = max(n for n in (1, 2) if self.bx % n == 0)
         self.pairs = pairs
         self.own = own
         self.locals = 8 * own
@@ -171,9 +171,9 @@
 
 def first_body(
     s, start_hbm, rows_hbm, slots_hbm, coupling_hbm, ids_ref,
-    field_ref, by_node_ref, by_atom_ref, line_ref, *refs
+    field_ref, by_atom_ref, wide_ref, *refs
 ):
-    *msg_refs, total_ref, weight_ref, start_ref, rows_ref, slots_ref, coupling_ref, tall_ref, wide_ref, low_ref, high_ref, sems, small_sems = refs
+    *msg_refs, total_ref, weight_ref, start_ref, rows_ref, slots_ref, coupling_ref, tall_ref, low_ref, high_ref, sems, small_sems = refs
     small = [
         pltpu.make_async_copy(rows_hbm, rows_ref, small_sems.at[0]),
         pltpu.make_async_copy(slots_hbm, slots_ref, small_sems.at[1]),
@@ -181,35 +181,28 @@
     ]
     for copy in small:
         copy.start()
-    few = s.few
-    copies = []
-    for n in range(s.bx // few):
-        span = pl.ds(n * few, few)
-        copies.append(pltpu.make_async_copy(start_hbm.at[span], start_ref.at[span], sems.at[n]))
-        copies[n].start()
+    whole = pltpu.make_async_copy(start_hbm, start_ref, sems.at[0])
+    whole.start()
     for copy in small:
         copy.wait()
-    selector = (ids_ref[...] == slots_ref[...]).astype(F32)
-    rows = jnp.dot(selector, rows_ref[0], precision=lax.Precision.HIGHEST, preferred_element_type=F32)
-    high, low = halves(rows)
-    low = low.astype(BF16).astype(F32)
-    tall_ref[...] = jnp.concatenate([high, low, high], axis=0).T
-    wide_ref[:, s.bz : s.bzp, :] = jnp.zeros((s.bx * s.by, s.bzp - s.bz, 3 * s.locals), F32)
+    chosen = (ids_ref[...] == slots_ref[...]).astype(F32).astype(BF16)
+    rows = rows_ref[0]
+    high = rows.astype(BF16)
+    low = (rows - high.astype(F32)).astype(BF16)
+    parts = [jnp.dot(chosen, part, preferred_element_type=F32) for part in (high, low)]
+    tall_ref[...] = jnp.concatenate(parts, axis=0).T
+    wide_ref[:, s.bz : s.bzp, :] = jnp.zeros((s.bx * s.by, s.bzp - s.bz, 2 * s.locals), F32)
     for g in range(s.bx * s.by):
         wide_ref[g, 0 : s.bz, :] = tall_ref[g * s.bz : (g + 1) * s.bz, :]
     for x in range(s.bx):
-        wide = wide_ref[x * s.by : (x + 1) * s.by].reshape(s.by * s.bzp, 3 * s.locals)
-        by_node_ref[x] = wide.astype(BF16)
-        by_atom_ref[x] = wide.T[0 : 2 * s.locals].astype(BF16)
-    line_ref[...] = wide_ref[:, 0, :]
+        wide = wide_ref[x * s.by : (x + 1) * s.by].reshape(s.by * s.bzp, 2 * s.locals)
+        by_atom_ref[x] = wide.T.astype(BF16)
     total = jnp.zeros((s.locals, s.waves), F32)
-    for n in range(s.bx // few):
-        copies[n].wait()
-        planes = start_ref[n * few : (n + 1) * few]
-        planes = jnp.concatenate([planes, jnp.zeros((few, s.by, s.bzp - s.bz, s.waves), F32)], axis=2)
-        field_ref[n * few : (n + 1) * few, 0 : s.by] = planes
-        for x in range(few):
-            total = total + split_sums(by_atom_ref[n * few + x], s.locals, planes[x].reshape(s.by * s.bzp, s.waves))
+    whole.wait()
+    for x in range(s.bx):
+        plane = jnp.concatenate([start_ref[x], jnp.zeros((s.by, s.bzp - s.bz, s.waves), F32)], axis=1)
+        field_ref[x, 0 : s.by] = plane
+        total = total + split_sums(by_atom_ref[x], s.locals, plane.reshape(s.by * s.bzp, s.waves))
     total_ref[...] = total
     half = 4 * s.own
     for x in range(s.bx):
@@ -224,6 +217,18 @@
     weight_ref[...] = jnp.broadcast_to(weight, weight_ref.shape)
 
 
+def node_body(s, wide_ref, by_node_ref, lowest_ref, lowest_by_node_ref):
+    for x in range(s.bx):
+        wide = wide_ref[x * s.by : (x + 1) * s.by].reshape(s.by * s.bzp, 2 * s.locals)
+        by_node_ref[x] = jnp.concatenate([wide, wide[:, 0 : s.locals]], axis=1).astype(BF16)
+    line = wide_ref[:, 0, :]
+    lowest_by_node_ref[...] = jnp.concatenate([line, line[:, 0 : s.locals]], axis=1).astype(BF16)
+    lowest = line.T
+    if s.z_plane > s.z_rows:
+        lowest = jnp.concatenate([lowest, jnp.zeros((2 * s.locals, s.z_plane - s.z_rows), F32)], axis=1)
+    lowest_ref[...] = lowest.astype(BF16)
+
+
 def put_sides(s, field_ref, x, y, x_ref, y_ref, xy_ref):
     for n in range(s.by):
         x_ref[n * s.span : (n + 1) * s.span] = field_ref[x, n, 0 : s.span, :]
@@ -278,7 +283,7 @@
 
 def cell_body(s, before_ref, from_x_ref, from_y_ref, from_xy_ref, part_ref, weight_ref, *refs):
     matrix_refs, refs = refs[: s.cells[0]], refs[s.cells[0] :]
-    field_ref, block_ref, *msg_refs, own_ref, sums_ref, x_ref, y_ref, xy_ref = refs
+    field_ref, sums_ref, *msg_refs, own_ref, x_ref, y_ref, xy_ref = refs
     del before_ref
     parts = get_sides(s, (from_x_ref, from_y_ref, from_xy_ref), x_ref, y_ref, xy_ref)
     rest = jnp.zeros((s.bzp - s.span, s.waves), F32)
@@ -296,7 +301,6 @@
     apply_cells(s, field_ref, matrix_refs, sums_ref)
     join_sides(s, sums_ref, x_ref, y_ref, xy_ref)
     send_sides(s, x_ref, y_ref, xy_ref, msg_refs, (total, total, total))
-    join_cells(s, sums_ref, block_ref)
 
 
 def apply_cells(s, field_ref, matrix_refs, sums_ref):
@@ -357,31 +361,38 @@
     return jnp.concatenate([high, high, low], axis=0).astype(BF16)
 
 
-def middle_body(s, block_ref, from_x_ref, from_y_ref, from_xy_ref, own_ref, by_node_ref, *refs):
-    field_ref, *msg_refs, x_ref, y_ref, xy_ref, low_ref, high_ref = refs
+def swap_body(s, block_ref, from_x_ref, from_y_ref, from_xy_ref, own_ref, lowest_by_node_ref, *refs):
+    *msg_refs, x_ref, y_ref, xy_ref, low_ref, high_ref = refs
+    x_part, y_part, corner = get_sides(s, (from_x_ref, from_y_ref, from_xy_ref), x_ref, y_ref, xy_ref)
+    stack = stacked(from_columns(s, [corner, x_part, y_part, own_ref[...]]))
+    low_ref[0 : s.z_rows] = jnp.dot(lowest_by_node_ref[...], stack, preferred_element_type=F32)
+    for x in range(s.bx):
+        low_ref[x * s.by : (x + 1) * s.by] += block_ref[x, :, 0, :]
+        high_ref[x * s.by : (x + 1) * s.by] = block_ref[x, :, s.bz, :]
+    for ref, z in ((low_ref, 0), (high_ref, s.bz)):
+        for n in range(s.by):
+            ref[n : n + 1] += x_ref[n * s.span + z : n * s.span + z + 1]
+        for n in range(s.bx):
+            ref[n * s.by : n * s.by + 1] += y_ref[n * s.span + z : n * s.span + z + 1]
+        ref[0:1] += xy_ref[z : z + 1]
+        blank(ref, s.z_rows)
+    put_z(s, msg_refs, low_ref, high_ref)
+
+
+def middle_body(s, block_ref, from_x_ref, from_y_ref, from_xy_ref, own_ref, by_node_ref, field_ref, x_ref, y_ref, xy_ref):
     x_part, y_part, corner = get_sides(s, (from_x_ref, from_y_ref, from_xy_ref), x_ref, y_ref, xy_ref)
     stack = stacked(from_columns(s, [corner, x_part, y_part, own_ref[...]]))
     for x in range(s.bx):
         image = jnp.dot(by_node_ref[x], stack, preferred_element_type=F32)
         field_ref[x, 0 : s.by] = image.reshape(s.by, s.bzp, s.waves) + block_ref[x]
     add_sides(s, field_ref, x_ref, y_ref, xy_ref)
-    for x in range(s.bx):
-        low_ref[x * s.by : (x + 1) * s.by] = field_ref[x, 0 : s.by, 0, :]
-        high_ref[x * s.by : (x + 1) * s.by] = field_ref[x, 0 : s.by, s.bz, :]
-    blank(low_ref, s.z_rows)
-    blank(high_ref, s.z_rows)
-    put_z(s, msg_refs, low_ref, high_ref)
-
-
-def sums_body(s, field_ref, by_atom_ref, line_ref, total_ref, lowest_ref):
+
+
+def sums_body(s, field_ref, by_atom_ref, total_ref):
     total = jnp.zeros((s.locals, s.waves), F32)
     for x in range(s.bx):
         total = total + split_sums(by_atom_ref[x], s.locals, field_ref[x, 0 : s.by].reshape(s.by * s.bzp, s.waves))
     total_ref[...] = total
-    lowest = line_ref[...].T[0 : 2 * s.locals]
-    if s.z_plane > s.z_rows:
-        lowest = jnp.concatenate([lowest, jnp.zeros((2 * s.locals, s.z_plane - s.z_rows), F32)], axis=1)
-    lowest_ref[...] = lowest.astype(BF16)
 
 
 def second_down_body(s, before_ref, total_ref, lowest_ref, *refs):
@@ -425,11 +436,13 @@
     copies = []
     for x in range(s.bx):
         image = jnp.dot(by_node_ref[x], stack, preferred_element_type=F32)
-        plane_ref[...] = image.reshape(s.by, s.bzp, s.waves) + block_ref[x]
-        plane_ref[:, 0, :] += below_ref[x * s.by : (x + 1) * s.by]
-        out_ref[x] = 2.0 * plane_ref[:, 0 : s.bz] - start_ref[x]
-        copies.append(pltpu.make_async_copy(out_ref.at[x], out_hbm.at[x], sems.at[x]))
-        copies[x].start()
+        plane_ref[x] = image.reshape(s.by, s.bzp, s.waves) + block_ref[x]
+        plane_ref[x, :, 0, :] += below_ref[x * s.by : (x + 1) * s.by]
+        out_ref[x] = 2.0 * plane_ref[x, :, 0 : s.bz] - start_ref[x]
+        if (x + 1) % s.few_out == 0:
+            span = pl.ds(x + 1 - s.few_out, s.few_out)
+            copies.append(pltpu.make_async_copy(out_ref.at[span], out_hbm.at[span], sems.at[x // s.few_out]))
+            copies[-1].start()
     for copy in copies:
         copy.wait()
 
@@ -517,15 +530,13 @@
     ids = local_atoms(own)[:, None]
     plane = s.by * s.bzp
     sides = s.side_rows()
-    sums = s.scratch(s.cells[2], s.bx + 1, s.by + 1, s.group)
-    field, by_node, by_atom, line, *msgs, total, weight = call(
+    field, by_atom, wide, *msgs, total, weight = call(
         first_body,
         s,
         [
             s.extended(),
-            jax.ShapeDtypeStruct((s.bx, plane, 3 * s.locals), BF16),
             jax.ShapeDtypeStruct((s.bx, 2 * s.locals, plane), BF16),
-            jax.ShapeDtypeStruct((s.z_rows, 3 * s.locals), F32),
+            jax.ShapeDtypeStruct((s.z_rows, s.bzp, 2 * s.locals), F32),
         ]
         + s.z_msgs(s.z_both, s.z_sums)
         + [s.rows(s.locals), s.rows(s.locals)],
@@ -534,11 +545,10 @@
             pltpu.VMEM(projectors.shape, F32),
             pltpu.VMEM(slot_atoms.shape, jnp.int32),
             pltpu.VMEM((1, atom_count), F32),
-            pltpu.VMEM((s.bx * s.by * s.bz, 3 * s.locals), F32),
-            pltpu.VMEM((s.bx * s.by, s.bzp, 3 * s.locals), F32),
+            pltpu.VMEM((s.bx * s.by * s.bz, 2 * s.locals), F32),
             s.scratch(s.z_both),
             s.scratch(s.z_sums),
-            pltpu.SemaphoreType.DMA((s.bx // s.few,)),
+            pltpu.SemaphoreType.DMA((1,)),
             pltpu.SemaphoreType.DMA((3,)),
         ],
         [wavefunctions, projectors, slot_atoms, atom_coupling[None, :], ids],
@@ -557,32 +567,43 @@
 
     def cells(field, msgs, part):
         received = along_xy(msgs, -1)
-        _, block, *msgs, mine = call(
+        _, sums, *msgs, mine = call(
             cell_body,
             s,
-            [s.extended(), s.block()] + s.side_msgs() + [s.rows(2 * own)],
-            [sums] + sides,
+            [s.extended(), jax.ShapeDtypeStruct((s.cells[2], s.bx + 1, s.by + 1, s.group, s.waves), F32)]
+            + s.side_msgs()
+            + [s.rows(2 * own)],
+            sides,
             [field] + received + [part, weight] + matrices,
             aliases={0: 0},
         )
-        return block, along_xy(msgs, 1), mine
+        received = along_xy(msgs, 1)
+        (block,) = call(join_cells, s, [s.block()], [], [sums])
+        return block, received, mine
 
     block, received, mine = cells(field, msgs, part)
-    field, *msgs = call(
-        middle_body,
-        s,
-        [s.extended()] + s.z_msgs(s.z_plane, s.z_plane),
+    by_node, lowest, lowest_by_node = call(
+        node_body,
+        s,
+        [
+            jax.ShapeDtypeStruct((s.bx, plane, 3 * s.locals), BF16),
+            jax.ShapeDtypeStruct((2 * s.locals, s.z_plane), BF16),
+            jax.ShapeDtypeStruct((s.z_rows, 3 * s.locals), BF16),
+        ],
+        [],
+        [wide],
+    )
+    msgs = call(
+        swap_body,
+        s,
+        s.z_msgs(s.z_plane, s.z_plane),
         sides + [s.scratch(s.z_plane), s.scratch(s.z_plane)],
-        [block] + received + [mine, by_node],
-    )
-    received = along_z(s, msgs)
-    total, lowest = call(
-        sums_body,
-        s,
-        [s.rows(s.locals), jax.ShapeDtypeStruct((2 * s.locals, s.z_plane), BF16)],
-        [],
-        [field, by_atom, line],
-    )
+        [block] + received + [mine, lowest_by_node],
+    )
+    swapped = along_z(s, msgs)
+    (field,) = call(middle_body, s, [s.extended()], sides, [block] + received + [mine, by_node])
+    received = swapped
+    (total,) = call(sums_body, s, [s.rows(s.locals)], [], [field, by_atom])
     field, *msgs, part = call(
         second_down_body,
         s,
@@ -608,9 +629,9 @@
         [
             s.scratch(s.z_sums),
             s.scratch(s.z_both),
-            s.scratch(s.by, s.bzp),
+            s.scratch(s.bx, s.by, s.bzp),
             s.scratch(s.bx, s.by, s.bz),
-            pltpu.SemaphoreType.DMA((s.bx,)),
+            pltpu.SemaphoreType.DMA((s.bx // s.few_out,)),
         ],
         [wavefunctions, block, total, by_node] + received,
         out_spaces={0: pltpu.HBM},

time: 54.3 us -> 53.2 us (0.980)
  waiting for transfers between devices: 23 us -> 21.4 us
    ppermute x15, waiting for transfers between devices: 23 us -> 21.4 us  [shifted(): return lax.ppermute(value, AXES, pairs)]
    pallas_call x11 -> x15, Pallas kernels: 14.1 us -> 14.6 us  [call(): pl.pallas_call(functools.partial(body, sizes, *extra), out_shape=outs, in...]
  transfers between devices with their start and end apart: 15 -> 15, of which waited for: 7 -> 7; matrix products, arithmetic and copies ran while one was open for 0% -> 0% of each run, Pallas kernels for 10% -> 13%
where the time goes in v5:
time: 53.2 us; the launch traced here: 53 us
  waiting for transfers between devices  21.4 us (40%)
  starting transfers between devices  16.7 us (31%)
  Pallas kernels  14.6 us (27%)
    ppermute x15, waiting for transfers between devices, shifted(): return lax.ppermute(value, AXES, pairs)  21.4 us
    ppermute x15, starting transfers between devices, shifted(): return lax.ppermute(value, AXES, pairs)  16.7 us
    pallas_call x15, Pallas kernels, call(): pl.pallas_call(functools.partial(body, sizes, *extra), out_shape=outs, in...  14.6 us
  transfers between devices with their start and end apart: 15, of which 7 were waited for; matrix products, arithmetic and copies ran while one was open for 0% of the time, Pallas kernels for 13%

profile of v5, /device:TPU:0, one launch (start us, length us, event | category | flops | bytes accessed | tf_op | source)
XLA Modules:
  0.0 53.0 jit_solution(8278126913680567284)
XLA Ops:
  0.2 2.5 %shard_map.55 = (f32[13,13,16,256]{3,2,1,0:T(8,128)S(1)}, bf16[12,32,192]{2,1,0:T(8,128)(2,1)S(1)}, f32[144,16,32]{2,1,0:T(8,128)S(1)}, bf16[176,256]{1,0:T(8,12...) custom-call(f32[12,12,12,256]{3,2,1,0:T(8,128)} %start_ref.1, f32[1,16,1728]{2,1,0:T(8,128)} %rows_hbm.1, ...), custom_call_target="tpu_custom_call" | custom-call | tf_op jit(solution)/shard_map/pallas_call | solution.py:102
  2.7 3.0 %collective-permute-start = (bf16[176,256]{1,0:T(8,128)(2,1)S(1)}, bf16[176,256]{1,0:T(8,128)(2,1)S(1)}, u32[]{:S(2)}, u32[]{:S(2)}) collective-permute-start(bf16[176,256]{1,0:T(8,128)(2,1)S(1)} %get-tuple-element.39), channel_id=1, source_target_pairs={{0,1},{1,0},{2,3},{3,2},{4,5},{5,4},{6,7},{7,6},{8,9},{9,8},{10,11... | collective-permute-start | bytes 270344 | tf_op jit(solution)/shard_map/ppermute | solution.py:29
  5.7 2.4 %shard_map.56.early_ref.refs_0_ = bf16[2,2,400,400]{3,2,1,0:T(8,128)(2,1)S(1)} custom-call(bf16[2,2,343,2,343]{4,3,2,1,0:T(2,128)(2,1)} %bitcast.19), custom_call_target="tpu_custom_call" | custom-call | tf_op jit(solution)/shard_map/pallas_call | solution.py:102
  8.5 0.6 %collective-permute-start.1 = (bf16[176,256]{1,0:T(8,128)(2,1)S(1)}, bf16[176,256]{1,0:T(8,128)(2,1)S(1)}, u32[]{:S(2)}, u32[]{:S(2)}) collective-permute-start(bf16[176,256]{1,0:T(8,128)(2,1)S(1)} %get-tuple-element.41), channel_id=1, source_target_pairs={{0,24},{1,25},{2,26},{3,27},{4,28},{5,29},{6,30},{7,31},{8,0},{9,1... | collective-permute-start | bytes 270344 | tf_op jit(solution)/shard_map/ppermute | solution.py:29
  9.1 3.6 %collective-permute-start.2 = (bf16[176,256]{1,0:T(8,128)(2,1)S(1)}, bf16[176,256]{1,0:T(8,128)(2,1)S(1)}, u32[]{:S(2)}, u32[]{:S(2)}) collective-permute-start(bf16[176,256]{1,0:T(8,128)(2,1)S(1)} %get-tuple-element.42), channel_id=1, source_target_pairs={{0,6},{1,7},{2,0},{3,1},{4,2},{5,3},{6,4},{7,5},{8,14},{9,15},{10,... | collective-permute-start | bytes 270344 | tf_op jit(solution)/shard_map/ppermute | solution.py:29
  12.7 1.1 %collective-permute-start.3 = (bf16[32,256]{1,0:T(8,128)(2,1)S(1)}, bf16[32,256]{1,0:T(8,128)(2,1)S(1)}, u32[]{:S(2)}, u32[]{:S(2)}) collective-permute-start(bf16[32,256]{1,0:T(8,128)(2,1)S(1)} %get-tuple-element.43), channel_id=1, source_target_pairs={{0,30},{1,31},{2,24},{3,25},{4,26},{5,27},{6,28},{7,29},{8,6},{9,7... | collective-permute-start | bytes 49160 | tf_op jit(solution)/shard_map/ppermute | solution.py:29
  13.8 2.4 %shard_map.58.refs_1_ = bf16[2,2,400,400]{3,2,1,0:T(8,128)(2,1)S(1)} custom-call(bf16[2,2,343,2,343]{4,3,2,1,0:T(2,128)(2,1)} %bitcast.20), custom_call_target="tpu_custom_call" | custom-call | tf_op jit(solution)/shard_map/pallas_call | solution.py:102
  16.3 1.2 %shard_map.59 = (f32[13,13,16,256]{3,2,1,0:T(8,128)S(1)}, f32[2,13,13,8,256]{4,3,2,1,0:T(8,128)S(1)}, bf16[176,256]{1,0:T(8,128)(2,1)S(1)}, bf16[176,256]{1,0:T(...) custom-call(f32[13,13,16,256]{3,2,1,0:T(8,128)S(1)} %get-tuple-element.40.befo, ...), custom_call_target="tpu_custom_call", output_to_operand_aliasing={{0}: (0, {})} | custom-call | tf_op jit(solution)/shard_map/pallas_call | solution.py:102
  17.5 0.6 %collective-permute-start.4 = (bf16[176,256]{1,0:T(8,128)(2,1)S(1)}, bf16[176,256]{1,0:T(8,128)(2,1)S(1)}, u32[]{:S(2)}, u32[]{:S(2)}) collective-permute-start(bf16[176,256]{1,0:T(8,128)(2,1)S(1)} %get-tuple-element.47), channel_id=1, source_target_pairs={{0,8},{1,9},{2,10},{3,11},{4,12},{5,13},{6,14},{7,15},{8,16},{9,17... | collective-permute-start | bytes 270344 | tf_op jit(solution)/shard_map/ppermute | solution.py:29
  18.1 1.0 %collective-permute-start.5 = (bf16[176,256]{1,0:T(8,128)(2,1)S(1)}, bf16[176,256]{1,0:T(8,128)(2,1)S(1)}, u32[]{:S(2)}, u32[]{:S(2)}) collective-permute-start(bf16[176,256]{1,0:T(8,128)(2,1)S(1)} %get-tuple-element.48), channel_id=1, source_target_pairs={{0,2},{1,3},{2,4},{3,5},{4,6},{5,7},{6,0},{7,1},{8,10},{9,11},{10,... | collective-permute-start | bytes 270344 | tf_op jit(solution)/shard_map/ppermute | solution.py:29
  20.2 4.9 %collective-permute-done.6.from_xy_ref = bf16[32,256]{1,0:T(8,128)(2,1)S(1)} collective-permute-done((bf16[32,256]{1,0:T(8,128)(2,1)S(1)}, bf16[32,256]{1,0:T(8,128)(2,1)S(1)}, u32[]{:S(2)}, u32[]{:S(2)}) %collective-permute-start.6) | collective-permute-done | bytes 16416 | tf_op jit(solution)/shard_map/ppermute | solution.py:29
  25.7 1.5 %collective-permute-start.7 = (bf16[288,256]{1,0:T(8,128)(2,1)S(1)}, bf16[288,256]{1,0:T(8,128)(2,1)S(1)}, u32[]{:S(2)}, u32[]{:S(2)}) collective-permute-start(bf16[288,256]{1,0:T(8,128)(2,1)S(1)} %shard_map.64), channel_id=1, source_target_pairs={{0,1},{1,0},{2,3},{3,2},{4,5},{5,4},{6,7},{7,6},{8,9},{9,8},{10,11... | collective-permute-start | bytes 442376 | tf_op jit(solution)/shard_map/ppermute | solution.py:29
  27.2 0.5 shard_map.62.field_ref.before_ref
  27.7 0.5 shard_map.63.total_ref
  28.2 3.4 %collective-permute-done.7.refs_0_ = bf16[288,256]{1,0:T(8,128)(2,1)S(1)} collective-permute-done((bf16[288,256]{1,0:T(8,128)(2,1)S(1)}, bf16[288,256]{1,0:T(8,128)(2,1)S(1)}, u32[]{:S(2)}, u32[]{:S(2)}) %collective-permute-start.7) | collective-permute-done | bytes 147488 | tf_op jit(solution)/shard_map/ppermute | solution.py:29
  32.1 1.8 %collective-permute-start.9 = (bf16[176,256]{1,0:T(8,128)(2,1)S(1)}, bf16[176,256]{1,0:T(8,128)(2,1)S(1)}, u32[]{:S(2)}, u32[]{:S(2)}) collective-permute-start(bf16[176,256]{1,0:T(8,128)(2,1)S(1)} %get-tuple-element.58), channel_id=1, source_target_pairs={{0,6},{1,7},{2,0},{3,1},{4,2},{5,3},{6,4},{7,5},{8,14},{9,15},{10,... | collective-permute-start | bytes 270344 | tf_op jit(solution)/shard_map/ppermute | solution.py:29
  34.0 3.2 %collective-permute-done.10.from_xy_ref = bf16[32,256]{1,0:T(8,128)(2,1)S(1)} collective-permute-done((bf16[32,256]{1,0:T(8,128)(2,1)S(1)}, bf16[32,256]{1,0:T(8,128)(2,1)S(1)}, u32[]{:S(2)}, u32[]{:S(2)}) %collective-permute-start.10) | collective-permute-done | bytes 16416 | tf_op jit(solution)/shard_map/ppermute | solution.py:29
  37.3 1.2 %shard_map.66 = (f32[13,13,16,256]{3,2,1,0:T(8,128)S(1)}, f32[2,13,13,8,256]{4,3,2,1,0:T(8,128)S(1)}, bf16[176,256]{1,0:T(8,128)(2,1)S(1)}, bf16[176,256]{1,0:T(...) custom-call(f32[13,13,16,256]{3,2,1,0:T(8,128)S(1)} %get-tuple-element.56.befo, ...), custom_call_target="tpu_custom_call", output_to_operand_aliasing={{0}: (0, {})} | custom-call | tf_op jit(solution)/shard_map/pallas_call | solution.py:102
  38.4 0.9 %collective-permute-start.11 = (bf16[176,256]{1,0:T(8,128)(2,1)S(1)}, bf16[176,256]{1,0:T(8,128)(2,1)S(1)}, u32[]{:S(2)}, u32[]{:S(2)}) collective-permute-start(bf16[176,256]{1,0:T(8,128)(2,1)S(1)} %get-tuple-element.62), channel_id=1, source_target_pairs={{0,8},{1,9},{2,10},{3,11},{4,12},{5,13},{6,14},{7,15},{8,16},{9,17... | collective-permute-start | bytes 270344 | tf_op jit(solution)/shard_map/ppermute | solution.py:29
  39.7 0.4 shard_map.67.before_ref
  40.2 6.3 %collective-permute-done.13.from_xy_ref = bf16[32,256]{1,0:T(8,128)(2,1)S(1)} collective-permute-done((bf16[32,256]{1,0:T(8,128)(2,1)S(1)}, bf16[32,256]{1,0:T(8,128)(2,1)S(1)}, u32[]{:S(2)}, u32[]{:S(2)}) %collective-permute-start.13) | collective-permute-done | bytes 16416 | tf_op jit(solution)/shard_map/ppermute | solution.py:29
  46.7 1.5 %collective-permute-start.14 = (bf16[176,256]{1,0:T(8,128)(2,1)S(1)}, bf16[176,256]{1,0:T(8,128)(2,1)S(1)}, u32[]{:S(2)}, u32[]{:S(2)}) collective-permute-start(bf16[176,256]{1,0:T(8,128)(2,1)S(1)} %get-tuple-element.68), channel_id=1, source_target_pairs={{0,1},{1,0},{2,3},{3,2},{4,5},{5,4},{6,7},{7,6},{8,9},{9,8},{10,11... | collective-permute-start | bytes 270344 | tf_op jit(solution)/shard_map/ppermute | solution.py:29
  48.2 3.0 %collective-permute-done.14.refs_0_ = bf16[176,256]{1,0:T(8,128)(2,1)S(1)} collective-permute-done((bf16[176,256]{1,0:T(8,128)(2,1)S(1)}, bf16[176,256]{1,0:T(8,128)(2,1)S(1)}, u32[]{:S(2)}, u32[]{:S(2)}) %collective-permute-start.14) | collective-permute-done | bytes 90144 | tf_op jit(solution)/shard_map/ppermute | solution.py:29
  51.2 1.7 %shard_map.69 = f32[12,12,12,256]{3,2,1,0:T(8,128)} custom-call(f32[12,12,12,256]{3,2,1,0:T(8,128)S(1)} %copy-done, f32[12,12,16,256]{3,2,1,0:T(8,128)S(1)} %get-tuple-element.66.block_ref, f32[16,256]{1,0:T(8,128)S(1)} %get-tuple-element.67.total_ref, bf16[12,192,48]{2,1,0:T(8,128)(2,1)S(1)} %get-tuple-element.52.by_node_ref, ...), custom_call_target="tpu_custom_call" | custom-call | tf_op jit(solution)/shard_map/pallas_call | solution.py:102
  (25 shorter events, 3.2 us)
Async XLA Ops:
  2.7 5.6 %collective-permute-start = (bf16[176,256]{1,0:T(8,128)(2,1)S(1)}, bf16[176,256]{1,0:T(8,128)(2,1)S(1)}, u32[]{:S(2)}, u32[]{:S(2)}) collective-permute-start(bf16[176,256]{1,0:T(8,128)(2,1)S(1)} %get-tuple-element.39), channel_id=1, source_target_pairs={{0,1},{1,0},{2,3},{3,2},{4,5},{5,4},{6,7},{7,6},{8,9},{9,8},{10,11... | collective-permute-start | bytes 270344 | tf_op jit(solution)/shard_map/ppermute | solution.py:29
  8.5 7.8 %collective-permute-start.1 = (bf16[176,256]{1,0:T(8,128)(2,1)S(1)}, bf16[176,256]{1,0:T(8,128)(2,1)S(1)}, u32[]{:S(2)}, u32[]{:S(2)}) collective-permute-start(bf16[176,256]{1,0:T(8,128)(2,1)S(1)} %get-tuple-element.41), channel_id=1, source_target_pairs={{0,24},{1,25},{2,26},{3,27},{4,28},{5,29},{6,30},{7,31},{8,0},{9,1... | collective-permute-start | bytes 270344 | tf_op jit(solution)/shard_map/ppermute | solution.py:29
  9.1 7.2 %collective-permute-start.2 = (bf16[176,256]{1,0:T(8,128)(2,1)S(1)}, bf16[176,256]{1,0:T(8,128)(2,1)S(1)}, u32[]{:S(2)}, u32[]{:S(2)}) collective-permute-start(bf16[176,256]{1,0:T(8,128)(2,1)S(1)} %get-tuple-element.42), channel_id=1, source_target_pairs={{0,6},{1,7},{2,0},{3,1},{4,2},{5,3},{6,4},{7,5},{8,14},{9,15},{10,... | collective-permute-start | bytes 270344 | tf_op jit(solution)/shard_map/ppermute | solution.py:29
  12.7 3.6 %collective-permute-start.3 = (bf16[32,256]{1,0:T(8,128)(2,1)S(1)}, bf16[32,256]{1,0:T(8,128)(2,1)S(1)}, u32[]{:S(2)}, u32[]{:S(2)}) collective-permute-start(bf16[32,256]{1,0:T(8,128)(2,1)S(1)} %get-tuple-element.43), channel_id=1, source_target_pairs={{0,30},{1,31},{2,24},{3,25},{4,26},{5,27},{6,28},{7,29},{8,6},{9,7... | collective-permute-start | bytes 49160 | tf_op jit(solution)/shard_map/ppermute | solution.py:29
  17.5 7.6 %collective-permute-start.4 = (bf16[176,256]{1,0:T(8,128)(2,1)S(1)}, bf16[176,256]{1,0:T(8,128)(2,1)S(1)}, u32[]{:S(2)}, u32[]{:S(2)}) collective-permute-start(bf16[176,256]{1,0:T(8,128)(2,1)S(1)} %get-tuple-element.47), channel_id=1, source_target_pairs={{0,8},{1,9},{2,10},{3,11},{4,12},{5,13},{6,14},{7,15},{8,16},{9,17... | collective-permute-start | bytes 270344 | tf_op jit(solution)/shard_map/ppermute | solution.py:29
  18.1 7.3 %collective-permute-start.5 = (bf16[176,256]{1,0:T(8,128)(2,1)S(1)}, bf16[176,256]{1,0:T(8,128)(2,1)S(1)}, u32[]{:S(2)}, u32[]{:S(2)}) collective-permute-start(bf16[176,256]{1,0:T(8,128)(2,1)S(1)} %get-tuple-element.48), channel_id=1, source_target_pairs={{0,2},{1,3},{2,4},{3,5},{4,6},{5,7},{6,0},{7,1},{8,10},{9,11},{10,... | collective-permute-start | bytes 270344 | tf_op jit(solution)/shard_map/ppermute | solution.py:29
  19.2 5.9 %collective-permute-start.6 = (bf16[32,256]{1,0:T(8,128)(2,1)S(1)}, bf16[32,256]{1,0:T(8,128)(2,1)S(1)}, u32[]{:S(2)}, u32[]{:S(2)}) collective-permute-start(bf16[32,256]{1,0:T(8,128)(2,1)S(1)} %get-tuple-element.49), channel_id=1, source_target_pairs={{0,10},{1,11},{2,12},{3,13},{4,14},{5,15},{6,8},{7,9},{8,18},{9,19... | collective-permute-start | bytes 49160 | tf_op jit(solution)/shard_map/ppermute | solution.py:29
  25.7 5.9 %collective-permute-start.7 = (bf16[288,256]{1,0:T(8,128)(2,1)S(1)}, bf16[288,256]{1,0:T(8,128)(2,1)S(1)}, u32[]{:S(2)}, u32[]{:S(2)}) collective-permute-start(bf16[288,256]{1,0:T(8,128)(2,1)S(1)} %shard_map.64), channel_id=1, source_target_pairs={{0,1},{1,0},{2,3},{3,2},{4,5},{5,4},{6,7},{7,6},{8,9},{9,8},{10,11... | collective-permute-start | bytes 442376 | tf_op jit(solution)/shard_map/ppermute | solution.py:29
  32.0 5.2 %collective-permute-start.8 = (bf16[176,256]{1,0:T(8,128)(2,1)S(1)}, bf16[176,256]{1,0:T(8,128)(2,1)S(1)}, u32[]{:S(2)}, u32[]{:S(2)}) collective-permute-start(bf16[176,256]{1,0:T(8,128)(2,1)S(1)} %get-tuple-element.57), channel_id=1, source_target_pairs={{0,24},{1,25},{2,26},{3,27},{4,28},{5,29},{6,30},{7,31},{8,0},{9,1... | collective-permute-start | bytes 270344 | tf_op jit(solution)/shard_map/ppermute | solution.py:29
  32.1 5.2 %collective-permute-start.9 = (bf16[176,256]{1,0:T(8,128)(2,1)S(1)}, bf16[176,256]{1,0:T(8,128)(2,1)S(1)}, u32[]{:S(2)}, u32[]{:S(2)}) collective-permute-start(bf16[176,256]{1,0:T(8,128)(2,1)S(1)} %get-tuple-element.58), channel_id=1, source_target_pairs={{0,6},{1,7},{2,0},{3,1},{4,2},{5,3},{6,4},{7,5},{8,14},{9,15},{10,... | collective-permute-start | bytes 270344 | tf_op jit(solution)/shard_map/ppermute | solution.py:29
  33.9 3.4 %collective-permute-start.10 = (bf16[32,256]{1,0:T(8,128)(2,1)S(1)}, bf16[32,256]{1,0:T(8,128)(2,1)S(1)}, u32[]{:S(2)}, u32[]{:S(2)}) collective-permute-start(bf16[32,256]{1,0:T(8,128)(2,1)S(1)} %get-tuple-element.59), channel_id=1, source_target_pairs={{0,30},{1,31},{2,24},{3,25},{4,26},{5,27},{6,28},{7,29},{8,6},{9,7... | collective-permute-start | bytes 49160 | tf_op jit(solution)/shard_map/ppermute | solution.py:29
  38.4 8.0 %collective-permute-start.11 = (bf16[176,256]{1,0:T(8,128)(2,1)S(1)}, bf16[176,256]{1,0:T(8,128)(2,1)S(1)}, u32[]{:S(2)}, u32[]{:S(2)}) collective-permute-start(bf16[176,256]{1,0:T(8,128)(2,1)S(1)} %get-tuple-element.62), channel_id=1, source_target_pairs={{0,8},{1,9},{2,10},{3,11},{4,12},{5,13},{6,14},{7,15},{8,16},{9,17... | collective-permute-start | bytes 270344 | tf_op jit(solution)/shard_map/ppermute | solution.py:29
  39.3 7.1 %collective-permute-start.12 = (bf16[176,256]{1,0:T(8,128)(2,1)S(1)}, bf16[176,256]{1,0:T(8,128)(2,1)S(1)}, u32[]{:S(2)}, u32[]{:S(2)}) collective-permute-start(bf16[176,256]{1,0:T(8,128)(2,1)S(1)} %get-tuple-element.63), channel_id=1, source_target_pairs={{0,2},{1,3},{2,4},{3,5},{4,6},{5,7},{6,0},{7,1},{8,10},{9,11},{10,... | collective-permute-start | bytes 270344 | tf_op jit(solution)/shard_map/ppermute | solution.py:29
  39.6 6.8 %collective-permute-start.13 = (bf16[32,256]{1,0:T(8,128)(2,1)S(1)}, bf16[32,256]{1,0:T(8,128)(2,1)S(1)}, u32[]{:S(2)}, u32[]{:S(2)}) collective-permute-start(bf16[32,256]{1,0:T(8,128)(2,1)S(1)} %get-tuple-element.64), channel_id=1, source_target_pairs={{0,10},{1,11},{2,12},{3,13},{4,14},{5,15},{6,8},{7,9},{8,18},{9,19... | collective-permute-start | bytes 49160 | tf_op jit(solution)/shard_map/ppermute | solution.py:29
  40.1 11.1 %copy-start = (f32[12,12,12,256]{3,2,1,0:T(8,128)S(1)}, f32[12,12,12,256]{3,2,1,0:T(8,128)}, u32[]{:S(2)}) copy-start(f32[12,12,12,256]{3,2,1,0:T(8,128)} %start_ref.1) | copy-start | bytes 5308420
  46.7 4.6 %collective-permute-start.14 = (bf16[176,256]{1,0:T(8,128)(2,1)S(1)}, bf16[176,256]{1,0:T(8,128)(2,1)S(1)}, u32[]{:S(2)}, u32[]{:S(2)}) collective-permute-start(bf16[176,256]{1,0:T(8,128)(2,1)S(1)} %get-tuple-element.68), channel_id=1, source_target_pairs={{0,1},{1,0},{2,3},{3,2},{4,5},{5,4},{6,7},{7,6},{8,9},{9,8},{10,11... | collective-permute-start | bytes 270344 | tf_op jit(solution)/shard_map/ppermute | solution.py:29

commit v6 on v5

--- a/solution.py
+++ b/solution.py
@@ -62,9 +62,9 @@
         self.z_rows = self.bx * self.by
         self.x_rows = self.by * self.span
         self.y_rows = self.bx * self.span
-        self.x_msg = up_to(self.x_rows + 4 * own, 16)
-        self.y_msg = up_to(self.y_rows + 4 * own, 16)
-        self.xy_msg = up_to(self.span + 4 * own, 16)
+        self.x_msg = up_to(self.x_rows + 4 * own, 8)
+        self.y_msg = up_to(self.y_rows + 4 * own, 8)
+        self.xy_msg = up_to(self.span + 4 * own, 8)
         self.z_plane = up_to(self.z_rows, 16)
         self.z_sums = up_to(8 * own, 16)
         self.z_both = up_to(self.z_rows + 8 * own, 16)

time: 53.2 us -> 52.5 us (0.987)
  waiting for transfers between devices: 21.4 us -> 20.8 us
    ppermute x15, waiting for transfers between devices: 21.4 us -> 20.8 us  [shifted(): return lax.ppermute(value, AXES, pairs)]
where the time goes in v6:
time: 52.5 us; the launch traced here: 52.4 us
  waiting for transfers between devices  20.8 us (40%)
  starting transfers between devices  16.7 us (32%)
  Pallas kernels  14.5 us (28%)
    ppermute x15, waiting for transfers between devices, shifted(): return lax.ppermute(value, AXES, pairs)  20.8 us
    ppermute x15, starting transfers between devices, shifted(): return lax.ppermute(value, AXES, pairs)  16.7 us
    pallas_call x15, Pallas kernels, call(): pl.pallas_call(functools.partial(body, sizes, *extra), out_shape=outs, in...  14.5 us
  transfers between devices with their start and end apart: 15, of which 7 were waited for; matrix products, arithmetic and copies ran while one was open for 0% of the time, Pallas kernels for 13%

profile of v6, /device:TPU:0, one launch (start us, length us, event | category | flops | bytes accessed | tf_op | source)
XLA Modules:
  0.0 52.4 jit_solution(2497120308456348955)
XLA Ops:
  0.2 2.5 %shard_map.55 = (f32[13,13,16,256]{3,2,1,0:T(8,128)S(1)}, bf16[12,32,192]{2,1,0:T(8,128)(2,1)S(1)}, f32[144,16,32]{2,1,0:T(8,128)S(1)}, bf16[176,256]{1,0:T(8,12...) custom-call(f32[12,12,12,256]{3,2,1,0:T(8,128)} %start_ref.1, f32[1,16,1728]{2,1,0:T(8,128)} %rows_hbm.1, ...), custom_call_target="tpu_custom_call" | custom-call | tf_op jit(solution)/shard_map/pallas_call | solution.py:102
  2.7 3.0 %collective-permute-start = (bf16[176,256]{1,0:T(8,128)(2,1)S(1)}, bf16[176,256]{1,0:T(8,128)(2,1)S(1)}, u32[]{:S(2)}, u32[]{:S(2)}) collective-permute-start(bf16[176,256]{1,0:T(8,128)(2,1)S(1)} %get-tuple-element.39), channel_id=1, source_target_pairs={{0,1},{1,0},{2,3},{3,2},{4,5},{5,4},{6,7},{7,6},{8,9},{9,8},{10,11... | collective-permute-start | bytes 270344 | tf_op jit(solution)/shard_map/ppermute | solution.py:29
  5.7 2.4 %shard_map.56.early_ref.refs_0_ = bf16[2,2,400,400]{3,2,1,0:T(8,128)(2,1)S(1)} custom-call(bf16[2,2,343,2,343]{4,3,2,1,0:T(2,128)(2,1)} %bitcast.19), custom_call_target="tpu_custom_call" | custom-call | tf_op jit(solution)/shard_map/pallas_call | solution.py:102
  8.4 0.6 %collective-permute-start.1 = (bf16[168,256]{1,0:T(8,128)(2,1)S(1)}, bf16[168,256]{1,0:T(8,128)(2,1)S(1)}, u32[]{:S(2)}, u32[]{:S(2)}) collective-permute-start(bf16[168,256]{1,0:T(8,128)(2,1)S(1)} %get-tuple-element.41), channel_id=1, source_target_pairs={{0,24},{1,25},{2,26},{3,27},{4,28},{5,29},{6,30},{7,31},{8,0},{9,1... | collective-permute-start | bytes 258056 | tf_op jit(solution)/shard_map/ppermute | solution.py:29
  9.0 3.6 %collective-permute-start.2 = (bf16[168,256]{1,0:T(8,128)(2,1)S(1)}, bf16[168,256]{1,0:T(8,128)(2,1)S(1)}, u32[]{:S(2)}, u32[]{:S(2)}) collective-permute-start(bf16[168,256]{1,0:T(8,128)(2,1)S(1)} %get-tuple-element.42), channel_id=1, source_target_pairs={{0,6},{1,7},{2,0},{3,1},{4,2},{5,3},{6,4},{7,5},{8,14},{9,15},{10,... | collective-permute-start | bytes 258056 | tf_op jit(solution)/shard_map/ppermute | solution.py:29
  12.6 1.1 %collective-permute-start.3 = (bf16[24,256]{1,0:T(8,128)(2,1)S(1)}, bf16[24,256]{1,0:T(8,128)(2,1)S(1)}, u32[]{:S(2)}, u32[]{:S(2)}) collective-permute-start(bf16[24,256]{1,0:T(8,128)(2,1)S(1)} %get-tuple-element.43), channel_id=1, source_target_pairs={{0,30},{1,31},{2,24},{3,25},{4,26},{5,27},{6,28},{7,29},{8,6},{9,7... | collective-permute-start | bytes 36872 | tf_op jit(solution)/shard_map/ppermute | solution.py:29
  13.7 2.4 %shard_map.58.refs_1_ = bf16[2,2,400,400]{3,2,1,0:T(8,128)(2,1)S(1)} custom-call(bf16[2,2,343,2,343]{4,3,2,1,0:T(2,128)(2,1)} %bitcast.20), custom_call_target="tpu_custom_call" | custom-call | tf_op jit(solution)/shard_map/pallas_call | solution.py:102
  16.2 1.2 %shard_map.59 = (f32[13,13,16,256]{3,2,1,0:T(8,128)S(1)}, f32[2,13,13,8,256]{4,3,2,1,0:T(8,128)S(1)}, bf16[168,256]{1,0:T(8,128)(2,1)S(1)}, bf16[168,256]{1,0:T(...) custom-call(f32[13,13,16,256]{3,2,1,0:T(8,128)S(1)} %get-tuple-element.40.befo, ...), custom_call_target="tpu_custom_call", output_to_operand_aliasing={{0}: (0, {})} | custom-call | tf_op jit(solution)/shard_map/pallas_call | solution.py:102
  17.4 0.6 %collective-permute-start.4 = (bf16[168,256]{1,0:T(8,128)(2,1)S(1)}, bf16[168,256]{1,0:T(8,128)(2,1)S(1)}, u32[]{:S(2)}, u32[]{:S(2)}) collective-permute-start(bf16[168,256]{1,0:T(8,128)(2,1)S(1)} %get-tuple-element.47), channel_id=1, source_target_pairs={{0,8},{1,9},{2,10},{3,11},{4,12},{5,13},{6,14},{7,15},{8,16},{9,17... | collective-permute-start | bytes 258056 | tf_op jit(solution)/shard_map/ppermute | solution.py:29
  18.0 1.1 %collective-permute-start.5 = (bf16[168,256]{1,0:T(8,128)(2,1)S(1)}, bf16[168,256]{1,0:T(8,128)(2,1)S(1)}, u32[]{:S(2)}, u32[]{:S(2)}) collective-permute-start(bf16[168,256]{1,0:T(8,128)(2,1)S(1)} %get-tuple-element.48), channel_id=1, source_target_pairs={{0,2},{1,3},{2,4},{3,5},{4,6},{5,7},{6,0},{7,1},{8,10},{9,11},{10,... | collective-permute-start | bytes 258056 | tf_op jit(solution)/shard_map/ppermute | solution.py:29
  20.0 4.9 %collective-permute-done.6.from_xy_ref = bf16[24,256]{1,0:T(8,128)(2,1)S(1)} collective-permute-done((bf16[24,256]{1,0:T(8,128)(2,1)S(1)}, bf16[24,256]{1,0:T(8,128)(2,1)S(1)}, u32[]{:S(2)}, u32[]{:S(2)}) %collective-permute-start.6) | collective-permute-done | bytes 12320 | tf_op jit(solution)/shard_map/ppermute | solution.py:29
  25.3 1.6 %collective-permute-start.7 = (bf16[288,256]{1,0:T(8,128)(2,1)S(1)}, bf16[288,256]{1,0:T(8,128)(2,1)S(1)}, u32[]{:S(2)}, u32[]{:S(2)}) collective-permute-start(bf16[288,256]{1,0:T(8,128)(2,1)S(1)} %shard_map.64), channel_id=1, source_target_pairs={{0,1},{1,0},{2,3},{3,2},{4,5},{5,4},{6,7},{7,6},{8,9},{9,8},{10,11... | collective-permute-start | bytes 442376 | tf_op jit(solution)/shard_map/ppermute | solution.py:29
  26.9 0.5 shard_map.62.field_ref.before_ref
  27.4 0.5 shard_map.63.total_ref
  27.9 3.4 %collective-permute-done.7.refs_0_ = bf16[288,256]{1,0:T(8,128)(2,1)S(1)} collective-permute-done((bf16[288,256]{1,0:T(8,128)(2,1)S(1)}, bf16[288,256]{1,0:T(8,128)(2,1)S(1)}, u32[]{:S(2)}, u32[]{:S(2)}) %collective-permute-start.7) | collective-permute-done | bytes 147488 | tf_op jit(solution)/shard_map/ppermute | solution.py:29
  31.7 1.8 %collective-permute-start.9 = (bf16[168,256]{1,0:T(8,128)(2,1)S(1)}, bf16[168,256]{1,0:T(8,128)(2,1)S(1)}, u32[]{:S(2)}, u32[]{:S(2)}) collective-permute-start(bf16[168,256]{1,0:T(8,128)(2,1)S(1)} %get-tuple-element.58), channel_id=1, source_target_pairs={{0,6},{1,7},{2,0},{3,1},{4,2},{5,3},{6,4},{7,5},{8,14},{9,15},{10,... | collective-permute-start | bytes 258056 | tf_op jit(solution)/shard_map/ppermute | solution.py:29
  33.7 3.1 %collective-permute-done.10.from_xy_ref = bf16[24,256]{1,0:T(8,128)(2,1)S(1)} collective-permute-done((bf16[24,256]{1,0:T(8,128)(2,1)S(1)}, bf16[24,256]{1,0:T(8,128)(2,1)S(1)}, u32[]{:S(2)}, u32[]{:S(2)}) %collective-permute-start.10) | collective-permute-done | bytes 12320 | tf_op jit(solution)/shard_map/ppermute | solution.py:29
  36.8 1.2 %shard_map.66 = (f32[13,13,16,256]{3,2,1,0:T(8,128)S(1)}, f32[2,13,13,8,256]{4,3,2,1,0:T(8,128)S(1)}, bf16[168,256]{1,0:T(8,128)(2,1)S(1)}, bf16[168,256]{1,0:T(...) custom-call(f32[13,13,16,256]{3,2,1,0:T(8,128)S(1)} %get-tuple-element.56.befo, ...), custom_call_target="tpu_custom_call", output_to_operand_aliasing={{0}: (0, {})} | custom-call | tf_op jit(solution)/shard_map/pallas_call | solution.py:102
  38.0 1.0 %collective-permute-start.11 = (bf16[168,256]{1,0:T(8,128)(2,1)S(1)}, bf16[168,256]{1,0:T(8,128)(2,1)S(1)}, u32[]{:S(2)}, u32[]{:S(2)}) collective-permute-start(bf16[168,256]{1,0:T(8,128)(2,1)S(1)} %get-tuple-element.62), channel_id=1, source_target_pairs={{0,8},{1,9},{2,10},{3,11},{4,12},{5,13},{6,14},{7,15},{8,16},{9,17... | collective-permute-start | bytes 258056 | tf_op jit(solution)/shard_map/ppermute | solution.py:29
  39.3 0.4 shard_map.67.before_ref
  39.8 6.1 %collective-permute-done.13.from_xy_ref = bf16[24,256]{1,0:T(8,128)(2,1)S(1)} collective-permute-done((bf16[24,256]{1,0:T(8,128)(2,1)S(1)}, bf16[24,256]{1,0:T(8,128)(2,1)S(1)}, u32[]{:S(2)}, u32[]{:S(2)}) %collective-permute-start.13) | collective-permute-done | bytes 12320 | tf_op jit(solution)/shard_map/ppermute | solution.py:29
  46.0 1.6 %collective-permute-start.14 = (bf16[176,256]{1,0:T(8,128)(2,1)S(1)}, bf16[176,256]{1,0:T(8,128)(2,1)S(1)}, u32[]{:S(2)}, u32[]{:S(2)}) collective-permute-start(bf16[176,256]{1,0:T(8,128)(2,1)S(1)} %get-tuple-element.68), channel_id=1, source_target_pairs={{0,1},{1,0},{2,3},{3,2},{4,5},{5,4},{6,7},{7,6},{8,9},{9,8},{10,11... | collective-permute-start | bytes 270344 | tf_op jit(solution)/shard_map/ppermute | solution.py:29
  47.6 3.0 %collective-permute-done.14.refs_0_ = bf16[176,256]{1,0:T(8,128)(2,1)S(1)} collective-permute-done((bf16[176,256]{1,0:T(8,128)(2,1)S(1)}, bf16[176,256]{1,0:T(8,128)(2,1)S(1)}, u32[]{:S(2)}, u32[]{:S(2)}) %collective-permute-start.14) | collective-permute-done | bytes 90144 | tf_op jit(solution)/shard_map/ppermute | solution.py:29
  50.6 1.7 %shard_map.69 = f32[12,12,12,256]{3,2,1,0:T(8,128)} custom-call(f32[12,12,12,256]{3,2,1,0:T(8,128)S(1)} %copy-done, f32[12,12,16,256]{3,2,1,0:T(8,128)S(1)} %get-tuple-element.66.block_ref, f32[16,256]{1,0:T(8,128)S(1)} %get-tuple-element.67.total_ref, bf16[12,192,48]{2,1,0:T(8,128)(2,1)S(1)} %get-tuple-element.52.by_node_ref, ...), custom_call_target="tpu_custom_call" | custom-call | tf_op jit(solution)/shard_map/pallas_call | solution.py:102
  (25 shorter events, 3.0 us)
Async XLA Ops:
  2.7 5.6 %collective-permute-start = (bf16[176,256]{1,0:T(8,128)(2,1)S(1)}, bf16[176,256]{1,0:T(8,128)(2,1)S(1)}, u32[]{:S(2)}, u32[]{:S(2)}) collective-permute-start(bf16[176,256]{1,0:T(8,128)(2,1)S(1)} %get-tuple-element.39), channel_id=1, source_target_pairs={{0,1},{1,0},{2,3},{3,2},{4,5},{5,4},{6,7},{7,6},{8,9},{9,8},{10,11... | collective-permute-start | bytes 270344 | tf_op jit(solution)/shard_map/ppermute | solution.py:29
  8.4 7.8 %collective-permute-start.1 = (bf16[168,256]{1,0:T(8,128)(2,1)S(1)}, bf16[168,256]{1,0:T(8,128)(2,1)S(1)}, u32[]{:S(2)}, u32[]{:S(2)}) collective-permute-start(bf16[168,256]{1,0:T(8,128)(2,1)S(1)} %get-tuple-element.41), channel_id=1, source_target_pairs={{0,24},{1,25},{2,26},{3,27},{4,28},{5,29},{6,30},{7,31},{8,0},{9,1... | collective-permute-start | bytes 258056 | tf_op jit(solution)/shard_map/ppermute | solution.py:29
  9.0 7.2 %collective-permute-start.2 = (bf16[168,256]{1,0:T(8,128)(2,1)S(1)}, bf16[168,256]{1,0:T(8,128)(2,1)S(1)}, u32[]{:S(2)}, u32[]{:S(2)}) collective-permute-start(bf16[168,256]{1,0:T(8,128)(2,1)S(1)} %get-tuple-element.42), channel_id=1, source_target_pairs={{0,6},{1,7},{2,0},{3,1},{4,2},{5,3},{6,4},{7,5},{8,14},{9,15},{10,... | collective-permute-start | bytes 258056 | tf_op jit(solution)/shard_map/ppermute | solution.py:29
  12.6 3.6 %collective-permute-start.3 = (bf16[24,256]{1,0:T(8,128)(2,1)S(1)}, bf16[24,256]{1,0:T(8,128)(2,1)S(1)}, u32[]{:S(2)}, u32[]{:S(2)}) collective-permute-start(bf16[24,256]{1,0:T(8,128)(2,1)S(1)} %get-tuple-element.43), channel_id=1, source_target_pairs={{0,30},{1,31},{2,24},{3,25},{4,26},{5,27},{6,28},{7,29},{8,6},{9,7... | collective-permute-start | bytes 36872 | tf_op jit(solution)/shard_map/ppermute | solution.py:29
  17.4 7.6 %collective-permute-start.4 = (bf16[168,256]{1,0:T(8,128)(2,1)S(1)}, bf16[168,256]{1,0:T(8,128)(2,1)S(1)}, u32[]{:S(2)}, u32[]{:S(2)}) collective-permute-start(bf16[168,256]{1,0:T(8,128)(2,1)S(1)} %get-tuple-element.47), channel_id=1, source_target_pairs={{0,8},{1,9},{2,10},{3,11},{4,12},{5,13},{6,14},{7,15},{8,16},{9,17... | collective-permute-start | bytes 258056 | tf_op jit(solution)/shard_map/ppermute | solution.py:29
  18.0 7.1 %collective-permute-start.5 = (bf16[168,256]{1,0:T(8,128)(2,1)S(1)}, bf16[168,256]{1,0:T(8,128)(2,1)S(1)}, u32[]{:S(2)}, u32[]{:S(2)}) collective-permute-start(bf16[168,256]{1,0:T(8,128)(2,1)S(1)} %get-tuple-element.48), channel_id=1, source_target_pairs={{0,2},{1,3},{2,4},{3,5},{4,6},{5,7},{6,0},{7,1},{8,10},{9,11},{10,... | collective-permute-start | bytes 258056 | tf_op jit(solution)/shard_map/ppermute | solution.py:29
  19.1 5.9 %collective-permute-start.6 = (bf16[24,256]{1,0:T(8,128)(2,1)S(1)}, bf16[24,256]{1,0:T(8,128)(2,1)S(1)}, u32[]{:S(2)}, u32[]{:S(2)}) collective-permute-start(bf16[24,256]{1,0:T(8,128)(2,1)S(1)} %get-tuple-element.49), channel_id=1, source_target_pairs={{0,10},{1,11},{2,12},{3,13},{4,14},{5,15},{6,8},{7,9},{8,18},{9,19... | collective-permute-start | bytes 36872 | tf_op jit(solution)/shard_map/ppermute | solution.py:29
  25.3 5.9 %collective-permute-start.7 = (bf16[288,256]{1,0:T(8,128)(2,1)S(1)}, bf16[288,256]{1,0:T(8,128)(2,1)S(1)}, u32[]{:S(2)}, u32[]{:S(2)}) collective-permute-start(bf16[288,256]{1,0:T(8,128)(2,1)S(1)} %shard_map.64), channel_id=1, source_target_pairs={{0,1},{1,0},{2,3},{3,2},{4,5},{5,4},{6,7},{7,6},{8,9},{9,8},{10,11... | collective-permute-start | bytes 442376 | tf_op jit(solution)/shard_map/ppermute | solution.py:29
  31.7 5.1 %collective-permute-start.8 = (bf16[168,256]{1,0:T(8,128)(2,1)S(1)}, bf16[168,256]{1,0:T(8,128)(2,1)S(1)}, u32[]{:S(2)}, u32[]{:S(2)}) collective-permute-start(bf16[168,256]{1,0:T(8,128)(2,1)S(1)} %get-tuple-element.57), channel_id=1, source_target_pairs={{0,24},{1,25},{2,26},{3,27},{4,28},{5,29},{6,30},{7,31},{8,0},{9,1... | collective-permute-start | bytes 258056 | tf_op jit(solution)/shard_map/ppermute | solution.py:29
  31.7 5.1 %collective-permute-start.9 = (bf16[168,256]{1,0:T(8,128)(2,1)S(1)}, bf16[168,256]{1,0:T(8,128)(2,1)S(1)}, u32[]{:S(2)}, u32[]{:S(2)}) collective-permute-start(bf16[168,256]{1,0:T(8,128)(2,1)S(1)} %get-tuple-element.58), channel_id=1, source_target_pairs={{0,6},{1,7},{2,0},{3,1},{4,2},{5,3},{6,4},{7,5},{8,14},{9,15},{10,... | collective-permute-start | bytes 258056 | tf_op jit(solution)/shard_map/ppermute | solution.py:29
  33.5 3.3 %collective-permute-start.10 = (bf16[24,256]{1,0:T(8,128)(2,1)S(1)}, bf16[24,256]{1,0:T(8,128)(2,1)S(1)}, u32[]{:S(2)}, u32[]{:S(2)}) collective-permute-start(bf16[24,256]{1,0:T(8,128)(2,1)S(1)} %get-tuple-element.59), channel_id=1, source_target_pairs={{0,30},{1,31},{2,24},{3,25},{4,26},{5,27},{6,28},{7,29},{8,6},{9,7... | collective-permute-start | bytes 36872 | tf_op jit(solution)/shard_map/ppermute | solution.py:29
  38.0 7.9 %collective-permute-start.11 = (bf16[168,256]{1,0:T(8,128)(2,1)S(1)}, bf16[168,256]{1,0:T(8,128)(2,1)S(1)}, u32[]{:S(2)}, u32[]{:S(2)}) collective-permute-start(bf16[168,256]{1,0:T(8,128)(2,1)S(1)} %get-tuple-element.62), channel_id=1, source_target_pairs={{0,8},{1,9},{2,10},{3,11},{4,12},{5,13},{6,14},{7,15},{8,16},{9,17... | collective-permute-start | bytes 258056 | tf_op jit(solution)/shard_map/ppermute | solution.py:29
  38.9 6.9 %collective-permute-start.12 = (bf16[168,256]{1,0:T(8,128)(2,1)S(1)}, bf16[168,256]{1,0:T(8,128)(2,1)S(1)}, u32[]{:S(2)}, u32[]{:S(2)}) collective-permute-start(bf16[168,256]{1,0:T(8,128)(2,1)S(1)} %get-tuple-element.63), channel_id=1, source_target_pairs={{0,2},{1,3},{2,4},{3,5},{4,6},{5,7},{6,0},{7,1},{8,10},{9,11},{10,... | collective-permute-start | bytes 258056 | tf_op jit(solution)/shard_map/ppermute | solution.py:29
  39.2 6.6 %collective-permute-start.13 = (bf16[24,256]{1,0:T(8,128)(2,1)S(1)}, bf16[24,256]{1,0:T(8,128)(2,1)S(1)}, u32[]{:S(2)}, u32[]{:S(2)}) collective-permute-start(bf16[24,256]{1,0:T(8,128)(2,1)S(1)} %get-tuple-element.64), channel_id=1, source_target_pairs={{0,10},{1,11},{2,12},{3,13},{4,14},{5,15},{6,8},{7,9},{8,18},{9,19... | collective-permute-start | bytes 36872 | tf_op jit(solution)/shard_map/ppermute | solution.py:29
  39.8 10.9 %copy-start = (f32[12,12,12,256]{3,2,1,0:T(8,128)S(1)}, f32[12,12,12,256]{3,2,1,0:T(8,128)}, u32[]{:S(2)}) copy-start(f32[12,12,12,256]{3,2,1,0:T(8,128)} %start_ref.1) | copy-start | bytes 5308420
  46.0 4.6 %collective-permute-start.14 = (bf16[176,256]{1,0:T(8,128)(2,1)S(1)}, bf16[176,256]{1,0:T(8,128)(2,1)S(1)}, u32[]{:S(2)}, u32[]{:S(2)}) collective-permute-start(bf16[176,256]{1,0:T(8,128)(2,1)S(1)} %get-tuple-element.68), channel_id=1, source_target_pairs={{0,1},{1,0},{2,3},{3,2},{4,5},{5,4},{6,7},{7,6},{8,9},{9,8},{10,11... | collective-permute-start | bytes 270344 | tf_op jit(solution)/shard_map/ppermute | solution.py:29

commit v7 on v6

--- a/solution.py
+++ b/solution.py
@@ -110,7 +110,7 @@
     )(*args)
 
 
-def local_atoms(own):
+def local_atoms(own, shape):
     sizes = [lax.axis_size(axis) for axis in AXES]
     here = [lax.axis_index(axis) for axis in AXES]
     ids = []
@@ -120,7 +120,11 @@
                 x, y, z = (lax.rem(h + n - d, n) for h, n, d in zip(here, sizes, (dx, dy, dz)))
                 owner = (x * sizes[1] + y) * sizes[2] + z
                 ids += [owner * own + a for a in range(own)]
-    return jnp.stack(ids).astype(jnp.int32)
+    row = lax.broadcasted_iota(jnp.int32, shape, 0)
+    table = jnp.zeros(shape, jnp.int32)
+    for n, atom in enumerate(ids):
+        table = jnp.where(row == n, atom, table)
+    return table
 
 
 def blank(rows_ref, first):
@@ -170,7 +174,7 @@
 
 
 def first_body(
-    s, start_hbm, rows_hbm, slots_hbm, coupling_hbm, ids_ref,
+    s, start_hbm, rows_hbm, slots_hbm, coupling_hbm,
     field_ref, by_atom_ref, wide_ref, *refs
 ):
     *msg_refs, total_ref, weight_ref, start_ref, rows_ref, slots_ref, coupling_ref, tall_ref, low_ref, high_ref, sems, small_sems = refs
@@ -185,7 +189,8 @@
     whole.start()
     for copy in small:
         copy.wait()
-    chosen = (ids_ref[...] == slots_ref[...]).astype(F32).astype(BF16)
+    slots = slots_ref[...]
+    chosen = (local_atoms(s.own, (s.locals, slots.shape[1])) == slots).astype(F32).astype(BF16)
     rows = rows_ref[0]
     high = rows.astype(BF16)
     low = (rows - high.astype(F32)).astype(BF16)
@@ -213,7 +218,7 @@
     put_split(high_ref, 0, total[half:])
     put_z(s, msg_refs, low_ref, high_ref)
     atoms = lax.broadcasted_iota(jnp.int32, (s.locals, coupling_ref.shape[1]), 1)
-    weight = jnp.sum(jnp.where(atoms == ids_ref[...], coupling_ref[...], 0.0), axis=1, keepdims=True)
+    weight = jnp.sum(jnp.where(atoms == local_atoms(s.own, atoms.shape), coupling_ref[...], 0.0), axis=1, keepdims=True)
     weight_ref[...] = jnp.broadcast_to(weight, weight_ref.shape)
 
 
@@ -527,7 +532,6 @@
         devices *= lax.axis_size(axis)
     own = atom_count // devices
     s = Sizes(wavefunctions.shape, cell_matrices.shape, own, lax.axis_size("gz") == 2)
-    ids = local_atoms(own)[:, None]
     plane = s.by * s.bzp
     sides = s.side_rows()
     field, by_atom, wide, *msgs, total, weight = call(
@@ -551,7 +555,7 @@
             pltpu.SemaphoreType.DMA((1,)),
             pltpu.SemaphoreType.DMA((3,)),
         ],
-        [wavefunctions, projectors, slot_atoms, atom_coupling[None, :], ids],
+        [wavefunctions, projectors, slot_atoms, atom_coupling[None, :]],
         spaces={0: pltpu.HBM, 1: pltpu.HBM, 2: pltpu.HBM, 3: pltpu.HBM},
     )
     matrices = [regrouped(s, cell_matrices, part) for part in range(s.cells[0])]

time: 52.5 us -> 52.4 us (level)
  no operation moved by 1% of the time
where the time goes in v7:
time: 52.4 us; the launch traced here: 52.2 us
  waiting for transfers between devices  20.8 us (40%)
  starting transfers between devices  16.8 us (32%)
  Pallas kernels  14.5 us (28%)
    ppermute x15, waiting for transfers between devices, shifted(): return lax.ppermute(value, AXES, pairs)  20.8 us
    ppermute x15, starting transfers between devices, shifted(): return lax.ppermute(value, AXES, pairs)  16.8 us
    pallas_call x15, Pallas kernels, call(): pl.pallas_call(functools.partial(body, sizes, *extra), out_shape=outs, in...  14.5 us
  transfers between devices with their start and end apart: 15, of which 7 were waited for; matrix products, arithmetic and copies ran while one was open for 0% of the time, Pallas kernels for 13%

profile of v7, /device:TPU:0, one launch (start us, length us, event | category | flops | bytes accessed | tf_op | source)
XLA Modules:
  0.0 52.2 jit_solution(14178894815012175302)
XLA Ops:
  0.0 2.5 %shard_map.55 = (f32[13,13,16,256]{3,2,1,0:T(8,128)S(1)}, bf16[12,32,192]{2,1,0:T(8,128)(2,1)S(1)}, f32[144,16,32]{2,1,0:T(8,128)S(1)}, bf16[176,256]{1,0:T(8,12...) custom-call(f32[12,12,12,256]{3,2,1,0:T(8,128)} %start_ref.1, f32[1,16,1728]{2,1,0:T(8,128)} %rows_hbm.1, ...), custom_call_target="tpu_custom_call" | custom-call | tf_op jit(solution)/shard_map/pallas_call | solution.py:102
  2.5 3.0 %collective-permute-start = (bf16[176,256]{1,0:T(8,128)(2,1)S(1)}, bf16[176,256]{1,0:T(8,128)(2,1)S(1)}, u32[]{:S(2)}, u32[]{:S(2)}) collective-permute-start(bf16[176,256]{1,0:T(8,128)(2,1)S(1)} %get-tuple-element.39), channel_id=1, source_target_pairs={{0,1},{1,0},{2,3},{3,2},{4,5},{5,4},{6,7},{7,6},{8,9},{9,8},{10,11... | collective-permute-start | bytes 270344 | tf_op jit(solution)/shard_map/ppermute | solution.py:29
  5.5 2.4 %shard_map.56.early_ref.refs_0_ = bf16[2,2,400,400]{3,2,1,0:T(8,128)(2,1)S(1)} custom-call(bf16[2,2,343,2,343]{4,3,2,1,0:T(2,128)(2,1)} %bitcast.2), custom_call_target="tpu_custom_call" | custom-call | tf_op jit(solution)/shard_map/pallas_call | solution.py:102
  8.3 0.6 %collective-permute-start.1 = (bf16[168,256]{1,0:T(8,128)(2,1)S(1)}, bf16[168,256]{1,0:T(8,128)(2,1)S(1)}, u32[]{:S(2)}, u32[]{:S(2)}) collective-permute-start(bf16[168,256]{1,0:T(8,128)(2,1)S(1)} %get-tuple-element.41), channel_id=1, source_target_pairs={{0,24},{1,25},{2,26},{3,27},{4,28},{5,29},{6,30},{7,31},{8,0},{9,1... | collective-permute-start | bytes 258056 | tf_op jit(solution)/shard_map/ppermute | solution.py:29
  8.9 3.6 %collective-permute-start.2 = (bf16[168,256]{1,0:T(8,128)(2,1)S(1)}, bf16[168,256]{1,0:T(8,128)(2,1)S(1)}, u32[]{:S(2)}, u32[]{:S(2)}) collective-permute-start(bf16[168,256]{1,0:T(8,128)(2,1)S(1)} %get-tuple-element.42), channel_id=1, source_target_pairs={{0,6},{1,7},{2,0},{3,1},{4,2},{5,3},{6,4},{7,5},{8,14},{9,15},{10,... | collective-permute-start | bytes 258056 | tf_op jit(solution)/shard_map/ppermute | solution.py:29
  12.5 1.1 %collective-permute-start.3 = (bf16[24,256]{1,0:T(8,128)(2,1)S(1)}, bf16[24,256]{1,0:T(8,128)(2,1)S(1)}, u32[]{:S(2)}, u32[]{:S(2)}) collective-permute-start(bf16[24,256]{1,0:T(8,128)(2,1)S(1)} %get-tuple-element.43), channel_id=1, source_target_pairs={{0,30},{1,31},{2,24},{3,25},{4,26},{5,27},{6,28},{7,29},{8,6},{9,7... | collective-permute-start | bytes 36872 | tf_op jit(solution)/shard_map/ppermute | solution.py:29
  13.6 2.4 %shard_map.58.refs_1_ = bf16[2,2,400,400]{3,2,1,0:T(8,128)(2,1)S(1)} custom-call(bf16[2,2,343,2,343]{4,3,2,1,0:T(2,128)(2,1)} %bitcast.3), custom_call_target="tpu_custom_call" | custom-call | tf_op jit(solution)/shard_map/pallas_call | solution.py:102
  16.1 1.2 %shard_map.59 = (f32[13,13,16,256]{3,2,1,0:T(8,128)S(1)}, f32[2,13,13,8,256]{4,3,2,1,0:T(8,128)S(1)}, bf16[168,256]{1,0:T(8,128)(2,1)S(1)}, bf16[168,256]{1,0:T(...) custom-call(f32[13,13,16,256]{3,2,1,0:T(8,128)S(1)} %get-tuple-element.40.befo, ...), custom_call_target="tpu_custom_call", output_to_operand_aliasing={{0}: (0, {})} | custom-call | tf_op jit(solution)/shard_map/pallas_call | solution.py:102
  17.2 0.6 %collective-permute-start.4 = (bf16[168,256]{1,0:T(8,128)(2,1)S(1)}, bf16[168,256]{1,0:T(8,128)(2,1)S(1)}, u32[]{:S(2)}, u32[]{:S(2)}) collective-permute-start(bf16[168,256]{1,0:T(8,128)(2,1)S(1)} %get-tuple-element.47), channel_id=1, source_target_pairs={{0,8},{1,9},{2,10},{3,11},{4,12},{5,13},{6,14},{7,15},{8,16},{9,17... | collective-permute-start | bytes 258056 | tf_op jit(solution)/shard_map/ppermute | solution.py:29
  17.9 1.1 %collective-permute-start.5 = (bf16[168,256]{1,0:T(8,128)(2,1)S(1)}, bf16[168,256]{1,0:T(8,128)(2,1)S(1)}, u32[]{:S(2)}, u32[]{:S(2)}) collective-permute-start(bf16[168,256]{1,0:T(8,128)(2,1)S(1)} %get-tuple-element.48), channel_id=1, source_target_pairs={{0,2},{1,3},{2,4},{3,5},{4,6},{5,7},{6,0},{7,1},{8,10},{9,11},{10,... | collective-permute-start | bytes 258056 | tf_op jit(solution)/shard_map/ppermute | solution.py:29
  19.9 5.0 %collective-permute-done.6.from_xy_ref = bf16[24,256]{1,0:T(8,128)(2,1)S(1)} collective-permute-done((bf16[24,256]{1,0:T(8,128)(2,1)S(1)}, bf16[24,256]{1,0:T(8,128)(2,1)S(1)}, u32[]{:S(2)}, u32[]{:S(2)}) %collective-permute-start.6) | collective-permute-done | bytes 12320 | tf_op jit(solution)/shard_map/ppermute | solution.py:29
  25.2 1.6 %collective-permute-start.7 = (bf16[288,256]{1,0:T(8,128)(2,1)S(1)}, bf16[288,256]{1,0:T(8,128)(2,1)S(1)}, u32[]{:S(2)}, u32[]{:S(2)}) collective-permute-start(bf16[288,256]{1,0:T(8,128)(2,1)S(1)} %shard_map.64), channel_id=1, source_target_pairs={{0,1},{1,0},{2,3},{3,2},{4,5},{5,4},{6,7},{7,6},{8,9},{9,8},{10,11... | collective-permute-start | bytes 442376 | tf_op jit(solution)/shard_map/ppermute | solution.py:29
  26.7 0.5 shard_map.62.field_ref.before_ref
  27.2 0.5 shard_map.63.total_ref
  27.7 3.4 %collective-permute-done.7.refs_0_ = bf16[288,256]{1,0:T(8,128)(2,1)S(1)} collective-permute-done((bf16[288,256]{1,0:T(8,128)(2,1)S(1)}, bf16[288,256]{1,0:T(8,128)(2,1)S(1)}, u32[]{:S(2)}, u32[]{:S(2)}) %collective-permute-start.7) | collective-permute-done | bytes 147488 | tf_op jit(solution)/shard_map/ppermute | solution.py:29
  31.6 1.8 %collective-permute-start.9 = (bf16[168,256]{1,0:T(8,128)(2,1)S(1)}, bf16[168,256]{1,0:T(8,128)(2,1)S(1)}, u32[]{:S(2)}, u32[]{:S(2)}) collective-permute-start(bf16[168,256]{1,0:T(8,128)(2,1)S(1)} %get-tuple-element.58), channel_id=1, source_target_pairs={{0,6},{1,7},{2,0},{3,1},{4,2},{5,3},{6,4},{7,5},{8,14},{9,15},{10,... | collective-permute-start | bytes 258056 | tf_op jit(solution)/shard_map/ppermute | solution.py:29
  33.6 3.1 %collective-permute-done.10.from_xy_ref = bf16[24,256]{1,0:T(8,128)(2,1)S(1)} collective-permute-done((bf16[24,256]{1,0:T(8,128)(2,1)S(1)}, bf16[24,256]{1,0:T(8,128)(2,1)S(1)}, u32[]{:S(2)}, u32[]{:S(2)}) %collective-permute-start.10) | collective-permute-done | bytes 12320 | tf_op jit(solution)/shard_map/ppermute | solution.py:29
  36.6 1.2 %shard_map.66 = (f32[13,13,16,256]{3,2,1,0:T(8,128)S(1)}, f32[2,13,13,8,256]{4,3,2,1,0:T(8,128)S(1)}, bf16[168,256]{1,0:T(8,128)(2,1)S(1)}, bf16[168,256]{1,0:T(...) custom-call(f32[13,13,16,256]{3,2,1,0:T(8,128)S(1)} %get-tuple-element.56.befo, ...), custom_call_target="tpu_custom_call", output_to_operand_aliasing={{0}: (0, {})} | custom-call | tf_op jit(solution)/shard_map/pallas_call | solution.py:102
  37.8 1.0 %collective-permute-start.11 = (bf16[168,256]{1,0:T(8,128)(2,1)S(1)}, bf16[168,256]{1,0:T(8,128)(2,1)S(1)}, u32[]{:S(2)}, u32[]{:S(2)}) collective-permute-start(bf16[168,256]{1,0:T(8,128)(2,1)S(1)} %get-tuple-element.62), channel_id=1, source_target_pairs={{0,8},{1,9},{2,10},{3,11},{4,12},{5,13},{6,14},{7,15},{8,16},{9,17... | collective-permute-start | bytes 258056 | tf_op jit(solution)/shard_map/ppermute | solution.py:29
  39.2 0.4 shard_map.67.before_ref
  39.6 6.1 %collective-permute-done.13.from_xy_ref = bf16[24,256]{1,0:T(8,128)(2,1)S(1)} collective-permute-done((bf16[24,256]{1,0:T(8,128)(2,1)S(1)}, bf16[24,256]{1,0:T(8,128)(2,1)S(1)}, u32[]{:S(2)}, u32[]{:S(2)}) %collective-permute-start.13) | collective-permute-done | bytes 12320 | tf_op jit(solution)/shard_map/ppermute | solution.py:29
  45.9 1.6 %collective-permute-start.14 = (bf16[176,256]{1,0:T(8,128)(2,1)S(1)}, bf16[176,256]{1,0:T(8,128)(2,1)S(1)}, u32[]{:S(2)}, u32[]{:S(2)}) collective-permute-start(bf16[176,256]{1,0:T(8,128)(2,1)S(1)} %get-tuple-element.68), channel_id=1, source_target_pairs={{0,1},{1,0},{2,3},{3,2},{4,5},{5,4},{6,7},{7,6},{8,9},{9,8},{10,11... | collective-permute-start | bytes 270344 | tf_op jit(solution)/shard_map/ppermute | solution.py:29
  47.4 3.0 %collective-permute-done.14.refs_0_ = bf16[176,256]{1,0:T(8,128)(2,1)S(1)} collective-permute-done((bf16[176,256]{1,0:T(8,128)(2,1)S(1)}, bf16[176,256]{1,0:T(8,128)(2,1)S(1)}, u32[]{:S(2)}, u32[]{:S(2)}) %collective-permute-start.14) | collective-permute-done | bytes 90144 | tf_op jit(solution)/shard_map/ppermute | solution.py:29
  50.5 1.7 %shard_map.69 = f32[12,12,12,256]{3,2,1,0:T(8,128)} custom-call(f32[12,12,12,256]{3,2,1,0:T(8,128)S(1)} %copy-done, f32[12,12,16,256]{3,2,1,0:T(8,128)S(1)} %get-tuple-element.66.block_ref, f32[16,256]{1,0:T(8,128)S(1)} %get-tuple-element.67.total_ref, bf16[12,192,48]{2,1,0:T(8,128)(2,1)S(1)} %get-tuple-element.52.by_node_ref, ...), custom_call_target="tpu_custom_call" | custom-call | tf_op jit(solution)/shard_map/pallas_call | solution.py:102
  (23 shorter events, 2.8 us)
Async XLA Ops:
  2.5 5.6 %collective-permute-start = (bf16[176,256]{1,0:T(8,128)(2,1)S(1)}, bf16[176,256]{1,0:T(8,128)(2,1)S(1)}, u32[]{:S(2)}, u32[]{:S(2)}) collective-permute-start(bf16[176,256]{1,0:T(8,128)(2,1)S(1)} %get-tuple-element.39), channel_id=1, source_target_pairs={{0,1},{1,0},{2,3},{3,2},{4,5},{5,4},{6,7},{7,6},{8,9},{9,8},{10,11... | collective-permute-start | bytes 270344 | tf_op jit(solution)/shard_map/ppermute | solution.py:29
  8.3 7.8 %collective-permute-start.1 = (bf16[168,256]{1,0:T(8,128)(2,1)S(1)}, bf16[168,256]{1,0:T(8,128)(2,1)S(1)}, u32[]{:S(2)}, u32[]{:S(2)}) collective-permute-start(bf16[168,256]{1,0:T(8,128)(2,1)S(1)} %get-tuple-element.41), channel_id=1, source_target_pairs={{0,24},{1,25},{2,26},{3,27},{4,28},{5,29},{6,30},{7,31},{8,0},{9,1... | collective-permute-start | bytes 258056 | tf_op jit(solution)/shard_map/ppermute | solution.py:29
  8.9 7.2 %collective-permute-start.2 = (bf16[168,256]{1,0:T(8,128)(2,1)S(1)}, bf16[168,256]{1,0:T(8,128)(2,1)S(1)}, u32[]{:S(2)}, u32[]{:S(2)}) collective-permute-start(bf16[168,256]{1,0:T(8,128)(2,1)S(1)} %get-tuple-element.42), channel_id=1, source_target_pairs={{0,6},{1,7},{2,0},{3,1},{4,2},{5,3},{6,4},{7,5},{8,14},{9,15},{10,... | collective-permute-start | bytes 258056 | tf_op jit(solution)/shard_map/ppermute | solution.py:29
  12.5 3.6 %collective-permute-start.3 = (bf16[24,256]{1,0:T(8,128)(2,1)S(1)}, bf16[24,256]{1,0:T(8,128)(2,1)S(1)}, u32[]{:S(2)}, u32[]{:S(2)}) collective-permute-start(bf16[24,256]{1,0:T(8,128)(2,1)S(1)} %get-tuple-element.43), channel_id=1, source_target_pairs={{0,30},{1,31},{2,24},{3,25},{4,26},{5,27},{6,28},{7,29},{8,6},{9,7... | collective-permute-start | bytes 36872 | tf_op jit(solution)/shard_map/ppermute | solution.py:29
  17.2 7.6 %collective-permute-start.4 = (bf16[168,256]{1,0:T(8,128)(2,1)S(1)}, bf16[168,256]{1,0:T(8,128)(2,1)S(1)}, u32[]{:S(2)}, u32[]{:S(2)}) collective-permute-start(bf16[168,256]{1,0:T(8,128)(2,1)S(1)} %get-tuple-element.47), channel_id=1, source_target_pairs={{0,8},{1,9},{2,10},{3,11},{4,12},{5,13},{6,14},{7,15},{8,16},{9,17... | collective-permute-start | bytes 258056 | tf_op jit(solution)/shard_map/ppermute | solution.py:29
  17.9 7.1 %collective-permute-start.5 = (bf16[168,256]{1,0:T(8,128)(2,1)S(1)}, bf16[168,256]{1,0:T(8,128)(2,1)S(1)}, u32[]{:S(2)}, u32[]{:S(2)}) collective-permute-start(bf16[168,256]{1,0:T(8,128)(2,1)S(1)} %get-tuple-element.48), channel_id=1, source_target_pairs={{0,2},{1,3},{2,4},{3,5},{4,6},{5,7},{6,0},{7,1},{8,10},{9,11},{10,... | collective-permute-start | bytes 258056 | tf_op jit(solution)/shard_map/ppermute | solution.py:29
  18.9 5.9 %collective-permute-start.6 = (bf16[24,256]{1,0:T(8,128)(2,1)S(1)}, bf16[24,256]{1,0:T(8,128)(2,1)S(1)}, u32[]{:S(2)}, u32[]{:S(2)}) collective-permute-start(bf16[24,256]{1,0:T(8,128)(2,1)S(1)} %get-tuple-element.49), channel_id=1, source_target_pairs={{0,10},{1,11},{2,12},{3,13},{4,14},{5,15},{6,8},{7,9},{8,18},{9,19... | collective-permute-start | bytes 36872 | tf_op jit(solution)/shard_map/ppermute | solution.py:29
  25.2 5.9 %collective-permute-start.7 = (bf16[288,256]{1,0:T(8,128)(2,1)S(1)}, bf16[288,256]{1,0:T(8,128)(2,1)S(1)}, u32[]{:S(2)}, u32[]{:S(2)}) collective-permute-start(bf16[288,256]{1,0:T(8,128)(2,1)S(1)} %shard_map.64), channel_id=1, source_target_pairs={{0,1},{1,0},{2,3},{3,2},{4,5},{5,4},{6,7},{7,6},{8,9},{9,8},{10,11... | collective-permute-start | bytes 442376 | tf_op jit(solution)/shard_map/ppermute | solution.py:29
  31.5 5.1 %collective-permute-start.8 = (bf16[168,256]{1,0:T(8,128)(2,1)S(1)}, bf16[168,256]{1,0:T(8,128)(2,1)S(1)}, u32[]{:S(2)}, u32[]{:S(2)}) collective-permute-start(bf16[168,256]{1,0:T(8,128)(2,1)S(1)} %get-tuple-element.57), channel_id=1, source_target_pairs={{0,24},{1,25},{2,26},{3,27},{4,28},{5,29},{6,30},{7,31},{8,0},{9,1... | collective-permute-start | bytes 258056 | tf_op jit(solution)/shard_map/ppermute | solution.py:29
  31.6 5.1 %collective-permute-start.9 = (bf16[168,256]{1,0:T(8,128)(2,1)S(1)}, bf16[168,256]{1,0:T(8,128)(2,1)S(1)}, u32[]{:S(2)}, u32[]{:S(2)}) collective-permute-start(bf16[168,256]{1,0:T(8,128)(2,1)S(1)} %get-tuple-element.58), channel_id=1, source_target_pairs={{0,6},{1,7},{2,0},{3,1},{4,2},{5,3},{6,4},{7,5},{8,14},{9,15},{10,... | collective-permute-start | bytes 258056 | tf_op jit(solution)/shard_map/ppermute | solution.py:29
  33.4 3.3 %collective-permute-start.10 = (bf16[24,256]{1,0:T(8,128)(2,1)S(1)}, bf16[24,256]{1,0:T(8,128)(2,1)S(1)}, u32[]{:S(2)}, u32[]{:S(2)}) collective-permute-start(bf16[24,256]{1,0:T(8,128)(2,1)S(1)} %get-tuple-element.59), channel_id=1, source_target_pairs={{0,30},{1,31},{2,24},{3,25},{4,26},{5,27},{6,28},{7,29},{8,6},{9,7... | collective-permute-start | bytes 36872 | tf_op jit(solution)/shard_map/ppermute | solution.py:29
  37.8 7.9 %collective-permute-start.11 = (bf16[168,256]{1,0:T(8,128)(2,1)S(1)}, bf16[168,256]{1,0:T(8,128)(2,1)S(1)}, u32[]{:S(2)}, u32[]{:S(2)}) collective-permute-start(bf16[168,256]{1,0:T(8,128)(2,1)S(1)} %get-tuple-element.62), channel_id=1, source_target_pairs={{0,8},{1,9},{2,10},{3,11},{4,12},{5,13},{6,14},{7,15},{8,16},{9,17... | collective-permute-start | bytes 258056 | tf_op jit(solution)/shard_map/ppermute | solution.py:29
  38.8 6.9 %collective-permute-start.12 = (bf16[168,256]{1,0:T(8,128)(2,1)S(1)}, bf16[168,256]{1,0:T(8,128)(2,1)S(1)}, u32[]{:S(2)}, u32[]{:S(2)}) collective-permute-start(bf16[168,256]{1,0:T(8,128)(2,1)S(1)} %get-tuple-element.63), channel_id=1, source_target_pairs={{0,2},{1,3},{2,4},{3,5},{4,6},{5,7},{6,0},{7,1},{8,10},{9,11},{10,... | collective-permute-start | bytes 258056 | tf_op jit(solution)/shard_map/ppermute | solution.py:29
  39.1 6.6 %collective-permute-start.13 = (bf16[24,256]{1,0:T(8,128)(2,1)S(1)}, bf16[24,256]{1,0:T(8,128)(2,1)S(1)}, u32[]{:S(2)}, u32[]{:S(2)}) collective-permute-start(bf16[24,256]{1,0:T(8,128)(2,1)S(1)} %get-tuple-element.64), channel_id=1, source_target_pairs={{0,10},{1,11},{2,12},{3,13},{4,14},{5,15},{6,8},{7,9},{8,18},{9,19... | collective-permute-start | bytes 36872 | tf_op jit(solution)/shard_map/ppermute | solution.py:29
  39.6 10.9 %copy-start = (f32[12,12,12,256]{3,2,1,0:T(8,128)S(1)}, f32[12,12,12,256]{3,2,1,0:T(8,128)}, u32[]{:S(2)}) copy-start(f32[12,12,12,256]{3,2,1,0:T(8,128)} %start_ref.1) | copy-start | bytes 5308420
  45.9 4.6 %collective-permute-start.14 = (bf16[176,256]{1,0:T(8,128)(2,1)S(1)}, bf16[176,256]{1,0:T(8,128)(2,1)S(1)}, u32[]{:S(2)}, u32[]{:S(2)}) collective-permute-start(bf16[176,256]{1,0:T(8,128)(2,1)S(1)} %get-tuple-element.68), channel_id=1, source_target_pairs={{0,1},{1,0},{2,3},{3,2},{4,5},{5,4},{6,7},{7,6},{8,9},{9,8},{10,11... | collective-permute-start | bytes 270344 | tf_op jit(solution)/shard_map/ppermute | solution.py:29

commit v8 on v7

--- a/solution.py
+++ b/solution.py
@@ -266,24 +266,42 @@
     field_ref[0, 0, 0 : s.span, :] += xy_ref[0 : s.span]
 
 
-def send_down(s, total, field_ref, msg_refs, part_ref, x_ref, y_ref, xy_ref):
-    put_sides(s, field_ref, 0, 0, x_ref, y_ref, xy_ref)
+def add_ends(s, x_ref, y_ref, xy_ref, z, plane_ref):
+    for n in range(s.by):
+        at = n * s.span + z
+        x_ref[at : at + 1] += plane_ref[n : n + 1]
+    for n in range(s.bx):
+        at = n * s.span + z
+        y_ref[at : at + 1] += plane_ref[n * s.by : n * s.by + 1]
+    xy_ref[z : z + 1] += plane_ref[0:1]
+
+
+def send_down(s, total, msg_refs, part_ref, x_ref, y_ref, xy_ref):
     corner, x_part, y_part, own_part = columns(s, total)
     part_ref[...] = own_part
     send_sides(s, x_ref, y_ref, xy_ref, msg_refs, (x_part, y_part, corner))
 
 
-def first_down_body(s, before_ref, total_ref, early_ref, *refs):
-    del before_ref, early_ref
+def first_down_body(s, field_ref, total_ref, early_ref, *refs):
+    del early_ref
     count = 2 - s.pairs
     received, refs = refs[:count], refs[count:]
-    field_ref, *msg_refs, part_ref, above_ref, below_ref, x_ref, y_ref, xy_ref = refs
+    *msg_refs, part_ref, above_ref, below_ref, x_ref, y_ref, xy_ref = refs
     get_z(s, received, above_ref, below_ref)
     half = 4 * s.own
     total = total_ref[...] + jnp.concatenate([get_split(below_ref, 0, half), get_split(above_ref, s.z_rows, half)], axis=0)
+    put_sides(s, field_ref, 0, 0, x_ref, y_ref, xy_ref)
+    add_ends(s, x_ref, y_ref, xy_ref, s.bz, above_ref)
+    send_down(s, total, msg_refs, part_ref, x_ref, y_ref, xy_ref)
+
+
+def first_fill_body(s, before_ref, sent_ref, *refs):
+    del before_ref, sent_ref
+    count = 2 - s.pairs
+    received, (field_ref, above_ref, below_ref) = refs[:count], refs[count:]
+    get_z(s, received, above_ref, below_ref)
     for x in range(s.bx):
         field_ref[x, 0 : s.by, s.bz, :] = above_ref[x * s.by : (x + 1) * s.by]
-    send_down(s, total, field_ref, msg_refs, part_ref, x_ref, y_ref, xy_ref)
 
 
 def cell_body(s, before_ref, from_x_ref, from_y_ref, from_xy_ref, part_ref, weight_ref, *refs):
@@ -400,17 +418,26 @@
     total_ref[...] = total
 
 
-def second_down_body(s, before_ref, total_ref, lowest_ref, *refs):
-    del before_ref
+def second_down_body(s, field_ref, total_ref, lowest_ref, *refs):
     count = 2 - s.pairs
     received, refs = refs[:count], refs[count:]
-    field_ref, *msg_refs, part_ref, above_ref, below_ref, x_ref, y_ref, xy_ref = refs
+    *msg_refs, part_ref, above_ref, below_ref, x_ref, y_ref, xy_ref = refs
+    get_z(s, received, above_ref, below_ref)
+    total = total_ref[...] + split_sums(lowest_ref[...], s.locals, below_ref[...])
+    put_sides(s, field_ref, 0, 0, x_ref, y_ref, xy_ref)
+    add_ends(s, x_ref, y_ref, xy_ref, s.bz, above_ref)
+    add_ends(s, x_ref, y_ref, xy_ref, 0, below_ref)
+    send_down(s, total, msg_refs, part_ref, x_ref, y_ref, xy_ref)
+
+
+def second_fill_body(s, before_ref, sent_ref, *refs):
+    del before_ref, sent_ref
+    count = 2 - s.pairs
+    received, (field_ref, above_ref, below_ref) = refs[:count], refs[count:]
     get_z(s, received, above_ref, below_ref)
     for x in range(s.bx):
         field_ref[x, 0 : s.by, s.bz, :] += above_ref[x * s.by : (x + 1) * s.by]
         field_ref[x, 0 : s.by, 0, :] += below_ref[x * s.by : (x + 1) * s.by]
-    total = total_ref[...] + split_sums(lowest_ref[...], s.locals, below_ref[...])
-    send_down(s, total, field_ref, msg_refs, part_ref, x_ref, y_ref, xy_ref)
 
 
 def fold_body(s, before_ref, from_x_ref, from_y_ref, from_xy_ref, own_ref, *refs):
@@ -560,17 +587,19 @@
     )
     matrices = [regrouped(s, cell_matrices, part) for part in range(s.cells[0])]
     received = along_z(s, msgs)
-    field, *msgs, part = call(
+    *msgs, part = call(
         first_down_body,
         s,
-        [s.extended()] + s.side_msgs() + [s.rows(2 * own)],
+        s.side_msgs() + [s.rows(2 * own)],
         [s.scratch(s.z_both), s.scratch(s.z_sums)] + sides,
         [field, total, matrices[0]] + received,
-        aliases={0: 0},
-    )
-
-    def cells(field, msgs, part):
+    )
+    fills = (first_fill_body, [s.scratch(s.z_both), s.scratch(s.z_sums)], received)
+
+    def cells(field, msgs, part, fills):
+        body, scratch, along = fills
         received = along_xy(msgs, -1)
+        (field,) = call(body, s, [s.extended()], scratch, [field, part] + along, aliases={0: 0})
         _, sums, *msgs, mine = call(
             cell_body,
             s,
@@ -585,7 +614,7 @@
         (block,) = call(join_cells, s, [s.block()], [], [sums])
         return block, received, mine
 
-    block, received, mine = cells(field, msgs, part)
+    block, received, mine = cells(field, msgs, part, fills)
     by_node, lowest, lowest_by_node = call(
         node_body,
         s,
@@ -608,15 +637,15 @@
     (field,) = call(middle_body, s, [s.extended()], sides, [block] + received + [mine, by_node])
     received = swapped
     (total,) = call(sums_body, s, [s.rows(s.locals)], [], [field, by_atom])
-    field, *msgs, part = call(
+    *msgs, part = call(
         second_down_body,
         s,
-        [s.extended()] + s.side_msgs() + [s.rows(2 * own)],
+        s.side_msgs() + [s.rows(2 * own)],
         [s.scratch(s.z_plane), s.scratch(s.z_plane)] + sides,
         [field, total, lowest] + received,
-        aliases={0: 0},
-    )
-    block, received, mine = cells(field, msgs, part)
+    )
+    fills = (second_fill_body, [s.scratch(s.z_plane), s.scratch(s.z_plane)], received)
+    block, received, mine = cells(field, msgs, part, fills)
     block, *msgs, total = call(
         fold_body,
         s,

time: 52.4 us -> 52.2 us (level)
    pallas_call x15 -> x17, Pallas kernels: 14.5 us -> 14.5 us  [call(): pl.pallas_call(functools.partial(body, sizes, *extra), out_shape=outs, in...]
  transfers between devices with their start and end apart: 15 -> 15, of which waited for: 7 -> 6; matrix products, arithmetic and copies ran while one was open for 0% -> 0% of each run, Pallas kernels for 13% -> 14%
where the time goes in v8:
time: 52.2 us; the launch traced here: 52 us
  waiting for transfers between devices  20.6 us (39%)
  starting transfers between devices  16.7 us (32%)
  Pallas kernels  14.5 us (28%)
    ppermute x15, waiting for transfers between devices, shifted(): return lax.ppermute(value, AXES, pairs)  20.6 us
    ppermute x15, starting transfers between devices, shifted(): return lax.ppermute(value, AXES, pairs)  16.7 us
    pallas_call x17, Pallas kernels, call(): pl.pallas_call(functools.partial(body, sizes, *extra), out_shape=outs, in...  14.5 us
  transfers between devices with their start and end apart: 15, of which 6 were waited for; matrix products, arithmetic and copies ran while one was open for 0% of the time, Pallas kernels for 14%

profile of v8, /device:TPU:0, one launch (start us, length us, event | category | flops | bytes accessed | tf_op | source)
XLA Modules:
  0.0 52.0 jit_solution(16830731378144087779)
XLA Ops:
  0.0 2.5 %shard_map.55 = (f32[13,13,16,256]{3,2,1,0:T(8,128)S(1)}, bf16[12,32,192]{2,1,0:T(8,128)(2,1)S(1)}, f32[144,16,32]{2,1,0:T(8,128)S(1)}, bf16[176,256]{1,0:T(8,12...) custom-call(f32[12,12,12,256]{3,2,1,0:T(8,128)} %start_ref.1, f32[1,16,1728]{2,1,0:T(8,128)} %rows_hbm.1, ...), custom_call_target="tpu_custom_call" | custom-call | tf_op jit(solution)/shard_map/pallas_call | solution.py:102
  2.5 3.0 %collective-permute-start = (bf16[176,256]{1,0:T(8,128)(2,1)S(1)}, bf16[176,256]{1,0:T(8,128)(2,1)S(1)}, u32[]{:S(2)}, u32[]{:S(2)}) collective-permute-start(bf16[176,256]{1,0:T(8,128)(2,1)S(1)} %get-tuple-element.37), channel_id=1, source_target_pairs={{0,1},{1,0},{2,3},{3,2},{4,5},{5,4},{6,7},{7,6},{8,9},{9,8},{10,11... | collective-permute-start | bytes 270344 | tf_op jit(solution)/shard_map/ppermute | solution.py:29
  5.5 2.4 %shard_map.56.early_ref.refs_0_ = bf16[2,2,400,400]{3,2,1,0:T(8,128)(2,1)S(1)} custom-call(bf16[2,2,343,2,343]{4,3,2,1,0:T(2,128)(2,1)} %bitcast.2), custom_call_target="tpu_custom_call" | custom-call | tf_op jit(solution)/shard_map/pallas_call | solution.py:102
  8.2 0.6 %collective-permute-start.1 = (bf16[168,256]{1,0:T(8,128)(2,1)S(1)}, bf16[168,256]{1,0:T(8,128)(2,1)S(1)}, u32[]{:S(2)}, u32[]{:S(2)}) collective-permute-start(bf16[168,256]{1,0:T(8,128)(2,1)S(1)} %get-tuple-element.39), channel_id=1, source_target_pairs={{0,24},{1,25},{2,26},{3,27},{4,28},{5,29},{6,30},{7,31},{8,0},{9,1... | collective-permute-start | bytes 258056 | tf_op jit(solution)/shard_map/ppermute | solution.py:29
  8.8 3.6 %collective-permute-start.2 = (bf16[168,256]{1,0:T(8,128)(2,1)S(1)}, bf16[168,256]{1,0:T(8,128)(2,1)S(1)}, u32[]{:S(2)}, u32[]{:S(2)}) collective-permute-start(bf16[168,256]{1,0:T(8,128)(2,1)S(1)} %get-tuple-element.40), channel_id=1, source_target_pairs={{0,6},{1,7},{2,0},{3,1},{4,2},{5,3},{6,4},{7,5},{8,14},{9,15},{10,... | collective-permute-start | bytes 258056 | tf_op jit(solution)/shard_map/ppermute | solution.py:29
  12.4 1.1 %collective-permute-start.3 = (bf16[24,256]{1,0:T(8,128)(2,1)S(1)}, bf16[24,256]{1,0:T(8,128)(2,1)S(1)}, u32[]{:S(2)}, u32[]{:S(2)}) collective-permute-start(bf16[24,256]{1,0:T(8,128)(2,1)S(1)} %get-tuple-element.41), channel_id=1, source_target_pairs={{0,30},{1,31},{2,24},{3,25},{4,26},{5,27},{6,28},{7,29},{8,6},{9,7... | collective-permute-start | bytes 36872 | tf_op jit(solution)/shard_map/ppermute | solution.py:29
  13.5 2.4 %shard_map.59.refs_1_ = bf16[2,2,400,400]{3,2,1,0:T(8,128)(2,1)S(1)} custom-call(bf16[2,2,343,2,343]{4,3,2,1,0:T(2,128)(2,1)} %bitcast.3), custom_call_target="tpu_custom_call" | custom-call | tf_op jit(solution)/shard_map/pallas_call | solution.py:102
  16.1 1.2 %shard_map.60 = (f32[13,13,16,256]{3,2,1,0:T(8,128)S(1)}, f32[2,13,13,8,256]{4,3,2,1,0:T(8,128)S(1)}, bf16[168,256]{1,0:T(8,128)(2,1)S(1)}, bf16[168,256]{1,0:T(...) custom-call(f32[13,13,16,256]{3,2,1,0:T(8,128)S(1)} %shard_map.58.before_ref, ...), custom_call_target="tpu_custom_call", output_to_operand_aliasing={{0}: (0, {})} | custom-call | tf_op jit(solution)/shard_map/pallas_call | solution.py:102
  17.3 0.5 %collective-permute-start.4 = (bf16[168,256]{1,0:T(8,128)(2,1)S(1)}, bf16[168,256]{1,0:T(8,128)(2,1)S(1)}, u32[]{:S(2)}, u32[]{:S(2)}) collective-permute-start(bf16[168,256]{1,0:T(8,128)(2,1)S(1)} %get-tuple-element.44), channel_id=1, source_target_pairs={{0,8},{1,9},{2,10},{3,11},{4,12},{5,13},{6,14},{7,15},{8,16},{9,17... | collective-permute-start | bytes 258056 | tf_op jit(solution)/shard_map/ppermute | solution.py:29
  17.8 1.2 %collective-permute-start.5 = (bf16[168,256]{1,0:T(8,128)(2,1)S(1)}, bf16[168,256]{1,0:T(8,128)(2,1)S(1)}, u32[]{:S(2)}, u32[]{:S(2)}) collective-permute-start(bf16[168,256]{1,0:T(8,128)(2,1)S(1)} %get-tuple-element.45), channel_id=1, source_target_pairs={{0,2},{1,3},{2,4},{3,5},{4,6},{5,7},{6,0},{7,1},{8,10},{9,11},{10,... | collective-permute-start | bytes 258056 | tf_op jit(solution)/shard_map/ppermute | solution.py:29
  19.9 5.0 %collective-permute-done.6.from_xy_ref = bf16[24,256]{1,0:T(8,128)(2,1)S(1)} collective-permute-done((bf16[24,256]{1,0:T(8,128)(2,1)S(1)}, bf16[24,256]{1,0:T(8,128)(2,1)S(1)}, u32[]{:S(2)}, u32[]{:S(2)}) %collective-permute-start.6) | collective-permute-done | bytes 12320 | tf_op jit(solution)/shard_map/ppermute | solution.py:29
  25.1 1.6 %collective-permute-start.7 = (bf16[288,256]{1,0:T(8,128)(2,1)S(1)}, bf16[288,256]{1,0:T(8,128)(2,1)S(1)}, u32[]{:S(2)}, u32[]{:S(2)}) collective-permute-start(bf16[288,256]{1,0:T(8,128)(2,1)S(1)} %shard_map.65), channel_id=1, source_target_pairs={{0,1},{1,0},{2,3},{3,2},{4,5},{5,4},{6,7},{7,6},{8,9},{9,8},{10,11... | collective-permute-start | bytes 442376 | tf_op jit(solution)/shard_map/ppermute | solution.py:29
  26.7 0.5 shard_map.63.field_ref.before_ref
  27.2 0.5 shard_map.64.total_ref
  27.6 3.4 %collective-permute-done.7.refs_0_ = bf16[288,256]{1,0:T(8,128)(2,1)S(1)} collective-permute-done((bf16[288,256]{1,0:T(8,128)(2,1)S(1)}, bf16[288,256]{1,0:T(8,128)(2,1)S(1)}, u32[]{:S(2)}, u32[]{:S(2)}) %collective-permute-start.7) | collective-permute-done | bytes 147488 | tf_op jit(solution)/shard_map/ppermute | solution.py:29
  31.3 1.8 %collective-permute-start.9 = (bf16[168,256]{1,0:T(8,128)(2,1)S(1)}, bf16[168,256]{1,0:T(8,128)(2,1)S(1)}, u32[]{:S(2)}, u32[]{:S(2)}) collective-permute-start(bf16[168,256]{1,0:T(8,128)(2,1)S(1)} %get-tuple-element.55), channel_id=1, source_target_pairs={{0,6},{1,7},{2,0},{3,1},{4,2},{5,3},{6,4},{7,5},{8,14},{9,15},{10,... | collective-permute-start | bytes 258056 | tf_op jit(solution)/shard_map/ppermute | solution.py:29
  33.5 2.9 %collective-permute-done.10.from_xy_ref = bf16[24,256]{1,0:T(8,128)(2,1)S(1)} collective-permute-done((bf16[24,256]{1,0:T(8,128)(2,1)S(1)}, bf16[24,256]{1,0:T(8,128)(2,1)S(1)}, u32[]{:S(2)}, u32[]{:S(2)}) %collective-permute-start.10) | collective-permute-done | bytes 12320 | tf_op jit(solution)/shard_map/ppermute | solution.py:29
  36.4 1.2 %shard_map.68 = (f32[13,13,16,256]{3,2,1,0:T(8,128)S(1)}, f32[2,13,13,8,256]{4,3,2,1,0:T(8,128)S(1)}, bf16[168,256]{1,0:T(8,128)(2,1)S(1)}, bf16[168,256]{1,0:T(...) custom-call(f32[13,13,16,256]{3,2,1,0:T(8,128)S(1)} %shard_map.67.before_ref, ...), custom_call_target="tpu_custom_call", output_to_operand_aliasing={{0}: (0, {})} | custom-call | tf_op jit(solution)/shard_map/pallas_call | solution.py:102
  37.6 1.0 %collective-permute-start.11 = (bf16[168,256]{1,0:T(8,128)(2,1)S(1)}, bf16[168,256]{1,0:T(8,128)(2,1)S(1)}, u32[]{:S(2)}, u32[]{:S(2)}) collective-permute-start(bf16[168,256]{1,0:T(8,128)(2,1)S(1)} %get-tuple-element.58), channel_id=1, source_target_pairs={{0,8},{1,9},{2,10},{3,11},{4,12},{5,13},{6,14},{7,15},{8,16},{9,17... | collective-permute-start | bytes 258056 | tf_op jit(solution)/shard_map/ppermute | solution.py:29
  38.9 0.4 shard_map.69.before_ref
  39.4 6.1 %collective-permute-done.13.from_xy_ref = bf16[24,256]{1,0:T(8,128)(2,1)S(1)} collective-permute-done((bf16[24,256]{1,0:T(8,128)(2,1)S(1)}, bf16[24,256]{1,0:T(8,128)(2,1)S(1)}, u32[]{:S(2)}, u32[]{:S(2)}) %collective-permute-start.13) | collective-permute-done | bytes 12320 | tf_op jit(solution)/shard_map/ppermute | solution.py:29
  45.6 1.6 %collective-permute-start.14 = (bf16[176,256]{1,0:T(8,128)(2,1)S(1)}, bf16[176,256]{1,0:T(8,128)(2,1)S(1)}, u32[]{:S(2)}, u32[]{:S(2)}) collective-permute-start(bf16[176,256]{1,0:T(8,128)(2,1)S(1)} %get-tuple-element.64), channel_id=1, source_target_pairs={{0,1},{1,0},{2,3},{3,2},{4,5},{5,4},{6,7},{7,6},{8,9},{9,8},{10,11... | collective-permute-start | bytes 270344 | tf_op jit(solution)/shard_map/ppermute | solution.py:29
  47.2 3.0 %collective-permute-done.14.refs_0_ = bf16[176,256]{1,0:T(8,128)(2,1)S(1)} collective-permute-done((bf16[176,256]{1,0:T(8,128)(2,1)S(1)}, bf16[176,256]{1,0:T(8,128)(2,1)S(1)}, u32[]{:S(2)}, u32[]{:S(2)}) %collective-permute-start.14) | collective-permute-done | bytes 90144 | tf_op jit(solution)/shard_map/ppermute | solution.py:29
  50.3 1.7 %shard_map.71 = f32[12,12,12,256]{3,2,1,0:T(8,128)} custom-call(f32[12,12,12,256]{3,2,1,0:T(8,128)S(1)} %copy-done, f32[12,12,16,256]{3,2,1,0:T(8,128)S(1)} %get-tuple-element.62.block_ref, f32[16,256]{1,0:T(8,128)S(1)} %get-tuple-element.63.total_ref, bf16[12,192,48]{2,1,0:T(8,128)(2,1)S(1)} %get-tuple-element.49.by_node_ref, ...), custom_call_target="tpu_custom_call" | custom-call | tf_op jit(solution)/shard_map/pallas_call | solution.py:102
  (25 shorter events, 2.7 us)
Async XLA Ops:
  2.5 5.6 %collective-permute-start = (bf16[176,256]{1,0:T(8,128)(2,1)S(1)}, bf16[176,256]{1,0:T(8,128)(2,1)S(1)}, u32[]{:S(2)}, u32[]{:S(2)}) collective-permute-start(bf16[176,256]{1,0:T(8,128)(2,1)S(1)} %get-tuple-element.37), channel_id=1, source_target_pairs={{0,1},{1,0},{2,3},{3,2},{4,5},{5,4},{6,7},{7,6},{8,9},{9,8},{10,11... | collective-permute-start | bytes 270344 | tf_op jit(solution)/shard_map/ppermute | solution.py:29
  8.2 7.9 %collective-permute-start.1 = (bf16[168,256]{1,0:T(8,128)(2,1)S(1)}, bf16[168,256]{1,0:T(8,128)(2,1)S(1)}, u32[]{:S(2)}, u32[]{:S(2)}) collective-permute-start(bf16[168,256]{1,0:T(8,128)(2,1)S(1)} %get-tuple-element.39), channel_id=1, source_target_pairs={{0,24},{1,25},{2,26},{3,27},{4,28},{5,29},{6,30},{7,31},{8,0},{9,1... | collective-permute-start | bytes 258056 | tf_op jit(solution)/shard_map/ppermute | solution.py:29
  8.8 7.3 %collective-permute-start.2 = (bf16[168,256]{1,0:T(8,128)(2,1)S(1)}, bf16[168,256]{1,0:T(8,128)(2,1)S(1)}, u32[]{:S(2)}, u32[]{:S(2)}) collective-permute-start(bf16[168,256]{1,0:T(8,128)(2,1)S(1)} %get-tuple-element.40), channel_id=1, source_target_pairs={{0,6},{1,7},{2,0},{3,1},{4,2},{5,3},{6,4},{7,5},{8,14},{9,15},{10,... | collective-permute-start | bytes 258056 | tf_op jit(solution)/shard_map/ppermute | solution.py:29
  12.4 3.7 %collective-permute-start.3 = (bf16[24,256]{1,0:T(8,128)(2,1)S(1)}, bf16[24,256]{1,0:T(8,128)(2,1)S(1)}, u32[]{:S(2)}, u32[]{:S(2)}) collective-permute-start(bf16[24,256]{1,0:T(8,128)(2,1)S(1)} %get-tuple-element.41), channel_id=1, source_target_pairs={{0,30},{1,31},{2,24},{3,25},{4,26},{5,27},{6,28},{7,29},{8,6},{9,7... | collective-permute-start | bytes 36872 | tf_op jit(solution)/shard_map/ppermute | solution.py:29
  17.3 7.6 %collective-permute-start.4 = (bf16[168,256]{1,0:T(8,128)(2,1)S(1)}, bf16[168,256]{1,0:T(8,128)(2,1)S(1)}, u32[]{:S(2)}, u32[]{:S(2)}) collective-permute-start(bf16[168,256]{1,0:T(8,128)(2,1)S(1)} %get-tuple-element.44), channel_id=1, source_target_pairs={{0,8},{1,9},{2,10},{3,11},{4,12},{5,13},{6,14},{7,15},{8,16},{9,17... | collective-permute-start | bytes 258056 | tf_op jit(solution)/shard_map/ppermute | solution.py:29
  17.8 7.1 %collective-permute-start.5 = (bf16[168,256]{1,0:T(8,128)(2,1)S(1)}, bf16[168,256]{1,0:T(8,128)(2,1)S(1)}, u32[]{:S(2)}, u32[]{:S(2)}) collective-permute-start(bf16[168,256]{1,0:T(8,128)(2,1)S(1)} %get-tuple-element.45), channel_id=1, source_target_pairs={{0,2},{1,3},{2,4},{3,5},{4,6},{5,7},{6,0},{7,1},{8,10},{9,11},{10,... | collective-permute-start | bytes 258056 | tf_op jit(solution)/shard_map/ppermute | solution.py:29
  19.0 5.9 %collective-permute-start.6 = (bf16[24,256]{1,0:T(8,128)(2,1)S(1)}, bf16[24,256]{1,0:T(8,128)(2,1)S(1)}, u32[]{:S(2)}, u32[]{:S(2)}) collective-permute-start(bf16[24,256]{1,0:T(8,128)(2,1)S(1)} %get-tuple-element.46), channel_id=1, source_target_pairs={{0,10},{1,11},{2,12},{3,13},{4,14},{5,15},{6,8},{7,9},{8,18},{9,19... | collective-permute-start | bytes 36872 | tf_op jit(solution)/shard_map/ppermute | solution.py:29
  25.1 5.9 %collective-permute-start.7 = (bf16[288,256]{1,0:T(8,128)(2,1)S(1)}, bf16[288,256]{1,0:T(8,128)(2,1)S(1)}, u32[]{:S(2)}, u32[]{:S(2)}) collective-permute-start(bf16[288,256]{1,0:T(8,128)(2,1)S(1)} %shard_map.65), channel_id=1, source_target_pairs={{0,1},{1,0},{2,3},{3,2},{4,5},{5,4},{6,7},{7,6},{8,9},{9,8},{10,11... | collective-permute-start | bytes 442376 | tf_op jit(solution)/shard_map/ppermute | solution.py:29
  31.3 5.1 %collective-permute-start.8 = (bf16[168,256]{1,0:T(8,128)(2,1)S(1)}, bf16[168,256]{1,0:T(8,128)(2,1)S(1)}, u32[]{:S(2)}, u32[]{:S(2)}) collective-permute-start(bf16[168,256]{1,0:T(8,128)(2,1)S(1)} %get-tuple-element.54), channel_id=1, source_target_pairs={{0,24},{1,25},{2,26},{3,27},{4,28},{5,29},{6,30},{7,31},{8,0},{9,1... | collective-permute-start | bytes 258056 | tf_op jit(solution)/shard_map/ppermute | solution.py:29
  31.3 5.1 %collective-permute-start.9 = (bf16[168,256]{1,0:T(8,128)(2,1)S(1)}, bf16[168,256]{1,0:T(8,128)(2,1)S(1)}, u32[]{:S(2)}, u32[]{:S(2)}) collective-permute-start(bf16[168,256]{1,0:T(8,128)(2,1)S(1)} %get-tuple-element.55), channel_id=1, source_target_pairs={{0,6},{1,7},{2,0},{3,1},{4,2},{5,3},{6,4},{7,5},{8,14},{9,15},{10,... | collective-permute-start | bytes 258056 | tf_op jit(solution)/shard_map/ppermute | solution.py:29
  33.1 3.3 %collective-permute-start.10 = (bf16[24,256]{1,0:T(8,128)(2,1)S(1)}, bf16[24,256]{1,0:T(8,128)(2,1)S(1)}, u32[]{:S(2)}, u32[]{:S(2)}) collective-permute-start(bf16[24,256]{1,0:T(8,128)(2,1)S(1)} %get-tuple-element.56), channel_id=1, source_target_pairs={{0,30},{1,31},{2,24},{3,25},{4,26},{5,27},{6,28},{7,29},{8,6},{9,7... | collective-permute-start | bytes 36872 | tf_op jit(solution)/shard_map/ppermute | solution.py:29
  37.6 7.9 %collective-permute-start.11 = (bf16[168,256]{1,0:T(8,128)(2,1)S(1)}, bf16[168,256]{1,0:T(8,128)(2,1)S(1)}, u32[]{:S(2)}, u32[]{:S(2)}) collective-permute-start(bf16[168,256]{1,0:T(8,128)(2,1)S(1)} %get-tuple-element.58), channel_id=1, source_target_pairs={{0,8},{1,9},{2,10},{3,11},{4,12},{5,13},{6,14},{7,15},{8,16},{9,17... | collective-permute-start | bytes 258056 | tf_op jit(solution)/shard_map/ppermute | solution.py:29
  38.6 6.9 %collective-permute-start.12 = (bf16[168,256]{1,0:T(8,128)(2,1)S(1)}, bf16[168,256]{1,0:T(8,128)(2,1)S(1)}, u32[]{:S(2)}, u32[]{:S(2)}) collective-permute-start(bf16[168,256]{1,0:T(8,128)(2,1)S(1)} %get-tuple-element.59), channel_id=1, source_target_pairs={{0,2},{1,3},{2,4},{3,5},{4,6},{5,7},{6,0},{7,1},{8,10},{9,11},{10,... | collective-permute-start | bytes 258056 | tf_op jit(solution)/shard_map/ppermute | solution.py:29
  38.8 6.6 %collective-permute-start.13 = (bf16[24,256]{1,0:T(8,128)(2,1)S(1)}, bf16[24,256]{1,0:T(8,128)(2,1)S(1)}, u32[]{:S(2)}, u32[]{:S(2)}) collective-permute-start(bf16[24,256]{1,0:T(8,128)(2,1)S(1)} %get-tuple-element.60), channel_id=1, source_target_pairs={{0,10},{1,11},{2,12},{3,13},{4,14},{5,15},{6,8},{7,9},{8,18},{9,19... | collective-permute-start | bytes 36872 | tf_op jit(solution)/shard_map/ppermute | solution.py:29
  39.4 10.9 %copy-start = (f32[12,12,12,256]{3,2,1,0:T(8,128)S(1)}, f32[12,12,12,256]{3,2,1,0:T(8,128)}, u32[]{:S(2)}) copy-start(f32[12,12,12,256]{3,2,1,0:T(8,128)} %start_ref.1) | copy-start | bytes 5308420
  45.6 4.6 %collective-permute-start.14 = (bf16[176,256]{1,0:T(8,128)(2,1)S(1)}, bf16[176,256]{1,0:T(8,128)(2,1)S(1)}, u32[]{:S(2)}, u32[]{:S(2)}) collective-permute-start(bf16[176,256]{1,0:T(8,128)(2,1)S(1)} %get-tuple-element.64), channel_id=1, source_target_pairs={{0,1},{1,0},{2,3},{3,2},{4,5},{5,4},{6,7},{7,6},{8,9},{9,8},{10,11... | collective-permute-start | bytes 270344 | tf_op jit(solution)/shard_map/ppermute | solution.py:29

commit v9 on v8

--- a/solution.py
+++ b/solution.py
@@ -203,6 +203,11 @@
         wide = wide_ref[x * s.by : (x + 1) * s.by].reshape(s.by * s.bzp, 2 * s.locals)
         by_atom_ref[x] = wide.T.astype(BF16)
     total = jnp.zeros((s.locals, s.waves), F32)
+    atoms = lax.broadcasted_iota(jnp.int32, (s.locals, coupling_ref.shape[1]), 1)
+    weight = jnp.sum(jnp.where(atoms == local_atoms(s.own, atoms.shape), coupling_ref[...], 0.0), axis=1, keepdims=True)
+    weight_ref[...] = jnp.broadcast_to(weight, weight_ref.shape)
+    blank(low_ref, s.z_rows)
+    blank(high_ref, 0)
     whole.wait()
     for x in range(s.bx):
         plane = jnp.concatenate([start_ref[x], jnp.zeros((s.by, s.bzp - s.bz, s.waves), F32)], axis=1)
@@ -212,14 +217,9 @@
     half = 4 * s.own
     for x in range(s.bx):
         low_ref[x * s.by : (x + 1) * s.by] = field_ref[x, 0 : s.by, 0, :]
-    blank(low_ref, s.z_rows)
-    blank(high_ref, 0)
     put_split(low_ref, s.z_rows, total[0:half])
     put_split(high_ref, 0, total[half:])
     put_z(s, msg_refs, low_ref, high_ref)
-    atoms = lax.broadcasted_iota(jnp.int32, (s.locals, coupling_ref.shape[1]), 1)
-    weight = jnp.sum(jnp.where(atoms == local_atoms(s.own, atoms.shape), coupling_ref[...], 0.0), axis=1, keepdims=True)
-    weight_ref[...] = jnp.broadcast_to(weight, weight_ref.shape)
 
 
 def node_body(s, wide_ref, by_node_ref, lowest_ref, lowest_by_node_ref):

time: 52.2 us -> 52.1 us (level)
  no operation moved by 1% of the time
where the time goes in v9:
time: 52.1 us; the launch traced here: 52 us
  waiting for transfers between devices  20.6 us (40%)
  starting transfers between devices  16.7 us (32%)
  Pallas kernels  14.5 us (28%)
    ppermute x15, waiting for transfers between devices, shifted(): return lax.ppermute(value, AXES, pairs)  20.6 us
    ppermute x15, starting transfers between devices, shifted(): return lax.ppermute(value, AXES, pairs)  16.7 us
    pallas_call x17, Pallas kernels, call(): pl.pallas_call(functools.partial(body, sizes, *extra), out_shape=outs, in...  14.5 us
  transfers between devices with their start and end apart: 15, of which 6 were waited for; matrix products, arithmetic and copies ran while one was open for 0% of the time, Pallas kernels for 14%

profile of v9, /device:TPU:0, one launch (start us, length us, event | category | flops | bytes accessed | tf_op | source)
XLA Modules:
  0.0 52.0 jit_solution(11414931752595722923)
XLA Ops:
  0.0 2.5 %shard_map.55 = (f32[13,13,16,256]{3,2,1,0:T(8,128)S(1)}, bf16[12,32,192]{2,1,0:T(8,128)(2,1)S(1)}, f32[144,16,32]{2,1,0:T(8,128)S(1)}, bf16[176,256]{1,0:T(8,12...) custom-call(f32[12,12,12,256]{3,2,1,0:T(8,128)} %start_ref.1, f32[1,16,1728]{2,1,0:T(8,128)} %rows_hbm.1, ...), custom_call_target="tpu_custom_call" | custom-call | tf_op jit(solution)/shard_map/pallas_call | solution.py:102
  2.5 3.0 %collective-permute-start = (bf16[176,256]{1,0:T(8,128)(2,1)S(1)}, bf16[176,256]{1,0:T(8,128)(2,1)S(1)}, u32[]{:S(2)}, u32[]{:S(2)}) collective-permute-start(bf16[176,256]{1,0:T(8,128)(2,1)S(1)} %get-tuple-element.37), channel_id=1, source_target_pairs={{0,1},{1,0},{2,3},{3,2},{4,5},{5,4},{6,7},{7,6},{8,9},{9,8},{10,11... | collective-permute-start | bytes 270344 | tf_op jit(solution)/shard_map/ppermute | solution.py:29
  5.5 2.4 %shard_map.56.early_ref.refs_0_ = bf16[2,2,400,400]{3,2,1,0:T(8,128)(2,1)S(1)} custom-call(bf16[2,2,343,2,343]{4,3,2,1,0:T(2,128)(2,1)} %bitcast.2), custom_call_target="tpu_custom_call" | custom-call | tf_op jit(solution)/shard_map/pallas_call | solution.py:102
  8.2 0.6 %collective-permute-start.1 = (bf16[168,256]{1,0:T(8,128)(2,1)S(1)}, bf16[168,256]{1,0:T(8,128)(2,1)S(1)}, u32[]{:S(2)}, u32[]{:S(2)}) collective-permute-start(bf16[168,256]{1,0:T(8,128)(2,1)S(1)} %get-tuple-element.39), channel_id=1, source_target_pairs={{0,24},{1,25},{2,26},{3,27},{4,28},{5,29},{6,30},{7,31},{8,0},{9,1... | collective-permute-start | bytes 258056 | tf_op jit(solution)/shard_map/ppermute | solution.py:29
  8.8 3.6 %collective-permute-start.2 = (bf16[168,256]{1,0:T(8,128)(2,1)S(1)}, bf16[168,256]{1,0:T(8,128)(2,1)S(1)}, u32[]{:S(2)}, u32[]{:S(2)}) collective-permute-start(bf16[168,256]{1,0:T(8,128)(2,1)S(1)} %get-tuple-element.40), channel_id=1, source_target_pairs={{0,6},{1,7},{2,0},{3,1},{4,2},{5,3},{6,4},{7,5},{8,14},{9,15},{10,... | collective-permute-start | bytes 258056 | tf_op jit(solution)/shard_map/ppermute | solution.py:29
  12.4 1.1 %collective-permute-start.3 = (bf16[24,256]{1,0:T(8,128)(2,1)S(1)}, bf16[24,256]{1,0:T(8,128)(2,1)S(1)}, u32[]{:S(2)}, u32[]{:S(2)}) collective-permute-start(bf16[24,256]{1,0:T(8,128)(2,1)S(1)} %get-tuple-element.41), channel_id=1, source_target_pairs={{0,30},{1,31},{2,24},{3,25},{4,26},{5,27},{6,28},{7,29},{8,6},{9,7... | collective-permute-start | bytes 36872 | tf_op jit(solution)/shard_map/ppermute | solution.py:29
  13.5 2.4 %shard_map.59.refs_1_ = bf16[2,2,400,400]{3,2,1,0:T(8,128)(2,1)S(1)} custom-call(bf16[2,2,343,2,343]{4,3,2,1,0:T(2,128)(2,1)} %bitcast.3), custom_call_target="tpu_custom_call" | custom-call | tf_op jit(solution)/shard_map/pallas_call | solution.py:102
  16.1 1.2 %shard_map.60 = (f32[13,13,16,256]{3,2,1,0:T(8,128)S(1)}, f32[2,13,13,8,256]{4,3,2,1,0:T(8,128)S(1)}, bf16[168,256]{1,0:T(8,128)(2,1)S(1)}, bf16[168,256]{1,0:T(...) custom-call(f32[13,13,16,256]{3,2,1,0:T(8,128)S(1)} %shard_map.58.before_ref, ...), custom_call_target="tpu_custom_call", output_to_operand_aliasing={{0}: (0, {})} | custom-call | tf_op jit(solution)/shard_map/pallas_call | solution.py:102
  17.3 0.5 %collective-permute-start.4 = (bf16[168,256]{1,0:T(8,128)(2,1)S(1)}, bf16[168,256]{1,0:T(8,128)(2,1)S(1)}, u32[]{:S(2)}, u32[]{:S(2)}) collective-permute-start(bf16[168,256]{1,0:T(8,128)(2,1)S(1)} %get-tuple-element.44), channel_id=1, source_target_pairs={{0,8},{1,9},{2,10},{3,11},{4,12},{5,13},{6,14},{7,15},{8,16},{9,17... | collective-permute-start | bytes 258056 | tf_op jit(solution)/shard_map/ppermute | solution.py:29
  17.8 1.2 %collective-permute-start.5 = (bf16[168,256]{1,0:T(8,128)(2,1)S(1)}, bf16[168,256]{1,0:T(8,128)(2,1)S(1)}, u32[]{:S(2)}, u32[]{:S(2)}) collective-permute-start(bf16[168,256]{1,0:T(8,128)(2,1)S(1)} %get-tuple-element.45), channel_id=1, source_target_pairs={{0,2},{1,3},{2,4},{3,5},{4,6},{5,7},{6,0},{7,1},{8,10},{9,11},{10,... | collective-permute-start | bytes 258056 | tf_op jit(solution)/shard_map/ppermute | solution.py:29
  19.9 5.0 %collective-permute-done.6.from_xy_ref = bf16[24,256]{1,0:T(8,128)(2,1)S(1)} collective-permute-done((bf16[24,256]{1,0:T(8,128)(2,1)S(1)}, bf16[24,256]{1,0:T(8,128)(2,1)S(1)}, u32[]{:S(2)}, u32[]{:S(2)}) %collective-permute-start.6) | collective-permute-done | bytes 12320 | tf_op jit(solution)/shard_map/ppermute | solution.py:29
  25.1 1.6 %collective-permute-start.7 = (bf16[288,256]{1,0:T(8,128)(2,1)S(1)}, bf16[288,256]{1,0:T(8,128)(2,1)S(1)}, u32[]{:S(2)}, u32[]{:S(2)}) collective-permute-start(bf16[288,256]{1,0:T(8,128)(2,1)S(1)} %shard_map.65), channel_id=1, source_target_pairs={{0,1},{1,0},{2,3},{3,2},{4,5},{5,4},{6,7},{7,6},{8,9},{9,8},{10,11... | collective-permute-start | bytes 442376 | tf_op jit(solution)/shard_map/ppermute | solution.py:29
  26.7 0.5 shard_map.63.field_ref.before_ref
  27.2 0.5 shard_map.64.total_ref
  27.6 3.4 %collective-permute-done.7.refs_0_ = bf16[288,256]{1,0:T(8,128)(2,1)S(1)} collective-permute-done((bf16[288,256]{1,0:T(8,128)(2,1)S(1)}, bf16[288,256]{1,0:T(8,128)(2,1)S(1)}, u32[]{:S(2)}, u32[]{:S(2)}) %collective-permute-start.7) | collective-permute-done | bytes 147488 | tf_op jit(solution)/shard_map/ppermute | solution.py:29
  31.3 1.8 %collective-permute-start.9 = (bf16[168,256]{1,0:T(8,128)(2,1)S(1)}, bf16[168,256]{1,0:T(8,128)(2,1)S(1)}, u32[]{:S(2)}, u32[]{:S(2)}) collective-permute-start(bf16[168,256]{1,0:T(8,128)(2,1)S(1)} %get-tuple-element.55), channel_id=1, source_target_pairs={{0,6},{1,7},{2,0},{3,1},{4,2},{5,3},{6,4},{7,5},{8,14},{9,15},{10,... | collective-permute-start | bytes 258056 | tf_op jit(solution)/shard_map/ppermute | solution.py:29
  33.5 2.9 %collective-permute-done.10.from_xy_ref = bf16[24,256]{1,0:T(8,128)(2,1)S(1)} collective-permute-done((bf16[24,256]{1,0:T(8,128)(2,1)S(1)}, bf16[24,256]{1,0:T(8,128)(2,1)S(1)}, u32[]{:S(2)}, u32[]{:S(2)}) %collective-permute-start.10) | collective-permute-done | bytes 12320 | tf_op jit(solution)/shard_map/ppermute | solution.py:29
  36.4 1.2 %shard_map.68 = (f32[13,13,16,256]{3,2,1,0:T(8,128)S(1)}, f32[2,13,13,8,256]{4,3,2,1,0:T(8,128)S(1)}, bf16[168,256]{1,0:T(8,128)(2,1)S(1)}, bf16[168,256]{1,0:T(...) custom-call(f32[13,13,16,256]{3,2,1,0:T(8,128)S(1)} %shard_map.67.before_ref, ...), custom_call_target="tpu_custom_call", output_to_operand_aliasing={{0}: (0, {})} | custom-call | tf_op jit(solution)/shard_map/pallas_call | solution.py:102
  37.6 1.0 %collective-permute-start.11 = (bf16[168,256]{1,0:T(8,128)(2,1)S(1)}, bf16[168,256]{1,0:T(8,128)(2,1)S(1)}, u32[]{:S(2)}, u32[]{:S(2)}) collective-permute-start(bf16[168,256]{1,0:T(8,128)(2,1)S(1)} %get-tuple-element.58), channel_id=1, source_target_pairs={{0,8},{1,9},{2,10},{3,11},{4,12},{5,13},{6,14},{7,15},{8,16},{9,17... | collective-permute-start | bytes 258056 | tf_op jit(solution)/shard_map/ppermute | solution.py:29
  38.9 0.4 shard_map.69.before_ref
  39.4 6.1 %collective-permute-done.13.from_xy_ref = bf16[24,256]{1,0:T(8,128)(2,1)S(1)} collective-permute-done((bf16[24,256]{1,0:T(8,128)(2,1)S(1)}, bf16[24,256]{1,0:T(8,128)(2,1)S(1)}, u32[]{:S(2)}, u32[]{:S(2)}) %collective-permute-start.13) | collective-permute-done | bytes 12320 | tf_op jit(solution)/shard_map/ppermute | solution.py:29
  45.6 1.6 %collective-permute-start.14 = (bf16[176,256]{1,0:T(8,128)(2,1)S(1)}, bf16[176,256]{1,0:T(8,128)(2,1)S(1)}, u32[]{:S(2)}, u32[]{:S(2)}) collective-permute-start(bf16[176,256]{1,0:T(8,128)(2,1)S(1)} %get-tuple-element.64), channel_id=1, source_target_pairs={{0,1},{1,0},{2,3},{3,2},{4,5},{5,4},{6,7},{7,6},{8,9},{9,8},{10,11... | collective-permute-start | bytes 270344 | tf_op jit(solution)/shard_map/ppermute | solution.py:29
  47.2 3.0 %collective-permute-done.14.refs_0_ = bf16[176,256]{1,0:T(8,128)(2,1)S(1)} collective-permute-done((bf16[176,256]{1,0:T(8,128)(2,1)S(1)}, bf16[176,256]{1,0:T(8,128)(2,1)S(1)}, u32[]{:S(2)}, u32[]{:S(2)}) %collective-permute-start.14) | collective-permute-done | bytes 90144 | tf_op jit(solution)/shard_map/ppermute | solution.py:29
  50.2 1.7 %shard_map.71 = f32[12,12,12,256]{3,2,1,0:T(8,128)} custom-call(f32[12,12,12,256]{3,2,1,0:T(8,128)S(1)} %copy-done, f32[12,12,16,256]{3,2,1,0:T(8,128)S(1)} %get-tuple-element.62.block_ref, f32[16,256]{1,0:T(8,128)S(1)} %get-tuple-element.63.total_ref, bf16[12,192,48]{2,1,0:T(8,128)(2,1)S(1)} %get-tuple-element.49.by_node_ref, ...), custom_call_target="tpu_custom_call" | custom-call | tf_op jit(solution)/shard_map/pallas_call | solution.py:102
  (25 shorter events, 2.7 us)
Async XLA Ops:
  2.5 5.6 %collective-permute-start = (bf16[176,256]{1,0:T(8,128)(2,1)S(1)}, bf16[176,256]{1,0:T(8,128)(2,1)S(1)}, u32[]{:S(2)}, u32[]{:S(2)}) collective-permute-start(bf16[176,256]{1,0:T(8,128)(2,1)S(1)} %get-tuple-element.37), channel_id=1, source_target_pairs={{0,1},{1,0},{2,3},{3,2},{4,5},{5,4},{6,7},{7,6},{8,9},{9,8},{10,11... | collective-permute-start | bytes 270344 | tf_op jit(solution)/shard_map/ppermute | solution.py:29
  8.2 7.9 %collective-permute-start.1 = (bf16[168,256]{1,0:T(8,128)(2,1)S(1)}, bf16[168,256]{1,0:T(8,128)(2,1)S(1)}, u32[]{:S(2)}, u32[]{:S(2)}) collective-permute-start(bf16[168,256]{1,0:T(8,128)(2,1)S(1)} %get-tuple-element.39), channel_id=1, source_target_pairs={{0,24},{1,25},{2,26},{3,27},{4,28},{5,29},{6,30},{7,31},{8,0},{9,1... | collective-permute-start | bytes 258056 | tf_op jit(solution)/shard_map/ppermute | solution.py:29
  8.8 7.3 %collective-permute-start.2 = (bf16[168,256]{1,0:T(8,128)(2,1)S(1)}, bf16[168,256]{1,0:T(8,128)(2,1)S(1)}, u32[]{:S(2)}, u32[]{:S(2)}) collective-permute-start(bf16[168,256]{1,0:T(8,128)(2,1)S(1)} %get-tuple-element.40), channel_id=1, source_target_pairs={{0,6},{1,7},{2,0},{3,1},{4,2},{5,3},{6,4},{7,5},{8,14},{9,15},{10,... | collective-permute-start | bytes 258056 | tf_op jit(solution)/shard_map/ppermute | solution.py:29
  12.4 3.7 %collective-permute-start.3 = (bf16[24,256]{1,0:T(8,128)(2,1)S(1)}, bf16[24,256]{1,0:T(8,128)(2,1)S(1)}, u32[]{:S(2)}, u32[]{:S(2)}) collective-permute-start(bf16[24,256]{1,0:T(8,128)(2,1)S(1)} %get-tuple-element.41), channel_id=1, source_target_pairs={{0,30},{1,31},{2,24},{3,25},{4,26},{5,27},{6,28},{7,29},{8,6},{9,7... | collective-permute-start | bytes 36872 | tf_op jit(solution)/shard_map/ppermute | solution.py:29
  17.3 7.6 %collective-permute-start.4 = (bf16[168,256]{1,0:T(8,128)(2,1)S(1)}, bf16[168,256]{1,0:T(8,128)(2,1)S(1)}, u32[]{:S(2)}, u32[]{:S(2)}) collective-permute-start(bf16[168,256]{1,0:T(8,128)(2,1)S(1)} %get-tuple-element.44), channel_id=1, source_target_pairs={{0,8},{1,9},{2,10},{3,11},{4,12},{5,13},{6,14},{7,15},{8,16},{9,17... | collective-permute-start | bytes 258056 | tf_op jit(solution)/shard_map/ppermute | solution.py:29
  17.8 7.1 %collective-permute-start.5 = (bf16[168,256]{1,0:T(8,128)(2,1)S(1)}, bf16[168,256]{1,0:T(8,128)(2,1)S(1)}, u32[]{:S(2)}, u32[]{:S(2)}) collective-permute-start(bf16[168,256]{1,0:T(8,128)(2,1)S(1)} %get-tuple-element.45), channel_id=1, source_target_pairs={{0,2},{1,3},{2,4},{3,5},{4,6},{5,7},{6,0},{7,1},{8,10},{9,11},{10,... | collective-permute-start | bytes 258056 | tf_op jit(solution)/shard_map/ppermute | solution.py:29
  19.0 5.9 %collective-permute-start.6 = (bf16[24,256]{1,0:T(8,128)(2,1)S(1)}, bf16[24,256]{1,0:T(8,128)(2,1)S(1)}, u32[]{:S(2)}, u32[]{:S(2)}) collective-permute-start(bf16[24,256]{1,0:T(8,128)(2,1)S(1)} %get-tuple-element.46), channel_id=1, source_target_pairs={{0,10},{1,11},{2,12},{3,13},{4,14},{5,15},{6,8},{7,9},{8,18},{9,19... | collective-permute-start | bytes 36872 | tf_op jit(solution)/shard_map/ppermute | solution.py:29
  25.1 5.9 %collective-permute-start.7 = (bf16[288,256]{1,0:T(8,128)(2,1)S(1)}, bf16[288,256]{1,0:T(8,128)(2,1)S(1)}, u32[]{:S(2)}, u32[]{:S(2)}) collective-permute-start(bf16[288,256]{1,0:T(8,128)(2,1)S(1)} %shard_map.65), channel_id=1, source_target_pairs={{0,1},{1,0},{2,3},{3,2},{4,5},{5,4},{6,7},{7,6},{8,9},{9,8},{10,11... | collective-permute-start | bytes 442376 | tf_op jit(solution)/shard_map/ppermute | solution.py:29
  31.3 5.1 %collective-permute-start.8 = (bf16[168,256]{1,0:T(8,128)(2,1)S(1)}, bf16[168,256]{1,0:T(8,128)(2,1)S(1)}, u32[]{:S(2)}, u32[]{:S(2)}) collective-permute-start(bf16[168,256]{1,0:T(8,128)(2,1)S(1)} %get-tuple-element.54), channel_id=1, source_target_pairs={{0,24},{1,25},{2,26},{3,27},{4,28},{5,29},{6,30},{7,31},{8,0},{9,1... | collective-permute-start | bytes 258056 | tf_op jit(solution)/shard_map/ppermute | solution.py:29
  31.3 5.1 %collective-permute-start.9 = (bf16[168,256]{1,0:T(8,128)(2,1)S(1)}, bf16[168,256]{1,0:T(8,128)(2,1)S(1)}, u32[]{:S(2)}, u32[]{:S(2)}) collective-permute-start(bf16[168,256]{1,0:T(8,128)(2,1)S(1)} %get-tuple-element.55), channel_id=1, source_target_pairs={{0,6},{1,7},{2,0},{3,1},{4,2},{5,3},{6,4},{7,5},{8,14},{9,15},{10,... | collective-permute-start | bytes 258056 | tf_op jit(solution)/shard_map/ppermute | solution.py:29
  33.1 3.3 %collective-permute-start.10 = (bf16[24,256]{1,0:T(8,128)(2,1)S(1)}, bf16[24,256]{1,0:T(8,128)(2,1)S(1)}, u32[]{:S(2)}, u32[]{:S(2)}) collective-permute-start(bf16[24,256]{1,0:T(8,128)(2,1)S(1)} %get-tuple-element.56), channel_id=1, source_target_pairs={{0,30},{1,31},{2,24},{3,25},{4,26},{5,27},{6,28},{7,29},{8,6},{9,7... | collective-permute-start | bytes 36872 | tf_op jit(solution)/shard_map/ppermute | solution.py:29
  37.6 7.9 %collective-permute-start.11 = (bf16[168,256]{1,0:T(8,128)(2,1)S(1)}, bf16[168,256]{1,0:T(8,128)(2,1)S(1)}, u32[]{:S(2)}, u32[]{:S(2)}) collective-permute-start(bf16[168,256]{1,0:T(8,128)(2,1)S(1)} %get-tuple-element.58), channel_id=1, source_target_pairs={{0,8},{1,9},{2,10},{3,11},{4,12},{5,13},{6,14},{7,15},{8,16},{9,17... | collective-permute-start | bytes 258056 | tf_op jit(solution)/shard_map/ppermute | solution.py:29
  38.6 6.9 %collective-permute-start.12 = (bf16[168,256]{1,0:T(8,128)(2,1)S(1)}, bf16[168,256]{1,0:T(8,128)(2,1)S(1)}, u32[]{:S(2)}, u32[]{:S(2)}) collective-permute-start(bf16[168,256]{1,0:T(8,128)(2,1)S(1)} %get-tuple-element.59), channel_id=1, source_target_pairs={{0,2},{1,3},{2,4},{3,5},{4,6},{5,7},{6,0},{7,1},{8,10},{9,11},{10,... | collective-permute-start | bytes 258056 | tf_op jit(solution)/shard_map/ppermute | solution.py:29
  38.8 6.6 %collective-permute-start.13 = (bf16[24,256]{1,0:T(8,128)(2,1)S(1)}, bf16[24,256]{1,0:T(8,128)(2,1)S(1)}, u32[]{:S(2)}, u32[]{:S(2)}) collective-permute-start(bf16[24,256]{1,0:T(8,128)(2,1)S(1)} %get-tuple-element.60), channel_id=1, source_target_pairs={{0,10},{1,11},{2,12},{3,13},{4,14},{5,15},{6,8},{7,9},{8,18},{9,19... | collective-permute-start | bytes 36872 | tf_op jit(solution)/shard_map/ppermute | solution.py:29
  39.4 10.9 %copy-start = (f32[12,12,12,256]{3,2,1,0:T(8,128)S(1)}, f32[12,12,12,256]{3,2,1,0:T(8,128)}, u32[]{:S(2)}) copy-start(f32[12,12,12,256]{3,2,1,0:T(8,128)} %start_ref.1) | copy-start | bytes 5308420
  45.6 4.6 %collective-permute-start.14 = (bf16[176,256]{1,0:T(8,128)(2,1)S(1)}, bf16[176,256]{1,0:T(8,128)(2,1)S(1)}, u32[]{:S(2)}, u32[]{:S(2)}) collective-permute-start(bf16[176,256]{1,0:T(8,128)(2,1)S(1)} %get-tuple-element.64), channel_id=1, source_target_pairs={{0,1},{1,0},{2,3},{3,2},{4,5},{5,4},{6,7},{7,6},{8,9},{9,8},{10,11... | collective-permute-start | bytes 270344 | tf_op jit(solution)/shard_map/ppermute | solution.py:29

commit v10 on v9

--- a/solution.py
+++ b/solution.py
@@ -202,7 +202,7 @@
     for x in range(s.bx):
         wide = wide_ref[x * s.by : (x + 1) * s.by].reshape(s.by * s.bzp, 2 * s.locals)
         by_atom_ref[x] = wide.T.astype(BF16)
-    total = jnp.zeros((s.locals, s.waves), F32)
+    sums = []
     atoms = lax.broadcasted_iota(jnp.int32, (s.locals, coupling_ref.shape[1]), 1)
     weight = jnp.sum(jnp.where(atoms == local_atoms(s.own, atoms.shape), coupling_ref[...], 0.0), axis=1, keepdims=True)
     weight_ref[...] = jnp.broadcast_to(weight, weight_ref.shape)
@@ -212,7 +212,8 @@
     for x in range(s.bx):
         plane = jnp.concatenate([start_ref[x], jnp.zeros((s.by, s.bzp - s.bz, s.waves), F32)], axis=1)
         field_ref[x, 0 : s.by] = plane
-        total = total + split_sums(by_atom_ref[x], s.locals, plane.reshape(s.by * s.bzp, s.waves))
+        sums.append(split_sums(by_atom_ref[x], s.locals, plane.reshape(s.by * s.bzp, s.waves)))
+    total = sum(sums[1:], sums[0])
     total_ref[...] = total
     half = 4 * s.own
     for x in range(s.bx):

time: 52.1 us -> 52.1 us (level)
  no operation moved by 1% of the time
where the time goes in v10:
time: 52.1 us; the launch traced here: 52 us
  waiting for transfers between devices  20.6 us (40%)
  starting transfers between devices  16.7 us (32%)
  Pallas kernels  14.5 us (28%)
    ppermute x15, waiting for transfers between devices, shifted(): return lax.ppermute(value, AXES, pairs)  20.6 us
    ppermute x15, starting transfers between devices, shifted(): return lax.ppermute(value, AXES, pairs)  16.7 us
    pallas_call x17, Pallas kernels, call(): pl.pallas_call(functools.partial(body, sizes, *extra), out_shape=outs, in...  14.5 us
  transfers between devices with their start and end apart: 15, of which 6 were waited for; matrix products, arithmetic and copies ran while one was open for 0% of the time, Pallas kernels for 14%

profile of v10, /device:TPU:0, one launch (start us, length us, event | category | flops | bytes accessed | tf_op | source)
XLA Modules:
  0.0 52.0 jit_solution(11414931752595722923)
XLA Ops:
  0.0 2.5 %shard_map.55 = (f32[13,13,16,256]{3,2,1,0:T(8,128)S(1)}, bf16[12,32,192]{2,1,0:T(8,128)(2,1)S(1)}, f32[144,16,32]{2,1,0:T(8,128)S(1)}, bf16[176,256]{1,0:T(8,12...) custom-call(f32[12,12,12,256]{3,2,1,0:T(8,128)} %start_ref.1, f32[1,16,1728]{2,1,0:T(8,128)} %rows_hbm.1, ...), custom_call_target="tpu_custom_call" | custom-call | tf_op jit(solution)/shard_map/pallas_call | solution.py:102
  2.5 3.0 %collective-permute-start = (bf16[176,256]{1,0:T(8,128)(2,1)S(1)}, bf16[176,256]{1,0:T(8,128)(2,1)S(1)}, u32[]{:S(2)}, u32[]{:S(2)}) collective-permute-start(bf16[176,256]{1,0:T(8,128)(2,1)S(1)} %get-tuple-element.37), channel_id=1, source_target_pairs={{0,1},{1,0},{2,3},{3,2},{4,5},{5,4},{6,7},{7,6},{8,9},{9,8},{10,11... | collective-permute-start | bytes 270344 | tf_op jit(solution)/shard_map/ppermute | solution.py:29
  5.5 2.4 %shard_map.56.early_ref.refs_0_ = bf16[2,2,400,400]{3,2,1,0:T(8,128)(2,1)S(1)} custom-call(bf16[2,2,343,2,343]{4,3,2,1,0:T(2,128)(2,1)} %bitcast.2), custom_call_target="tpu_custom_call" | custom-call | tf_op jit(solution)/shard_map/pallas_call | solution.py:102
  8.2 0.6 %collective-permute-start.1 = (bf16[168,256]{1,0:T(8,128)(2,1)S(1)}, bf16[168,256]{1,0:T(8,128)(2,1)S(1)}, u32[]{:S(2)}, u32[]{:S(2)}) collective-permute-start(bf16[168,256]{1,0:T(8,128)(2,1)S(1)} %get-tuple-element.39), channel_id=1, source_target_pairs={{0,24},{1,25},{2,26},{3,27},{4,28},{5,29},{6,30},{7,31},{8,0},{9,1... | collective-permute-start | bytes 258056 | tf_op jit(solution)/shard_map/ppermute | solution.py:29
  8.8 3.6 %collective-permute-start.2 = (bf16[168,256]{1,0:T(8,128)(2,1)S(1)}, bf16[168,256]{1,0:T(8,128)(2,1)S(1)}, u32[]{:S(2)}, u32[]{:S(2)}) collective-permute-start(bf16[168,256]{1,0:T(8,128)(2,1)S(1)} %get-tuple-element.40), channel_id=1, source_target_pairs={{0,6},{1,7},{2,0},{3,1},{4,2},{5,3},{6,4},{7,5},{8,14},{9,15},{10,... | collective-permute-start | bytes 258056 | tf_op jit(solution)/shard_map/ppermute | solution.py:29
  12.4 1.1 %collective-permute-start.3 = (bf16[24,256]{1,0:T(8,128)(2,1)S(1)}, bf16[24,256]{1,0:T(8,128)(2,1)S(1)}, u32[]{:S(2)}, u32[]{:S(2)}) collective-permute-start(bf16[24,256]{1,0:T(8,128)(2,1)S(1)} %get-tuple-element.41), channel_id=1, source_target_pairs={{0,30},{1,31},{2,24},{3,25},{4,26},{5,27},{6,28},{7,29},{8,6},{9,7... | collective-permute-start | bytes 36872 | tf_op jit(solution)/shard_map/ppermute | solution.py:29
  13.5 2.4 %shard_map.59.refs_1_ = bf16[2,2,400,400]{3,2,1,0:T(8,128)(2,1)S(1)} custom-call(bf16[2,2,343,2,343]{4,3,2,1,0:T(2,128)(2,1)} %bitcast.3), custom_call_target="tpu_custom_call" | custom-call | tf_op jit(solution)/shard_map/pallas_call | solution.py:102
  16.1 1.2 %shard_map.60 = (f32[13,13,16,256]{3,2,1,0:T(8,128)S(1)}, f32[2,13,13,8,256]{4,3,2,1,0:T(8,128)S(1)}, bf16[168,256]{1,0:T(8,128)(2,1)S(1)}, bf16[168,256]{1,0:T(...) custom-call(f32[13,13,16,256]{3,2,1,0:T(8,128)S(1)} %shard_map.58.before_ref, ...), custom_call_target="tpu_custom_call", output_to_operand_aliasing={{0}: (0, {})} | custom-call | tf_op jit(solution)/shard_map/pallas_call | solution.py:102
  17.3 0.5 %collective-permute-start.4 = (bf16[168,256]{1,0:T(8,128)(2,1)S(1)}, bf16[168,256]{1,0:T(8,128)(2,1)S(1)}, u32[]{:S(2)}, u32[]{:S(2)}) collective-permute-start(bf16[168,256]{1,0:T(8,128)(2,1)S(1)} %get-tuple-element.44), channel_id=1, source_target_pairs={{0,8},{1,9},{2,10},{3,11},{4,12},{5,13},{6,14},{7,15},{8,16},{9,17... | collective-permute-start | bytes 258056 | tf_op jit(solution)/shard_map/ppermute | solution.py:29
  17.8 1.2 %collective-permute-start.5 = (bf16[168,256]{1,0:T(8,128)(2,1)S(1)}, bf16[168,256]{1,0:T(8,128)(2,1)S(1)}, u32[]{:S(2)}, u32[]{:S(2)}) collective-permute-start(bf16[168,256]{1,0:T(8,128)(2,1)S(1)} %get-tuple-element.45), channel_id=1, source_target_pairs={{0,2},{1,3},{2,4},{3,5},{4,6},{5,7},{6,0},{7,1},{8,10},{9,11},{10,... | collective-permute-start | bytes 258056 | tf_op jit(solution)/shard_map/ppermute | solution.py:29
  19.9 5.0 %collective-permute-done.6.from_xy_ref = bf16[24,256]{1,0:T(8,128)(2,1)S(1)} collective-permute-done((bf16[24,256]{1,0:T(8,128)(2,1)S(1)}, bf16[24,256]{1,0:T(8,128)(2,1)S(1)}, u32[]{:S(2)}, u32[]{:S(2)}) %collective-permute-start.6) | collective-permute-done | bytes 12320 | tf_op jit(solution)/shard_map/ppermute | solution.py:29
  25.1 1.6 %collective-permute-start.7 = (bf16[288,256]{1,0:T(8,128)(2,1)S(1)}, bf16[288,256]{1,0:T(8,128)(2,1)S(1)}, u32[]{:S(2)}, u32[]{:S(2)}) collective-permute-start(bf16[288,256]{1,0:T(8,128)(2,1)S(1)} %shard_map.65), channel_id=1, source_target_pairs={{0,1},{1,0},{2,3},{3,2},{4,5},{5,4},{6,7},{7,6},{8,9},{9,8},{10,11... | collective-permute-start | bytes 442376 | tf_op jit(solution)/shard_map/ppermute | solution.py:29
  26.7 0.5 shard_map.63.field_ref.before_ref
  27.2 0.5 shard_map.64.total_ref
  27.6 3.4 %collective-permute-done.7.refs_0_ = bf16[288,256]{1,0:T(8,128)(2,1)S(1)} collective-permute-done((bf16[288,256]{1,0:T(8,128)(2,1)S(1)}, bf16[288,256]{1,0:T(8,128)(2,1)S(1)}, u32[]{:S(2)}, u32[]{:S(2)}) %collective-permute-start.7) | collective-permute-done | bytes 147488 | tf_op jit(solution)/shard_map/ppermute | solution.py:29
  31.3 1.8 %collective-permute-start.9 = (bf16[168,256]{1,0:T(8,128)(2,1)S(1)}, bf16[168,256]{1,0:T(8,128)(2,1)S(1)}, u32[]{:S(2)}, u32[]{:S(2)}) collective-permute-start(bf16[168,256]{1,0:T(8,128)(2,1)S(1)} %get-tuple-element.55), channel_id=1, source_target_pairs={{0,6},{1,7},{2,0},{3,1},{4,2},{5,3},{6,4},{7,5},{8,14},{9,15},{10,... | collective-permute-start | bytes 258056 | tf_op jit(solution)/shard_map/ppermute | solution.py:29
  33.5 2.9 %collective-permute-done.10.from_xy_ref = bf16[24,256]{1,0:T(8,128)(2,1)S(1)} collective-permute-done((bf16[24,256]{1,0:T(8,128)(2,1)S(1)}, bf16[24,256]{1,0:T(8,128)(2,1)S(1)}, u32[]{:S(2)}, u32[]{:S(2)}) %collective-permute-start.10) | collective-permute-done | bytes 12320 | tf_op jit(solution)/shard_map/ppermute | solution.py:29
  36.4 1.2 %shard_map.68 = (f32[13,13,16,256]{3,2,1,0:T(8,128)S(1)}, f32[2,13,13,8,256]{4,3,2,1,0:T(8,128)S(1)}, bf16[168,256]{1,0:T(8,128)(2,1)S(1)}, bf16[168,256]{1,0:T(...) custom-call(f32[13,13,16,256]{3,2,1,0:T(8,128)S(1)} %shard_map.67.before_ref, ...), custom_call_target="tpu_custom_call", output_to_operand_aliasing={{0}: (0, {})} | custom-call | tf_op jit(solution)/shard_map/pallas_call | solution.py:102
  37.6 1.0 %collective-permute-start.11 = (bf16[168,256]{1,0:T(8,128)(2,1)S(1)}, bf16[168,256]{1,0:T(8,128)(2,1)S(1)}, u32[]{:S(2)}, u32[]{:S(2)}) collective-permute-start(bf16[168,256]{1,0:T(8,128)(2,1)S(1)} %get-tuple-element.58), channel_id=1, source_target_pairs={{0,8},{1,9},{2,10},{3,11},{4,12},{5,13},{6,14},{7,15},{8,16},{9,17... | collective-permute-start | bytes 258056 | tf_op jit(solution)/shard_map/ppermute | solution.py:29
  38.9 0.4 shard_map.69.before_ref
  39.4 6.1 %collective-permute-done.13.from_xy_ref = bf16[24,256]{1,0:T(8,128)(2,1)S(1)} collective-permute-done((bf16[24,256]{1,0:T(8,128)(2,1)S(1)}, bf16[24,256]{1,0:T(8,128)(2,1)S(1)}, u32[]{:S(2)}, u32[]{:S(2)}) %collective-permute-start.13) | collective-permute-done | bytes 12320 | tf_op jit(solution)/shard_map/ppermute | solution.py:29
  45.6 1.6 %collective-permute-start.14 = (bf16[176,256]{1,0:T(8,128)(2,1)S(1)}, bf16[176,256]{1,0:T(8,128)(2,1)S(1)}, u32[]{:S(2)}, u32[]{:S(2)}) collective-permute-start(bf16[176,256]{1,0:T(8,128)(2,1)S(1)} %get-tuple-element.64), channel_id=1, source_target_pairs={{0,1},{1,0},{2,3},{3,2},{4,5},{5,4},{6,7},{7,6},{8,9},{9,8},{10,11... | collective-permute-start | bytes 270344 | tf_op jit(solution)/shard_map/ppermute | solution.py:29
  47.2 3.0 %collective-permute-done.14.refs_0_ = bf16[176,256]{1,0:T(8,128)(2,1)S(1)} collective-permute-done((bf16[176,256]{1,0:T(8,128)(2,1)S(1)}, bf16[176,256]{1,0:T(8,128)(2,1)S(1)}, u32[]{:S(2)}, u32[]{:S(2)}) %collective-permute-start.14) | collective-permute-done | bytes 90144 | tf_op jit(solution)/shard_map/ppermute | solution.py:29
  50.2 1.7 %shard_map.71 = f32[12,12,12,256]{3,2,1,0:T(8,128)} custom-call(f32[12,12,12,256]{3,2,1,0:T(8,128)S(1)} %copy-done, f32[12,12,16,256]{3,2,1,0:T(8,128)S(1)} %get-tuple-element.62.block_ref, f32[16,256]{1,0:T(8,128)S(1)} %get-tuple-element.63.total_ref, bf16[12,192,48]{2,1,0:T(8,128)(2,1)S(1)} %get-tuple-element.49.by_node_ref, ...), custom_call_target="tpu_custom_call" | custom-call | tf_op jit(solution)/shard_map/pallas_call | solution.py:102
  (25 shorter events, 2.7 us)
Async XLA Ops:
  2.5 5.6 %collective-permute-start = (bf16[176,256]{1,0:T(8,128)(2,1)S(1)}, bf16[176,256]{1,0:T(8,128)(2,1)S(1)}, u32[]{:S(2)}, u32[]{:S(2)}) collective-permute-start(bf16[176,256]{1,0:T(8,128)(2,1)S(1)} %get-tuple-element.37), channel_id=1, source_target_pairs={{0,1},{1,0},{2,3},{3,2},{4,5},{5,4},{6,7},{7,6},{8,9},{9,8},{10,11... | collective-permute-start | bytes 270344 | tf_op jit(solution)/shard_map/ppermute | solution.py:29
  8.2 7.9 %collective-permute-start.1 = (bf16[168,256]{1,0:T(8,128)(2,1)S(1)}, bf16[168,256]{1,0:T(8,128)(2,1)S(1)}, u32[]{:S(2)}, u32[]{:S(2)}) collective-permute-start(bf16[168,256]{1,0:T(8,128)(2,1)S(1)} %get-tuple-element.39), channel_id=1, source_target_pairs={{0,24},{1,25},{2,26},{3,27},{4,28},{5,29},{6,30},{7,31},{8,0},{9,1... | collective-permute-start | bytes 258056 | tf_op jit(solution)/shard_map/ppermute | solution.py:29
  8.8 7.3 %collective-permute-start.2 = (bf16[168,256]{1,0:T(8,128)(2,1)S(1)}, bf16[168,256]{1,0:T(8,128)(2,1)S(1)}, u32[]{:S(2)}, u32[]{:S(2)}) collective-permute-start(bf16[168,256]{1,0:T(8,128)(2,1)S(1)} %get-tuple-element.40), channel_id=1, source_target_pairs={{0,6},{1,7},{2,0},{3,1},{4,2},{5,3},{6,4},{7,5},{8,14},{9,15},{10,... | collective-permute-start | bytes 258056 | tf_op jit(solution)/shard_map/ppermute | solution.py:29
  12.4 3.7 %collective-permute-start.3 = (bf16[24,256]{1,0:T(8,128)(2,1)S(1)}, bf16[24,256]{1,0:T(8,128)(2,1)S(1)}, u32[]{:S(2)}, u32[]{:S(2)}) collective-permute-start(bf16[24,256]{1,0:T(8,128)(2,1)S(1)} %get-tuple-element.41), channel_id=1, source_target_pairs={{0,30},{1,31},{2,24},{3,25},{4,26},{5,27},{6,28},{7,29},{8,6},{9,7... | collective-permute-start | bytes 36872 | tf_op jit(solution)/shard_map/ppermute | solution.py:29
  17.3 7.6 %collective-permute-start.4 = (bf16[168,256]{1,0:T(8,128)(2,1)S(1)}, bf16[168,256]{1,0:T(8,128)(2,1)S(1)}, u32[]{:S(2)}, u32[]{:S(2)}) collective-permute-start(bf16[168,256]{1,0:T(8,128)(2,1)S(1)} %get-tuple-element.44), channel_id=1, source_target_pairs={{0,8},{1,9},{2,10},{3,11},{4,12},{5,13},{6,14},{7,15},{8,16},{9,17... | collective-permute-start | bytes 258056 | tf_op jit(solution)/shard_map/ppermute | solution.py:29
  17.8 7.1 %collective-permute-start.5 = (bf16[168,256]{1,0:T(8,128)(2,1)S(1)}, bf16[168,256]{1,0:T(8,128)(2,1)S(1)}, u32[]{:S(2)}, u32[]{:S(2)}) collective-permute-start(bf16[168,256]{1,0:T(8,128)(2,1)S(1)} %get-tuple-element.45), channel_id=1, source_target_pairs={{0,2},{1,3},{2,4},{3,5},{4,6},{5,7},{6,0},{7,1},{8,10},{9,11},{10,... | collective-permute-start | bytes 258056 | tf_op jit(solution)/shard_map/ppermute | solution.py:29
  19.0 5.9 %collective-permute-start.6 = (bf16[24,256]{1,0:T(8,128)(2,1)S(1)}, bf16[24,256]{1,0:T(8,128)(2,1)S(1)}, u32[]{:S(2)}, u32[]{:S(2)}) collective-permute-start(bf16[24,256]{1,0:T(8,128)(2,1)S(1)} %get-tuple-element.46), channel_id=1, source_target_pairs={{0,10},{1,11},{2,12},{3,13},{4,14},{5,15},{6,8},{7,9},{8,18},{9,19... | collective-permute-start | bytes 36872 | tf_op jit(solution)/shard_map/ppermute | solution.py:29
  25.1 5.9 %collective-permute-start.7 = (bf16[288,256]{1,0:T(8,128)(2,1)S(1)}, bf16[288,256]{1,0:T(8,128)(2,1)S(1)}, u32[]{:S(2)}, u32[]{:S(2)}) collective-permute-start(bf16[288,256]{1,0:T(8,128)(2,1)S(1)} %shard_map.65), channel_id=1, source_target_pairs={{0,1},{1,0},{2,3},{3,2},{4,5},{5,4},{6,7},{7,6},{8,9},{9,8},{10,11... | collective-permute-start | bytes 442376 | tf_op jit(solution)/shard_map/ppermute | solution.py:29
  31.3 5.1 %collective-permute-start.8 = (bf16[168,256]{1,0:T(8,128)(2,1)S(1)}, bf16[168,256]{1,0:T(8,128)(2,1)S(1)}, u32[]{:S(2)}, u32[]{:S(2)}) collective-permute-start(bf16[168,256]{1,0:T(8,128)(2,1)S(1)} %get-tuple-element.54), channel_id=1, source_target_pairs={{0,24},{1,25},{2,26},{3,27},{4,28},{5,29},{6,30},{7,31},{8,0},{9,1... | collective-permute-start | bytes 258056 | tf_op jit(solution)/shard_map/ppermute | solution.py:29
  31.3 5.1 %collective-permute-start.9 = (bf16[168,256]{1,0:T(8,128)(2,1)S(1)}, bf16[168,256]{1,0:T(8,128)(2,1)S(1)}, u32[]{:S(2)}, u32[]{:S(2)}) collective-permute-start(bf16[168,256]{1,0:T(8,128)(2,1)S(1)} %get-tuple-element.55), channel_id=1, source_target_pairs={{0,6},{1,7},{2,0},{3,1},{4,2},{5,3},{6,4},{7,5},{8,14},{9,15},{10,... | collective-permute-start | bytes 258056 | tf_op jit(solution)/shard_map/ppermute | solution.py:29
  33.1 3.3 %collective-permute-start.10 = (bf16[24,256]{1,0:T(8,128)(2,1)S(1)}, bf16[24,256]{1,0:T(8,128)(2,1)S(1)}, u32[]{:S(2)}, u32[]{:S(2)}) collective-permute-start(bf16[24,256]{1,0:T(8,128)(2,1)S(1)} %get-tuple-element.56), channel_id=1, source_target_pairs={{0,30},{1,31},{2,24},{3,25},{4,26},{5,27},{6,28},{7,29},{8,6},{9,7... | collective-permute-start | bytes 36872 | tf_op jit(solution)/shard_map/ppermute | solution.py:29
  37.6 7.9 %collective-permute-start.11 = (bf16[168,256]{1,0:T(8,128)(2,1)S(1)}, bf16[168,256]{1,0:T(8,128)(2,1)S(1)}, u32[]{:S(2)}, u32[]{:S(2)}) collective-permute-start(bf16[168,256]{1,0:T(8,128)(2,1)S(1)} %get-tuple-element.58), channel_id=1, source_target_pairs={{0,8},{1,9},{2,10},{3,11},{4,12},{5,13},{6,14},{7,15},{8,16},{9,17... | collective-permute-start | bytes 258056 | tf_op jit(solution)/shard_map/ppermute | solution.py:29
  38.6 6.9 %collective-permute-start.12 = (bf16[168,256]{1,0:T(8,128)(2,1)S(1)}, bf16[168,256]{1,0:T(8,128)(2,1)S(1)}, u32[]{:S(2)}, u32[]{:S(2)}) collective-permute-start(bf16[168,256]{1,0:T(8,128)(2,1)S(1)} %get-tuple-element.59), channel_id=1, source_target_pairs={{0,2},{1,3},{2,4},{3,5},{4,6},{5,7},{6,0},{7,1},{8,10},{9,11},{10,... | collective-permute-start | bytes 258056 | tf_op jit(solution)/shard_map/ppermute | solution.py:29
  38.8 6.6 %collective-permute-start.13 = (bf16[24,256]{1,0:T(8,128)(2,1)S(1)}, bf16[24,256]{1,0:T(8,128)(2,1)S(1)}, u32[]{:S(2)}, u32[]{:S(2)}) collective-permute-start(bf16[24,256]{1,0:T(8,128)(2,1)S(1)} %get-tuple-element.60), channel_id=1, source_target_pairs={{0,10},{1,11},{2,12},{3,13},{4,14},{5,15},{6,8},{7,9},{8,18},{9,19... | collective-permute-start | bytes 36872 | tf_op jit(solution)/shard_map/ppermute | solution.py:29
  39.4 10.9 %copy-start = (f32[12,12,12,256]{3,2,1,0:T(8,128)S(1)}, f32[12,12,12,256]{3,2,1,0:T(8,128)}, u32[]{:S(2)}) copy-start(f32[12,12,12,256]{3,2,1,0:T(8,128)} %start_ref.1) | copy-start | bytes 5308420
  45.6 4.6 %collective-permute-start.14 = (bf16[176,256]{1,0:T(8,128)(2,1)S(1)}, bf16[176,256]{1,0:T(8,128)(2,1)S(1)}, u32[]{:S(2)}, u32[]{:S(2)}) collective-permute-start(bf16[176,256]{1,0:T(8,128)(2,1)S(1)} %get-tuple-element.64), channel_id=1, source_target_pairs={{0,1},{1,0},{2,3},{3,2},{4,5},{5,4},{6,7},{7,6},{8,9},{9,8},{10,11... | collective-permute-start | bytes 270344 | tf_op jit(solution)/shard_map/ppermute | solution.py:29
